TPU v7x, 32 devices: a whole 2x2x4 slice. The times are simulated.
32 devices in a mesh: gx: 4 (over y, x), gz: 8 (over z, core).
Axes of the slice: x: 2, y: 2, z: 4, core: 2. Of those that a mesh axis runs over, the one named last changes fastest.
Arguments:
- source: float32 [64, 16, 1024], P('gx', None, 'gz'), may hold values from -14 to 14
- previous: float32 [64, 16, 1024], P('gx', None, 'gz'), may hold values from -6 to 6
- coefficients: float32 [3, 8, 2, 128], P(None, 'gx', None, 'gz'), may hold values from 0.3 to 3
- stiffness: float32 [8, 8], replicated, may hold values from -0.2 to 2.5, as said below
- fdm_vectors: float32 [8, 8], replicated, may hold values from -0.1 to 1.2
- fdm_values: float32 [8], replicated, may hold values from 0.1 to 10
- coarse_inverse: float32 [64, 64], P(('gx', 'gz')), may hold values from -0.004 to 0.008, as said below
- vertex_map: int32 [8, 8, 2, 128], P(None, 'gx', None, 'gz'), may hold values from 0 to 63, as said below
Outputs:
- new_solution: float32 [64, 16, 1024], P('gx', None, 'gz')
- new_residual: float32 [64, 16, 1024], P('gx', None, 'gz')
Inputs may be any that keep to these rules, and one draw needn't show every extreme that they name: stiffness is symmetric. coarse_inverse is symmetric. `vertex_map`: corners of elements that meet at one grid vertex carry the same number; each number labels the vertices of one aligned block of 2 x 3 x 8 grid vertices along the three dimensions; every number occurs.
All inputs are finite; a program needn't handle non-finite values.
Results may differ from a plain program's by a relative error of at most 0.00012.
Values sent between devices are 32-bit elements; how exact they have to be, the bound alone decides.
No kernel may reach another device: no remote copies, remote signals or barrier semaphores. Data moves between devices by JAX's collectives and lax.ppermute only.
A program may use at most 64 MiB of HBM per device.

v0:
```python
import jax
import jax.numpy as jnp
from jax import lax
from jax.sharding import PartitionSpec as P

GLL_POINTS = [
    -1.0,
    -0.8717401485096066,
    -0.5917001814331423,
    -0.2092992179024789,
    0.2092992179024789,
    0.5917001814331423,
    0.8717401485096066,
    1.0,
]
GLL_WEIGHTS = [
    0.03571428571428571,
    0.21070422714350603,
    0.34112269248350435,
    0.4124587946587038,
    0.4124587946587038,
    0.34112269248350435,
    0.21070422714350603,
    0.03571428571428571,
]


def with_halo(cells, sides, width):
    for axis, dim in sides:
        count = lax.axis_size(axis)
        head = lax.slice_in_dim(cells, 0, width, axis=dim)
        tail = lax.slice_in_dim(cells, cells.shape[dim] - width, cells.shape[dim], axis=dim)
        cells = jnp.concatenate(
            [
                lax.ppermute(tail, axis, [(i, (i + 1) % count) for i in range(count)]),
                cells,
                lax.ppermute(head, axis, [((i + 1) % count, i) for i in range(count)]),
            ],
            axis=dim,
        )
    return cells


def node_weights(length):
    return jnp.tile(jnp.array(GLL_WEIGHTS, dtype=jnp.float32), length // 8)


def block_matrix(matrix, length):
    return jnp.kron(jnp.eye(length // 8, dtype=jnp.float32), matrix)


def contract_axis(values, matrix, axis_number):
    blocked = block_matrix(matrix, values.shape[axis_number])
    if axis_number == 0:
        return jnp.einsum("pyz,ip->iyz", values, blocked, precision=lax.Precision.HIGHEST)
    if axis_number == 1:
        return jnp.einsum("xpz,jp->xjz", values, blocked, precision=lax.Precision.HIGHEST)
    return jnp.einsum("xyp,kp->xyk", values, blocked, precision=lax.Precision.HIGHEST)


def combine_pairs(padded, axis_number):
    length = padded.shape[axis_number] - 2
    middle = lax.slice_in_dim(padded, 1, length + 1, axis=axis_number)
    upper = lax.slice_in_dim(padded, 2, length + 2, axis=axis_number)
    lower = lax.slice_in_dim(padded, 0, length, axis=axis_number)
    layout = [1, 1, 1]
    layout[axis_number] = length
    position = (jnp.arange(length) % 8).reshape(layout)
    return middle + jnp.where(position == 7, upper, 0.0) + jnp.where(position == 0, lower, 0.0)


def assemble(values):
    padded = with_halo(values, (("gx", 0),), 1)
    summed = combine_pairs(padded, 0)
    summed = combine_pairs(jnp.pad(summed, ((0, 0), (1, 1), (0, 0))), 1)
    padded = with_halo(summed, (("gz", 2),), 1)
    return combine_pairs(padded, 2)


def periodic_count(length):
    position = jnp.arange(length) % 8
    return jnp.where((position == 0) | (position == 7), 2.0, 1.0).astype(jnp.float32)


def copy_counts(rows_x, rows_y, spanwise_rows):
    row_index = jnp.arange(rows_y)
    along_y = jnp.where((row_index == 0) | (row_index == rows_y - 1), 1.0, periodic_count(rows_y))
    return (
        periodic_count(rows_x)[:, None, None]
        * along_y[None, :, None]
        * periodic_count(spanwise_rows)[None, None, :]
    )


def spread(layer):
    return jnp.repeat(jnp.repeat(jnp.repeat(layer, 8, axis=0), 8, axis=1), 8, axis=2)


def apply_operator(values, spreads, stiffness):
    weight_x = node_weights(values.shape[0])[:, None, None]
    weight_y = node_weights(values.shape[1])[None, :, None]
    weight_z = node_weights(values.shape[2])[None, None, :]
    result = spreads[0] * contract_axis(values, stiffness, 0) * weight_y * weight_z
    result = result + spreads[1] * contract_axis(values, stiffness, 1) * weight_x * weight_z
    return result + spreads[2] * contract_axis(values, stiffness, 2) * weight_x * weight_y


def local_solve(values, spreads, vectors, eigen):
    moved = contract_axis(values, vectors.T, 0)
    moved = contract_axis(moved, vectors.T, 1)
    moved = contract_axis(moved, vectors.T, 2)
    lam_x = jnp.tile(eigen, values.shape[0] // 8)[:, None, None]
    lam_y = jnp.tile(eigen, values.shape[1] // 8)[None, :, None]
    lam_z = jnp.tile(eigen, values.shape[2] // 8)[None, None, :]
    moved = moved / (spreads[0] * lam_x + spreads[1] * lam_y + spreads[2] * lam_z)
    moved = contract_axis(moved, vectors, 0)
    moved = contract_axis(moved, vectors, 1)
    return contract_axis(moved, vectors, 2)


def corner_matrix(length):
    points = jnp.array(GLL_POINTS, dtype=jnp.float32)
    basis = jnp.stack([(1.0 - points) / 2.0, (1.0 + points) / 2.0])
    return jnp.kron(jnp.eye(length // 8, dtype=jnp.float32), basis.T)


def restrict(weighted):
    rows_x, rows_y, spanwise_rows = weighted.shape
    reduced_value = jnp.einsum(
        "xyz,zc->xyc", weighted, corner_matrix(spanwise_rows), precision=lax.Precision.HIGHEST
    )
    reduced_value = jnp.einsum(
        "xyc,yb->xbc", reduced_value, corner_matrix(rows_y), precision=lax.Precision.HIGHEST
    )
    reduced_value = jnp.einsum(
        "xbc,xa->abc", reduced_value, corner_matrix(rows_x), precision=lax.Precision.HIGHEST
    )
    reduced_value = reduced_value.reshape(rows_x // 8, 2, rows_y // 8, 2, spanwise_rows // 8, 2)
    return reduced_value.transpose(1, 3, 5, 0, 2, 4).reshape(
        8, rows_x // 8, rows_y // 8, spanwise_rows // 8
    )


def prolong(corner_values, rows_x, rows_y, spanwise_rows):
    arranged = corner_values.reshape(2, 2, 2, rows_x // 8, rows_y // 8, spanwise_rows // 8)
    arranged = arranged.transpose(3, 0, 4, 1, 5, 2).reshape(
        rows_x // 4, rows_y // 4, spanwise_rows // 4
    )
    result = jnp.einsum(
        "abc,xa->xbc", arranged, corner_matrix(rows_x), precision=lax.Precision.HIGHEST
    )
    result = jnp.einsum(
        "xbc,yb->xyc", result, corner_matrix(rows_y), precision=lax.Precision.HIGHEST
    )
    return jnp.einsum(
        "xyc,zc->xyz", result, corner_matrix(spanwise_rows), precision=lax.Precision.HIGHEST
    )


def body(
    source, previous, coefficients, stiffness, fdm_vectors, fdm_values, coarse_inverse, vertex_map
):
    rows_x, rows_y, spanwise_rows = source.shape
    count_coarse = coarse_inverse.shape[1]
    copies = copy_counts(rows_x, rows_y, spanwise_rows)
    keep = (jnp.arange(rows_y) < rows_y - 1).astype(jnp.float32).reshape(1, rows_y, 1)
    spreads = [spread(coefficients[component]) for component in range(3)]
    start = keep * assemble(previous) / copies
    residual = keep * assemble(source - apply_operator(start, spreads, stiffness))
    corner_sums = restrict(residual / copies)
    partial_value = jax.ops.segment_sum(
        corner_sums.reshape(-1), vertex_map.reshape(-1), num_segments=count_coarse
    )
    coarse_rhs = lax.psum(partial_value, ("gx", "gz"))
    own_values = jnp.dot(coarse_inverse, coarse_rhs, precision=lax.Precision.HIGHEST)
    coarse_values = lax.all_gather(own_values, ("gx", "gz"), axis=0, tiled=True)
    local_part = local_solve(residual, spreads, fdm_vectors, fdm_values)
    coarse_part = prolong(coarse_values[vertex_map], rows_x, rows_y, spanwise_rows)
    precond = keep * (assemble(local_part) + coarse_part)
    numerator = lax.psum(jnp.sum(residual * precond / copies), ("gx", "gz"))
    image = keep * assemble(apply_operator(precond, spreads, stiffness))
    denominator = lax.psum(jnp.sum(precond * image / copies), ("gx", "gz"))
    alpha = numerator / denominator
    return (start + alpha * precond, residual - alpha * image)


def solution(mesh):
    placed = (
        P("gx", None, "gz"),
        P("gx", None, "gz"),
        P(None, "gx", None, "gz"),
        P(),
        P(),
        P(),
        P(("gx", "gz"), None),
        P(None, "gx", None, "gz"),
    )
    return jax.shard_map(
        body,
        mesh=mesh,
        in_specs=placed,
        out_specs=(P("gx", None, "gz"), P("gx", None, "gz")),
        check_vma=False,
    )
```

profile of v0, /device:TPU:0, one launch (start us, length us, event | category | flops | bytes accessed | tf_op | source)
XLA Modules:
  0.0 211.5 jit_solution(5846801020661909079)
XLA Ops:
  1.4 2.9 %collective-permute-start.1 = (f32[1,16,128]{2,0,1:T(1,128)S(1)}, f32[1,16,128]{2,0,1:T(1,128)S(1)}, u32[]{:S(2)}, u32[]{:S(2)}) collective-permute-start(f32[1,16,128]{2,0,1:T(1,128)S(1)} %bitcast.115), channel_id=1, source_target_pairs={{0,8},{8,16},{16,24},{24,0},{1,9},{9,17},{17,25},{25,1},{2,10},{10... | collective-permute-start | bytes 24584 | tf_op jit(solution)/shard_map/ppermute | solution.py:35
  10.8 1.8 broadcast_multiply_fusion.1
  14.2 3.0 %collective-permute-start.2 = (f32[16,16,1]{2,0,1:T(8,128)}, f32[16,16,1]{2,0,1:T(8,128)}, u32[]{:S(2)}, u32[]{:S(2)}) collective-permute-start(f32[16,16,1]{2,0,1:T(8,128)} %get-tuple-element.27), channel_id=1, source_target_pairs={{1,0},{2,1},{3,2},{4,3},{5,4},{6,5},{7,6},{0,7},{9,8},{10,9},{11,1... | collective-permute-start | bytes 3080 | tf_op jit(solution)/shard_map/ppermute | solution.py:37
  21.5 2.2 %reshape.297 = f32[128,128,1]{1,0,2:T(8,128)} reshape(f32[16,8,16,8]{3,2,1,0:T(8,128)} %get-tuple-element.33) | data formatting | bytes 131072 | tf_op jit(solution)/shard_map/jit(kron)/mul | solution.py:49
  24.5 1.2 multiply_divide_fusion.3
  29.1 1.5 collective-permute-start.4
  31.1 1.4 reshape.284
  32.5 1.3 reshape.303
  33.9 1.3 mul.592
  39.2 3.0 %collective-permute-start.6 = (f32[16,16,1]{2,0,1:T(8,128)S(1)}, f32[16,16,1]{2,0,1:T(8,128)S(1)}, u32[]{:S(2)}, u32[]{:S(2)}) collective-permute-start(f32[16,16,1]{2,0,1:T(8,128)S(1)} %get-tuple-element.23), channel_id=1, source_target_pairs={{1,0},{2,1},{3,2},{4,3},{5,4},{6,5},{7,6},{0,7},{9,8},{10,9},{11,1... | collective-permute-start | bytes 3080 | tf_op jit(solution)/shard_map/ppermute | solution.py:37
  44.7 3.7 %collective-permute-done.7 = f32[16,16,1]{2,0,1:T(8,128)S(1)} collective-permute-done((f32[16,16,1]{2,0,1:T(8,128)S(1)}, f32[16,16,1]{2,0,1:T(8,128)S(1)}, u32[]{:S(2)}, u32[]{:S(2)}) %collective-permute-start.7) | collective-permute-done | bytes 1056 | tf_op jit(solution)/shard_map/ppermute | solution.py:35
  51.0 4.2 %scatter_custom_fusion = f32[64]{0:T(128)S(1)} fusion(s32[512]{0:T(512)} %reshape.284, f32[512]{0:T(512)S(1)} %reshape.286, f32[]{:T(128)} %constant.105.clone.1), kind=kCustom, calls=%fused_computation.162 | custom fusion | flops 512 | bytes 768 | tf_op jit(solution)/shard_map/scatter-add | solution.py:171
  55.2 37.9 %psum.21 = f32[64]{0:T(128)S(1)} all-reduce(f32[64]{0:T(128)S(1)} %scatter_custom_fusion), channel_id=1, replica_groups=mesh['gx'=4,'gz'=8] {'gx','gz'}, use_global_device_ids=true, to_apply=%region_1.2 | all-reduce | flops 64 | bytes 512 | tf_op jit(solution)/shard_map/psum | solution.py:174
  93.4 41.3 %all-reduce.4 = f32[64]{0:T(128)S(1)} all-reduce(f32[64]{0:T(128)S(1)} %dynamic-update-slice), channel_id=1, replica_groups=mesh['gx'=4,'gz'=8] {'gx','gz'}, use_global_device_ids=true, to_apply=%add.4 | all-reduce | flops 64 | bytes 512
  134.8 3.3 %gather_fusion = f32[512]{0:T(512)S(1)} fusion(f32[64]{0:T(128)S(1)} %all-reduce.4, s32[1024]{0:T(1024)S(1)} %pad_clamp_fusion), kind=kCustom, calls=%fused_computation | custom fusion | bytes 6144 | tf_op jit(solution)/shard_map/gather | solution.py:178
  140.9 3.3 %collective-permute-start.8 = (f32[1,16,128]{2,0,1:T(1,128)S(1)}, f32[1,16,128]{2,0,1:T(1,128)S(1)}, u32[]{:S(2)}, u32[]{:S(2)}) collective-permute-start(f32[1,16,128]{2,0,1:T(1,128)S(1)} %get-tuple-element.21), channel_id=1, source_target_pairs={{8,0},{16,8},{24,16},{0,24},{9,1},{17,9},{25,17},{1,25},{10,2},{18... | collective-permute-start | bytes 24584 | tf_op jit(solution)/shard_map/ppermute | solution.py:37
  145.5 3.2 %collective-permute-done.9 = f32[1,16,128]{2,0,1:T(1,128)S(1)} collective-permute-done((f32[1,16,128]{2,0,1:T(1,128)S(1)}, f32[1,16,128]{2,0,1:T(1,128)S(1)}, u32[]{:S(2)}, u32[]{:S(2)}) %collective-permute-start.9) | collective-permute-done | bytes 8224 | tf_op jit(solution)/shard_map/ppermute | solution.py:35
  149.9 2.8 %collective-permute-done.10 = f32[16,16,1]{2,0,1:T(8,128)S(1)} collective-permute-done((f32[16,16,1]{2,0,1:T(8,128)S(1)}, f32[16,16,1]{2,0,1:T(8,128)S(1)}, u32[]{:S(2)}, u32[]{:S(2)}) %collective-permute-start.10) | collective-permute-done | bytes 1056 | tf_op jit(solution)/shard_map/ppermute | solution.py:37
  152.8 2.5 %collective-permute-done.11 = f32[16,16,1]{2,0,1:T(8,128)S(1)} collective-permute-done((f32[16,16,1]{2,0,1:T(8,128)S(1)}, f32[16,16,1]{2,0,1:T(8,128)S(1)}, u32[]{:S(2)}, u32[]{:S(2)}) %collective-permute-start.11) | collective-permute-done | bytes 1056 | tf_op jit(solution)/shard_map/ppermute | solution.py:35
  157.9 2.0 collective-permute-start.13
  159.9 1.6 collective-permute-done.12
  163.3 3.2 %collective-permute-done.14 = f32[16,16,1]{2,0,1:T(8,128)S(1)} collective-permute-done((f32[16,16,1]{2,0,1:T(8,128)S(1)}, f32[16,16,1]{2,0,1:T(8,128)S(1)}, u32[]{:S(2)}, u32[]{:S(2)}) %collective-permute-start.14) | collective-permute-done | bytes 1056 | tf_op jit(solution)/shard_map/ppermute | solution.py:37
  166.5 2.6 %collective-permute-done.15 = f32[16,16,1]{2,0,1:T(8,128)S(1)} collective-permute-done((f32[16,16,1]{2,0,1:T(8,128)S(1)}, f32[16,16,1]{2,0,1:T(8,128)S(1)}, u32[]{:S(2)}, u32[]{:S(2)}) %collective-permute-start.15) | collective-permute-done | bytes 1056 | tf_op jit(solution)/shard_map/ppermute | solution.py:35
  170.0 37.5 %all-reduce.5 = (f32[]{:T(128)}, f32[]{:T(128)}) all-reduce(f32[]{:T(128)} %get-tuple-element.9, f32[]{:T(128)} %get-tuple-element.8), channel_id=1, replica_groups=mesh['gx'=4,'gz'=8] {'gx','gz'}, use_global_device_ids=true, to_apply=%region_3.4 | all-reduce | flops 2 | bytes 16 | tf_op jit(solution)/shard_map/psum | solution.py:180
  (207 shorter events, 39.7 us)
Async XLA Ops:
  0.6 92.4 %copy-start = (f32[2,64]{1,0:T(2,128)S(1)}, f32[2,64]{1,0:T(2,128)}, u32[]{:S(2)}) copy-start(f32[2,64]{1,0:T(2,128)} %param.26) | copy-start | bytes 1540
  1.4 11.8 %collective-permute-start.1 = (f32[1,16,128]{2,0,1:T(1,128)S(1)}, f32[1,16,128]{2,0,1:T(1,128)S(1)}, u32[]{:S(2)}, u32[]{:S(2)}) collective-permute-start(f32[1,16,128]{2,0,1:T(1,128)S(1)} %bitcast.115), channel_id=1, source_target_pairs={{0,8},{8,16},{16,24},{24,0},{1,9},{9,17},{17,25},{25,1},{2,10},{10... | collective-permute-start | bytes 24584 | tf_op jit(solution)/shard_map/ppermute | solution.py:35
  4.3 8.9 %collective-permute-start = (f32[1,16,128]{2,0,1:T(1,128)S(1)}, f32[1,16,128]{2,0,1:T(1,128)S(1)}, u32[]{:S(2)}, u32[]{:S(2)}) collective-permute-start(f32[1,16,128]{2,0,1:T(1,128)S(1)} %bitcast.114), channel_id=1, source_target_pairs={{8,0},{16,8},{24,16},{0,24},{9,1},{17,9},{25,17},{1,25},{10,2},{18... | collective-permute-start | bytes 24584 | tf_op jit(solution)/shard_map/ppermute | solution.py:37
  5.3 8.0 %copy-start.21 = (pred[16]{0:T(512)(128)(4,1)}, pred[16]{0:T(512)(128)(4,1)S(1)}, u32[]{:S(2)}) copy-start(pred[16]{0:T(512)(128)(4,1)S(1)} %get-tuple-element.40) | copy-start | bytes 52
  5.3 8.0 %copy-start.23 = (pred[16]{0:T(512)(128)(4,1)}, pred[16]{0:T(512)(128)(4,1)S(1)}, u32[]{:S(2)}) copy-start(pred[16]{0:T(512)(128)(4,1)S(1)} %get-tuple-element.41) | copy-start | bytes 52
  14.2 9.6 %collective-permute-start.2 = (f32[16,16,1]{2,0,1:T(8,128)}, f32[16,16,1]{2,0,1:T(8,128)}, u32[]{:S(2)}, u32[]{:S(2)}) collective-permute-start(f32[16,16,1]{2,0,1:T(8,128)} %get-tuple-element.27), channel_id=1, source_target_pairs={{1,0},{2,1},{3,2},{4,3},{5,4},{6,5},{7,6},{0,7},{9,8},{10,9},{11,1... | collective-permute-start | bytes 3080 | tf_op jit(solution)/shard_map/ppermute | solution.py:37
  17.2 6.6 %collective-permute-start.3 = (f32[16,16,1]{2,0,1:T(8,128)}, f32[16,16,1]{2,0,1:T(8,128)}, u32[]{:S(2)}, u32[]{:S(2)}) collective-permute-start(f32[16,16,1]{2,0,1:T(8,128)} %get-tuple-element.28), channel_id=1, source_target_pairs={{0,1},{1,2},{2,3},{3,4},{4,5},{5,6},{6,7},{7,0},{8,9},{9,10},{10,1... | collective-permute-start | bytes 3080 | tf_op jit(solution)/shard_map/ppermute | solution.py:35
  17.9 8.9 %copy-start.26 = (f32[16]{0:T(128)}, f32[16]{0:T(128)S(1)}, u32[]{:S(2)}) copy-start(f32[16]{0:T(128)S(1)} %mul.550) | copy-start | bytes 196
  29.1 9.0 %collective-permute-start.4 = (f32[1,16,128]{2,0,1:T(1,128)}, f32[1,16,128]{2,0,1:T(1,128)}, u32[]{:S(2)}, u32[]{:S(2)}) collective-permute-start(f32[1,16,128]{2,0,1:T(1,128)} %get-tuple-element.25), channel_id=1, source_target_pairs={{8,0},{16,8},{24,16},{0,24},{9,1},{17,9},{25,17},{1,25},{10,2},{18... | collective-permute-start | bytes 24584 | tf_op jit(solution)/shard_map/ppermute | solution.py:37
  30.6 7.5 %collective-permute-start.5 = (f32[1,16,128]{2,0,1:T(1,128)}, f32[1,16,128]{2,0,1:T(1,128)}, u32[]{:S(2)}, u32[]{:S(2)}) collective-permute-start(f32[1,16,128]{2,0,1:T(1,128)} %get-tuple-element.26), channel_id=1, source_target_pairs={{0,8},{8,16},{16,24},{24,0},{1,9},{9,17},{17,25},{25,1},{2,10},{10... | collective-permute-start | bytes 24584 | tf_op jit(solution)/shard_map/ppermute | solution.py:35
  37.1 5.6 %copy-start.2 = (f32[16,8,16,8]{3,2,1,0:T(8,128)S(1)}, f32[16,8,16,8]{3,2,1,0:T(8,128)}, u32[]{:S(2)}) copy-start(f32[16,8,16,8]{3,2,1,0:T(8,128)} %get-tuple-element.31) | copy-start | bytes 196612
  39.2 5.5 %collective-permute-start.6 = (f32[16,16,1]{2,0,1:T(8,128)S(1)}, f32[16,16,1]{2,0,1:T(8,128)S(1)}, u32[]{:S(2)}, u32[]{:S(2)}) collective-permute-start(f32[16,16,1]{2,0,1:T(8,128)S(1)} %get-tuple-element.23), channel_id=1, source_target_pairs={{1,0},{2,1},{3,2},{4,3},{5,4},{6,5},{7,6},{0,7},{9,8},{10,9},{11,1... | collective-permute-start | bytes 3080 | tf_op jit(solution)/shard_map/ppermute | solution.py:37
  42.2 6.2 %collective-permute-start.7 = (f32[16,16,1]{2,0,1:T(8,128)S(1)}, f32[16,16,1]{2,0,1:T(8,128)S(1)}, u32[]{:S(2)}, u32[]{:S(2)}) collective-permute-start(f32[16,16,1]{2,0,1:T(8,128)S(1)} %get-tuple-element.24), channel_id=1, source_target_pairs={{0,1},{1,2},{2,3},{3,4},{4,5},{5,6},{6,7},{7,0},{8,9},{9,10},{10,1... | collective-permute-start | bytes 3080 | tf_op jit(solution)/shard_map/ppermute | solution.py:35
  43.2 5.2 %copy-start.37 = (f32[128]{0:T(128)S(1)}, f32[128]{0:T(128)}, u32[]{:S(2)}) copy-start(f32[128]{0:T(128)} %or_select_fusion) | copy-start | bytes 1540
  43.7 4.7 %copy-start.30 = (pred[128]{0:T(512)(128)(4,1)S(1)}, pred[128]{0:T(512)(128)(4,1)}, u32[]{:S(2)}) copy-start(pred[128]{0:T(512)(128)(4,1)} %get-tuple-element.44) | copy-start | bytes 388
  140.9 4.6 %collective-permute-start.8 = (f32[1,16,128]{2,0,1:T(1,128)S(1)}, f32[1,16,128]{2,0,1:T(1,128)S(1)}, u32[]{:S(2)}, u32[]{:S(2)}) collective-permute-start(f32[1,16,128]{2,0,1:T(1,128)S(1)} %get-tuple-element.21), channel_id=1, source_target_pairs={{8,0},{16,8},{24,16},{0,24},{9,1},{17,9},{25,17},{1,25},{10,2},{18... | collective-permute-start | bytes 24584 | tf_op jit(solution)/shard_map/ppermute | solution.py:37
  144.1 4.6 %collective-permute-start.9 = (f32[1,16,128]{2,0,1:T(1,128)S(1)}, f32[1,16,128]{2,0,1:T(1,128)S(1)}, u32[]{:S(2)}, u32[]{:S(2)}) collective-permute-start(f32[1,16,128]{2,0,1:T(1,128)S(1)} %get-tuple-element.22), channel_id=1, source_target_pairs={{0,8},{8,16},{16,24},{24,0},{1,9},{9,17},{17,25},{25,1},{2,10},{10... | collective-permute-start | bytes 24584 | tf_op jit(solution)/shard_map/ppermute | solution.py:35
  149.0 3.8 %collective-permute-start.10 = (f32[16,16,1]{2,0,1:T(8,128)S(1)}, f32[16,16,1]{2,0,1:T(8,128)S(1)}, u32[]{:S(2)}, u32[]{:S(2)}) collective-permute-start(f32[16,16,1]{2,0,1:T(8,128)S(1)} %get-tuple-element.19), channel_id=1, source_target_pairs={{1,0},{2,1},{3,2},{4,3},{5,4},{6,5},{7,6},{0,7},{9,8},{10,9},{11,1... | collective-permute-start | bytes 3080 | tf_op jit(solution)/shard_map/ppermute | solution.py:37
  149.1 6.2 %collective-permute-start.11 = (f32[16,16,1]{2,0,1:T(8,128)S(1)}, f32[16,16,1]{2,0,1:T(8,128)S(1)}, u32[]{:S(2)}, u32[]{:S(2)}) collective-permute-start(f32[16,16,1]{2,0,1:T(8,128)S(1)} %get-tuple-element.20), channel_id=1, source_target_pairs={{0,1},{1,2},{2,3},{3,4},{4,5},{5,6},{6,7},{7,0},{8,9},{9,10},{10,1... | collective-permute-start | bytes 3080 | tf_op jit(solution)/shard_map/ppermute | solution.py:35
  149.9 5.7 %copy-start.9 = (f32[128,128,1]{1,0,2:T(8,128)S(1)}, f32[128,128,1]{1,0,2:T(8,128)}, u32[]{:S(2)}) copy-start(f32[128,128,1]{1,0,2:T(8,128)} %reshape.297) | copy-start | bytes 196612
  157.8 3.7 %collective-permute-start.12 = (f32[1,16,128]{2,0,1:T(1,128)S(1)}, f32[1,16,128]{2,0,1:T(1,128)S(1)}, u32[]{:S(2)}, u32[]{:S(2)}) collective-permute-start(f32[1,16,128]{2,0,1:T(1,128)S(1)} %get-tuple-element.17), channel_id=1, source_target_pairs={{8,0},{16,8},{24,16},{0,24},{9,1},{17,9},{25,17},{1,25},{10,2},{18... | collective-permute-start | bytes 24584 | tf_op jit(solution)/shard_map/ppermute | solution.py:37
  157.9 4.6 %collective-permute-start.13 = (f32[1,16,128]{2,0,1:T(1,128)S(1)}, f32[1,16,128]{2,0,1:T(1,128)S(1)}, u32[]{:S(2)}, u32[]{:S(2)}) collective-permute-start(f32[1,16,128]{2,0,1:T(1,128)S(1)} %get-tuple-element.18), channel_id=1, source_target_pairs={{0,8},{8,16},{16,24},{24,0},{1,9},{9,17},{17,25},{25,1},{2,10},{10... | collective-permute-start | bytes 24584 | tf_op jit(solution)/shard_map/ppermute | solution.py:35
  162.8 3.8 %collective-permute-start.14 = (f32[16,16,1]{2,0,1:T(8,128)S(1)}, f32[16,16,1]{2,0,1:T(8,128)S(1)}, u32[]{:S(2)}, u32[]{:S(2)}) collective-permute-start(f32[16,16,1]{2,0,1:T(8,128)S(1)} %get-tuple-element.15), channel_id=1, source_target_pairs={{1,0},{2,1},{3,2},{4,3},{5,4},{6,5},{7,6},{0,7},{9,8},{10,9},{11,1... | collective-permute-start | bytes 3080 | tf_op jit(solution)/shard_map/ppermute | solution.py:37
  162.9 6.2 %collective-permute-start.15 = (f32[16,16,1]{2,0,1:T(8,128)S(1)}, f32[16,16,1]{2,0,1:T(8,128)S(1)}, u32[]{:S(2)}, u32[]{:S(2)}) collective-permute-start(f32[16,16,1]{2,0,1:T(8,128)S(1)} %get-tuple-element.16), channel_id=1, source_target_pairs={{0,1},{1,2},{2,3},{3,4},{4,5},{5,6},{6,7},{7,0},{8,9},{9,10},{10,1... | collective-permute-start | bytes 3080 | tf_op jit(solution)/shard_map/ppermute | solution.py:35
  (36 other events, 53.4 us)
where the time goes:
time: 213 us; the launch traced here: 211 us
  blocking collectives  117 us (55%)
  local copies, waits for them, and re-layouts  30.8 us (14%)
  waiting for transfers between devices  22.7 us (11%)
  starting transfers between devices  18.3 us (9%)
  other arithmetic  14.9 us (7%)
  matrix products  5.23 us (2%)
  between operations  2.77 us (1%)
    unnamed x1, blocking collectives  41.3 us
    psum x1, blocking collectives, body(): coarse_rhs = lax.psum(partial_value, ('gx', 'gz'))  37.9 us
    psum x1, blocking collectives, body(): numerator = lax.psum(jnp.sum(residual * precond / copies), ('gx', 'gz'))  37.5 us
    ppermute x8, waiting for transfers between devices, with_halo(): lax.ppermute(tail, axis, [(i, (i + 1) % count) for i in range(count)])  13 us
    ppermute x8, starting transfers between devices, with_halo(): lax.ppermute(head, axis, [((i + 1) % count, i) for i in range(count)])  12 us
    ppermute x8, waiting for transfers between devices, with_halo(): lax.ppermute(head, axis, [((i + 1) % count, i) for i in range(count)])  9.75 us
    unnamed x93, local copies, waits for them, and re-layouts  9.32 us
    ppermute x8, starting transfers between devices, with_halo(): lax.ppermute(tail, axis, [(i, (i + 1) % count) for i in range(count)])  6.33 us
  transfers between devices with their start and end apart: 16, of which 10 were waited for; matrix products, arithmetic and copies ran while one was open for 10% of the time, Pallas kernels for 0%

commit v1 on v0

v1 whole, which is shorter than its diff:
```python
import functools

import jax
import jax.numpy as jnp
import numpy as np
from jax import lax
from jax.experimental import pallas as pl
from jax.experimental.pallas import tpu as pltpu
from jax.sharding import PartitionSpec as P

POINTS = [
    -1.0,
    -0.8717401485096066,
    -0.5917001814331423,
    -0.2092992179024789,
    0.2092992179024789,
    0.5917001814331423,
    0.8717401485096066,
    1.0,
]
WEIGHTS = [
    0.03571428571428571,
    0.21070422714350603,
    0.34112269248350435,
    0.4124587946587038,
    0.4124587946587038,
    0.34112269248350435,
    0.21070422714350603,
    0.03571428571428571,
]
LOW = [(1.0 - s) / 2.0 for s in POINTS]
HIGH = [(1.0 + s) / 2.0 for s in POINTS]
EXACT = lax.Precision.HIGHEST

ROWS = 16
LANES = 128
WIDE = 256
HALO = 32
PAIRS = ((0, 0), (0, 1), (1, 1))
GROUP_X = ([1.0] * 8 + LOW, [0.0] * 8 + HIGH)
INVERSE_X = [0.5] + [1.0] * 6 + [0.5] + [0.5] + [1.0] * 6 + [0.5]


def iota(shape, dim):
    return lax.broadcasted_iota(jnp.int32, shape, dim)


def pick(index, values):
    result = jnp.full(index.shape, values[0], jnp.float32)
    for i in range(1, 8):
        result = jnp.where(index == i, values[i], result)
    return result


def even_index(axis):
    return lax.rem(lax.axis_index(axis), 2) == 0


class Geometry:
    def __init__(self, lanes):
        shape = (2, 8, lanes)
        self.element_y, self.row, lane = iota(shape, 0), iota(shape, 1), iota(shape, 2)
        self.position = lane & 7
        self.first = self.position == 0
        self.last = self.position == 7
        self.edge = self.first | self.last
        self.weight_y = pick(self.row, WEIGHTS)
        self.weight_z = pick(self.position, WEIGHTS)
        self.inverse_z = jnp.where(self.edge, 0.5, 1.0)
        self.wall = (self.element_y == 1) & (self.row == 7)
        inner = ((self.element_y == 0) & (self.row == 7)) | ((self.element_y == 1) & (self.row == 0))
        self.inverse_y = jnp.where(inner, 0.5, 1.0)
        self.keep = jnp.where(self.wall, 0.0, 1.0)
        self.lanes = lanes

    def pair_y(self, v):
        lower, upper = v[0], v[1]
        row = self.row[0]
        up = jnp.where(row == 7, pltpu.roll(upper, 7, 0), 0.0)
        down = jnp.where(row == 0, pltpu.roll(lower, 1, 0), 0.0)
        return jnp.stack([lower + up, upper + down])

    def pair_z(self, v):
        flat = v.reshape(16, self.lanes)
        after = pltpu.roll(flat, self.lanes - 1, 1).reshape(v.shape)
        before = pltpu.roll(flat, 1, 1).reshape(v.shape)
        return v + jnp.where(self.edge, jnp.where(self.last, after, before), 0.0)

    def pair(self, v):
        return self.pair_z(self.pair_y(v))


def contract_x(rows, matrix, i, transpose=False):
    total = None
    for p in range(8):
        factor = matrix[p, i] if transpose else matrix[i, p]
        term = factor * rows[p]
        total = term if total is None else total + term
    return total


def contract_y(v, diagonals):
    total = diagonals[0] * v
    for d in range(1, 8):
        rolled = jnp.stack([pltpu.roll(v[e], 8 - d, 0) for e in range(2)])
        total = total + diagonals[d] * rolled
    return total


def contract_z(flat, block):
    pieces = [
        jnp.dot(
            flat[:, at : at + LANES], block, precision=EXACT, preferred_element_type=jnp.float32
        )
        for at in range(0, flat.shape[1], LANES)
    ]
    return pieces[0] if len(pieces) == 1 else jnp.concatenate(pieces, axis=1)


def wide_diagonals(ref, which, lanes):
    one = [ref[which, d] for d in range(8)]
    return [jnp.concatenate([c] * (lanes // LANES), axis=1)[None] for c in one]


def metric(ref, component, element, lanes):
    at = (component * 2 + element) * 2
    return jnp.stack([jnp.broadcast_to(ref[at + e : at + e + 1, :lanes], (8, lanes)) for e in range(2)])


def apply_rows(geo, source_ref, along_z, metrics, stiffness, diagonals):
    lanes = geo.lanes
    rows = [source_ref[x].reshape(2, 8, lanes) for x in range(ROWS)]
    result = []
    for element in range(2):
        cx, cy, cz = metrics[element]
        factor_x = cx * geo.weight_y * geo.weight_z
        factor_y = cy * geo.weight_z
        factor_z = cz * geo.weight_y
        own = rows[element * 8 : element * 8 + 8]
        for i in range(8):
            x = element * 8 + i
            term_y = factor_y * contract_y(own[i], diagonals)
            term_z = factor_z * along_z[x * 16 : x * 16 + 16].reshape(2, 8, lanes)
            result.append(factor_x * contract_x(own, stiffness, i) + WEIGHTS[i] * (term_y + term_z))
    return result


def join_middle(rows):
    middle = rows[7] + rows[8]
    return rows[:7] + [middle, middle] + rows[9:]


def prepare_kernel(stiffness, vectors, blocks, diagonals):
    spread_rows = (iota((LANES, 8), 0) & 7 == iota((LANES, 8), 1)).astype(jnp.float32)
    same = (iota((LANES, LANES), 0) >> 3) == (iota((LANES, LANES), 1) >> 3)
    unit = (iota((8, 8), 0) == iota((8, 8), 1)).astype(jnp.float32)

    def dot(a, b, dims):
        return lax.dot_general(a, b, ((dims), ((), ())), precision=EXACT, preferred_element_type=jnp.float32)

    def block(matrix):
        half = dot(spread_rows, matrix, ((1,), (0,)))
        return jnp.where(same, dot(half, spread_rows, ((1,), (1,))), 0.0)

    def put_diagonals(at, matrix):
        row, column = iota((8, 8), 0), iota((8, 8), 1)
        for d in range(8):
            chosen = jnp.where(column == ((row + d) & 7), matrix, 0.0)
            diagonals[at, d] = jnp.broadcast_to(jnp.sum(chosen, axis=1, keepdims=True), (8, LANES))

    k, s = stiffness[...], vectors[...]
    k_turned, s_turned = dot(k, unit, ((0,), (0,))), dot(s, unit, ((0,), (0,)))
    blocks[0] = block(k_turned)
    blocks[1] = block(s)
    blocks[2] = block(s_turned)
    put_diagonals(0, k)
    put_diagonals(1, s_turned)
    put_diagonals(2, s)


def pack_kernel(source, previous, coefficients, first, second, metrics, scratch):
    even = even_index("gz")
    scratch[...] = jnp.zeros_like(scratch)
    for c in range(3):
        for element in range(2):
            at = (c * 2 + element) * 2
            scratch[at : at + 2, :] = coefficients[c, element]
    widen = (iota((16, LANES), 0) == (iota((16, LANES), 1) >> 3)).astype(jnp.float32)
    spread = jnp.dot(scratch[...], widen, precision=EXACT, preferred_element_type=jnp.float32)
    metrics[...] = spread
    group = iota((8 * ROWS, LANES), 1) // HALO
    parts = [
        ref[lo : lo + 8].reshape(8 * ROWS, LANES) for ref in (previous, source) for lo in (0, 8)
    ]
    for to_right, out in ((even, first), (jnp.logical_not(even), second)):
        base = jnp.where(to_right, HALO, 0)
        packed = None
        for k, part in enumerate(parts):
            moved = pltpu.roll(part, lax.rem(base + HALO * k, LANES), 1)
            packed = moved if packed is None else jnp.where(group == k, moved, packed)
        out[0:8] = packed.reshape(8, ROWS, LANES)
        out[8] = spread


def start_kernel(
    source, previous, own_metrics, first, second, stiffness, blocks, diagonals,
    start, rest, metrics, message_a, message_b, field,
):
    even = even_index("gz")
    lane = iota((ROWS, LANES), 1)

    def beyond(plane, right_shift, left_shift, fill):
        a, b = first[plane], second[plane]
        right, left = jnp.where(even, a, b), jnp.where(even, b, a)
        if right_shift:
            right = pltpu.roll(right, right_shift, 1)
        if left_shift:
            left = pltpu.roll(left, left_shift, 1)
        return jnp.where(lane < HALO, right, jnp.where(lane >= LANES - HALO, left, fill))

    def wide(ref, x, kind):
        slot = 2 * kind + x // 8
        right_shift = (LANES - HALO * slot) % LANES
        left_shift = (LANES - HALO - HALO * slot) % LANES
        return jnp.concatenate([ref[x], beyond(x % 8, right_shift, left_shift, 0.0)], axis=1).reshape(2, 8, WIDE)

    geo = Geometry(WIDE)
    metrics[:, :LANES] = own_metrics[...]
    metrics[:, LANES:] = beyond(8, 0, 0, 1.0)
    factor = geo.keep * geo.inverse_y * geo.inverse_z
    rows = [geo.pair(wide(previous, x, 0)) * (factor * INVERSE_X[x]) for x in range(ROWS)]
    rows = join_middle(rows)
    faces = (rows[0], rows[15])
    rows[0] = rows[15] = jnp.zeros_like(rows[0])
    for x in range(ROWS):
        field[x] = rows[x].reshape(ROWS, WIDE)
        start[x] = rows[x].reshape(ROWS, WIDE)[:, :LANES]
    along_z = contract_z(field[...].reshape(ROWS * ROWS, WIDE), blocks[0])
    factors = [[metric(metrics, c, e, WIDE) for c in range(3)] for e in range(2)]
    applied = apply_rows(geo, field, along_z, factors, stiffness, wide_diagonals(diagonals, 0, WIDE))
    for x in range(ROWS):
        rest[x] = (wide(source, x, 1) - applied[x]).reshape(ROWS, WIDE)
    even_x = even_index("gx")

    def choose(right, left):
        return jnp.where(even_x, right, left), jnp.where(even_x, left, right)

    for at, right, left in (
        (0, faces[1].reshape(ROWS, WIDE), faces[0].reshape(ROWS, WIDE)),
        (16, rest[15], rest[0]),
    ):
        message_a[at : at + 16], message_b[at : at + 16] = choose(right, left)
    for c in range(3):
        at = 32 + 2 * c
        right, left = metrics[(c * 2 + 1) * 2 : (c * 2 + 1) * 2 + 2], metrics[c * 4 : c * 4 + 2]
        message_a[at : at + 2], message_b[at : at + 2] = choose(right, left)
    message_a[38:40] = jnp.zeros((2, WIDE), jnp.float32)
    message_b[38:40] = jnp.zeros((2, WIDE), jnp.float32)


def face_metric(ref_right, ref_left, c, even, right):
    def rows(ref):
        return jnp.stack([jnp.broadcast_to(ref[32 + 2 * c + e : 33 + 2 * c + e], (8, WIDE)) for e in range(2)])

    a, b = rows(ref_right), rows(ref_left)
    return jnp.where(even, a, b) if right else jnp.where(even, b, a)


def solve_kernel(
    start, rest, metrics, own_a, own_b, got_a, got_b, stiffness, vectors, eigen, blocks, diagonals,
    new_start, residual, local, message_a, message_b, sums, field,
):
    even = even_index("gx")
    geo = Geometry(WIDE)
    factors = [[metric(metrics, c, e, WIDE) for c in range(3)] for e in range(2)]

    def sided(a, b, at):
        one, two = a[at : at + 16].reshape(2, 8, WIDE), b[at : at + 16].reshape(2, 8, WIDE)
        return jnp.where(even, one, two), jnp.where(even, two, one)

    mine, theirs = sided(own_a, own_b, 0), sided(got_a, got_b, 0)
    right, left = mine[0] + theirs[0], mine[1] + theirs[1]
    other_rest = sided(got_a, got_b, 16)
    for x in range(1, 15):
        new_start[x] = start[x]
    new_start[0] = left.reshape(ROWS, WIDE)[:, :LANES]
    new_start[15] = right.reshape(ROWS, WIDE)[:, :LANES]

    stiff = wide_diagonals(diagonals, 0, WIDE)
    rows = [rest[x].reshape(2, 8, WIDE) for x in range(ROWS)]
    for element, near, face, across, far, side in ((0, 0, left, 7, 1, False), (1, 7, right, 0, 0, True)):
        cx, cy, cz = factors[element]
        other = [face_metric(got_a, got_b, c, even, side) for c in range(3)]
        weights = geo.weight_y * geo.weight_z
        scaled = cx * weights * face
        for i in range(8):
            if i != near:
                rows[element * 8 + i] = rows[element * 8 + i] - stiffness[i, near] * scaled
        along_z = contract_z(face.reshape(ROWS, WIDE), blocks[0]).reshape(2, 8, WIDE)
        taken = stiffness[near, near] * scaled + stiffness[across, across] * (other[0] * weights * face)
        taken = taken + WEIGHTS[0] * (
            (cy + other[1]) * geo.weight_z * contract_y(face, stiff) + (cz + other[2]) * geo.weight_y * along_z
        )
        x = element * 8 + near
        rows[x] = rows[x] + other_rest[far] - taken
    rows = [geo.pair(v) * geo.keep for v in join_middle(rows)]
    weight = geo.inverse_y * geo.inverse_z
    parts = [None, None]
    for x in range(ROWS):
        field[x] = rows[x].reshape(ROWS, WIDE)
        residual[x] = rows[x].reshape(ROWS, WIDE)[:, :LANES]
        for a in range(2):
            if GROUP_X[a][x] * INVERSE_X[x] != 0.0:
                term = (GROUP_X[a][x] * INVERSE_X[x]) * rows[x][:, :, :LANES]
                parts[a] = term if parts[a] is None else parts[a] + term

    def down(v):
        return jnp.sum(v.reshape(ROWS, LANES), axis=0, keepdims=True)

    for a in range(2):
        sums[a : a + 1] = down(parts[a] * weight[:, :, :LANES])

    forward, backward = wide_diagonals(diagonals, 1, WIDE), wide_diagonals(diagonals, 2, WIDE)
    moved = []
    for element in range(2):
        own = [field[element * 8 + p].reshape(2, 8, WIDE) for p in range(8)]
        for i in range(8):
            moved.append(contract_y(contract_x(own, vectors, i, True), forward).reshape(ROWS, WIDE))
    spectral = contract_z(jnp.concatenate(moved, axis=0), blocks[1])
    lam = [eigen[i] for i in range(8)]
    lam_y, lam_z = pick(geo.row, lam), pick(geo.position, lam)
    divided = []
    for element in range(2):
        cx, cy, cz = factors[element]
        base = cy * lam_y + cz * lam_z
        for i in range(8):
            x = element * 8 + i
            value = spectral[x * 16 : x * 16 + 16].reshape(2, 8, WIDE)
            divided.append((value / (cx * lam[i] + base)).reshape(ROWS, WIDE))
    back = contract_z(jnp.concatenate(divided, axis=0), blocks[2])
    solved = []
    for element in range(2):
        own = [
            contract_y(back[x * 16 : x * 16 + 16].reshape(2, 8, WIDE), backward)
            for x in range(element * 8, element * 8 + 8)
        ]
        solved += [contract_x(own, vectors, i) for i in range(8)]
    total = None
    for x in range(ROWS):
        term = solved[x][:, :, :LANES] * residual[x].reshape(2, 8, LANES)
        total = term if total is None else total + term
    sums[2:3] = down(total)
    sums[3:8] = jnp.zeros((5, LANES), jnp.float32)
    solved = [(geo.pair(v) * geo.keep).reshape(ROWS, WIDE) for v in join_middle(solved)]
    for x in range(ROWS):
        local[x] = solved[x]
    message_a[...] = jnp.where(even, solved[15], solved[0])
    message_b[...] = jnp.where(even, solved[0], solved[15])


def group_lanes(lanes, group):
    lane = iota((1, lanes), 1)
    signed = jnp.where(lane < lanes // 2 + lanes // 4, lane, lane - lanes) if lanes > LANES else lane
    element, position = signed >> 3, lane & 7
    low, high = pick(position, LOW), pick(position, HIGH)
    here = jnp.where((element >> 3) == group, low, 0.0)
    return here + jnp.where(((element + 1) >> 3) == group, high, 0.0)


def image_kernel(
    local, metrics, got_a, got_b, stiffness, labels, coarse, sums, blocks, diagonals,
    local_own, image, message_a, message_b, payload, field,
):
    even = even_index("gx")
    geo = Geometry(WIDE)
    one, two = got_a[...], got_b[...]
    for x in range(ROWS):
        value = local[x]
        if x == 0:
            value = value + jnp.where(even, two, one)
        if x == 15:
            value = value + jnp.where(even, one, two)
        field[x] = value
        local_own[x] = value[:, :LANES]
    along_z = contract_z(field[...].reshape(ROWS * ROWS, WIDE), blocks[0])
    factors = [[metric(metrics, c, e, WIDE) for c in range(3)] for e in range(2)]
    applied = apply_rows(geo, field, along_z, factors, stiffness, wide_diagonals(diagonals, 0, WIDE))

    total, parts = None, [None, None]
    for x in range(ROWS):
        own = applied[x][:, :, :LANES]
        term = own * local_own[x].reshape(2, 8, LANES)
        total = term if total is None else total + term
        for a in range(2):
            if GROUP_X[a][x] != 0.0:
                term = GROUP_X[a][x] * own
                parts[a] = term if parts[a] is None else parts[a] + term
    keep = geo.keep[:, :, :LANES]

    def down(v):
        return jnp.sum(v.reshape(ROWS, LANES), axis=0, keepdims=True)

    applied = [(geo.pair(v) * geo.keep).reshape(ROWS, WIDE)[:, :LANES] for v in join_middle(applied)]
    for x in range(ROWS):
        image[x] = applied[x]
    message_a[...] = jnp.where(even, applied[15], applied[0])
    message_b[...] = jnp.where(even, applied[0], applied[15])

    groups = [group_lanes(LANES, b) for b in range(3)]
    stacked = jnp.concatenate(groups + [jnp.zeros((5, LANES), jnp.float32)], axis=0)
    stiff_z = contract_z(stacked, blocks[0])
    weight_z = pick(iota((1, LANES), 1) & 7, WEIGHTS)
    kept = [[1.0] * 8, [1.0] * 7 + [0.0]]
    mass_y = [sum(w * k for w, k in zip(WEIGHTS, line)) for line in kept]
    inner = None
    for i in range(7):
        for j in range(7):
            inner = stiffness[i, j] if inner is None else inner + stiffness[i, j]
    border = stiffness[7, 7]
    for i in range(7):
        border = border + stiffness[i, 7] + stiffness[7, i]
    stiff_y = [inner + border, inner]
    matrix_rows = []
    for a, b in PAIRS:
        across, along = jnp.zeros((1, LANES), jnp.float32), jnp.zeros((1, LANES), jnp.float32)
        for element in range(2):
            fa = GROUP_X[a][element * 8 : element * 8 + 8]
            fb = GROUP_X[b][element * 8 : element * 8 + 8]
            if not (any(fa) and any(fb)):
                continue
            mass_x = sum(w * p * q for w, p, q in zip(WEIGHTS, fa, fb))
            stiff_x = None
            for i in range(8):
                for j in range(8):
                    if fa[i] * fb[j] != 0.0:
                        term = (fa[i] * fb[j]) * stiffness[i, j]
                        stiff_x = term if stiff_x is None else stiff_x + term
            for e in range(2):
                cx, cy, cz = (metrics[(c * 2 + element) * 2 + e, :LANES].reshape(1, LANES) for c in range(3))
                across = across + cx * (stiff_x * mass_y[e]) + cy * (stiff_y[e] * mass_x)
                along = along + cz * (mass_x * mass_y[e])
        across = across * weight_z
        for k in range(3):
            matrix_rows.append(across * groups[k] + along * stiff_z[k : k + 1])
    zero = jnp.zeros((1, LANES), jnp.float32)
    lines = [sums[0:1], sums[1:2]] + [down(part * keep) for part in parts] + matrix_rows
    lines = jnp.concatenate(lines + [sums[2:3], down(total), zero], axis=0)
    lane = iota((LANES, LANES), 1) & 7
    node = iota((LANES, LANES), 0)
    element, position = node >> 3, node & 7
    low, high = pick(position, LOW), pick(position, HIGH)
    columns = jnp.where(lane == (element >> 3), low, 0.0) + jnp.where(lane == ((element + 1) >> 3), high, 0.0)
    columns = jnp.where(lane == 3, 1.0, jnp.where(lane < 3, columns, 0.0))
    reduced = jnp.dot(lines, columns, precision=EXACT, preferred_element_type=jnp.float32)
    mine = (iota((16, LANES), 1) >> 3) == iota((16, LANES), 0)
    row = jnp.sum(jnp.where(mine, reduced, 0.0), axis=0, keepdims=True)
    place = iota((1, LANES), 1)
    for a in range(2):
        for b in range(3):
            corner, x, z = 4 * a + (b == 2), a, (0, 8, 15)[b]
            number = labels[corner, x, 0, z].astype(jnp.float32)
            row = jnp.where(place == 8 * (3 * a + b) + 4, number, row)
    if coarse is None:
        below = zero
    else:
        per, count = coarse.shape
        below = [coarse[i : i + 1, :] for i in range(per)]
        if per * count < LANES:
            below.append(jnp.zeros((1, LANES - per * count), jnp.float32))
        below = jnp.concatenate(below, axis=1)
    block = jnp.concatenate([row, below] * 4, axis=0)
    copies = payload.shape[0] // 8
    payload[...] = jnp.broadcast_to(block[None], (copies, 8, LANES)).reshape(copies * 8, LANES)


def lane_tables():
    one = np.zeros((8, LANES), np.float32)
    two = np.zeros((8, LANES), np.float32)
    top = np.zeros((8, LANES), np.float32)
    for a in range(2):
        for b in range(3):
            one[6, 8 * a + b], two[3 * a + b, 8 * a + b], top[0, 8 * a + b] = 1.0, 1.0, 1.0
            one[6, 8 * (2 + a) + b], two[3 * a + b, 8 * (2 + a) + b] = 2.0, 1.0
            top[1, 8 * (2 + a) + b] = 1.0
    for p, (a, other) in enumerate(PAIRS):
        for b in range(3):
            for c in range(3):
                at = 8 * (4 + 3 * p + b) + c
                one[3 * a + b, at] = 1.0 if a == other else 2.0
                two[3 * other + c, at] = 1.0
                top[1, at] = 1.0
    one[6, 8 * 13 + 3], two[6, 8 * 13 + 3], top[0, 8 * 13 + 3] = 1.0, 1.0, 1.0
    one[6, 8 * 14 + 3], two[6, 8 * 14 + 3], top[1, 8 * 14 + 3] = 1.0, 1.0, 1.0
    return np.stack([one, two, top])


def final_kernel(
    devices, spans, count, per,
    start, residual, local, image, got_a, got_b, far_a, far_b, metrics, stiffness, blocks, diagonals, tables,
    gathered, given, new_solution, new_residual, values,
):
    even = even_index("gx")
    geo = Geometry(WIDE)
    rows = gathered[pl.ds(0, devices, stride=2), :]
    place = iota((1, LANES), 1)
    if given is None:
        spot = iota((devices, count), 1)
        hits = []
        rhs = [jnp.zeros((1, devices), jnp.float32) for _ in range(per)]
        owner = iota((devices, devices), 1)
        for k in range(6):
            label = rows[:, 8 * k + 4 : 8 * k + 5].astype(jnp.int32)
            at = 8 * (k // 3) + k % 3
            value = rows[:, at : at + 1]
            hits.append(spot == label)
            for q in range(per):
                chosen = jnp.where(owner * per + q == label, value, 0.0)
                rhs[q] = rhs[q] + jnp.sum(chosen, axis=0, keepdims=True)
        inverse = gathered[pl.ds(1, devices, stride=2), :]
        coarse = None
        for q in range(per):
            term = jnp.dot(
                rhs[q], inverse[:, q * count : q * count + count], precision=EXACT,
                preferred_element_type=jnp.float32,
            )
            coarse = term if coarse is None else coarse + term
        columns = [jnp.sum(jnp.where(hit, coarse, 0.0), axis=1, keepdims=True) for hit in hits]
        kept = jnp.zeros((devices, LANES), jnp.float32)
        for k in range(6):
            kept = jnp.where(iota((devices, LANES), 1) == k, columns[k], kept)
        values[...] = kept
    else:
        columns = [given[:, k : k + 1] for k in range(6)]
        values[...] = given[...]
    one, two = tables[0, 6:7, :], tables[1, 6:7, :]
    for k in range(6):
        one = one + columns[k] * tables[0, k : k + 1, :]
        two = two + columns[k] * tables[1, k : k + 1, :]
    product = jnp.sum(rows * one * two, axis=0, keepdims=True)
    numerator = jnp.sum(product * tables[2, 0:1, :], axis=1, keepdims=True)
    denominator = jnp.sum(product * tables[2, 1:2, :], axis=1, keepdims=True)
    alpha = numerator / denominator

    gx, gz = lax.axis_index("gx"), lax.axis_index("gz")
    before_x = lax.rem(gx + devices // spans - 1, devices // spans)
    before_z = lax.rem(gz + spans - 1, spans)
    here = values[pl.ds(gx * spans + gz, 1), :]
    behind = values[pl.ds(gx * spans + before_z, 1), :]
    aside = values[pl.ds(before_x * spans + gz, 1), :]
    corner = values[pl.ds(before_x * spans + before_z, 1), :]
    functions = [group_lanes(WIDE, b) for b in (-1, 0, 1, 2)]

    def along(line, back, a):
        total = back[:, 3 * a + 1 : 3 * a + 2] * functions[0]
        for b in range(3):
            total = total + line[:, 3 * a + b : 3 * a + b + 1] * functions[1 + b]
        return total

    lines = [along(here, behind, 0), along(here, behind, 1), along(aside, corner, 0)]
    flat = jnp.concatenate(lines + [jnp.zeros((5, WIDE), jnp.float32)], axis=0)
    stiff_lines = contract_z(flat, blocks[0])
    wide = [jnp.broadcast_to(line, (8, WIDE))[None] for line in lines]
    stiff_wide = [jnp.broadcast_to(stiff_lines[a : a + 1], (8, WIDE))[None] for a in range(3)]
    stiff_keep = contract_y(geo.keep, wide_diagonals(diagonals, 0, WIDE))

    def spread(c, weights_x, stiff_x, weight, side):
        cx, cy, cz = c
        plain = flat_x = turned = None
        for a, w, s in zip(side, weights_x, stiff_x):
            if s is not None:
                flat_x = s * wide[a] if flat_x is None else flat_x + s * wide[a]
            if w != 0.0:
                plain = w * wide[a] if plain is None else plain + w * wide[a]
                turned = w * stiff_wide[a] if turned is None else turned + w * stiff_wide[a]
        return cx * flat_x + weight * (cy * plain + cz * turned)

    def folded(c):
        return (
            c[0] * (geo.weight_y * geo.weight_z * geo.keep),
            c[1] * (geo.weight_z * stiff_keep),
            c[2] * (geo.weight_y * geo.keep),
        )

    def stiff_of(i, line):
        total = None
        for p in range(8):
            if line[p] != 0.0:
                term = stiffness[i, p] * line[p] if line[p] != 1.0 else stiffness[i, p]
                total = term if total is None else total + term
        return total

    applied = []
    for element in range(2):
        c = folded([metric(metrics, k, element, WIDE) for k in range(3)])
        for i in range(8):
            x = element * 8 + i
            parts = [GROUP_X[a][element * 8 : element * 8 + 8] for a in range(2)]
            stiff_x = [stiff_of(i, line) for line in parts]
            applied.append(spread(c, [GROUP_X[a][x] for a in range(2)], stiff_x, WEIGHTS[i], (0, 1)))
    other = folded([face_metric(far_a, far_b, k, even, False) for k in range(3)])
    applied[0] = applied[0] + spread(other, [1.0, 0.0], [stiff_of(7, HIGH), stiff_of(7, LOW)], WEIGHTS[7], (0, 2))
    other = folded([face_metric(far_a, far_b, k, even, True) for k in range(3)])
    applied[15] = applied[15] + spread(other, [1.0], [stiff_of(0, [1.0] * 8)], WEIGHTS[0], (1,))

    applied = join_middle(applied)
    first, second = got_a[...], got_b[...]
    keep = geo.keep[:, :, :LANES].reshape(ROWS, LANES)
    for x in range(ROWS):
        value = (geo.pair(applied[x]) * geo.keep).reshape(ROWS, WIDE)[:, :LANES] + image[x]
        if x == 0:
            value = value + jnp.where(even, second, first)
        if x == 15:
            value = value + jnp.where(even, first, second)
        new_residual[x] = residual[x] - alpha * value
        coarse_line = None
        for a in range(2):
            if GROUP_X[a][x] != 0.0:
                term = GROUP_X[a][x] * lines[a][:, :LANES]
                coarse_line = term if coarse_line is None else coarse_line + term
        new_solution[x] = start[x] + alpha * (local[x] + keep * coarse_line)


VMEM = pl.BlockSpec(memory_space=pltpu.VMEM)
SMEM = pl.BlockSpec(memory_space=pltpu.SMEM)


def call(kernel, shapes, specs, scratch, name):
    return pl.pallas_call(
        kernel,
        out_shape=[jax.ShapeDtypeStruct(shape, jnp.float32) for shape in shapes],
        in_specs=specs,
        out_specs=[VMEM] * len(shapes),
        scratch_shapes=[pltpu.VMEM(shape, jnp.float32) for shape in scratch],
        compiler_params=pltpu.CompilerParams(vmem_limit_bytes=16 * 1024 * 1024),
        name=name,
    )


def swap(first, second, axis):
    size = lax.axis_size(axis)
    odd = [(i, (i + 1) % size) for i in range(1, size, 2)]
    one = lax.ppermute(first, axis, [(i, i ^ 1) for i in range(size)])
    two = lax.ppermute(second, axis, odd + [(b, a) for a, b in odd])
    return one, two


def body(
    source, previous, coefficients, stiffness, fdm_vectors, fdm_values, coarse_inverse, vertex_map
):
    assert source.shape == (ROWS, ROWS, LANES)
    spans = lax.axis_size("gz")
    devices = lax.axis_size("gx") * spans
    per, count = coarse_inverse.shape
    block, wide = (ROWS, ROWS, LANES), (ROWS, ROWS, WIDE)
    halo = (9, ROWS, LANES)

    first, second, own_metrics = call(
        pack_kernel, [halo, halo, (16, LANES)], [VMEM] * 3, [(16, 16)], "pack"
    )(source, previous, coefficients)
    first, second = swap(first, second, "gz")
    blocks, diagonals = call(
        prepare_kernel, [(3, LANES, LANES), (3, 8, 8, LANES)], [VMEM] * 2, [], "prepare"
    )(stiffness, fdm_vectors)

    message = (40, WIDE)
    start, rest, metrics, own_a, own_b = call(
        start_kernel,
        [block, wide, (16, WIDE), message, message],
        [VMEM] * 5 + [SMEM, VMEM, VMEM],
        [wide],
        "start",
    )(source, previous, own_metrics, first, second, stiffness, blocks, diagonals)
    far_a, far_b = swap(own_a, own_b, "gx")

    start, residual, local, face_a, face_b, sums = call(
        solve_kernel,
        [block, block, wide, (ROWS, WIDE), (ROWS, WIDE), (8, LANES)],
        [VMEM] * 7 + [SMEM] * 3 + [VMEM] * 2,
        [wide],
        "solve",
    )(
        start, rest, metrics, own_a, own_b, far_a, far_b,
        stiffness, fdm_vectors, fdm_values, blocks, diagonals,
    )
    face_a, face_b = swap(face_a, face_b, "gx")

    small = per * count <= LANES
    kernel = image_kernel
    operands = [local, metrics, face_a, face_b, stiffness, vertex_map, coarse_inverse, sums, blocks, diagonals]
    specs = [VMEM] * 4 + [SMEM, SMEM] + [VMEM] * 4
    if not small:
        del operands[6], specs[6]

        def kernel(*refs):
            image_kernel(*refs[:6], None, *refs[6:])

    local, image, side_a, side_b, payload = call(
        kernel,
        [block, block, (ROWS, LANES), (ROWS, LANES), (2 * devices, LANES)],
        specs,
        [wide],
        "image",
    )(*operands)
    side_a, side_b = swap(side_a, side_b, "gx")
    gathered = lax.all_to_all(payload.reshape(devices, 2, LANES), ("gx", "gz"), 0, 0)
    gathered = gathered.reshape(2 * devices, LANES)

    tables = jnp.asarray(lane_tables())
    operands = [
        start, residual, local, image, side_a, side_b, far_a, far_b, metrics, stiffness, blocks, diagonals,
        tables, gathered,
    ]
    specs = [VMEM] * 9 + [SMEM] + [VMEM] * 4
    finish = functools.partial(final_kernel, devices, spans, count, per)
    if small:

        def kernel(*refs):
            finish(*refs[:14], None, *refs[14:])

    else:
        kernel = finish
        rows = gathered[0::2]
        keys = [8 * k + 4 for k in range(6)]
        labels = rows[:, jnp.array(keys)].astype(jnp.int32)
        parts = rows[:, jnp.array([8 * (k // 3) + k % 3 for k in range(6)])]
        rhs = jnp.zeros((count,), jnp.float32).at[labels.reshape(-1)].add(parts.reshape(-1))
        own = jnp.dot(coarse_inverse, rhs, precision=EXACT)
        coarse = lax.all_gather(own, ("gx", "gz"), axis=0, tiled=True)
        operands.append(jnp.pad(coarse[labels], ((0, 0), (0, LANES - 6))))
        specs.append(VMEM)
    return tuple(call(kernel, [block, block], specs, [(devices, LANES)], "finish")(*operands))


def solution(mesh):
    placed = (
        P("gx", None, "gz"),
        P("gx", None, "gz"),
        P(None, "gx", None, "gz"),
        P(),
        P(),
        P(),
        P(("gx", "gz"), None),
        P(None, "gx", None, "gz"),
    )
    return jax.shard_map(
        body,
        mesh=mesh,
        in_specs=placed,
        out_specs=(P("gx", None, "gz"), P("gx", None, "gz")),
        check_vma=False,
    )
```

time: 213 us -> 43.6 us (0.20)
  blocking collectives: 117 us -> 0 us
  local copies, waits for them, and re-layouts: 30.8 us -> 3.85 us
  other arithmetic: 14.9 us -> 0 us
  waiting for transfers between devices: 22.7 us -> 10.4 us
  Pallas kernels: 0 us -> 10 us
  matrix products: 5.23 us -> 0 us
    psum x2 -> x0, blocking collectives: 75.4 us -> none  [the longest x1 37.9 us: body(): coarse_rhs = lax.psum(partial_value, ('gx', 'gz'))]
    unnamed x1 -> x0, blocking collectives: 41.3 us -> none
    ppermute x16 -> x8, waiting for transfers between devices: 22.7 us -> 9.54 us  [the longest x4 7.27 us: swap(): two = lax.ppermute(second, axis, odd + [(b, a) for a, b in odd])]
    pallas_call x0 -> x6, Pallas kernels: none -> 10 us  [the longest x1 2.61 us: body(): call(kernel, [block, block, (ROWS, LANES), (ROWS, LANES), (2 * devices, L...]
    mul x13 -> x0, local copies, waits for them, and re-layouts: 7.82 us -> none  [the longest x6 4.07 us: block_matrix(): return jnp.kron(jnp.eye(length // 8, dtype=jnp.float32), matrix)]
    unnamed x93 -> x20, local copies, waits for them, and re-layouts: 9.32 us -> 3.85 us
    reshape x18 -> x0, local copies, waits for them, and re-layouts: 5.41 us -> none  [the longest x9 4.74 us: spread(): jnp.repeat(jnp.repeat(jnp.repeat(layer, 8, axis=0), 8, axis=1), 8, axis=2)]
    dot_general x19 -> x0, matrix products: 5.23 us -> none  [the longest x4 1.11 us: contract_axis(): jnp.einsum('xyp,kp->xyk', values, blocked, precision=lax.Precision.HIGHEST)]
  transfers between devices with their start and end apart: 16 -> 9, of which waited for: 10 -> 8; matrix products, arithmetic and copies ran while one was open for 10% -> 0% of each run, Pallas kernels for 0% -> 3%
where the time goes in v1:
time: 43.6 us; the launch traced here: 43.4 us
  starting transfers between devices  18.5 us (42%)
  waiting for transfers between devices  10.4 us (24%)
  Pallas kernels  10 us (23%)
  local copies, waits for them, and re-layouts  3.85 us (9%)
  between operations  0.71 us (2%)
    ppermute x4, starting transfers between devices, swap(): two = lax.ppermute(second, axis, odd + [(b, a) for a, b in odd])  10.1 us
    ppermute x4, waiting for transfers between devices, swap(): two = lax.ppermute(second, axis, odd + [(b, a) for a, b in odd])  7.27 us
    ppermute x4, starting transfers between devices, swap(): one = lax.ppermute(first, axis, [(i, i ^ 1) for i in range(size)])  4.51 us
    all_to_all x1, starting transfers between devices, body(): lax.all_to_all(payload.reshape(devices, 2, LANES), ('gx', 'gz'), 0, 0)  3.85 us
    unnamed x20, local copies, waits for them, and re-layouts  3.85 us
    pallas_call x1, Pallas kernels, body(): call(kernel, [block, block, (ROWS, LANES), (ROWS, LANES), (2 * devices, L...  2.61 us
    pallas_call x1, Pallas kernels, body(): call(solve_kernel, [block, block, wide, (ROWS, WIDE), (ROWS, WIDE), (8, L...  2.38 us
    ppermute x4, waiting for transfers between devices, swap(): one = lax.ppermute(first, axis, [(i, i ^ 1) for i in range(size)])  2.27 us
  transfers between devices with their start and end apart: 9, of which 8 were waited for; matrix products, arithmetic and copies ran while one was open for 0% of the time, Pallas kernels for 3%

profile of v1, /device:TPU:0, one launch (start us, length us, event | category | flops | bytes accessed | tf_op | source)
XLA Modules:
  0.0 43.4 jit_solution(12462787025016422652)
XLA Ops:
  0.6 0.9 %copy-done = f32[16,16,128]{2,1,0:T(8,128)S(1)} copy-done((f32[16,16,128]{2,1,0:T(8,128)S(1)}, f32[16,16,128]{2,1,0:T(8,128)}, u32[]{:S(2)}) %copy-start) | copy-done | bytes 131096
  1.5 0.9 %copy-done.2 = f32[16,16,128]{2,1,0:T(8,128)S(1)} copy-done((f32[16,16,128]{2,1,0:T(8,128)S(1)}, f32[16,16,128]{2,1,0:T(8,128)}, u32[]{:S(2)}) %copy-start.2) | copy-done | bytes 131096
  2.4 0.7 %copy-done.7 = f32[3,2,2,16]{3,2,1,0:T(2,128)S(1)} copy-done((f32[3,2,2,16]{3,2,1,0:T(2,128)S(1)}, f32[3,2,2,16]{3,2,1,0:T(2,128)}, u32[]{:S(2)}) %copy-start.7) | copy-done | bytes 792
  3.9 4.7 %collective-permute-start.1 = (f32[9,16,128]{2,1,0:T(8,128)S(1)}, f32[9,16,128]{2,1,0:T(8,128)S(1)}, u32[]{:S(2)}, u32[]{:S(2)}) collective-permute-start(f32[9,16,128]{2,1,0:T(8,128)S(1)} %get-tuple-element.25), channel_id=1, source_target_pairs={{1,2},{3,4},{5,6},{7,0},{2,1},{4,3},{6,5},{0,7},{9,10},{11,12},{13... | collective-permute-start | bytes 221192 | tf_op jit(solution)/shard_map/ppermute | solution.py:643
  8.6 1.3 %prepare.1 = (f32[3,128,128]{2,1,0:T(8,128)S(1)}, f32[3,8,8,128]{3,2,1,0:T(8,128)S(1)}) custom-call(f32[8,8]{1,0:T(8,128)S(1)} %copy-done.3, f32[8,8]{1,0:T(8,128)S(1)} %copy-done.4), custom_call_target="tpu_custom_call" | custom-call | tf_op jit(solution)/shard_map/prepare/pallas_call | solution.py:661
  9.9 0.8 %collective-permute-done.1.second = f32[9,16,128]{2,1,0:T(8,128)S(1)} collective-permute-done((f32[9,16,128]{2,1,0:T(8,128)S(1)}, f32[9,16,128]{2,1,0:T(8,128)S(1)}, u32[]{:S(2)}, u32[]{:S(2)}) %collective-permute-start.1) | collective-permute-done | bytes 73760 | tf_op jit(solution)/shard_map/ppermute | solution.py:643
  10.7 1.3 %start.1 = (f32[16,16,128]{2,1,0:T(8,128)S(1)}, f32[16,16,256]{2,1,0:T(8,128)S(1)}, f32[16,256]{1,0:T(8,128)S(1)}, f32[40,256]{1,0:T(8,128)S(1)}, f32[40,256]{1,0:T(8,128)S(1)}) custom-call(f32[16,16,128]{2,1,0:T(8,128)S(1)} %copy-done.1, f32[16,16,128]{2,1,0:T(8,128)S(1)} %copy-done.2, f32[16,128]{1,0:T(8,128)S(1)} %get-tuple-element.23.own_metrics, ...), custom_call_target="tpu_custom_call" | custom-call | tf_op jit(solution)/shard_map/start/pallas_call | solution.py:666
  12.0 1.6 %collective-permute-start.2 = (f32[40,256]{1,0:T(8,128)S(1)}, f32[40,256]{1,0:T(8,128)S(1)}, u32[]{:S(2)}, u32[]{:S(2)}) collective-permute-start(f32[40,256]{1,0:T(8,128)S(1)} %get-tuple-element.31.own_a), channel_id=1, source_target_pairs={{0,8},{8,0},{16,24},{24,16},{1,9},{9,1},{17,25},{25,17},{2,10},{10... | collective-permute-start | bytes 122888 | tf_op jit(solution)/shard_map/ppermute | solution.py:642
  13.6 1.5 %collective-permute-start.3 = (f32[40,256]{1,0:T(8,128)S(1)}, f32[40,256]{1,0:T(8,128)S(1)}, u32[]{:S(2)}, u32[]{:S(2)}) collective-permute-start(f32[40,256]{1,0:T(8,128)S(1)} %get-tuple-element.32.own_b), channel_id=1, source_target_pairs={{8,16},{24,0},{16,8},{0,24},{9,17},{25,1},{17,9},{1,25},{10,18},{2... | collective-permute-start | bytes 122888 | tf_op jit(solution)/shard_map/ppermute | solution.py:643
  15.1 1.1 %collective-permute-done.2.got_a.refs_6_ = f32[40,256]{1,0:T(8,128)S(1)} collective-permute-done((f32[40,256]{1,0:T(8,128)S(1)}, f32[40,256]{1,0:T(8,128)S(1)}, u32[]{:S(2)}, u32[]{:S(2)}) %collective-permute-start.2) | collective-permute-done | bytes 40992 | tf_op jit(solution)/shard_map/ppermute | solution.py:642
  16.2 2.3 %collective-permute-done.3.got_b.refs_7_ = f32[40,256]{1,0:T(8,128)S(1)} collective-permute-done((f32[40,256]{1,0:T(8,128)S(1)}, f32[40,256]{1,0:T(8,128)S(1)}, u32[]{:S(2)}, u32[]{:S(2)}) %collective-permute-start.3) | collective-permute-done | bytes 40992 | tf_op jit(solution)/shard_map/ppermute | solution.py:643
  18.5 0.7 %copy-done.9 = f32[8]{0:T(128)S(1)} copy-done((f32[8]{0:T(128)S(1)}, f32[8]{0:T(128)}, u32[]{:S(2)}) %copy-start.9) | copy-done | bytes 56
  19.1 2.4 %solve.1 = (f32[16,16,128]{2,1,0:T(8,128)S(1)}, f32[16,16,128]{2,1,0:T(8,128)S(1)}, f32[16,16,256]{2,1,0:T(8,128)S(1)}, f32[16,256]{1,0:T(8,128)S(1)}, f32[16,256]{1,0:T(8,128)S(1)}, /*index=5*/f32[8,128]{1,0:T(8,128)S(1)}) custom-call(f32[16,16,128]{2,1,0:T(8,128)S(1)} %get-tuple-element.28.start, f32[16,16,256]{2,1,0:T(8,128)S(1)} %get-tuple-element.29.rest, ...), custom_call_target="tpu_custom_call" | custom-call | tf_op jit(solution)/shard_map/solve/pallas_call | solution.py:675
  22.1 2.4 %collective-permute-start.5 = (f32[16,256]{1,0:T(8,128)S(1)}, f32[16,256]{1,0:T(8,128)S(1)}, u32[]{:S(2)}, u32[]{:S(2)}) collective-permute-start(f32[16,256]{1,0:T(8,128)S(1)} %get-tuple-element.37), channel_id=1, source_target_pairs={{8,16},{24,0},{16,8},{0,24},{9,17},{25,1},{17,9},{1,25},{10,18},{2... | collective-permute-start | bytes 49160 | tf_op jit(solution)/shard_map/ppermute | solution.py:643
  24.6 0.8 %collective-permute-done.4.got_a = f32[16,256]{1,0:T(8,128)S(1)} collective-permute-done((f32[16,256]{1,0:T(8,128)S(1)}, f32[16,256]{1,0:T(8,128)S(1)}, u32[]{:S(2)}, u32[]{:S(2)}) %collective-permute-start.4) | collective-permute-done | bytes 16416 | tf_op jit(solution)/shard_map/ppermute | solution.py:642
  25.3 1.4 %collective-permute-done.5.got_b = f32[16,256]{1,0:T(8,128)S(1)} collective-permute-done((f32[16,256]{1,0:T(8,128)S(1)}, f32[16,256]{1,0:T(8,128)S(1)}, u32[]{:S(2)}, u32[]{:S(2)}) %collective-permute-start.5) | collective-permute-done | bytes 16416 | tf_op jit(solution)/shard_map/ppermute | solution.py:643
  26.8 0.7 %copy-done.8 = f32[2,64]{1,0:T(2,128)S(1)} copy-done((f32[2,64]{1,0:T(2,128)S(1)}, f32[2,64]{1,0:T(2,128)}, u32[]{:S(2)}) %copy-start.8) | copy-done | bytes 536
  27.5 2.6 %image.1 = (f32[16,16,128]{2,1,0:T(8,128)S(1)}, f32[16,16,128]{2,1,0:T(8,128)S(1)}, f32[16,128]{1,0:T(8,128)S(1)}, f32[16,128]{1,0:T(8,128)S(1)}, f32[64,128]{1,0:T(8,128)}) custom-call(f32[16,16,256]{2,1,0:T(8,128)S(1)} %get-tuple-element.35.local, f32[16,256]{1,0:T(8,128)S(1)} %get-tuple-element.30.metrics.refs_8_, ...), custom_call_target="tpu_custom_call" | custom-call | tf_op jit(solution)/shard_map/image/pallas_call | solution.py:697
  30.1 3.8 %all-to-all-start = ((f32[32,2,128]{2,1,0:T(2,128)}), f32[32,2,128]{2,1,0:T(2,128)S(1)}, u32[]{:S(2)}, u32[]{:S(2)}) async-start(f32[32,2,128]{2,1,0:T(2,128)} %bitcast), calls=%async_computation | async-start | bytes 65536 | tf_op jit(solution)/shard_map/all_to_all | solution.py:705
  33.9 1.8 %collective-permute-start.6 = (f32[16,128]{1,0:T(8,128)S(1)}, f32[16,128]{1,0:T(8,128)S(1)}, u32[]{:S(2)}, u32[]{:S(2)}) collective-permute-start(f32[16,128]{1,0:T(8,128)S(1)} %get-tuple-element.41), channel_id=1, source_target_pairs={{0,8},{8,0},{16,24},{24,16},{1,9},{9,1},{17,25},{25,17},{2,10},{10... | collective-permute-start | bytes 24584 | tf_op jit(solution)/shard_map/ppermute | solution.py:642
  35.8 1.5 %collective-permute-start.7 = (f32[16,128]{1,0:T(8,128)S(1)}, f32[16,128]{1,0:T(8,128)S(1)}, u32[]{:S(2)}, u32[]{:S(2)}) collective-permute-start(f32[16,128]{1,0:T(8,128)S(1)} %get-tuple-element.42), channel_id=1, source_target_pairs={{8,16},{24,0},{16,8},{0,24},{9,17},{25,1},{17,9},{1,25},{10,18},{2... | collective-permute-start | bytes 24584 | tf_op jit(solution)/shard_map/ppermute | solution.py:643
  37.7 2.7 %collective-permute-done.7.refs_5_ = f32[16,128]{1,0:T(8,128)S(1)} collective-permute-done((f32[16,128]{1,0:T(8,128)S(1)}, f32[16,128]{1,0:T(8,128)S(1)}, u32[]{:S(2)}, u32[]{:S(2)}) %collective-permute-start.7) | collective-permute-done | bytes 8224 | tf_op jit(solution)/shard_map/ppermute | solution.py:643
  40.3 0.8 %all-to-all-done = f32[32,2,128]{2,1,0:T(2,128)S(1)} async-done(((f32[32,2,128]{2,1,0:T(2,128)}), f32[32,2,128]{2,1,0:T(2,128)S(1)}, u32[]{:S(2)}, u32[]{:S(2)}) %all-to-all-start) | async-done | bytes 32800 | tf_op jit(solution)/shard_map/all_to_all | solution.py:705
  41.2 2.2 %finish.1 = (f32[16,16,128]{2,1,0:T(8,128)}, f32[16,16,128]{2,1,0:T(8,128)}) custom-call(f32[16,16,128]{2,1,0:T(8,128)S(1)} %get-tuple-element.33.refs_0_, f32[16,16,128]{2,1,0:T(8,128)S(1)} %get-tuple-element.34.refs_1_, f32[16,16,128]{2,1,0:T(8,128)S(1)} %get-tuple-element.39.refs_2_, f32[16,16,128]{2,1,0:T(8,128)S(1)} %get-tuple-element.40.refs_3_, ...), custom_call_target="tpu_custom_call" | custom-call | tf_op jit(solution)/shard_map/finish/pallas_call | solution.py:731
  (20 shorter events, 1.8 us)
Async XLA Ops:
  0.6 0.9 %copy-start = (f32[16,16,128]{2,1,0:T(8,128)S(1)}, f32[16,16,128]{2,1,0:T(8,128)}, u32[]{:S(2)}) copy-start(f32[16,16,128]{2,1,0:T(8,128)} %source.3) | copy-start | bytes 393220
  1.5 0.9 %copy-start.2 = (f32[16,16,128]{2,1,0:T(8,128)S(1)}, f32[16,16,128]{2,1,0:T(8,128)}, u32[]{:S(2)}) copy-start(f32[16,16,128]{2,1,0:T(8,128)} %previous.3) | copy-start | bytes 393220
  2.4 0.7 %copy-start.7 = (f32[3,2,2,16]{3,2,1,0:T(2,128)S(1)}, f32[3,2,2,16]{3,2,1,0:T(2,128)}, u32[]{:S(2)}) copy-start(f32[3,2,2,16]{3,2,1,0:T(2,128)} %coefficients.1) | copy-start | bytes 2308
  3.1 5.5 %copy-start.3 = (f32[8,8]{1,0:T(8,128)S(1)}, f32[8,8]{1,0:T(8,128)}, u32[]{:S(2)}) copy-start(f32[8,8]{1,0:T(8,128)} %refs_9_.1) | copy-start | bytes 772
  3.1 5.5 %copy-start.4 = (f32[8,8]{1,0:T(8,128)S(1)}, f32[8,8]{1,0:T(8,128)}, u32[]{:S(2)}) copy-start(f32[8,8]{1,0:T(8,128)} %vectors.3) | copy-start | bytes 772
  3.1 7.6 %copy-start.1 = (f32[16,16,128]{2,1,0:T(8,128)S(1)}, f32[16,16,128]{2,1,0:T(8,128)}, u32[]{:S(2)}) copy-start(f32[16,16,128]{2,1,0:T(8,128)} %source.3) | copy-start | bytes 393220
  3.4 6.5 %collective-permute-start = (f32[9,16,128]{2,1,0:T(8,128)S(1)}, f32[9,16,128]{2,1,0:T(8,128)S(1)}, u32[]{:S(2)}, u32[]{:S(2)}) collective-permute-start(f32[9,16,128]{2,1,0:T(8,128)S(1)} %get-tuple-element.24), channel_id=1, source_target_pairs={{0,1},{1,0},{2,3},{3,2},{4,5},{5,4},{6,7},{7,6},{8,9},{9,8},{10,11... | collective-permute-start | bytes 221192 | tf_op jit(solution)/shard_map/ppermute | solution.py:642
  3.9 6.9 %collective-permute-start.1 = (f32[9,16,128]{2,1,0:T(8,128)S(1)}, f32[9,16,128]{2,1,0:T(8,128)S(1)}, u32[]{:S(2)}, u32[]{:S(2)}) collective-permute-start(f32[9,16,128]{2,1,0:T(8,128)S(1)} %get-tuple-element.25), channel_id=1, source_target_pairs={{1,2},{3,4},{5,6},{7,0},{2,1},{4,3},{6,5},{0,7},{9,10},{11,12},{13... | collective-permute-start | bytes 221192 | tf_op jit(solution)/shard_map/ppermute | solution.py:643
  12.0 4.1 %collective-permute-start.2 = (f32[40,256]{1,0:T(8,128)S(1)}, f32[40,256]{1,0:T(8,128)S(1)}, u32[]{:S(2)}, u32[]{:S(2)}) collective-permute-start(f32[40,256]{1,0:T(8,128)S(1)} %get-tuple-element.31.own_a), channel_id=1, source_target_pairs={{0,8},{8,0},{16,24},{24,16},{1,9},{9,1},{17,25},{25,17},{2,10},{10... | collective-permute-start | bytes 122888 | tf_op jit(solution)/shard_map/ppermute | solution.py:642
  13.6 4.9 %collective-permute-start.3 = (f32[40,256]{1,0:T(8,128)S(1)}, f32[40,256]{1,0:T(8,128)S(1)}, u32[]{:S(2)}, u32[]{:S(2)}) collective-permute-start(f32[40,256]{1,0:T(8,128)S(1)} %get-tuple-element.32.own_b), channel_id=1, source_target_pairs={{8,16},{24,0},{16,8},{0,24},{9,17},{25,1},{17,9},{1,25},{10,18},{2... | collective-permute-start | bytes 122888 | tf_op jit(solution)/shard_map/ppermute | solution.py:643
  18.5 0.7 %copy-start.9 = (f32[8]{0:T(128)S(1)}, f32[8]{0:T(128)}, u32[]{:S(2)}) copy-start(f32[8]{0:T(128)} %eigen.1) | copy-start | bytes 100
  19.1 7.6 %copy-start.5 = (s32[8,2,2,16]{3,2,1,0:T(2,128)S(1)}, s32[8,2,2,16]{3,2,1,0:T(2,128)}, u32[]{:S(2)}) copy-start(s32[8,2,2,16]{3,2,1,0:T(2,128)} %labels.1) | copy-start | bytes 6148
  21.5 3.8 %collective-permute-start.4 = (f32[16,256]{1,0:T(8,128)S(1)}, f32[16,256]{1,0:T(8,128)S(1)}, u32[]{:S(2)}, u32[]{:S(2)}) collective-permute-start(f32[16,256]{1,0:T(8,128)S(1)} %get-tuple-element.36), channel_id=1, source_target_pairs={{0,8},{8,0},{16,24},{24,16},{1,9},{9,1},{17,25},{25,17},{2,10},{10... | collective-permute-start | bytes 49160 | tf_op jit(solution)/shard_map/ppermute | solution.py:642
  22.1 4.6 %collective-permute-start.5 = (f32[16,256]{1,0:T(8,128)S(1)}, f32[16,256]{1,0:T(8,128)S(1)}, u32[]{:S(2)}, u32[]{:S(2)}) collective-permute-start(f32[16,256]{1,0:T(8,128)S(1)} %get-tuple-element.37), channel_id=1, source_target_pairs={{8,16},{24,0},{16,8},{0,24},{9,17},{25,1},{17,9},{1,25},{10,18},{2... | collective-permute-start | bytes 49160 | tf_op jit(solution)/shard_map/ppermute | solution.py:643
  26.8 0.7 %copy-start.8 = (f32[2,64]{1,0:T(2,128)S(1)}, f32[2,64]{1,0:T(2,128)}, u32[]{:S(2)}) copy-start(f32[2,64]{1,0:T(2,128)} %coarse.1) | copy-start | bytes 1540
  30.1 11.1 %all-to-all-start = ((f32[32,2,128]{2,1,0:T(2,128)}), f32[32,2,128]{2,1,0:T(2,128)S(1)}, u32[]{:S(2)}, u32[]{:S(2)}) async-start(f32[32,2,128]{2,1,0:T(2,128)} %bitcast), calls=%async_computation | async-start | bytes 65536 | tf_op jit(solution)/shard_map/all_to_all | solution.py:705
  33.9 7.2 %copy-start.6 = (f32[3,8,128]{2,1,0:T(8,128)S(1)}, f32[3,8,128]{2,1,0:T(8,128)}, u32[]{:S(2)}) copy-start(f32[3,8,128]{2,1,0:T(8,128)} %constant.2.clone.refs_12_) | copy-start | bytes 36868
  33.9 3.7 %collective-permute-start.6 = (f32[16,128]{1,0:T(8,128)S(1)}, f32[16,128]{1,0:T(8,128)S(1)}, u32[]{:S(2)}, u32[]{:S(2)}) collective-permute-start(f32[16,128]{1,0:T(8,128)S(1)} %get-tuple-element.41), channel_id=1, source_target_pairs={{0,8},{8,0},{16,24},{24,16},{1,9},{9,1},{17,25},{25,17},{2,10},{10... | collective-permute-start | bytes 24584 | tf_op jit(solution)/shard_map/ppermute | solution.py:642
  35.8 4.6 %collective-permute-start.7 = (f32[16,128]{1,0:T(8,128)S(1)}, f32[16,128]{1,0:T(8,128)S(1)}, u32[]{:S(2)}, u32[]{:S(2)}) collective-permute-start(f32[16,128]{1,0:T(8,128)S(1)} %get-tuple-element.42), channel_id=1, source_target_pairs={{8,16},{24,0},{16,8},{0,24},{9,17},{25,1},{17,9},{1,25},{10,18},{2... | collective-permute-start | bytes 24584 | tf_op jit(solution)/shard_map/ppermute | solution.py:643

commit v2 on v1

v2 whole, which is shorter than its diff:
```python
import functools

import jax
import jax.numpy as jnp
import numpy as np
from jax import lax
from jax.experimental import pallas as pl
from jax.experimental.pallas import tpu as pltpu
from jax.sharding import PartitionSpec as P

POINTS = [
    -1.0,
    -0.8717401485096066,
    -0.5917001814331423,
    -0.2092992179024789,
    0.2092992179024789,
    0.5917001814331423,
    0.8717401485096066,
    1.0,
]
WEIGHTS = [
    0.03571428571428571,
    0.21070422714350603,
    0.34112269248350435,
    0.4124587946587038,
    0.4124587946587038,
    0.34112269248350435,
    0.21070422714350603,
    0.03571428571428571,
]
ONES = [1.0] * 8
LOW = [(1.0 - s) / 2.0 for s in POINTS]
HIGH = [(1.0 + s) / 2.0 for s in POINTS]
EXACT = lax.Precision.HIGHEST

ROWS = 16
LANES = 128
WIDE = 256
HALO = 32
PAIRS = ((0, 0), (0, 1), (1, 1))
GROUP_X = (ONES + LOW, [0.0] * 8 + HIGH)
INVERSE_X = [0.5] + [1.0] * 6 + [0.5] + [0.5] + [1.0] * 6 + [0.5]


def iota(shape, dim):
    return lax.broadcasted_iota(jnp.int32, shape, dim)


def pick(index, values):
    result = jnp.full(index.shape, values[0], jnp.float32)
    for i in range(1, 8):
        result = jnp.where(index == i, values[i], result)
    return result


def even_index(axis):
    return lax.rem(lax.axis_index(axis), 2) == 0


class Geometry:
    def __init__(self, lanes):
        shape = (2, 8, lanes)
        self.element_y, self.row, lane = iota(shape, 0), iota(shape, 1), iota(shape, 2)
        self.position = lane & 7
        self.first = self.position == 0
        self.last = self.position == 7
        self.edge = self.first | self.last
        self.weight_y = pick(self.row, WEIGHTS)
        self.weight_z = pick(self.position, WEIGHTS)
        self.inverse_z = jnp.where(self.edge, 0.5, 1.0)
        self.wall = (self.element_y == 1) & (self.row == 7)
        inner = ((self.element_y == 0) & (self.row == 7)) | ((self.element_y == 1) & (self.row == 0))
        self.inverse_y = jnp.where(inner, 0.5, 1.0)
        self.keep = jnp.where(self.wall, 0.0, 1.0)
        self.lanes = lanes

    def pair_y(self, v):
        lower, upper = v[0], v[1]
        row = self.row[0]
        up = jnp.where(row == 7, pltpu.roll(upper, 7, 0), 0.0)
        down = jnp.where(row == 0, pltpu.roll(lower, 1, 0), 0.0)
        return jnp.stack([lower + up, upper + down])

    def pair_z(self, v):
        flat = v.reshape(16, self.lanes)
        after = pltpu.roll(flat, self.lanes - 1, 1).reshape(v.shape)
        before = pltpu.roll(flat, 1, 1).reshape(v.shape)
        return v + jnp.where(self.edge, jnp.where(self.last, after, before), 0.0)

    def pair(self, v):
        return self.pair_z(self.pair_y(v))

    def assemble(self, v):
        return self.pair(v) * self.keep


def solid(v):
    return v.reshape(ROWS, v.shape[-1])


def split(v):
    return v.reshape(2, 8, v.shape[-1])


def own(v):
    return v[..., :LANES]


def down(v):
    return jnp.sum(v.reshape(ROWS, LANES), axis=0, keepdims=True)


def line_of(ref, at, lanes):
    row = ref[at : at + 1, :]
    return jnp.concatenate([row] * (lanes // LANES), axis=1)[None]


def contract_x(rows, table, i, transpose=False):
    total = None
    for p in range(8):
        factor = line_of(table, p * 8 + i if transpose else i * 8 + p, WIDE)
        term = factor * rows[p]
        total = term if total is None else total + term
    return total


def contract_y(v, diagonals):
    total = diagonals[0] * v
    for d in range(1, 8):
        rolled = jnp.stack([pltpu.roll(v[e], 8 - d, 0) for e in range(2)])
        total = total + diagonals[d] * rolled
    return total


def thirds(v):
    high = v.astype(jnp.bfloat16)
    rest = v - high.astype(jnp.float32)
    middle = rest.astype(jnp.bfloat16)
    return high, middle, (rest - middle.astype(jnp.float32)).astype(jnp.bfloat16)


def contract_z(flat, upper, lower, which):
    pieces = []
    for at in range(0, flat.shape[1], LANES):
        high, middle, low = thirds(flat[:, at : at + LANES])
        one = jnp.dot(
            jnp.concatenate([high, middle], axis=1), upper[which], preferred_element_type=jnp.float32
        )
        two = jnp.dot(jnp.concatenate([low, high], axis=1), lower[which], preferred_element_type=jnp.float32)
        pieces.append(one[:, :LANES] + (one[:, LANES:] + two))
    return pieces[0] if len(pieces) == 1 else jnp.concatenate(pieces, axis=1)


def wide_diagonals(ref, which):
    return [jnp.concatenate([ref[which, d]] * (WIDE // LANES), axis=1)[None] for d in range(8)]


def metric(ref, component, element):
    at = (component * 2 + element) * 2
    return jnp.stack([jnp.broadcast_to(ref[at + e : at + e + 1, :], (8, WIDE)) for e in range(2)])


def scaled_metrics(geo, c):
    return c[0] * geo.weight_y * geo.weight_z, c[1] * geo.weight_z, c[2] * geo.weight_y


def stored_factors(ref, element):
    return [split(ref[c, element]) for c in range(3)]


def apply_rows(rows, along_z, factors, stiffness, diagonals):
    result = []
    for element in range(2):
        factor_x, factor_y, factor_z = factors[element]
        inside = rows[element * 8 : element * 8 + 8]
        for i in range(8):
            x = element * 8 + i
            term_y = factor_y * contract_y(inside[i], diagonals)
            term_z = factor_z * split(along_z[x * 16 : x * 16 + 16])
            result.append(factor_x * contract_x(inside, stiffness, i) + WEIGHTS[i] * (term_y + term_z))
    return result


def join_middle(rows):
    middle = rows[7] + rows[8]
    return rows[:7] + [middle, middle] + rows[9:]


def group_lanes(lanes, group):
    lane = iota((1, lanes), 1)
    signed = jnp.where(lane < lanes // 2 + lanes // 4, lane, lane - lanes) if lanes > LANES else lane
    element, position = signed >> 3, lane & 7
    low, high = pick(position, LOW), pick(position, HIGH)
    here = jnp.where((element >> 3) == group, low, 0.0)
    return here + jnp.where(((element + 1) >> 3) == group, high, 0.0)


def pack_kernel(source, previous, coefficients, first, second, metrics, near_source, near_previous, raw, scratch, ready):
    copies = [
        pltpu.make_async_copy(source, near_source, ready.at[0]),
        pltpu.make_async_copy(previous, near_previous, ready.at[1]),
        pltpu.make_async_copy(coefficients, raw, ready.at[2]),
    ]
    for copy in copies:
        copy.start()
    even = even_index("gz")
    scratch[...] = jnp.zeros_like(scratch)
    widen = (iota((16, LANES), 0) == (iota((16, LANES), 1) >> 3)).astype(jnp.float32)
    for copy in copies:
        copy.wait()
    for c in range(3):
        for element in range(2):
            at = (c * 2 + element) * 2
            scratch[at : at + 2, :] = raw[c, element]
    spread = jnp.dot(scratch[...], widen, precision=EXACT, preferred_element_type=jnp.float32)
    metrics[...] = spread
    group = iota((8 * ROWS, LANES), 1) // HALO
    parts = [
        ref[lo : lo + 8].reshape(8 * ROWS, LANES) for ref in (near_previous, near_source) for lo in (0, 8)
    ]
    for to_right, out in ((even, first), (jnp.logical_not(even), second)):
        base = jnp.where(to_right, HALO, 0)
        packed = None
        for k, part in enumerate(parts):
            moved = pltpu.roll(part, lax.rem(base + HALO * k, LANES), 1)
            packed = moved if packed is None else jnp.where(group == k, moved, packed)
        out[0:8] = packed.reshape(8, ROWS, LANES)
        out[8] = spread


def prepare_kernel(
    with_coarse, metrics, stiffness, vectors, eigen, labels, coarse, tables,
    upper, lower, diagonals, stiff_table, vector_table, lam, lines, fixed, near_tables,
):
    near_tables[...] = tables[...]
    repeat = (iota((LANES, 8), 0) & 7 == iota((LANES, 8), 1)).astype(jnp.float32)
    same = (iota((LANES, LANES), 0) >> 3) == (iota((LANES, LANES), 1) >> 3)
    unit = (iota((8, 8), 0) == iota((8, 8), 1)).astype(jnp.float32)
    row, column = iota((8, 8), 0), iota((8, 8), 1)

    def dot(a, b, dims):
        return lax.dot_general(a, b, (dims, ((), ())), precision=EXACT, preferred_element_type=jnp.float32)

    def put_block(at, matrix):
        half = dot(repeat, matrix, ((1,), (0,)))
        block = jnp.where(same, dot(half, repeat, ((1,), (1,))), 0.0)
        high, middle, low = thirds(block)
        both = jnp.concatenate([high, middle], axis=1)
        upper[at] = jnp.concatenate([both, both], axis=0)
        lower[at] = jnp.concatenate([high, low], axis=0)

    def put_diagonals(at, matrix):
        for d in range(8):
            chosen = jnp.where(column == ((row + d) & 7), matrix, 0.0)
            diagonals[at, d] = jnp.broadcast_to(jnp.sum(chosen, axis=1, keepdims=True), (8, LANES))

    def put_table(out, matrix):
        tall = (iota((64, 8), 0) >> 3 == iota((64, 8), 1)).astype(jnp.float32)
        chosen = jnp.where(iota((64, 8), 0) & 7 == iota((64, 8), 1), dot(tall, matrix, ((1,), (0,))), 0.0)
        out[...] = jnp.broadcast_to(jnp.sum(chosen, axis=1, keepdims=True), (64, LANES))

    k, s = stiffness[...], vectors[...]
    k_turned, s_turned = dot(k, unit, ((0,), (0,))), dot(s, unit, ((0,), (0,)))
    for at, matrix in enumerate((k_turned, s, s_turned)):
        put_block(at, matrix)
    for at, matrix in enumerate((k, s_turned, s)):
        put_diagonals(at, matrix)
    put_table(stiff_table, k)
    put_table(vector_table, s)
    values = [eigen[i] for i in range(8)]
    lam[0] = pick(iota((8, LANES), 0), values)
    lam[1] = pick(iota((8, LANES), 1) & 7, values)
    stiff_lines = []
    for at, line in enumerate((ONES, LOW, HIGH)):
        total = jnp.sum(k * pick(column, line), axis=1, keepdims=True)
        stiff_lines.append(jnp.broadcast_to(total, (8, LANES)))
        lines[at] = stiff_lines[at]

    groups = [group_lanes(LANES, b) for b in range(3)]
    stacked = jnp.concatenate(groups + [jnp.zeros((13, LANES), jnp.float32)], axis=0)
    stiff_z = contract_z(stacked, upper, lower, 0)
    weight_z = pick(iota((1, LANES), 1) & 7, WEIGHTS)
    node = iota((8, LANES), 0)
    mass_y = [sum(WEIGHTS), sum(WEIGHTS[:7])]
    last = jnp.broadcast_to(k[:, 7:8], (8, LANES))
    inner = jnp.where(node == 7, 0.0, stiff_lines[0] - last)
    stiff_y = [jnp.sum(v, axis=0, keepdims=True) for v in (stiff_lines[0], inner)]
    at = 0
    for a, b in PAIRS:
        across, along = jnp.zeros((1, LANES), jnp.float32), jnp.zeros((1, LANES), jnp.float32)
        for element in range(2):
            fa = GROUP_X[a][element * 8 : element * 8 + 8]
            fb = GROUP_X[b][element * 8 : element * 8 + 8]
            if not (any(fa) and any(fb)):
                continue
            mass_x = sum(w * p * q for w, p, q in zip(WEIGHTS, fa, fb))
            applied = stiff_lines[0 if fb == ONES else 1 + b]
            stiff_x = jnp.sum(applied * pick(node, fa), axis=0, keepdims=True)
            for e in range(2):
                cx, cy, cz = (metrics[(c * 2 + element) * 2 + e, :].reshape(1, LANES) for c in range(3))
                across = across + cx * (stiff_x * mass_y[e]) + cy * (stiff_y[e] * mass_x)
                along = along + cz * (mass_x * mass_y[e])
        across = across * weight_z
        for b in range(3):
            fixed[at : at + 1] = across * groups[b] + along * stiff_z[b : b + 1]
            at += 1
    fixed[9:16] = jnp.zeros((7, LANES), jnp.float32)
    place = iota((1, LANES), 1)
    numbers = jnp.zeros((1, LANES), jnp.float32)
    for a in range(2):
        for b in range(3):
            corner, x, z = 4 * a + (b == 2), a, (0, 8, 15)[b]
            number = labels[corner, x, 0, z].astype(jnp.float32)
            numbers = jnp.where(place == 8 * (3 * a + b) + 4, number, numbers)
    fixed[16:17] = numbers
    below = jnp.zeros((1, LANES), jnp.float32)
    if with_coarse:
        per, count = coarse.shape
        below = [coarse[i : i + 1, :] for i in range(per)]
        if per * count < LANES:
            below.append(jnp.zeros((1, LANES - per * count), jnp.float32))
        below = jnp.concatenate(below, axis=1)
    fixed[17:18] = below
    fixed[18:24] = jnp.zeros((6, LANES), jnp.float32)


def start_kernel(
    source, previous, own_metrics, first, second, stiffness, upper, lower, diagonals,
    start, rest, metrics, factors, message_a, message_b,
):
    even = even_index("gz")
    lane = iota((ROWS, LANES), 1)

    def beyond(plane, right_shift, left_shift, fill):
        a, b = first[plane], second[plane]
        right, left = jnp.where(even, a, b), jnp.where(even, b, a)
        if right_shift:
            right = pltpu.roll(right, right_shift, 1)
        if left_shift:
            left = pltpu.roll(left, left_shift, 1)
        return jnp.where(lane < HALO, right, jnp.where(lane >= LANES - HALO, left, fill))

    def wide(ref, x, kind):
        slot = 2 * kind + x // 8
        right_shift = (LANES - HALO * slot) % LANES
        left_shift = (LANES - HALO - HALO * slot) % LANES
        return split(jnp.concatenate([ref[x], beyond(x % 8, right_shift, left_shift, 0.0)], axis=1))

    geo = Geometry(WIDE)
    metrics[:, :LANES] = own_metrics[...]
    metrics[:, LANES:] = beyond(8, 0, 0, 1.0)
    factor = geo.keep * geo.inverse_y * geo.inverse_z
    rows = [geo.pair(wide(previous, x, 0)) * (factor * INVERSE_X[x]) for x in range(ROWS)]
    rows = join_middle(rows)
    faces = (rows[0], rows[15])
    rows[0] = rows[15] = jnp.zeros_like(rows[0])
    for x in range(ROWS):
        start[x] = solid(own(rows[x]))
    along_z = contract_z(jnp.concatenate([solid(v) for v in rows], axis=0), upper, lower, 0)
    scaled = [scaled_metrics(geo, [metric(metrics, c, e) for c in range(3)]) for e in range(2)]
    for e in range(2):
        for c in range(3):
            factors[c, e] = solid(scaled[e][c])
    applied = apply_rows(rows, along_z, scaled, stiffness, wide_diagonals(diagonals, 0))
    for x in range(ROWS):
        rest[x] = solid(wide(source, x, 1) - applied[x])
    even_x = even_index("gx")

    def choose(right, left):
        return jnp.where(even_x, right, left), jnp.where(even_x, left, right)

    for at, right, left in ((0, solid(faces[1]), solid(faces[0])), (16, rest[15], rest[0])):
        message_a[at : at + 16], message_b[at : at + 16] = choose(right, left)
    for c in range(3):
        at = 32 + 2 * c
        right, left = metrics[(c * 2 + 1) * 2 : (c * 2 + 1) * 2 + 2], metrics[c * 4 : c * 4 + 2]
        message_a[at : at + 2], message_b[at : at + 2] = choose(right, left)
    message_a[38:40] = jnp.zeros((2, WIDE), jnp.float32)
    message_b[38:40] = jnp.zeros((2, WIDE), jnp.float32)


def sided(even, a, b, at, size=16):
    one, two = a[at : at + size], b[at : at + size]
    return jnp.where(even, one, two), jnp.where(even, two, one)


def face_metrics(even, a, b):
    sides = [[], []]
    for c in range(3):
        for side, pair in enumerate(sided(even, a, b, 32 + 2 * c, 2)):
            sides[side].append(jnp.stack([jnp.broadcast_to(pair[e : e + 1], (8, WIDE)) for e in range(2)]))
    return sides


def coarse_pieces(geo, factors, stiff_keep, functions, stiff_functions):
    factor_x, factor_y, factor_z = factors
    kept_x, kept_y, kept_z = factor_x * geo.keep, factor_y * stiff_keep, factor_z * geo.keep
    result = []
    for plain, turned in zip(functions, stiff_functions):
        result.append(
            (geo.assemble(kept_x * plain[None]), geo.assemble(kept_y * plain[None] + kept_z * turned[None]))
        )
    return result


def wide_functions(upper, lower):
    functions = [group_lanes(WIDE, b) for b in (-1, 0, 1, 2)]
    stacked = jnp.concatenate(functions + [jnp.zeros((12, WIDE), jnp.float32)], axis=0)
    turned = contract_z(stacked, upper, lower, 0)
    return functions, [turned[b : b + 1] for b in range(4)]


def kept_stiffness(geo, lines, stiffness):
    row = iota((8, LANES), 0)
    last = jnp.zeros((8, LANES), jnp.float32)
    for j in range(8):
        last = jnp.where(row == j, stiffness[j * 8 + 7 : j * 8 + 8, :], last)
    both = jnp.stack([lines[0], lines[0] - last])
    return jnp.concatenate([both] * (WIDE // LANES), axis=2)


def ready_kernel(rest, metrics, factors, lam, stiffness, lines, upper, lower, known, inverse, pieces):
    geo = Geometry(WIDE)
    rows = join_middle([split(rest[x]) for x in range(ROWS)])
    for x in range(1, ROWS - 1):
        known[x] = solid(geo.assemble(rows[x]))
    known[0] = known[15] = jnp.zeros((ROWS, WIDE), jnp.float32)
    lam_y = jnp.concatenate([lam[0]] * (WIDE // LANES), axis=1)[None]
    lam_z = jnp.concatenate([lam[1]] * (WIDE // LANES), axis=1)[None]
    for element in range(2):
        cx, cy, cz = (metric(metrics, c, element) for c in range(3))
        base = cy * lam_y + cz * lam_z
        for i in range(8):
            inverse[element * 8 + i] = solid(1.0 / (cx * line_of(lam.at[0], i, WIDE) + base))
    functions, turned = wide_functions(upper, lower)
    stiff_keep = kept_stiffness(geo, lines, stiffness)
    for element in range(2):
        made = coarse_pieces(geo, stored_factors(factors, element), stiff_keep, functions, turned)
        for b in range(4):
            for k in range(2):
                pieces[element, k, b] = solid(own(made[b][k]))


def solve_kernel(
    rest, known, factors, inverse, own_a, own_b, got_a, got_b,
    stiffness, vectors, upper, lower, diagonals,
    start_faces, residual, local, message_a, message_b, sums,
):
    even = even_index("gx")
    geo = Geometry(WIDE)
    mine, theirs = sided(even, own_a, own_b, 0), sided(even, got_a, got_b, 0)
    right, left = split(mine[0] + theirs[0]), split(mine[1] + theirs[1])
    start_faces[0], start_faces[1] = solid(own(left)), solid(own(right))
    other_right, other_left = (split(v) for v in sided(even, got_a, got_b, 16))
    metrics_right, metrics_left = face_metrics(even, got_a, got_b)
    stiff = wide_diagonals(diagonals, 0)
    along_z = contract_z(jnp.concatenate([solid(left), solid(right)], axis=0), upper, lower, 0)
    rows = [split(known[x]) for x in range(ROWS)]
    for element, near, face, across, arrived, other, turned in (
        (0, 0, left, 7, other_left, metrics_left, along_z[:16]),
        (1, 7, right, 0, other_right, metrics_right, along_z[16:]),
    ):
        mine = stored_factors(factors, element)
        theirs = scaled_metrics(geo, other)
        scaled = mine[0] * face
        beside = line_of(stiffness, near * 9, WIDE) * scaled
        beside = beside + line_of(stiffness, across * 9, WIDE) * (theirs[0] * face)
        beside = beside + WEIGHTS[0] * (
            (mine[1] + theirs[1]) * contract_y(face, stiff) + (mine[2] + theirs[2]) * split(turned)
        )
        x = element * 8 + near
        rows[x] = geo.assemble(split(rest[x]) + arrived - beside)
        moved = geo.assemble(scaled)
        for i in range(8):
            if i != near:
                change = line_of(stiffness, i * 8 + near, WIDE) * moved
                x = element * 8 + i
                rows[x] = rows[x] - change
                if x in (7, 8):
                    rows[15 - x] = rows[15 - x] - change
    parts = [None, None]
    for x in range(ROWS):
        residual[x] = solid(own(rows[x]))
        for a in range(2):
            if GROUP_X[a][x] * INVERSE_X[x] != 0.0:
                term = (GROUP_X[a][x] * INVERSE_X[x]) * own(rows[x])
                parts[a] = term if parts[a] is None else parts[a] + term
    weight = own(geo.inverse_y * geo.inverse_z)
    for a in range(2):
        sums[a : a + 1] = down(parts[a] * weight)

    forward, backward = wide_diagonals(diagonals, 1), wide_diagonals(diagonals, 2)
    moved = []
    for element in range(2):
        inside = rows[element * 8 : element * 8 + 8]
        moved += [solid(contract_y(contract_x(inside, vectors, i, True), forward)) for i in range(8)]
    spectral = contract_z(jnp.concatenate(moved, axis=0), upper, lower, 1)
    divided = [spectral[x * 16 : x * 16 + 16] * inverse[x] for x in range(ROWS)]
    back = contract_z(jnp.concatenate(divided, axis=0), upper, lower, 2)
    solved = []
    for element in range(2):
        inside = [
            contract_y(split(back[x * 16 : x * 16 + 16]), backward) for x in range(element * 8, element * 8 + 8)
        ]
        solved += [contract_x(inside, vectors, i) for i in range(8)]
    total = None
    for x in range(ROWS):
        term = own(solved[x]) * own(rows[x])
        total = term if total is None else total + term
    sums[2:3] = down(total)
    sums[3:8] = jnp.zeros((5, LANES), jnp.float32)
    solved = [geo.assemble(v) for v in join_middle(solved)]
    for x in range(ROWS):
        local[x] = solid(solved[x])
    beside = []
    for element, near in ((0, 0), (1, 7)):
        total = None
        for p in range(8):
            if p != near:
                term = line_of(stiffness, near * 8 + p, WIDE) * solved[element * 8 + p]
                total = term if total is None else total + term
        beside.append(solid(total))
    for at, left_row, right_row in ((0, solid(solved[0]), solid(solved[15])), (16, beside[0], beside[1])):
        message_a[at : at + 16] = jnp.where(even, right_row, left_row)
        message_b[at : at + 16] = jnp.where(even, left_row, right_row)


def ahead_kernel(
    local, factors, far_a, far_b, stiffness, lines, upper, lower, diagonals,
    image, sums, face_factors, face_pieces,
):
    even = even_index("gx")
    geo = Geometry(WIDE)
    rows = [split(local[x]) for x in range(ROWS)]
    rows[0] = rows[15] = jnp.zeros_like(rows[0])
    along_z = contract_z(jnp.concatenate([solid(v) for v in rows], axis=0), upper, lower, 0)
    scaled = [stored_factors(factors, e) for e in range(2)]
    applied = apply_rows(rows, along_z, scaled, stiffness, wide_diagonals(diagonals, 0))
    total, parts = None, [None, None]
    for x in range(1, ROWS - 1):
        term = own(applied[x]) * own(rows[x])
        total = term if total is None else total + term
        for a in range(2):
            if GROUP_X[a][x] != 0.0:
                term = GROUP_X[a][x] * own(applied[x])
                parts[a] = term if parts[a] is None else parts[a] + term
    for at, value in enumerate(parts + [total]):
        sums[at : at + 1] = down(value * own(geo.keep))
    sums[3:8] = jnp.zeros((5, LANES), jnp.float32)
    joined = join_middle(applied)
    for x in range(1, ROWS - 1):
        image[x] = solid(own(geo.assemble(joined[x])))
    image[0] = image[15] = jnp.zeros((ROWS, LANES), jnp.float32)
    functions, turned = wide_functions(upper, lower)
    stiff_keep = kept_stiffness(geo, lines, stiffness)
    for side, raw in enumerate(face_metrics(even, far_a, far_b)):
        theirs = scaled_metrics(geo, raw)
        for c in range(3):
            face_factors[side, c] = solid(theirs[c])
        made = coarse_pieces(geo, theirs, stiff_keep, functions, turned)
        for b in range(4):
            for k in range(2):
                face_pieces[side, k, b] = solid(own(made[b][k]))


def image_kernel(
    known, factors, face_factors, own_a, own_b, got_a, got_b, first_sums, second_sums, fixed,
    stiffness, lines, upper, lower, diagonals,
    image, faces, payload,
):
    even = even_index("gx")
    geo = Geometry(WIDE)
    stiff = wide_diagonals(diagonals, 0)
    mine, theirs = sided(even, own_a, own_b, 0), sided(even, got_a, got_b, 0)
    mine_beside, theirs_beside = sided(even, own_a, own_b, 16), sided(even, got_a, got_b, 16)
    values = [mine[side] + theirs[side] for side in range(2)]
    along_z = contract_z(jnp.concatenate(values, axis=0), upper, lower, 0)
    extra = [second_sums[a : a + 1] for a in range(3)]
    rows = [known[x] for x in range(ROWS)]
    for side, element, near, across in ((0, 1, 7, 0), (1, 0, 0, 7)):
        value, arrived = split(values[side]), split(theirs[side])
        faces[1 - side] = solid(own(value))
        here, there = stored_factors(factors, element), [split(face_factors[side, c]) for c in range(3)]
        along_y, turned = contract_y(value, stiff), split(along_z[side * 16 : side * 16 + 16])
        beside = split(mine_beside[side])
        ours = here[0] * (beside + line_of(stiffness, near * 9, WIDE) * value)
        ours = ours + WEIGHTS[0] * (here[1] * along_y + here[2] * turned)
        other = there[0] * (split(theirs_beside[side]) + line_of(stiffness, across * 9, WIDE) * value)
        other = other + WEIGHTS[0] * (there[1] * along_y + there[2] * turned)
        rows[element * 8 + near] = solid(own(geo.assemble(ours + other)))
        spread = here[0] * value
        moved = solid(own(geo.assemble(spread)))
        for i in range(8):
            if i != near:
                change = stiffness[i * 8 + near : i * 8 + near + 1, :] * moved
                x = element * 8 + i
                rows[x] = rows[x] + change
                if x in (7, 8):
                    rows[15 - x] = rows[15 - x] + change
        near_only = own(spread * geo.keep)
        kept = own(ours * geo.keep)
        for a in range(2):
            line = GROUP_X[a][element * 8 : element * 8 + 8]
            if any(line):
                at = 0 if line == ONES else 1 + a
                factor = lines[at, near : near + 1, :]
                if line[near] != 0.0:
                    factor = factor - line[near] * stiffness[near * 9 : near * 9 + 1, :]
                    extra[a] = extra[a] + down(line[near] * kept)
                extra[a] = extra[a] + factor * down(near_only)
        extra[2] = extra[2] + down(own(beside) * near_only + own(value) * kept)
    for x in range(ROWS):
        image[x] = rows[x]
    zero = jnp.zeros((1, LANES), jnp.float32)
    table = jnp.concatenate(
        [first_sums[0:2], extra[0], extra[1], fixed[0:9], first_sums[2:3], extra[2], zero], axis=0
    )
    lane = iota((LANES, LANES), 1) & 7
    node = iota((LANES, LANES), 0)
    element, position = node >> 3, node & 7
    low, high = pick(position, LOW), pick(position, HIGH)
    columns = jnp.where(lane == (element >> 3), low, 0.0) + jnp.where(lane == ((element + 1) >> 3), high, 0.0)
    columns = jnp.where(lane == 3, 1.0, jnp.where(lane < 3, columns, 0.0))
    reduced = jnp.dot(table, columns, precision=EXACT, preferred_element_type=jnp.float32)
    mine = (iota((16, LANES), 1) >> 3) == iota((16, LANES), 0)
    row = jnp.sum(jnp.where(mine, reduced, 0.0), axis=0, keepdims=True) + fixed[16:17]
    block = jnp.concatenate([row, fixed[17:18]] * 4, axis=0)
    copies = payload.shape[0] // 8
    payload[...] = jnp.broadcast_to(block[None], (copies, 8, LANES)).reshape(copies * 8, LANES)


def lane_tables():
    one = np.zeros((8, LANES), np.float32)
    two = np.zeros((8, LANES), np.float32)
    top = np.zeros((8, LANES), np.float32)
    for a in range(2):
        for b in range(3):
            one[6, 8 * a + b], two[3 * a + b, 8 * a + b], top[0, 8 * a + b] = 1.0, 1.0, 1.0
            one[6, 8 * (2 + a) + b], two[3 * a + b, 8 * (2 + a) + b] = 2.0, 1.0
            top[1, 8 * (2 + a) + b] = 1.0
    for p, (a, other) in enumerate(PAIRS):
        for b in range(3):
            for c in range(3):
                at = 8 * (4 + 3 * p + b) + c
                one[3 * a + b, at] = 1.0 if a == other else 2.0
                two[3 * other + c, at] = 1.0
                top[1, at] = 1.0
    one[6, 8 * 13 + 3], two[6, 8 * 13 + 3], top[0, 8 * 13 + 3] = 1.0, 1.0, 1.0
    one[6, 8 * 14 + 3], two[6, 8 * 14 + 3], top[1, 8 * 14 + 3] = 1.0, 1.0, 1.0
    return np.stack([one, two, top])


def final_kernel(
    devices, spans, count, per,
    start, start_faces, residual, local, faces, image, pieces, face_pieces, lines, tables,
    gathered, given, new_solution, new_residual, values,
):
    rows = gathered[pl.ds(0, devices, stride=2), :]
    if given is None:
        spot = iota((devices, count), 1)
        hits = []
        rhs = [jnp.zeros((1, devices), jnp.float32) for _ in range(per)]
        owner = iota((devices, devices), 1)
        for k in range(6):
            label = rows[:, 8 * k + 4 : 8 * k + 5].astype(jnp.int32)
            at = 8 * (k // 3) + k % 3
            value = rows[:, at : at + 1]
            hits.append(spot == label)
            for q in range(per):
                chosen = jnp.where(owner * per + q == label, value, 0.0)
                rhs[q] = rhs[q] + jnp.sum(chosen, axis=0, keepdims=True)
        inverse = gathered[pl.ds(1, devices, stride=2), :]
        coarse = None
        for q in range(per):
            term = jnp.dot(
                rhs[q], inverse[:, q * count : q * count + count], precision=EXACT,
                preferred_element_type=jnp.float32,
            )
            coarse = term if coarse is None else coarse + term
        columns = [jnp.sum(jnp.where(hit, coarse, 0.0), axis=1, keepdims=True) for hit in hits]
        kept = jnp.zeros((devices, LANES), jnp.float32)
        for k in range(6):
            kept = jnp.where(iota((devices, LANES), 1) == k, columns[k], kept)
        values[...] = kept
    else:
        columns = [given[:, k : k + 1] for k in range(6)]
        values[...] = given[...]
    one, two = tables[0, 6:7, :], tables[1, 6:7, :]
    for k in range(6):
        one = one + columns[k] * tables[0, k : k + 1, :]
        two = two + columns[k] * tables[1, k : k + 1, :]
    product = jnp.sum(rows * one * two, axis=0, keepdims=True)
    numerator = jnp.sum(product * tables[2, 0:1, :], axis=1, keepdims=True)
    denominator = jnp.sum(product * tables[2, 1:2, :], axis=1, keepdims=True)
    alpha = numerator / denominator

    gx, gz = lax.axis_index("gx"), lax.axis_index("gz")
    before_x = lax.rem(gx + devices // spans - 1, devices // spans)
    before_z = lax.rem(gz + spans - 1, spans)
    here = values[pl.ds(gx * spans + gz, 1), :]
    behind = values[pl.ds(gx * spans + before_z, 1), :]
    aside = values[pl.ds(before_x * spans + gz, 1), :]
    corner = values[pl.ds(before_x * spans + before_z, 1), :]
    functions = [group_lanes(LANES, b) for b in range(3)]

    def four(line, back, a):
        return [back[:, 3 * a + 1 : 3 * a + 2]] + [line[:, 3 * a + b : 3 * a + b + 1] for b in range(3)]

    def mix(numbers, ref):
        total = numbers[0] * ref[0]
        for b in range(1, 4):
            total = total + numbers[b] * ref[b]
        return total

    near, right, left = four(here, behind, 0), four(here, behind, 1), four(aside, corner, 0)
    line_near = sum(near[1 + b] * functions[b] for b in range(3))
    line_right = sum(right[1 + b] * functions[b] for b in range(3))
    whole = [mix(near, pieces.at[0, k]) for k in range(2)]
    low = [mix(near, pieces.at[1, k]) for k in range(2)]
    high = [mix(right, pieces.at[1, k]) for k in range(2)]

    def stiff(line, i):
        return lines[line, i : i + 1, :]

    extra = [stiff(0, i) * whole[0] + WEIGHTS[i] * whole[1] for i in range(8)]
    for i in range(8):
        extra.append(
            stiff(1, i) * low[0] + stiff(2, i) * high[0] + WEIGHTS[i] * (LOW[i] * low[1] + HIGH[i] * high[1])
        )
    extra = join_middle(extra)
    beyond_x, beyond_w = face_pieces.at[1, 0], face_pieces.at[1, 1]
    extra[0] = extra[0] + (
        stiff(1, 7) * mix(left, beyond_x) + stiff(2, 7) * mix(near, beyond_x) + WEIGHTS[7] * mix(near, beyond_w)
    )
    extra[15] = extra[15] + stiff(0, 0) * mix(right, face_pieces.at[0, 0]) + WEIGHTS[0] * mix(right, face_pieces.at[0, 1])
    keep = solid(Geometry(LANES).keep)
    for x in range(ROWS):
        begin = start_faces[x // 15] if x in (0, 15) else start[x]
        mine = faces[x // 15] if x in (0, 15) else local[x, :, :LANES]
        new_residual[x] = residual[x] - alpha * (image[x] + extra[x])
        coarse_line = GROUP_X[0][x] * line_near
        if GROUP_X[1][x] != 0.0:
            coarse_line = coarse_line + GROUP_X[1][x] * line_right
        new_solution[x] = begin + alpha * (mine + keep * coarse_line)


VMEM = pl.BlockSpec(memory_space=pltpu.VMEM)
SMEM = pl.BlockSpec(memory_space=pltpu.SMEM)
FAR = pl.BlockSpec(memory_space=pltpu.HBM)


def call(kernel, shapes, specs, name, scratch=()):
    def leaf(shape):
        kind = jnp.float32
        if shape[0] == "half":
            shape, kind = shape[1:], jnp.bfloat16
        return jax.ShapeDtypeStruct(shape, kind)

    return pl.pallas_call(
        kernel,
        out_shape=[leaf(shape) for shape in shapes],
        in_specs=specs,
        out_specs=[VMEM] * len(shapes),
        scratch_shapes=list(scratch),
        compiler_params=pltpu.CompilerParams(vmem_limit_bytes=16 * 1024 * 1024),
        name=name,
    )


def swap(first, second, axis):
    size = lax.axis_size(axis)
    odd = [(i, (i + 1) % size) for i in range(1, size, 2)]
    one = lax.ppermute(first, axis, [(i, i ^ 1) for i in range(size)])
    two = lax.ppermute(second, axis, odd + [(b, a) for a, b in odd])
    return one, two


def body(
    source, previous, coefficients, stiffness, fdm_vectors, fdm_values, coarse_inverse, vertex_map
):
    assert source.shape == (ROWS, ROWS, LANES)
    spans = lax.axis_size("gz")
    devices = lax.axis_size("gx") * spans
    per, count = coarse_inverse.shape
    small = per * count <= LANES
    block, wide, face = (ROWS, ROWS, LANES), (ROWS, ROWS, WIDE), (ROWS, LANES)
    halo = (9, ROWS, LANES)

    first, second, own_metrics, source, previous = call(
        pack_kernel,
        [halo, halo, face, block, block],
        [FAR] * 3,
        "pack",
        [pltpu.VMEM(coefficients.shape, jnp.float32), pltpu.VMEM((16, 16), jnp.float32), pltpu.SemaphoreType.DMA((3,))],
    )(*(pltpu.with_memory_space_constraint(v, pltpu.HBM) for v in (source, previous, coefficients)))
    first, second = swap(first, second, "gz")
    upper, lower, diagonals, stiff, vectors, lam, lines, fixed, tables = call(
        functools.partial(prepare_kernel, small),
        [
            ("half", 3, WIDE, WIDE), ("half", 3, WIDE, LANES), (3, 8, 8, LANES),
            (64, LANES), (64, LANES), (2, 8, LANES), (3, 8, LANES), (24, LANES), (3, 8, LANES),
        ],
        [VMEM] * 3 + [SMEM] * 2 + [VMEM if small else FAR, VMEM],
        "prepare",
    )(own_metrics, stiffness, fdm_vectors, fdm_values, vertex_map, coarse_inverse, jnp.asarray(lane_tables()))

    message = (40, WIDE)
    start, rest, metrics, factors, own_a, own_b = call(
        start_kernel,
        [block, wide, (16, WIDE), (3, 2, ROWS, WIDE), message, message],
        [VMEM] * 9,
        "start",
    )(source, previous, own_metrics, first, second, stiff, upper, lower, diagonals)
    far_a, far_b = swap(own_a, own_b, "gx")
    known, inverse, pieces = call(
        ready_kernel, [wide, wide, (2, 2, 4, ROWS, LANES)], [VMEM] * 8, "ready"
    )(rest, metrics, factors, lam, stiff, lines, upper, lower)

    message = (32, WIDE)
    start_faces, residual, local, side_a, side_b, sums = call(
        solve_kernel,
        [(2, ROWS, LANES), block, wide, message, message, (8, LANES)],
        [VMEM] * 13,
        "solve",
    )(rest, known, factors, inverse, own_a, own_b, far_a, far_b, stiff, vectors, upper, lower, diagonals)
    got_a, got_b = swap(side_a, side_b, "gx")
    image, more_sums, face_factors, face_pieces = call(
        ahead_kernel,
        [block, (8, LANES), (2, 3, ROWS, WIDE), (2, 2, 4, ROWS, LANES)],
        [VMEM] * 9,
        "ahead",
    )(local, factors, far_a, far_b, stiff, lines, upper, lower, diagonals)

    image, faces, payload = call(
        image_kernel, [block, (2, ROWS, LANES), (2 * devices, LANES)], [VMEM] * 15, "image"
    )(
        image, factors, face_factors, side_a, side_b, got_a, got_b, sums, more_sums, fixed,
        stiff, lines, upper, lower, diagonals,
    )
    gathered = lax.all_to_all(payload.reshape(devices, 2, LANES), ("gx", "gz"), 0, 0)
    gathered = gathered.reshape(2 * devices, LANES)

    operands = [
        start, start_faces, residual, local, faces, image, pieces, face_pieces, lines,
        tables, gathered,
    ]
    finish = functools.partial(final_kernel, devices, spans, count, per)
    if small:

        def kernel(*refs):
            finish(*refs[:11], None, *refs[11:])

    else:
        kernel = finish
        rows = gathered[0::2]
        labels = rows[:, jnp.array([8 * k + 4 for k in range(6)])].astype(jnp.int32)
        parts = rows[:, jnp.array([8 * (k // 3) + k % 3 for k in range(6)])]
        rhs = jnp.zeros((count,), jnp.float32).at[labels.reshape(-1)].add(parts.reshape(-1))
        mine = jnp.dot(coarse_inverse, rhs, precision=EXACT)
        coarse = lax.all_gather(mine, ("gx", "gz"), axis=0, tiled=True)
        operands.append(jnp.pad(coarse[labels], ((0, 0), (0, LANES - 6))))
    return tuple(
        call(kernel, [block, block], [VMEM] * len(operands), "finish", [pltpu.VMEM((devices, LANES), jnp.float32)])(
            *operands
        )
    )


def solution(mesh):
    placed = (
        P("gx", None, "gz"),
        P("gx", None, "gz"),
        P(None, "gx", None, "gz"),
        P(),
        P(),
        P(),
        P(("gx", "gz"), None),
        P(None, "gx", None, "gz"),
    )
    return jax.shard_map(
        body,
        mesh=mesh,
        in_specs=placed,
        out_specs=(P("gx", None, "gz"), P("gx", None, "gz")),
        check_vma=False,
    )
```

time: 43.6 us -> 36 us (0.83)
  blocking collectives: 0 us -> 10.9 us
  starting transfers between devices: 18.5 us -> 11.3 us
  waiting for transfers between devices: 10.4 us -> 4.79 us
  local copies, waits for them, and re-layouts: 3.85 us -> 0.03 us
  Pallas kernels: 10 us -> 8.01 us
    all_to_all x0 -> x1, blocking collectives: none -> 10.9 us  [body(): lax.all_to_all(payload.reshape(devices, 2, LANES), ('gx', 'gz'), 0, 0)]
    all_to_all x1 -> x0, starting transfers between devices: 3.85 us -> none  [body(): lax.all_to_all(payload.reshape(devices, 2, LANES), ('gx', 'gz'), 0, 0)]
    unnamed x20 -> x12, local copies, waits for them, and re-layouts: 3.85 us -> 0.03 us
    ppermute x4 -> x3, waiting for transfers between devices: 7.27 us -> 3.84 us  [swap(): two = lax.ppermute(second, axis, odd + [(b, a) for a, b in odd])]
    pallas_call x6 -> x8, Pallas kernels: 10 us -> 8.01 us  [the longest x1 2.01 us: body(): call(functools.partial(prepare_kernel, small), [('half', 3, WIDE, WIDE),...]
    ppermute x4 -> x3, starting transfers between devices: 4.51 us -> 2.67 us  [swap(): one = lax.ppermute(first, axis, [(i, i ^ 1) for i in range(size)])]
    ppermute x4 -> x3, starting transfers between devices: 10.1 us -> 8.65 us  [swap(): two = lax.ppermute(second, axis, odd + [(b, a) for a, b in odd])]
    ppermute x4 -> x3, waiting for transfers between devices: 2.27 us -> 0.95 us  [swap(): one = lax.ppermute(first, axis, [(i, i ^ 1) for i in range(size)])]
  transfers between devices with their start and end apart: 9 -> 6, of which waited for: 8 -> 5; matrix products, arithmetic and copies ran while one was open for 0% -> 0% of each run, Pallas kernels for 3% -> 9%
where the time goes in v2:
time: 36 us; the launch traced here: 35.8 us
  starting transfers between devices  11.3 us (31%)
  blocking collectives  10.9 us (30%)
  Pallas kernels  8.01 us (22%)
  waiting for transfers between devices  4.79 us (13%)
  between operations  0.75 us (2%)
    all_to_all x1, blocking collectives, body(): lax.all_to_all(payload.reshape(devices, 2, LANES), ('gx', 'gz'), 0, 0)  10.9 us
    ppermute x3, starting transfers between devices, swap(): two = lax.ppermute(second, axis, odd + [(b, a) for a, b in odd])  8.65 us
    ppermute x3, waiting for transfers between devices, swap(): two = lax.ppermute(second, axis, odd + [(b, a) for a, b in odd])  3.84 us
    ppermute x3, starting transfers between devices, swap(): one = lax.ppermute(first, axis, [(i, i ^ 1) for i in range(size)])  2.67 us
    pallas_call x1, Pallas kernels, body(): call(functools.partial(prepare_kernel, small), [('half', 3, WIDE, WIDE),...  2.01 us
    pallas_call x1, Pallas kernels, body(): call(kernel, [block, block], [VMEM] * len(operands), 'finish', [pltpu.VME...  1.31 us
    pallas_call x1, Pallas kernels, body(): call(solve_kernel, [(2, ROWS, LANES), block, wide, message, message, (8,...  1.27 us
    pallas_call x1, Pallas kernels, body(): call(pack_kernel, [halo, halo, face, block, block], [FAR] * 3, 'pack', [p...  1.22 us
  transfers between devices with their start and end apart: 6, of which 5 were waited for; matrix products, arithmetic and copies ran while one was open for 0% of the time, Pallas kernels for 9%

profile of v2, /device:TPU:0, one launch (start us, length us, event | category | flops | bytes accessed | tf_op | source)
XLA Modules:
  0.0 35.8 jit_solution(8503512488480350990)
XLA Ops:
  0.6 0.0 copy-start.1
  0.7 0.0 copy-start.3
  0.7 1.2 %pack.1 = (f32[9,16,128]{2,1,0:T(8,128)S(1)}, f32[9,16,128]{2,1,0:T(8,128)S(1)}, f32[16,128]{1,0:T(8,128)S(1)}, f32[16,16,128]{2,1,0:T(8,128)S(1)}, f32[16,16,128]{2,1,0:T(8,128)S(1)}) custom-call(f32[16,16,128]{2,1,0:T(8,128)} %source.1, f32[16,16,128]{2,1,0:T(8,128)} %previous.1, f32[3,2,2,16]{3,2,1,0:T(2,128)} %coefficients.1), custom_call_target="tpu_custom_call" | custom-call | tf_op jit(solution)/shard_map/pack/pallas_call | solution.py:789
  1.9 0.0 copy-start.2
  1.9 0.5 %collective-permute-start = (f32[9,16,128]{2,1,0:T(8,128)S(1)}, f32[9,16,128]{2,1,0:T(8,128)S(1)}, u32[]{:S(2)}, u32[]{:S(2)}) collective-permute-start(f32[9,16,128]{2,1,0:T(8,128)S(1)} %get-tuple-element.41), channel_id=1, source_target_pairs={{0,1},{1,0},{2,3},{3,2},{4,5},{5,4},{6,7},{7,6},{8,9},{9,8},{10,11... | collective-permute-start | bytes 221192 | tf_op jit(solution)/shard_map/ppermute | solution.py:773
  2.4 4.7 %collective-permute-start.1 = (f32[9,16,128]{2,1,0:T(8,128)S(1)}, f32[9,16,128]{2,1,0:T(8,128)S(1)}, u32[]{:S(2)}, u32[]{:S(2)}) collective-permute-start(f32[9,16,128]{2,1,0:T(8,128)S(1)} %get-tuple-element.42), channel_id=1, source_target_pairs={{1,2},{3,4},{5,6},{7,0},{2,1},{4,3},{6,5},{0,7},{9,10},{11,12},{13... | collective-permute-start | bytes 221192 | tf_op jit(solution)/shard_map/ppermute | solution.py:774
  7.2 2.0 %prepare.1 = (bf16[3,256,256]{2,1,0:T(8,128)(2,1)S(1)}, bf16[3,256,128]{2,1,0:T(8,128)(2,1)S(1)}, f32[3,8,8,128]{3,2,1,0:T(8,128)S(1)}, f32[64,128]{1,0:T(8,128)...) custom-call(f32[16,128]{1,0:T(8,128)S(1)} %get-tuple-element.40.metr, ...), custom_call_target="tpu_custom_call" | custom-call | tf_op jit(solution)/shard_map/prepare/pallas_call | solution.py:797
  9.2 0.0 collective-permute-done.first
  9.2 0.1 collective-permute-done.1.second
  9.3 0.7 %start.1 = (f32[16,16,128]{2,1,0:T(8,128)S(1)}, f32[16,16,256]{2,1,0:T(8,128)S(1)}, f32[16,256]{1,0:T(8,128)S(1)}, f32[3,2,16,256]{3,2,1,0:T(8,128)S(1)}, f32[40,256]{1,0:T(8,128)S(1)}, /*index=5*/f32[40,256]{1,0:T(8,128)S(1)}) custom-call(f32[16,16,128]{2,1,0:T(8,128)S(1)} %get-tuple-element.38.source, f32[16,16,128]{2,1,0:T(8,128)S(1)} %get-tuple-element.39.previous, ...), custom_call_target="tpu_custom_call" | custom-call | tf_op jit(solution)/shard_map/start/pallas_call | solution.py:808
  10.0 1.6 %collective-permute-start.2 = (f32[40,256]{1,0:T(8,128)S(1)}, f32[40,256]{1,0:T(8,128)S(1)}, u32[]{:S(2)}, u32[]{:S(2)}) collective-permute-start(f32[40,256]{1,0:T(8,128)S(1)} %get-tuple-element.55.own_a), channel_id=1, source_target_pairs={{0,8},{8,0},{16,24},{24,16},{1,9},{9,1},{17,25},{25,17},{2,10},{10... | collective-permute-start | bytes 122888 | tf_op jit(solution)/shard_map/ppermute | solution.py:773
  11.6 1.5 %collective-permute-start.3 = (f32[40,256]{1,0:T(8,128)S(1)}, f32[40,256]{1,0:T(8,128)S(1)}, u32[]{:S(2)}, u32[]{:S(2)}) collective-permute-start(f32[40,256]{1,0:T(8,128)S(1)} %get-tuple-element.56.own_b), channel_id=1, source_target_pairs={{8,16},{24,0},{16,8},{0,24},{9,17},{25,1},{17,9},{1,25},{10,18},{2... | collective-permute-start | bytes 122888 | tf_op jit(solution)/shard_map/ppermute | solution.py:774
  13.1 0.4 %ready.1 = (f32[16,16,256]{2,1,0:T(8,128)S(1)}, f32[16,16,256]{2,1,0:T(8,128)S(1)}, f32[2,2,4,16,128]{4,3,2,1,0:T(8,128)S(1)}) custom-call(f32[16,16,256]{2,1,0:T(8,128)S(1)} %get-tuple-element.48.rest, f32[16,256]{1,0:T(8,128)S(1)} %get-tuple-element.49.metrics, f32[3,2,16,256]{3,2,1,0:T(8,128)S(1)} %get-tuple-element.50.factors, ...), custom_call_target="tpu_custom_call" | custom-call | tf_op jit(solution)/shard_map/ready/pallas_call | solution.py:815
  13.4 0.7 %collective-permute-done.2.got_a.far_a = f32[40,256]{1,0:T(8,128)S(1)} collective-permute-done((f32[40,256]{1,0:T(8,128)S(1)}, f32[40,256]{1,0:T(8,128)S(1)}, u32[]{:S(2)}, u32[]{:S(2)}) %collective-permute-start.2) | collective-permute-done | bytes 40992 | tf_op jit(solution)/shard_map/ppermute | solution.py:773
  14.1 2.3 %collective-permute-done.3.got_b.far_b = f32[40,256]{1,0:T(8,128)S(1)} collective-permute-done((f32[40,256]{1,0:T(8,128)S(1)}, f32[40,256]{1,0:T(8,128)S(1)}, u32[]{:S(2)}, u32[]{:S(2)}) %collective-permute-start.3) | collective-permute-done | bytes 40992 | tf_op jit(solution)/shard_map/ppermute | solution.py:774
  16.5 1.3 %solve.1 = (f32[2,16,128]{2,1,0:T(8,128)S(1)}, f32[16,16,128]{2,1,0:T(8,128)S(1)}, f32[16,16,256]{2,1,0:T(8,128)S(1)}, f32[32,256]{1,0:T(8,128)S(1)}, f32[32,256]{1,0:T(8,128)S(1)}, /*index=5*/f32[8,128]{1,0:T(8,128)S(1)}) custom-call(f32[16,16,256]{2,1,0:T(8,128)S(1)} %get-tuple-element.48.rest, f32[16,16,256]{2,1,0:T(8,128)S(1)} %get-tuple-element.53.known, ...), custom_call_target="tpu_custom_call" | custom-call | tf_op jit(solution)/shard_map/solve/pallas_call | solution.py:820
  17.7 0.6 %collective-permute-start.4 = (f32[32,256]{1,0:T(8,128)S(1)}, f32[32,256]{1,0:T(8,128)S(1)}, u32[]{:S(2)}, u32[]{:S(2)}) collective-permute-start(f32[32,256]{1,0:T(8,128)S(1)} %get-tuple-element.63.own_a), channel_id=1, source_target_pairs={{0,8},{8,0},{16,24},{24,16},{1,9},{9,1},{17,25},{25,17},{2,10},{10... | collective-permute-start | bytes 98312 | tf_op jit(solution)/shard_map/ppermute | solution.py:773
  18.3 2.4 %collective-permute-start.5 = (f32[32,256]{1,0:T(8,128)S(1)}, f32[32,256]{1,0:T(8,128)S(1)}, u32[]{:S(2)}, u32[]{:S(2)}) collective-permute-start(f32[32,256]{1,0:T(8,128)S(1)} %get-tuple-element.64.own_b), channel_id=1, source_target_pairs={{8,16},{24,0},{16,8},{0,24},{9,17},{25,1},{17,9},{1,25},{10,18},{2... | collective-permute-start | bytes 98312 | tf_op jit(solution)/shard_map/ppermute | solution.py:774
  20.8 0.7 %ahead.1 = (f32[16,16,128]{2,1,0:T(8,128)S(1)}, f32[8,128]{1,0:T(8,128)S(1)}, f32[2,3,16,256]{3,2,1,0:T(8,128)S(1)}, f32[2,2,4,16,128]{4,3,2,1,0:T(8,128)S(1)}) custom-call(f32[16,16,256]{2,1,0:T(8,128)S(1)} %get-tuple-element.60.local.refs_3_, f32[3,2,16,256]{3,2,1,0:T(8,128)S(1)} %get-tuple-element.50.factors, ...), custom_call_target="tpu_custom_call" | custom-call | tf_op jit(solution)/shard_map/ahead/pallas_call | solution.py:827
  21.5 0.2 collective-permute-done.4.got_a
  21.7 1.4 %collective-permute-done.5.got_b = f32[32,256]{1,0:T(8,128)S(1)} collective-permute-done((f32[32,256]{1,0:T(8,128)S(1)}, f32[32,256]{1,0:T(8,128)S(1)}, u32[]{:S(2)}, u32[]{:S(2)}) %collective-permute-start.5) | collective-permute-done | bytes 32800 | tf_op jit(solution)/shard_map/ppermute | solution.py:774
  23.2 0.4 %image.1 = (f32[16,16,128]{2,1,0:T(8,128)S(1)}, f32[2,16,128]{2,1,0:T(8,128)S(1)}, f32[64,128]{1,0:T(8,128)S(1)}) custom-call(f32[16,16,128]{2,1,0:T(8,128)S(1)} %get-tuple-element.61.known, f32[3,2,16,256]{3,2,1,0:T(8,128)S(1)} %get-tuple-element.50.factors, f32[2,3,16,256]{3,2,1,0:T(8,128)S(1)} %get-tuple-element.62.face_factors, ...), custom_call_target="tpu_custom_call" | custom-call | tf_op jit(solution)/shard_map/image/pallas_call | solution.py:834
  23.6 10.9 %all_to_all.5 = f32[32,2,128]{2,1,0:T(2,128)S(1)} all-to-all(f32[32,2,128]{2,1,0:T(2,128)S(1)} %bitcast.3), channel_id=1, replica_groups=mesh['gx'=4,'gz'=8] {'gx','gz'}, dimensions={0} | all-to-all | bytes 65536 | tf_op jit(solution)/shard_map/all_to_all | solution.py:840
  34.5 1.3 %finish.1 = (f32[16,16,128]{2,1,0:T(8,128)}, f32[16,16,128]{2,1,0:T(8,128)}) custom-call(f32[16,16,128]{2,1,0:T(8,128)S(1)} %get-tuple-element.47.refs_0_, f32[2,16,128]{2,1,0:T(8,128)S(1)} %get-tuple-element.58.refs_1_, f32[16,16,128]{2,1,0:T(8,128)S(1)} %get-tuple-element.59.refs_2_, f32[16,16,256]{2,1,0:T(8,128)S(1)} %get-tuple-element.60.local.refs_3_, ...), custom_call_target="tpu_custom_call" | custom-call | tf_op jit(solution)/shard_map/finish/pallas_call | solution.py:863
  (9 shorter events, 0.0 us)
Async XLA Ops:
  0.6 6.5 %copy-start = (s32[8,2,2,16]{3,2,1,0:T(2,128)S(1)}, s32[8,2,2,16]{3,2,1,0:T(2,128)}, u32[]{:S(2)}) copy-start(s32[8,2,2,16]{3,2,1,0:T(2,128)} %labels.1) | copy-start | bytes 6148
  0.6 6.5 %copy-start.1 = (f32[3,8,128]{2,1,0:T(8,128)S(1)}, f32[3,8,128]{2,1,0:T(8,128)}, u32[]{:S(2)}) copy-start(f32[3,8,128]{2,1,0:T(8,128)} %constant.2.clone.tables) | copy-start | bytes 36868
  0.7 6.5 %copy-start.3 = (f32[8,8]{1,0:T(8,128)S(1)}, f32[8,8]{1,0:T(8,128)}, u32[]{:S(2)}) copy-start(f32[8,8]{1,0:T(8,128)} %vectors.1) | copy-start | bytes 772
  1.9 5.3 %copy-start.2 = (f32[8,8]{1,0:T(8,128)S(1)}, f32[8,8]{1,0:T(8,128)}, u32[]{:S(2)}) copy-start(f32[8,8]{1,0:T(8,128)} %stiffness.1) | copy-start | bytes 772
  1.9 7.3 %collective-permute-start = (f32[9,16,128]{2,1,0:T(8,128)S(1)}, f32[9,16,128]{2,1,0:T(8,128)S(1)}, u32[]{:S(2)}, u32[]{:S(2)}) collective-permute-start(f32[9,16,128]{2,1,0:T(8,128)S(1)} %get-tuple-element.41), channel_id=1, source_target_pairs={{0,1},{1,0},{2,3},{3,2},{4,5},{5,4},{6,7},{7,6},{8,9},{9,8},{10,11... | collective-permute-start | bytes 221192 | tf_op jit(solution)/shard_map/ppermute | solution.py:773
  2.4 4.7 %copy-start.4 = (f32[2,64]{1,0:T(2,128)S(1)}, f32[2,64]{1,0:T(2,128)}, u32[]{:S(2)}) copy-start(f32[2,64]{1,0:T(2,128)} %coarse.1) | copy-start | bytes 1540
  2.4 4.7 %copy-start.5 = (f32[8]{0:T(128)S(1)}, f32[8]{0:T(128)}, u32[]{:S(2)}) copy-start(f32[8]{0:T(128)} %eigen.1) | copy-start | bytes 100
  2.4 6.9 %collective-permute-start.1 = (f32[9,16,128]{2,1,0:T(8,128)S(1)}, f32[9,16,128]{2,1,0:T(8,128)S(1)}, u32[]{:S(2)}, u32[]{:S(2)}) collective-permute-start(f32[9,16,128]{2,1,0:T(8,128)S(1)} %get-tuple-element.42), channel_id=1, source_target_pairs={{1,2},{3,4},{5,6},{7,0},{2,1},{4,3},{6,5},{0,7},{9,10},{11,12},{13... | collective-permute-start | bytes 221192 | tf_op jit(solution)/shard_map/ppermute | solution.py:774
  10.0 4.1 %collective-permute-start.2 = (f32[40,256]{1,0:T(8,128)S(1)}, f32[40,256]{1,0:T(8,128)S(1)}, u32[]{:S(2)}, u32[]{:S(2)}) collective-permute-start(f32[40,256]{1,0:T(8,128)S(1)} %get-tuple-element.55.own_a), channel_id=1, source_target_pairs={{0,8},{8,0},{16,24},{24,16},{1,9},{9,1},{17,25},{25,17},{2,10},{10... | collective-permute-start | bytes 122888 | tf_op jit(solution)/shard_map/ppermute | solution.py:773
  11.6 4.9 %collective-permute-start.3 = (f32[40,256]{1,0:T(8,128)S(1)}, f32[40,256]{1,0:T(8,128)S(1)}, u32[]{:S(2)}, u32[]{:S(2)}) collective-permute-start(f32[40,256]{1,0:T(8,128)S(1)} %get-tuple-element.56.own_b), channel_id=1, source_target_pairs={{8,16},{24,0},{16,8},{0,24},{9,17},{25,1},{17,9},{1,25},{10,18},{2... | collective-permute-start | bytes 122888 | tf_op jit(solution)/shard_map/ppermute | solution.py:774
  17.7 4.0 %collective-permute-start.4 = (f32[32,256]{1,0:T(8,128)S(1)}, f32[32,256]{1,0:T(8,128)S(1)}, u32[]{:S(2)}, u32[]{:S(2)}) collective-permute-start(f32[32,256]{1,0:T(8,128)S(1)} %get-tuple-element.63.own_a), channel_id=1, source_target_pairs={{0,8},{8,0},{16,24},{24,16},{1,9},{9,1},{17,25},{25,17},{2,10},{10... | collective-permute-start | bytes 98312 | tf_op jit(solution)/shard_map/ppermute | solution.py:773
  18.3 4.8 %collective-permute-start.5 = (f32[32,256]{1,0:T(8,128)S(1)}, f32[32,256]{1,0:T(8,128)S(1)}, u32[]{:S(2)}, u32[]{:S(2)}) collective-permute-start(f32[32,256]{1,0:T(8,128)S(1)} %get-tuple-element.64.own_b), channel_id=1, source_target_pairs={{8,16},{24,0},{16,8},{0,24},{9,17},{25,1},{17,9},{1,25},{10,18},{2... | collective-permute-start | bytes 98312 | tf_op jit(solution)/shard_map/ppermute | solution.py:774

commit v3 on v2

--- a/solution.py
+++ b/solution.py
@@ -37,6 +37,11 @@
 LANES = 128
 WIDE = 256
 HALO = 32
+DEEP, SHALLOW = 25, 17
+SLOT = DEEP + SHALLOW
+FIRST_FIELDS = ((0, 24), (41, 17), (75, 17))
+SECOND_FIELDS = ((0, 8), (16, 8), (32, 8), (48, 8))
+FIRST_ROWS, SECOND_ROWS = 56, 40
 PAIRS = ((0, 0), (0, 1), (1, 1))
 GROUP_X = (ONES + LOW, [0.0] * 8 + HIGH)
 INVERSE_X = [0.5] + [1.0] * 6 + [0.5] + [0.5] + [1.0] * 6 + [0.5]
@@ -184,6 +189,26 @@
 def join_middle(rows):
     middle = rows[7] + rows[8]
     return rows[:7] + [middle, middle] + rows[9:]
+
+
+def fold(parts, fields):
+    lane = iota((8, LANES), 1)
+    result = parts[0]
+    for part, (offset, half) in list(zip(parts, fields))[1:]:
+        taken = ((lane - offset + half) & (LANES - 1)) < 2 * half
+        result = jnp.where(taken, pltpu.roll(part, offset, 1), result)
+    return result
+
+
+def unfold(packed, field, fill=0.0):
+    offset, half = field
+    lane = iota((8, LANES), 1)
+    moved = pltpu.roll(packed, LANES - offset, 1) if offset else packed
+    return jnp.where(((lane + half) & (LANES - 1)) < 2 * half, moved, fill)
+
+
+def widen(tile, pieces):
+    return jnp.concatenate([tile, jnp.concatenate(pieces, axis=0)], axis=1)
 
 
 def group_lanes(lanes, group):
@@ -214,18 +239,21 @@
             scratch[at : at + 2, :] = raw[c, element]
     spread = jnp.dot(scratch[...], widen, precision=EXACT, preferred_element_type=jnp.float32)
     metrics[...] = spread
-    group = iota((8 * ROWS, LANES), 1) // HALO
-    parts = [
-        ref[lo : lo + 8].reshape(8 * ROWS, LANES) for ref in (near_previous, near_source) for lo in (0, 8)
-    ]
+    slot = iota((8, LANES), 1)
     for to_right, out in ((even, first), (jnp.logical_not(even), second)):
-        base = jnp.where(to_right, HALO, 0)
-        packed = None
-        for k, part in enumerate(parts):
-            moved = pltpu.roll(part, lax.rem(base + HALO * k, LANES), 1)
-            packed = moved if packed is None else jnp.where(group == k, moved, packed)
-        out[0:8] = packed.reshape(8, ROWS, LANES)
-        out[8] = spread
+        for tile in range(11):
+            packed = None
+            for k in range(3):
+                n = 3 * tile + k
+                if n >= 2 * ROWS:
+                    break
+                for ref, width, at in ((near_previous, DEEP, SLOT * k), (near_source, SHALLOW, SLOT * k + DEEP)):
+                    shift = jnp.where(to_right, (at + width) % LANES, at)
+                    moved = pltpu.roll(ref[n // 2, 8 * (n % 2) : 8 * (n % 2) + 8], shift, 1)
+                    packed = moved if packed is None else jnp.where(slot >= at, moved, packed)
+            out[tile] = packed
+        out[11] = spread[:8]
+        out[12] = spread[8:]
 
 
 def prepare_kernel(
@@ -326,31 +354,33 @@
 
 def start_kernel(
     source, previous, own_metrics, first, second, stiffness, upper, lower, diagonals,
-    start, rest, metrics, factors, message_a, message_b,
+    start, rest, metrics, factors, halves, message_a, message_b,
 ):
     even = even_index("gz")
-    lane = iota((ROWS, LANES), 1)
-
-    def beyond(plane, right_shift, left_shift, fill):
-        a, b = first[plane], second[plane]
-        right, left = jnp.where(even, a, b), jnp.where(even, b, a)
-        if right_shift:
-            right = pltpu.roll(right, right_shift, 1)
-        if left_shift:
-            left = pltpu.roll(left, left_shift, 1)
-        return jnp.where(lane < HALO, right, jnp.where(lane >= LANES - HALO, left, fill))
-
-    def wide(ref, x, kind):
-        slot = 2 * kind + x // 8
-        right_shift = (LANES - HALO * slot) % LANES
-        left_shift = (LANES - HALO - HALO * slot) % LANES
-        return split(jnp.concatenate([ref[x], beyond(x % 8, right_shift, left_shift, 0.0)], axis=1))
+    lane = iota((8, LANES), 1)
+    one, two = first[...], second[...]
+    from_right, from_left = jnp.where(even, one, two), jnp.where(even, two, one)
+
+    def beyond(n, at, width):
+        at = at + SLOT * (n % 3)
+        right, left = from_right[n // 3], from_left[n // 3]
+        if at:
+            right = pltpu.roll(right, LANES - at, 1)
+        left = pltpu.roll(left, (LANES - width - at) % LANES, 1)
+        return jnp.where(lane < width, right, jnp.where(lane >= LANES - width, left, 0.0))
+
+    def wide(ref, x, at, width):
+        return split(widen(ref[x], [beyond(2 * x + e, at, width) for e in range(2)]))
 
     geo = Geometry(WIDE)
     metrics[:, :LANES] = own_metrics[...]
-    metrics[:, LANES:] = beyond(8, 0, 0, 1.0)
+    for e in range(2):
+        right, left = from_right[11 + e], from_left[11 + e]
+        metrics[8 * e : 8 * e + 8, LANES:] = jnp.where(
+            lane < HALO, right, jnp.where(lane >= LANES - HALO, left, 1.0)
+        )
     factor = geo.keep * geo.inverse_y * geo.inverse_z
-    rows = [geo.pair(wide(previous, x, 0)) * (factor * INVERSE_X[x]) for x in range(ROWS)]
+    rows = [geo.pair(wide(previous, x, 0, DEEP)) * (factor * INVERSE_X[x]) for x in range(ROWS)]
     rows = join_middle(rows)
     faces = (rows[0], rows[15])
     rows[0] = rows[15] = jnp.zeros_like(rows[0])
@@ -363,33 +393,44 @@
             factors[c, e] = solid(scaled[e][c])
     applied = apply_rows(rows, along_z, scaled, stiffness, wide_diagonals(diagonals, 0))
     for x in range(ROWS):
-        rest[x] = solid(wide(source, x, 1) - applied[x])
+        rest[x] = solid(wide(source, x, DEEP, SHALLOW) - applied[x])
+    halves[0], halves[1] = solid(faces[0]), solid(faces[1])
+    messages = []
+    for side, x in ((0, 0), (1, 15)):
+        half, value = halves[side], rest[x]
+        rows = [metrics[(c * 2 + side) * 2 : (c * 2 + side) * 2 + 2] for c in range(3)]
+        rows = jnp.concatenate(rows + [jnp.ones((2, WIDE), jnp.float32)], axis=0)
+        lower_fold = fold([half[:8, LANES:], value[:8, LANES:], rows[:, LANES:]], FIRST_FIELDS)
+        upper_fold = fold([half[8:, LANES:], value[8:, LANES:]], FIRST_FIELDS[:2])
+        messages.append(
+            jnp.concatenate([half[:, :LANES], value[:, :LANES], lower_fold, upper_fold, rows[:, :LANES]], axis=0)
+        )
     even_x = even_index("gx")
-
-    def choose(right, left):
-        return jnp.where(even_x, right, left), jnp.where(even_x, left, right)
-
-    for at, right, left in ((0, solid(faces[1]), solid(faces[0])), (16, rest[15], rest[0])):
-        message_a[at : at + 16], message_b[at : at + 16] = choose(right, left)
-    for c in range(3):
-        at = 32 + 2 * c
-        right, left = metrics[(c * 2 + 1) * 2 : (c * 2 + 1) * 2 + 2], metrics[c * 4 : c * 4 + 2]
-        message_a[at : at + 2], message_b[at : at + 2] = choose(right, left)
-    message_a[38:40] = jnp.zeros((2, WIDE), jnp.float32)
-    message_b[38:40] = jnp.zeros((2, WIDE), jnp.float32)
-
-
-def sided(even, a, b, at, size=16):
-    one, two = a[at : at + size], b[at : at + size]
-    return jnp.where(even, one, two), jnp.where(even, two, one)
-
-
-def face_metrics(even, a, b):
-    sides = [[], []]
-    for c in range(3):
-        for side, pair in enumerate(sided(even, a, b, 32 + 2 * c, 2)):
-            sides[side].append(jnp.stack([jnp.broadcast_to(pair[e : e + 1], (8, WIDE)) for e in range(2)]))
-    return sides
+    message_a[...] = jnp.where(even_x, messages[1], messages[0])
+    message_b[...] = jnp.where(even_x, messages[0], messages[1])
+
+
+def both_sides(even, a, b):
+    one, two = a[...], b[...]
+    return jnp.where(even, two, one), jnp.where(even, one, two)
+
+
+def read_first(message):
+    lower_fold, upper_fold = message[32:40], message[40:48]
+    half, value = (
+        widen(message[16 * k : 16 * k + 16], [unfold(lower_fold, FIRST_FIELDS[k]), unfold(upper_fold, FIRST_FIELDS[k])])
+        for k in range(2)
+    )
+    rows = widen(message[48:56], [unfold(lower_fold, FIRST_FIELDS[2], 1.0)])
+    metrics = [
+        jnp.stack([jnp.broadcast_to(rows[2 * c + e : 2 * c + e + 1], (8, WIDE)) for e in range(2)]) for c in range(3)
+    ]
+    return split(half), split(value), metrics
+
+
+def read_second(message):
+    pieces = [unfold(message[32:40], field) for field in SECOND_FIELDS]
+    return widen(message[0:16], pieces[:2]), widen(message[16:32], pieces[2:])
 
 
 def coarse_pieces(geo, factors, stiff_keep, functions, stiff_functions):
@@ -442,34 +483,33 @@
 
 
 def solve_kernel(
-    rest, known, factors, inverse, own_a, own_b, got_a, got_b,
+    rest, known, factors, inverse, halves, got_a, got_b,
     stiffness, vectors, upper, lower, diagonals,
-    start_faces, residual, local, message_a, message_b, sums,
+    start_faces, residual, local, face_values, face_factors, message_a, message_b, sums,
 ):
     even = even_index("gx")
     geo = Geometry(WIDE)
-    mine, theirs = sided(even, own_a, own_b, 0), sided(even, got_a, got_b, 0)
-    right, left = split(mine[0] + theirs[0]), split(mine[1] + theirs[1])
-    start_faces[0], start_faces[1] = solid(own(left)), solid(own(right))
-    other_right, other_left = (split(v) for v in sided(even, got_a, got_b, 16))
-    metrics_right, metrics_left = face_metrics(even, got_a, got_b)
+    arrived = [read_first(message) for message in both_sides(even, got_a, got_b)]
+    values = [split(halves[side]) + arrived[side][0] for side in range(2)]
     stiff = wide_diagonals(diagonals, 0)
-    along_z = contract_z(jnp.concatenate([solid(left), solid(right)], axis=0), upper, lower, 0)
+    along_z = contract_z(jnp.concatenate([solid(v) for v in values], axis=0), upper, lower, 0)
     rows = [split(known[x]) for x in range(ROWS)]
-    for element, near, face, across, arrived, other, turned in (
-        (0, 0, left, 7, other_left, metrics_left, along_z[:16]),
-        (1, 7, right, 0, other_right, metrics_right, along_z[16:]),
-    ):
+    for side, near, across in ((0, 0, 7), (1, 7, 0)):
+        face, element = values[side], side
+        start_faces[side] = solid(own(face))
         mine = stored_factors(factors, element)
-        theirs = scaled_metrics(geo, other)
+        theirs = scaled_metrics(geo, arrived[side][2])
+        for c in range(3):
+            face_factors[side, c] = solid(theirs[c])
         scaled = mine[0] * face
         beside = line_of(stiffness, near * 9, WIDE) * scaled
         beside = beside + line_of(stiffness, across * 9, WIDE) * (theirs[0] * face)
         beside = beside + WEIGHTS[0] * (
-            (mine[1] + theirs[1]) * contract_y(face, stiff) + (mine[2] + theirs[2]) * split(turned)
+            (mine[1] + theirs[1]) * contract_y(face, stiff)
+            + (mine[2] + theirs[2]) * split(along_z[side * 16 : side * 16 + 16])
         )
         x = element * 8 + near
-        rows[x] = geo.assemble(split(rest[x]) + arrived - beside)
+        rows[x] = geo.assemble(split(rest[x]) + arrived[side][1] - beside)
         moved = geo.assemble(scaled)
         for i in range(8):
             if i != near:
@@ -512,24 +552,25 @@
     solved = [geo.assemble(v) for v in join_middle(solved)]
     for x in range(ROWS):
         local[x] = solid(solved[x])
-    beside = []
-    for element, near in ((0, 0), (1, 7)):
+    messages = []
+    for side, near in ((0, 0), (1, 7)):
         total = None
         for p in range(8):
             if p != near:
-                term = line_of(stiffness, near * 8 + p, WIDE) * solved[element * 8 + p]
+                term = line_of(stiffness, near * 8 + p, WIDE) * solved[side * 8 + p]
                 total = term if total is None else total + term
-        beside.append(solid(total))
-    for at, left_row, right_row in ((0, solid(solved[0]), solid(solved[15])), (16, beside[0], beside[1])):
-        message_a[at : at + 16] = jnp.where(even, right_row, left_row)
-        message_b[at : at + 16] = jnp.where(even, left_row, right_row)
+        value, beside = solid(solved[side * 8 + near]), solid(total)
+        face_values[side, 0], face_values[side, 1] = value, beside
+        folded = fold([v[at : at + 8, LANES:] for v in (value, beside) for at in (0, 8)], SECOND_FIELDS)
+        messages.append(jnp.concatenate([value[:, :LANES], beside[:, :LANES], folded], axis=0))
+    message_a[...] = jnp.where(even, messages[1], messages[0])
+    message_b[...] = jnp.where(even, messages[0], messages[1])
 
 
 def ahead_kernel(
-    local, factors, far_a, far_b, stiffness, lines, upper, lower, diagonals,
-    image, sums, face_factors, face_pieces,
+    local, factors, face_factors, stiffness, lines, upper, lower, diagonals,
+    image, sums, face_pieces,
 ):
-    even = even_index("gx")
     geo = Geometry(WIDE)
     rows = [split(local[x]) for x in range(ROWS)]
     rows[0] = rows[15] = jnp.zeros_like(rows[0])
@@ -553,10 +594,8 @@
     image[0] = image[15] = jnp.zeros((ROWS, LANES), jnp.float32)
     functions, turned = wide_functions(upper, lower)
     stiff_keep = kept_stiffness(geo, lines, stiffness)
-    for side, raw in enumerate(face_metrics(even, far_a, far_b)):
-        theirs = scaled_metrics(geo, raw)
-        for c in range(3):
-            face_factors[side, c] = solid(theirs[c])
+    for side in range(2):
+        theirs = [split(face_factors[side, c]) for c in range(3)]
         made = coarse_pieces(geo, theirs, stiff_keep, functions, turned)
         for b in range(4):
             for k in range(2):
@@ -564,28 +603,27 @@
 
 
 def image_kernel(
-    known, factors, face_factors, own_a, own_b, got_a, got_b, first_sums, second_sums, fixed,
+    known, factors, face_factors, face_values, got_a, got_b, first_sums, second_sums, fixed,
     stiffness, lines, upper, lower, diagonals,
     image, faces, payload,
 ):
     even = even_index("gx")
     geo = Geometry(WIDE)
     stiff = wide_diagonals(diagonals, 0)
-    mine, theirs = sided(even, own_a, own_b, 0), sided(even, got_a, got_b, 0)
-    mine_beside, theirs_beside = sided(even, own_a, own_b, 16), sided(even, got_a, got_b, 16)
-    values = [mine[side] + theirs[side] for side in range(2)]
+    arrived = [read_second(message) for message in both_sides(even, got_a, got_b)]
+    values = [face_values[side, 0] + arrived[side][0] for side in range(2)]
     along_z = contract_z(jnp.concatenate(values, axis=0), upper, lower, 0)
     extra = [second_sums[a : a + 1] for a in range(3)]
     rows = [known[x] for x in range(ROWS)]
-    for side, element, near, across in ((0, 1, 7, 0), (1, 0, 0, 7)):
-        value, arrived = split(values[side]), split(theirs[side])
-        faces[1 - side] = solid(own(value))
+    for side, near, across in ((0, 0, 7), (1, 7, 0)):
+        element, value = side, split(values[side])
+        faces[side] = solid(own(value))
         here, there = stored_factors(factors, element), [split(face_factors[side, c]) for c in range(3)]
         along_y, turned = contract_y(value, stiff), split(along_z[side * 16 : side * 16 + 16])
-        beside = split(mine_beside[side])
+        beside = split(face_values[side, 1])
         ours = here[0] * (beside + line_of(stiffness, near * 9, WIDE) * value)
         ours = ours + WEIGHTS[0] * (here[1] * along_y + here[2] * turned)
-        other = there[0] * (split(theirs_beside[side]) + line_of(stiffness, across * 9, WIDE) * value)
+        other = there[0] * (split(arrived[side][1]) + line_of(stiffness, across * 9, WIDE) * value)
         other = other + WEIGHTS[0] * (there[1] * along_y + there[2] * turned)
         rows[element * 8 + near] = solid(own(geo.assemble(ours + other)))
         spread = here[0] * value
@@ -728,11 +766,11 @@
             stiff(1, i) * low[0] + stiff(2, i) * high[0] + WEIGHTS[i] * (LOW[i] * low[1] + HIGH[i] * high[1])
         )
     extra = join_middle(extra)
-    beyond_x, beyond_w = face_pieces.at[1, 0], face_pieces.at[1, 1]
+    beyond_x, beyond_w = face_pieces.at[0, 0], face_pieces.at[0, 1]
     extra[0] = extra[0] + (
         stiff(1, 7) * mix(left, beyond_x) + stiff(2, 7) * mix(near, beyond_x) + WEIGHTS[7] * mix(near, beyond_w)
     )
-    extra[15] = extra[15] + stiff(0, 0) * mix(right, face_pieces.at[0, 0]) + WEIGHTS[0] * mix(right, face_pieces.at[0, 1])
+    extra[15] = extra[15] + stiff(0, 0) * mix(right, face_pieces.at[1, 0]) + WEIGHTS[0] * mix(right, face_pieces.at[1, 1])
     keep = solid(Geometry(LANES).keep)
     for x in range(ROWS):
         begin = start_faces[x // 15] if x in (0, 15) else start[x]
@@ -784,7 +822,7 @@
     per, count = coarse_inverse.shape
     small = per * count <= LANES
     block, wide, face = (ROWS, ROWS, LANES), (ROWS, ROWS, WIDE), (ROWS, LANES)
-    halo = (9, ROWS, LANES)
+    halo = (13, 8, LANES)
 
     first, second, own_metrics, source, previous = call(
         pack_kernel,
@@ -804,10 +842,10 @@
         "prepare",
     )(own_metrics, stiffness, fdm_vectors, fdm_values, vertex_map, coarse_inverse, jnp.asarray(lane_tables()))
 
-    message = (40, WIDE)
-    start, rest, metrics, factors, own_a, own_b = call(
+    message = (FIRST_ROWS, LANES)
+    start, rest, metrics, factors, halves, own_a, own_b = call(
         start_kernel,
-        [block, wide, (16, WIDE), (3, 2, ROWS, WIDE), message, message],
+        [block, wide, (16, WIDE), (3, 2, ROWS, WIDE), (2, ROWS, WIDE), message, message],
         [VMEM] * 9,
         "start",
     )(source, previous, own_metrics, first, second, stiff, upper, lower, diagonals)
@@ -816,25 +854,25 @@
         ready_kernel, [wide, wide, (2, 2, 4, ROWS, LANES)], [VMEM] * 8, "ready"
     )(rest, metrics, factors, lam, stiff, lines, upper, lower)
 
-    message = (32, WIDE)
-    start_faces, residual, local, side_a, side_b, sums = call(
+    message = (SECOND_ROWS, LANES)
+    start_faces, residual, local, face_values, face_factors, side_a, side_b, sums = call(
         solve_kernel,
-        [(2, ROWS, LANES), block, wide, message, message, (8, LANES)],
-        [VMEM] * 13,
+        [(2, ROWS, LANES), block, wide, (2, 2, ROWS, WIDE), (2, 3, ROWS, WIDE), message, message, (8, LANES)],
+        [VMEM] * 12,
         "solve",
-    )(rest, known, factors, inverse, own_a, own_b, far_a, far_b, stiff, vectors, upper, lower, diagonals)
+    )(rest, known, factors, inverse, halves, far_a, far_b, stiff, vectors, upper, lower, diagonals)
     got_a, got_b = swap(side_a, side_b, "gx")
-    image, more_sums, face_factors, face_pieces = call(
+    image, more_sums, face_pieces = call(
         ahead_kernel,
-        [block, (8, LANES), (2, 3, ROWS, WIDE), (2, 2, 4, ROWS, LANES)],
-        [VMEM] * 9,
+        [block, (8, LANES), (2, 2, 4, ROWS, LANES)],
+        [VMEM] * 8,
         "ahead",
-    )(local, factors, far_a, far_b, stiff, lines, upper, lower, diagonals)
+    )(local, factors, face_factors, stiff, lines, upper, lower, diagonals)
 
     image, faces, payload = call(
-        image_kernel, [block, (2, ROWS, LANES), (2 * devices, LANES)], [VMEM] * 15, "image"
+        image_kernel, [block, (2, ROWS, LANES), (2 * devices, LANES)], [VMEM] * 14, "image"
     )(
-        image, factors, face_factors, side_a, side_b, got_a, got_b, sums, more_sums, fixed,
+        image, factors, face_factors, face_values, got_a, got_b, sums, more_sums, fixed,
         stiff, lines, upper, lower, diagonals,
     )
     gathered = lax.all_to_all(payload.reshape(devices, 2, LANES), ("gx", "gz"), 0, 0)

time: 36 us -> 35.5 us (0.986)
  transfers between devices with their start and end apart: 6 -> 6, of which waited for: 5 -> 4; matrix products, arithmetic and copies ran while one was open for 0% -> 0% of each run, Pallas kernels for 9% -> 9%
where the time goes in v3:
time: 35.5 us; the launch traced here: 35.3 us
  starting transfers between devices  11.3 us (32%)
  blocking collectives  10.8 us (30%)
  Pallas kernels  8.11 us (23%)
  waiting for transfers between devices  4.45 us (13%)
  between operations  0.75 us (2%)
    all_to_all x1, blocking collectives, body(): lax.all_to_all(payload.reshape(devices, 2, LANES), ('gx', 'gz'), 0, 0)  10.8 us
    ppermute x3, starting transfers between devices, swap(): two = lax.ppermute(second, axis, odd + [(b, a) for a, b in odd])  8.65 us
    ppermute x3, waiting for transfers between devices, swap(): two = lax.ppermute(second, axis, odd + [(b, a) for a, b in odd])  3.83 us
    ppermute x3, starting transfers between devices, swap(): one = lax.ppermute(first, axis, [(i, i ^ 1) for i in range(size)])  2.6 us
    pallas_call x1, Pallas kernels, body(): call(functools.partial(prepare_kernel, small), [('half', 3, WIDE, WIDE),...  2.01 us
    pallas_call x1, Pallas kernels, body(): call(solve_kernel, [(2, ROWS, LANES), block, wide, (2, 2, ROWS, WIDE), (2...  1.35 us
    pallas_call x1, Pallas kernels, body(): call(kernel, [block, block], [VMEM] * len(operands), 'finish', [pltpu.VME...  1.31 us
    pallas_call x1, Pallas kernels, body(): call(pack_kernel, [halo, halo, face, block, block], [FAR] * 3, 'pack', [p...  1.22 us
  transfers between devices with their start and end apart: 6, of which 4 were waited for; matrix products, arithmetic and copies ran while one was open for 0% of the time, Pallas kernels for 9%

profile of v3, /device:TPU:0, one launch (start us, length us, event | category | flops | bytes accessed | tf_op | source)
XLA Modules:
  0.0 35.3 jit_solution(14707652316594386277)
XLA Ops:
  0.6 0.0 copy-start.1
  0.7 0.0 copy-start.3
  0.7 1.2 %pack.1 = (f32[13,8,128]{2,1,0:T(8,128)S(1)}, f32[13,8,128]{2,1,0:T(8,128)S(1)}, f32[16,128]{1,0:T(8,128)S(1)}, f32[16,16,128]{2,1,0:T(8,128)S(1)}, f32[16,16,128]{2,1,0:T(8,128)S(1)}) custom-call(f32[16,16,128]{2,1,0:T(8,128)} %source.1, f32[16,16,128]{2,1,0:T(8,128)} %previous.1, f32[3,2,2,16]{3,2,1,0:T(2,128)} %coefficients.1), custom_call_target="tpu_custom_call" | custom-call | tf_op jit(solution)/shard_map/pack/pallas_call | solution.py:827
  1.9 0.0 copy-start.2
  1.9 0.5 %collective-permute-start = (f32[13,8,128]{2,1,0:T(8,128)S(1)}, f32[13,8,128]{2,1,0:T(8,128)S(1)}, u32[]{:S(2)}, u32[]{:S(2)}) collective-permute-start(f32[13,8,128]{2,1,0:T(8,128)S(1)} %get-tuple-element.43), channel_id=1, source_target_pairs={{0,1},{1,0},{2,3},{3,2},{4,5},{5,4},{6,7},{7,6},{8,9},{9,8},{10,11... | collective-permute-start | bytes 159752 | tf_op jit(solution)/shard_map/ppermute | solution.py:811
  2.4 4.7 %collective-permute-start.1 = (f32[13,8,128]{2,1,0:T(8,128)S(1)}, f32[13,8,128]{2,1,0:T(8,128)S(1)}, u32[]{:S(2)}, u32[]{:S(2)}) collective-permute-start(f32[13,8,128]{2,1,0:T(8,128)S(1)} %get-tuple-element.44), channel_id=1, source_target_pairs={{1,2},{3,4},{5,6},{7,0},{2,1},{4,3},{6,5},{0,7},{9,10},{11,12},{13... | collective-permute-start | bytes 159752 | tf_op jit(solution)/shard_map/ppermute | solution.py:812
  7.2 2.0 %prepare.1 = (bf16[3,256,256]{2,1,0:T(8,128)(2,1)S(1)}, bf16[3,256,128]{2,1,0:T(8,128)(2,1)S(1)}, f32[3,8,8,128]{3,2,1,0:T(8,128)S(1)}, f32[64,128]{1,0:T(8,128)...) custom-call(f32[16,128]{1,0:T(8,128)S(1)} %get-tuple-element.42.metr, ...), custom_call_target="tpu_custom_call" | custom-call | tf_op jit(solution)/shard_map/prepare/pallas_call | solution.py:835
  9.2 0.0 collective-permute-done.first
  9.2 0.0 collective-permute-done.1.second
  9.2 0.7 %start.1 = (f32[16,16,128]{2,1,0:T(8,128)S(1)}, f32[16,16,256]{2,1,0:T(8,128)S(1)}, f32[16,256]{1,0:T(8,128)S(1)}, f32[3,2,16,256]{3,2,1,0:T(8,128)S(1)}, f32[2,...) custom-call(f32[16,16,128]{2,1,0:T(8,128)S(1)} %get-tuple-element.40.source, ...), custom_call_target="tpu_custom_call" | custom-call | tf_op jit(solution)/shard_map/start/pallas_call | solution.py:846
  9.9 1.5 %collective-permute-start.2 = (f32[56,128]{1,0:T(8,128)S(1)}, f32[56,128]{1,0:T(8,128)S(1)}, u32[]{:S(2)}, u32[]{:S(2)}) collective-permute-start(f32[56,128]{1,0:T(8,128)S(1)} %get-tuple-element.58), channel_id=1, source_target_pairs={{0,8},{8,0},{16,24},{24,16},{1,9},{9,1},{17,25},{25,17},{2,10},{10... | collective-permute-start | bytes 86024 | tf_op jit(solution)/shard_map/ppermute | solution.py:811
  11.5 1.5 %collective-permute-start.3 = (f32[56,128]{1,0:T(8,128)S(1)}, f32[56,128]{1,0:T(8,128)S(1)}, u32[]{:S(2)}, u32[]{:S(2)}) collective-permute-start(f32[56,128]{1,0:T(8,128)S(1)} %get-tuple-element.59), channel_id=1, source_target_pairs={{8,16},{24,0},{16,8},{0,24},{9,17},{25,1},{17,9},{1,25},{10,18},{2... | collective-permute-start | bytes 86024 | tf_op jit(solution)/shard_map/ppermute | solution.py:812
  13.0 0.4 %ready.1 = (f32[16,16,256]{2,1,0:T(8,128)S(1)}, f32[16,16,256]{2,1,0:T(8,128)S(1)}, f32[2,2,4,16,128]{4,3,2,1,0:T(8,128)S(1)}) custom-call(f32[16,16,256]{2,1,0:T(8,128)S(1)} %get-tuple-element.50.rest, f32[16,256]{1,0:T(8,128)S(1)} %get-tuple-element.51.metrics, f32[3,2,16,256]{3,2,1,0:T(8,128)S(1)} %get-tuple-element.52.factors, ...), custom_call_target="tpu_custom_call" | custom-call | tf_op jit(solution)/shard_map/ready/pallas_call | solution.py:853
  13.3 0.5 %collective-permute-done.2.got_a = f32[56,128]{1,0:T(8,128)S(1)} collective-permute-done((f32[56,128]{1,0:T(8,128)S(1)}, f32[56,128]{1,0:T(8,128)S(1)}, u32[]{:S(2)}, u32[]{:S(2)}) %collective-permute-start.2) | collective-permute-done | bytes 28704 | tf_op jit(solution)/shard_map/ppermute | solution.py:811
  13.9 2.4 %collective-permute-done.3.got_b = f32[56,128]{1,0:T(8,128)S(1)} collective-permute-done((f32[56,128]{1,0:T(8,128)S(1)}, f32[56,128]{1,0:T(8,128)S(1)}, u32[]{:S(2)}, u32[]{:S(2)}) %collective-permute-start.3) | collective-permute-done | bytes 28704 | tf_op jit(solution)/shard_map/ppermute | solution.py:812
  16.2 1.4 %solve.1 = (f32[2,16,128]{2,1,0:T(8,128)S(1)}, f32[16,16,128]{2,1,0:T(8,128)S(1)}, f32[16,16,256]{2,1,0:T(8,128)S(1)}, f32[2,2,16,256]{3,2,1,0:T(8,128)S(1)}, f3...) custom-call(f32[16,16,256]{2,1,0:T(8,128)S(1)} %get-tuple-element.50.rest, ...), custom_call_target="tpu_custom_call" | custom-call | tf_op jit(solution)/shard_map/solve/pallas_call | solution.py:858
  17.6 0.6 %collective-permute-start.4 = (f32[40,128]{1,0:T(8,128)S(1)}, f32[40,128]{1,0:T(8,128)S(1)}, u32[]{:S(2)}, u32[]{:S(2)}) collective-permute-start(f32[40,128]{1,0:T(8,128)S(1)} %get-tuple-element.67), channel_id=1, source_target_pairs={{0,8},{8,0},{16,24},{24,16},{1,9},{9,1},{17,25},{25,17},{2,10},{10... | collective-permute-start | bytes 61448 | tf_op jit(solution)/shard_map/ppermute | solution.py:811
  18.1 2.4 %collective-permute-start.5 = (f32[40,128]{1,0:T(8,128)S(1)}, f32[40,128]{1,0:T(8,128)S(1)}, u32[]{:S(2)}, u32[]{:S(2)}) collective-permute-start(f32[40,128]{1,0:T(8,128)S(1)} %get-tuple-element.68), channel_id=1, source_target_pairs={{8,16},{24,0},{16,8},{0,24},{9,17},{25,1},{17,9},{1,25},{10,18},{2... | collective-permute-start | bytes 61448 | tf_op jit(solution)/shard_map/ppermute | solution.py:812
  20.6 0.7 %ahead.1 = (f32[16,16,128]{2,1,0:T(8,128)S(1)}, f32[8,128]{1,0:T(8,128)S(1)}, f32[2,2,4,16,128]{4,3,2,1,0:T(8,128)S(1)}) custom-call(f32[16,16,256]{2,1,0:T(8,128)S(1)} %get-tuple-element.63.local.refs_3_, f32[3,2,16,256]{3,2,1,0:T(8,128)S(1)} %get-tuple-element.52.factors, f32[2,3,16,256]{3,2,1,0:T(8,128)S(1)} %get-tuple-element.64.face_factors, ...), custom_call_target="tpu_custom_call" | custom-call | tf_op jit(solution)/shard_map/ahead/pallas_call | solution.py:865
  21.3 0.1 collective-permute-done.4.got_a
  21.4 1.4 %collective-permute-done.5.got_b = f32[40,128]{1,0:T(8,128)S(1)} collective-permute-done((f32[40,128]{1,0:T(8,128)S(1)}, f32[40,128]{1,0:T(8,128)S(1)}, u32[]{:S(2)}, u32[]{:S(2)}) %collective-permute-start.5) | collective-permute-done | bytes 20512 | tf_op jit(solution)/shard_map/ppermute | solution.py:812
  22.8 0.4 %image.1 = (f32[16,16,128]{2,1,0:T(8,128)S(1)}, f32[2,16,128]{2,1,0:T(8,128)S(1)}, f32[64,128]{1,0:T(8,128)S(1)}) custom-call(f32[16,16,128]{2,1,0:T(8,128)S(1)} %get-tuple-element.65.known, f32[3,2,16,256]{3,2,1,0:T(8,128)S(1)} %get-tuple-element.52.factors, f32[2,3,16,256]{3,2,1,0:T(8,128)S(1)} %get-tuple-element.64.face_factors, ...), custom_call_target="tpu_custom_call" | custom-call | tf_op jit(solution)/shard_map/image/pallas_call | solution.py:872
  23.3 10.8 %all_to_all.5 = f32[32,2,128]{2,1,0:T(2,128)S(1)} all-to-all(f32[32,2,128]{2,1,0:T(2,128)S(1)} %bitcast.3), channel_id=1, replica_groups=mesh['gx'=4,'gz'=8] {'gx','gz'}, dimensions={0} | all-to-all | bytes 65536 | tf_op jit(solution)/shard_map/all_to_all | solution.py:878
  34.0 1.3 %finish.1 = (f32[16,16,128]{2,1,0:T(8,128)}, f32[16,16,128]{2,1,0:T(8,128)}) custom-call(f32[16,16,128]{2,1,0:T(8,128)S(1)} %get-tuple-element.49.refs_0_, f32[2,16,128]{2,1,0:T(8,128)S(1)} %get-tuple-element.61.refs_1_, f32[16,16,128]{2,1,0:T(8,128)S(1)} %get-tuple-element.62.refs_2_, f32[16,16,256]{2,1,0:T(8,128)S(1)} %get-tuple-element.63.local.refs_3_, ...), custom_call_target="tpu_custom_call" | custom-call | tf_op jit(solution)/shard_map/finish/pallas_call | solution.py:901
  (9 shorter events, 0.0 us)
Async XLA Ops:
  0.6 6.5 %copy-start = (s32[8,2,2,16]{3,2,1,0:T(2,128)S(1)}, s32[8,2,2,16]{3,2,1,0:T(2,128)}, u32[]{:S(2)}) copy-start(s32[8,2,2,16]{3,2,1,0:T(2,128)} %labels.1) | copy-start | bytes 6148
  0.6 6.5 %copy-start.1 = (f32[3,8,128]{2,1,0:T(8,128)S(1)}, f32[3,8,128]{2,1,0:T(8,128)}, u32[]{:S(2)}) copy-start(f32[3,8,128]{2,1,0:T(8,128)} %constant.2.clone.tables) | copy-start | bytes 36868
  0.7 6.5 %copy-start.3 = (f32[8,8]{1,0:T(8,128)S(1)}, f32[8,8]{1,0:T(8,128)}, u32[]{:S(2)}) copy-start(f32[8,8]{1,0:T(8,128)} %vectors.1) | copy-start | bytes 772
  1.9 5.3 %copy-start.2 = (f32[8,8]{1,0:T(8,128)S(1)}, f32[8,8]{1,0:T(8,128)}, u32[]{:S(2)}) copy-start(f32[8,8]{1,0:T(8,128)} %stiffness.1) | copy-start | bytes 772
  1.9 7.3 %collective-permute-start = (f32[13,8,128]{2,1,0:T(8,128)S(1)}, f32[13,8,128]{2,1,0:T(8,128)S(1)}, u32[]{:S(2)}, u32[]{:S(2)}) collective-permute-start(f32[13,8,128]{2,1,0:T(8,128)S(1)} %get-tuple-element.43), channel_id=1, source_target_pairs={{0,1},{1,0},{2,3},{3,2},{4,5},{5,4},{6,7},{7,6},{8,9},{9,8},{10,11... | collective-permute-start | bytes 159752 | tf_op jit(solution)/shard_map/ppermute | solution.py:811
  2.4 4.7 %copy-start.4 = (f32[2,64]{1,0:T(2,128)S(1)}, f32[2,64]{1,0:T(2,128)}, u32[]{:S(2)}) copy-start(f32[2,64]{1,0:T(2,128)} %coarse.1) | copy-start | bytes 1540
  2.4 4.7 %copy-start.5 = (f32[8]{0:T(128)S(1)}, f32[8]{0:T(128)}, u32[]{:S(2)}) copy-start(f32[8]{0:T(128)} %eigen.1) | copy-start | bytes 100
  2.4 6.8 %collective-permute-start.1 = (f32[13,8,128]{2,1,0:T(8,128)S(1)}, f32[13,8,128]{2,1,0:T(8,128)S(1)}, u32[]{:S(2)}, u32[]{:S(2)}) collective-permute-start(f32[13,8,128]{2,1,0:T(8,128)S(1)} %get-tuple-element.44), channel_id=1, source_target_pairs={{1,2},{3,4},{5,6},{7,0},{2,1},{4,3},{6,5},{0,7},{9,10},{11,12},{13... | collective-permute-start | bytes 159752 | tf_op jit(solution)/shard_map/ppermute | solution.py:812
  9.9 3.9 %collective-permute-start.2 = (f32[56,128]{1,0:T(8,128)S(1)}, f32[56,128]{1,0:T(8,128)S(1)}, u32[]{:S(2)}, u32[]{:S(2)}) collective-permute-start(f32[56,128]{1,0:T(8,128)S(1)} %get-tuple-element.58), channel_id=1, source_target_pairs={{0,8},{8,0},{16,24},{24,16},{1,9},{9,1},{17,25},{25,17},{2,10},{10... | collective-permute-start | bytes 86024 | tf_op jit(solution)/shard_map/ppermute | solution.py:811
  11.5 4.8 %collective-permute-start.3 = (f32[56,128]{1,0:T(8,128)S(1)}, f32[56,128]{1,0:T(8,128)S(1)}, u32[]{:S(2)}, u32[]{:S(2)}) collective-permute-start(f32[56,128]{1,0:T(8,128)S(1)} %get-tuple-element.59), channel_id=1, source_target_pairs={{8,16},{24,0},{16,8},{0,24},{9,17},{25,1},{17,9},{1,25},{10,18},{2... | collective-permute-start | bytes 86024 | tf_op jit(solution)/shard_map/ppermute | solution.py:812
  17.6 3.8 %collective-permute-start.4 = (f32[40,128]{1,0:T(8,128)S(1)}, f32[40,128]{1,0:T(8,128)S(1)}, u32[]{:S(2)}, u32[]{:S(2)}) collective-permute-start(f32[40,128]{1,0:T(8,128)S(1)} %get-tuple-element.67), channel_id=1, source_target_pairs={{0,8},{8,0},{16,24},{24,16},{1,9},{9,1},{17,25},{25,17},{2,10},{10... | collective-permute-start | bytes 61448 | tf_op jit(solution)/shard_map/ppermute | solution.py:811
  18.1 4.7 %collective-permute-start.5 = (f32[40,128]{1,0:T(8,128)S(1)}, f32[40,128]{1,0:T(8,128)S(1)}, u32[]{:S(2)}, u32[]{:S(2)}) collective-permute-start(f32[40,128]{1,0:T(8,128)S(1)} %get-tuple-element.68), channel_id=1, source_target_pairs={{8,16},{24,0},{16,8},{0,24},{9,17},{25,1},{17,9},{1,25},{10,18},{2... | collective-permute-start | bytes 61448 | tf_op jit(solution)/shard_map/ppermute | solution.py:812

commit v4 on v3

--- a/solution.py
+++ b/solution.py
@@ -40,7 +40,7 @@
 DEEP, SHALLOW = 25, 17
 SLOT = DEEP + SHALLOW
 FIRST_FIELDS = ((0, 24), (41, 17), (75, 17))
-SECOND_FIELDS = ((0, 8), (16, 8), (32, 8), (48, 8))
+SECOND_FIELDS = ((0, 16), (32, 16), (64, 16), (96, 16))
 FIRST_ROWS, SECOND_ROWS = 56, 40
 PAIRS = ((0, 0), (0, 1), (1, 1))
 GROUP_X = (ONES + LOW, [0.0] * 8 + HIGH)
@@ -120,9 +120,25 @@
     return jnp.concatenate([row] * (lanes // LANES), axis=1)[None]
 
 
-def contract_x(rows, table, i, transpose=False):
+def weighted(factors, rows):
+    total = None
+    for factor, row in zip(factors, rows):
+        total = factor * row if total is None else total + factor * row
+    return total
+
+
+def divisors_of(geo, c, lam):
+    lam_y = jnp.concatenate([lam[0]] * (WIDE // LANES), axis=1)[None]
+    lam_z = jnp.concatenate([lam[1]] * (WIDE // LANES), axis=1)[None]
+    base = c[1] * lam_y + c[2] * lam_z
+    return [1.0 / (c[0] * line_of(lam.at[0], i, WIDE) + base) for i in range(8)]
+
+
+def contract_x(rows, table, i, transpose=False, without=None):
     total = None
     for p in range(8):
+        if p == without:
+            continue
         factor = line_of(table, p * 8 + i if transpose else i * 8 + p, WIDE)
         term = factor * rows[p]
         total = term if total is None else total + term
@@ -258,7 +274,7 @@
 
 def prepare_kernel(
     with_coarse, metrics, stiffness, vectors, eigen, labels, coarse, tables,
-    upper, lower, diagonals, stiff_table, vector_table, lam, lines, fixed, near_tables,
+    upper, lower, diagonals, stiff_table, vector_table, bend, lam, lines, fixed, near_tables,
 ):
     near_tables[...] = tables[...]
     repeat = (iota((LANES, 8), 0) & 7 == iota((LANES, 8), 1)).astype(jnp.float32)
@@ -295,6 +311,10 @@
         put_diagonals(at, matrix)
     put_table(stiff_table, k)
     put_table(vector_table, s)
+    for side, near in ((0, 0), (1, 7)):
+        chosen = jnp.where(column == near, 0.0, s_turned * k[near : near + 1, :])
+        total = jnp.sum(chosen, axis=1, keepdims=True)
+        bend[8 * side : 8 * side + 8] = jnp.broadcast_to(total, (8, LANES))
     values = [eigen[i] for i in range(8)]
     lam[0] = pick(iota((8, LANES), 0), values)
     lam[1] = pick(iota((8, LANES), 1) & 7, values)
@@ -353,8 +373,8 @@
 
 
 def start_kernel(
-    source, previous, own_metrics, first, second, stiffness, upper, lower, diagonals,
-    start, rest, metrics, factors, halves, message_a, message_b,
+    source, previous, own_metrics, first, second, stiffness, vectors, bend, lam, upper, lower, diagonals,
+    start, known, factors, halves, remainders, spectrum, inverse, message_a, message_b, common, metrics,
 ):
     even = even_index("gz")
     lane = iota((8, LANES), 1)
@@ -392,22 +412,52 @@
         for c in range(3):
             factors[c, e] = solid(scaled[e][c])
     applied = apply_rows(rows, along_z, scaled, stiffness, wide_diagonals(diagonals, 0))
-    for x in range(ROWS):
-        rest[x] = solid(wide(source, x, DEEP, SHALLOW) - applied[x])
+    rest = [wide(source, x, DEEP, SHALLOW) - applied[x] for x in range(ROWS)]
     halves[0], halves[1] = solid(faces[0]), solid(faces[1])
+    remainders[0], remainders[1] = solid(rest[0]), solid(rest[15])
     messages = []
     for side, x in ((0, 0), (1, 15)):
-        half, value = halves[side], rest[x]
+        half, value = solid(faces[side]), solid(rest[x])
         rows = [metrics[(c * 2 + side) * 2 : (c * 2 + side) * 2 + 2] for c in range(3)]
         rows = jnp.concatenate(rows + [jnp.ones((2, WIDE), jnp.float32)], axis=0)
         lower_fold = fold([half[:8, LANES:], value[:8, LANES:], rows[:, LANES:]], FIRST_FIELDS)
         upper_fold = fold([half[8:, LANES:], value[8:, LANES:]], FIRST_FIELDS[:2])
-        messages.append(
-            jnp.concatenate([half[:, :LANES], value[:, :LANES], lower_fold, upper_fold, rows[:, :LANES]], axis=0)
-        )
+        messages += [half[:, :LANES], value[:, :LANES], lower_fold, upper_fold, rows[:, :LANES]]
+    messages = jnp.concatenate(messages, axis=0)
+    common[...] = messages
+    message_a[: 2 * FIRST_ROWS], message_b[: 2 * FIRST_ROWS] = messages, messages
+
+    rest = join_middle(rest)
+    zero = jnp.zeros((2, 8, WIDE), jnp.float32)
+    rest = [zero] + [geo.assemble(v) for v in rest[1:15]] + [zero]
+    forward = wide_diagonals(diagonals, 1)
+    moved = []
+    for element in range(2):
+        inside = rest[element * 8 : element * 8 + 8]
+        moved += [solid(contract_y(contract_x(inside, vectors, i, True, 7 * element), forward)) for i in range(8)]
+    for x in range(ROWS):
+        known[x] = solid(rest[x])
+    transformed = contract_z(jnp.concatenate(moved, axis=0), upper, lower, 1)
+    damped = []
+    for element in range(2):
+        divisors = divisors_of(geo, [metric(metrics, c, element) for c in range(3)], lam)
+        for i in range(8):
+            x = element * 8 + i
+            value = split(transformed[x * 16 : x * 16 + 16])
+            spectrum[x], inverse[x] = solid(value), solid(divisors[i])
+            damped.append(value * divisors[i])
+    messages = []
+    for side, near in ((0, 0), (1, 7)):
+        inside, across = damped[side * 8 : side * 8 + 8], damped[8 - side * 8 : 16 - side * 8]
+        value = contract_x(inside, vectors, near)
+        beside = weighted([line_of(bend, side * 8 + i, WIDE) for i in range(8)], inside)
+        beside = beside + line_of(stiffness, near * 8 + 7 - near, WIDE) * contract_x(across, vectors, near)
+        value, beside = solid(value), solid(beside)
+        folded = fold([v[at : at + 8, LANES:] for v in (value, beside) for at in (0, 8)], SECOND_FIELDS)
+        messages.append(jnp.concatenate([value[:, :LANES], beside[:, :LANES], folded], axis=0))
     even_x = even_index("gx")
-    message_a[...] = jnp.where(even_x, messages[1], messages[0])
-    message_b[...] = jnp.where(even_x, messages[0], messages[1])
+    message_a[2 * FIRST_ROWS :] = jnp.where(even_x, messages[1], messages[0])
+    message_b[2 * FIRST_ROWS :] = jnp.where(even_x, messages[0], messages[1])
 
 
 def both_sides(even, a, b):
@@ -460,198 +510,175 @@
     return jnp.concatenate([both] * (WIDE // LANES), axis=2)
 
 
-def ready_kernel(rest, metrics, factors, lam, stiffness, lines, upper, lower, known, inverse, pieces):
+def ready_kernel(factors, stiffness, lines, upper, lower, pieces, waves, stiff_keep):
     geo = Geometry(WIDE)
-    rows = join_middle([split(rest[x]) for x in range(ROWS)])
-    for x in range(1, ROWS - 1):
-        known[x] = solid(geo.assemble(rows[x]))
-    known[0] = known[15] = jnp.zeros((ROWS, WIDE), jnp.float32)
-    lam_y = jnp.concatenate([lam[0]] * (WIDE // LANES), axis=1)[None]
-    lam_z = jnp.concatenate([lam[1]] * (WIDE // LANES), axis=1)[None]
+    functions, turned = wide_functions(upper, lower)
+    for b in range(4):
+        waves[b : b + 1], waves[4 + b : 5 + b] = functions[b], turned[b]
+    along_y = kept_stiffness(geo, lines, stiffness)
+    stiff_keep[...] = solid(along_y)
     for element in range(2):
-        cx, cy, cz = (metric(metrics, c, element) for c in range(3))
-        base = cy * lam_y + cz * lam_z
-        for i in range(8):
-            inverse[element * 8 + i] = solid(1.0 / (cx * line_of(lam.at[0], i, WIDE) + base))
-    functions, turned = wide_functions(upper, lower)
-    stiff_keep = kept_stiffness(geo, lines, stiffness)
-    for element in range(2):
-        made = coarse_pieces(geo, stored_factors(factors, element), stiff_keep, functions, turned)
+        made = coarse_pieces(geo, stored_factors(factors, element), along_y, functions, turned)
         for b in range(4):
             for k in range(2):
                 pieces[element, k, b] = solid(own(made[b][k]))
 
 
 def solve_kernel(
-    rest, known, factors, inverse, halves, got_a, got_b,
-    stiffness, vectors, upper, lower, diagonals,
-    start_faces, residual, local, face_values, face_factors, message_a, message_b, sums,
+    known, factors, halves, remainders, spectrum, inverse, got_a, got_b, got_c, _,
+    stiffness, vectors, bend, lam, upper, lower, diagonals,
+    start_faces, residual, local, beside, face_factors, sums,
 ):
     even = even_index("gx")
     geo = Geometry(WIDE)
-    arrived = [read_first(message) for message in both_sides(even, got_a, got_b)]
-    values = [split(halves[side]) + arrived[side][0] for side in range(2)]
+    sides = both_sides(even, got_a, got_b)
+    beyond = got_c[...]
+    at = [side[: 2 * FIRST_ROWS] for side in sides]
+    near = [read_first(at[0][FIRST_ROWS:]), read_first(at[1][:FIRST_ROWS])]
+    far = [read_first(at[0][:FIRST_ROWS]), read_first(at[1][FIRST_ROWS:])]
+    last = [read_first(beyond[FIRST_ROWS:]), read_first(beyond[:FIRST_ROWS])]
+    mine = [stored_factors(factors, e) for e in range(2)]
+    near_factors, far_factors, last_factors = ([scaled_metrics(geo, v[2]) for v in group] for group in (near, far, last))
+    for side in range(2):
+        for c in range(3):
+            face_factors[side, c] = solid(near_factors[side][c])
+    values = [split(halves[side]) + near[side][0] for side in range(2)]
+    values += [far[side][0] + last[side][0] for side in range(2)]
+    remains = [split(remainders[side]) + near[side][1] for side in range(2)]
+    remains += [far[side][1] + last[side][1] for side in range(2)]
+    beside_left = [near_factors[0], mine[1], last_factors[0], far_factors[1]]
+    beside_right = [mine[0], near_factors[1], far_factors[0], last_factors[1]]
     stiff = wide_diagonals(diagonals, 0)
     along_z = contract_z(jnp.concatenate([solid(v) for v in values], axis=0), upper, lower, 0)
-    rows = [split(known[x]) for x in range(ROWS)]
-    for side, near, across in ((0, 0, 7), (1, 7, 0)):
-        face, element = values[side], side
-        start_faces[side] = solid(own(face))
-        mine = stored_factors(factors, element)
-        theirs = scaled_metrics(geo, arrived[side][2])
-        for c in range(3):
-            face_factors[side, c] = solid(theirs[c])
-        scaled = mine[0] * face
-        beside = line_of(stiffness, near * 9, WIDE) * scaled
-        beside = beside + line_of(stiffness, across * 9, WIDE) * (theirs[0] * face)
-        beside = beside + WEIGHTS[0] * (
-            (mine[1] + theirs[1]) * contract_y(face, stiff)
-            + (mine[2] + theirs[2]) * split(along_z[side * 16 : side * 16 + 16])
+    first, last_corner = line_of(stiffness, 0, WIDE), line_of(stiffness, 63, WIDE)
+    cross = line_of(stiffness, 7, WIDE)
+    totals, into_left, into_right = [], [], []
+    for k in range(4):
+        one, two, value = beside_left[k], beside_right[k], values[k]
+        left, right = one[0] * value, two[0] * value
+        taken = last_corner * left + first * right + WEIGHTS[0] * (
+            (one[1] + two[1]) * contract_y(value, stiff) + (one[2] + two[2]) * split(along_z[k * 16 : k * 16 + 16])
         )
-        x = element * 8 + near
-        rows[x] = geo.assemble(split(rest[x]) + arrived[side][1] - beside)
-        moved = geo.assemble(scaled)
+        totals.append(geo.assemble(remains[k] - taken))
+        into_left.append(geo.assemble(left) if k != 2 else None)
+        into_right.append(geo.assemble(right) if k != 3 else None)
+    for side in range(2):
+        start_faces[side] = solid(own(values[side]))
+
+    moved = [into_right[0], into_left[1]]
+    rows = [own(split(known[x])) for x in range(ROWS)]
+    rows[0], rows[15] = own(totals[0]), own(totals[1])
+    for side, face in ((0, 0), (1, 7)):
         for i in range(8):
-            if i != near:
-                change = line_of(stiffness, i * 8 + near, WIDE) * moved
-                x = element * 8 + i
+            if i != face:
+                change = line_of(stiffness, i * 8 + face, LANES) * own(moved[side])
+                x = side * 8 + i
                 rows[x] = rows[x] - change
                 if x in (7, 8):
                     rows[15 - x] = rows[15 - x] - change
     parts = [None, None]
     for x in range(ROWS):
-        residual[x] = solid(own(rows[x]))
+        residual[x] = solid(rows[x])
         for a in range(2):
             if GROUP_X[a][x] * INVERSE_X[x] != 0.0:
-                term = (GROUP_X[a][x] * INVERSE_X[x]) * own(rows[x])
+                term = (GROUP_X[a][x] * INVERSE_X[x]) * rows[x]
                 parts[a] = term if parts[a] is None else parts[a] + term
     weight = own(geo.inverse_y * geo.inverse_z)
     for a in range(2):
         sums[a : a + 1] = down(parts[a] * weight)
 
     forward, backward = wide_diagonals(diagonals, 1), wide_diagonals(diagonals, 2)
+    fields = totals + [into_left[0], into_left[1], into_left[3], into_right[0], into_right[1], into_right[2]]
+    flat = jnp.concatenate([solid(contract_y(v, forward)) for v in fields], axis=0)
+    flat = contract_z(flat, upper, lower, 1)
+    flat = [split(flat[k * 16 : k * 16 + 16]) for k in range(len(fields))]
+    totals, into_left = flat[:4], {0: flat[4], 1: flat[5], 3: flat[6]}
+    into_right = {0: flat[7], 1: flat[8], 2: flat[9]}
+
+    def vector(p, i):
+        return line_of(vectors, p * 8 + i, WIDE)
+
+    def changes(element, total, close, distant):
+        face, other = 7 * element, 7 - 7 * element
+        crossed = cross * distant
+        return [
+            vector(face, i) * total - line_of(bend, element * 8 + i, WIDE) * close - vector(other, i) * crossed
+            for i in range(8)
+        ]
+
     moved = []
-    for element in range(2):
-        inside = rows[element * 8 : element * 8 + 8]
-        moved += [solid(contract_y(contract_x(inside, vectors, i, True), forward)) for i in range(8)]
-    spectral = contract_z(jnp.concatenate(moved, axis=0), upper, lower, 1)
-    divided = [spectral[x * 16 : x * 16 + 16] * inverse[x] for x in range(ROWS)]
-    back = contract_z(jnp.concatenate(divided, axis=0), upper, lower, 2)
+    for element, change in enumerate(
+        (changes(0, totals[0], into_right[0], into_left[1]), changes(1, totals[1], into_left[1], into_right[0]))
+    ):
+        moved += [solid((split(spectrum[element * 8 + i]) + change[i]) * split(inverse[element * 8 + i])) for i in range(8)]
+    for side in range(2):
+        value, partial = (split(v) for v in read_second(sides[side][2 * FIRST_ROWS :]))
+        near_element, far_element = 1 - side, side
+        if side == 0:
+            close = changes(1, totals[0], into_left[0], into_right[2])
+            distant = changes(0, totals[2], into_right[2], into_left[0])
+        else:
+            close = changes(0, totals[1], into_right[1], into_left[3])
+            distant = changes(1, totals[3], into_left[3], into_right[1])
+        face = 7 * near_element
+        close = [a * b for a, b in zip(close, divisors_of(geo, near[side][2], lam))]
+        distant = [a * b for a, b in zip(distant, divisors_of(geo, far[side][2], lam))]
+        value = value + weighted([vector(face, i) for i in range(8)], close)
+        partial = partial + weighted([line_of(bend, near_element * 8 + i, WIDE) for i in range(8)], close)
+        partial = partial + cross * weighted([vector(face, i) for i in range(8)], distant)
+        moved += [solid(value), solid(partial)]
+
+    back = contract_z(jnp.concatenate(moved, axis=0), upper, lower, 2)
+    back = [contract_y(split(back[k * 16 : k * 16 + 16]), backward) for k in range(ROWS + 4)]
     solved = []
     for element in range(2):
-        inside = [
-            contract_y(split(back[x * 16 : x * 16 + 16]), backward) for x in range(element * 8, element * 8 + 8)
-        ]
+        inside = back[element * 8 : element * 8 + 8]
         solved += [contract_x(inside, vectors, i) for i in range(8)]
     total = None
     for x in range(ROWS):
-        term = own(solved[x]) * own(rows[x])
+        term = own(solved[x]) * rows[x]
         total = term if total is None else total + term
     sums[2:3] = down(total)
     sums[3:8] = jnp.zeros((5, LANES), jnp.float32)
-    solved = [geo.assemble(v) for v in join_middle(solved)]
+    solved = join_middle(solved)
+    solved[0], solved[15] = solved[0] + back[16], solved[15] + back[18]
     for x in range(ROWS):
-        local[x] = solid(solved[x])
-    messages = []
-    for side, near in ((0, 0), (1, 7)):
-        total = None
-        for p in range(8):
-            if p != near:
-                term = line_of(stiffness, near * 8 + p, WIDE) * solved[side * 8 + p]
-                total = term if total is None else total + term
-        value, beside = solid(solved[side * 8 + near]), solid(total)
-        face_values[side, 0], face_values[side, 1] = value, beside
-        folded = fold([v[at : at + 8, LANES:] for v in (value, beside) for at in (0, 8)], SECOND_FIELDS)
-        messages.append(jnp.concatenate([value[:, :LANES], beside[:, :LANES], folded], axis=0))
-    message_a[...] = jnp.where(even, messages[1], messages[0])
-    message_b[...] = jnp.where(even, messages[0], messages[1])
-
-
-def ahead_kernel(
-    local, factors, face_factors, stiffness, lines, upper, lower, diagonals,
-    image, sums, face_pieces,
+        local[x] = solid(geo.assemble(solved[x]))
+    for side in range(2):
+        beside[side] = solid(geo.assemble(back[17 + 2 * side]))
+
+
+def image_kernel(
+    local, factors, face_factors, beside, sums, fixed, stiffness, lines, upper, lower, diagonals,
+    image, payload,
 ):
     geo = Geometry(WIDE)
     rows = [split(local[x]) for x in range(ROWS)]
-    rows[0] = rows[15] = jnp.zeros_like(rows[0])
     along_z = contract_z(jnp.concatenate([solid(v) for v in rows], axis=0), upper, lower, 0)
     scaled = [stored_factors(factors, e) for e in range(2)]
-    applied = apply_rows(rows, along_z, scaled, stiffness, wide_diagonals(diagonals, 0))
+    stiff = wide_diagonals(diagonals, 0)
+    applied = apply_rows(rows, along_z, scaled, stiffness, stiff)
     total, parts = None, [None, None]
-    for x in range(1, ROWS - 1):
+    for x in range(ROWS):
         term = own(applied[x]) * own(rows[x])
         total = term if total is None else total + term
         for a in range(2):
             if GROUP_X[a][x] != 0.0:
                 term = GROUP_X[a][x] * own(applied[x])
                 parts[a] = term if parts[a] is None else parts[a] + term
-    for at, value in enumerate(parts + [total]):
-        sums[at : at + 1] = down(value * own(geo.keep))
-    sums[3:8] = jnp.zeros((5, LANES), jnp.float32)
-    joined = join_middle(applied)
-    for x in range(1, ROWS - 1):
-        image[x] = solid(own(geo.assemble(joined[x])))
-    image[0] = image[15] = jnp.zeros((ROWS, LANES), jnp.float32)
-    functions, turned = wide_functions(upper, lower)
-    stiff_keep = kept_stiffness(geo, lines, stiffness)
-    for side in range(2):
-        theirs = [split(face_factors[side, c]) for c in range(3)]
-        made = coarse_pieces(geo, theirs, stiff_keep, functions, turned)
-        for b in range(4):
-            for k in range(2):
-                face_pieces[side, k, b] = solid(own(made[b][k]))
-
-
-def image_kernel(
-    known, factors, face_factors, face_values, got_a, got_b, first_sums, second_sums, fixed,
-    stiffness, lines, upper, lower, diagonals,
-    image, faces, payload,
-):
-    even = even_index("gx")
-    geo = Geometry(WIDE)
-    stiff = wide_diagonals(diagonals, 0)
-    arrived = [read_second(message) for message in both_sides(even, got_a, got_b)]
-    values = [face_values[side, 0] + arrived[side][0] for side in range(2)]
-    along_z = contract_z(jnp.concatenate(values, axis=0), upper, lower, 0)
-    extra = [second_sums[a : a + 1] for a in range(3)]
-    rows = [known[x] for x in range(ROWS)]
-    for side, near, across in ((0, 0, 7), (1, 7, 0)):
-        element, value = side, split(values[side])
-        faces[side] = solid(own(value))
-        here, there = stored_factors(factors, element), [split(face_factors[side, c]) for c in range(3)]
-        along_y, turned = contract_y(value, stiff), split(along_z[side * 16 : side * 16 + 16])
-        beside = split(face_values[side, 1])
-        ours = here[0] * (beside + line_of(stiffness, near * 9, WIDE) * value)
-        ours = ours + WEIGHTS[0] * (here[1] * along_y + here[2] * turned)
-        other = there[0] * (split(arrived[side][1]) + line_of(stiffness, across * 9, WIDE) * value)
-        other = other + WEIGHTS[0] * (there[1] * along_y + there[2] * turned)
-        rows[element * 8 + near] = solid(own(geo.assemble(ours + other)))
-        spread = here[0] * value
-        moved = solid(own(geo.assemble(spread)))
-        for i in range(8):
-            if i != near:
-                change = stiffness[i * 8 + near : i * 8 + near + 1, :] * moved
-                x = element * 8 + i
-                rows[x] = rows[x] + change
-                if x in (7, 8):
-                    rows[15 - x] = rows[15 - x] + change
-        near_only = own(spread * geo.keep)
-        kept = own(ours * geo.keep)
-        for a in range(2):
-            line = GROUP_X[a][element * 8 : element * 8 + 8]
-            if any(line):
-                at = 0 if line == ONES else 1 + a
-                factor = lines[at, near : near + 1, :]
-                if line[near] != 0.0:
-                    factor = factor - line[near] * stiffness[near * 9 : near * 9 + 1, :]
-                    extra[a] = extra[a] + down(line[near] * kept)
-                extra[a] = extra[a] + factor * down(near_only)
-        extra[2] = extra[2] + down(own(beside) * near_only + own(value) * kept)
+    extra = [down(value * own(geo.keep)) for value in parts + [total]]
+    for side, x, across in ((0, 0, 63), (1, 15, 0)):
+        there = [split(face_factors[side, c]) for c in range(3)]
+        other = there[0] * (split(beside[side]) + line_of(stiffness, across, WIDE) * rows[x])
+        turned = split(along_z[x * 16 : x * 16 + 16])
+        other = other + WEIGHTS[0] * (there[1] * contract_y(rows[x], stiff) + there[2] * turned)
+        applied[x] = applied[x] + other
+    applied = join_middle(applied)
     for x in range(ROWS):
-        image[x] = rows[x]
+        image[x] = solid(own(geo.assemble(applied[x])))
     zero = jnp.zeros((1, LANES), jnp.float32)
     table = jnp.concatenate(
-        [first_sums[0:2], extra[0], extra[1], fixed[0:9], first_sums[2:3], extra[2], zero], axis=0
+        [sums[0:2], extra[0], extra[1], fixed[0:9], sums[2:3], extra[2], zero], axis=0
     )
     lane = iota((LANES, LANES), 1) & 7
     node = iota((LANES, LANES), 0)
@@ -690,7 +717,7 @@
 
 def final_kernel(
     devices, spans, count, per,
-    start, start_faces, residual, local, faces, image, pieces, face_pieces, lines, tables,
+    start, start_faces, residual, local, image, pieces, face_factors, waves, stiff_keep, lines, tables,
     gathered, given, new_solution, new_residual, values,
 ):
     rows = gathered[pl.ds(0, devices, stride=2), :]
@@ -739,7 +766,6 @@
     behind = values[pl.ds(gx * spans + before_z, 1), :]
     aside = values[pl.ds(before_x * spans + gz, 1), :]
     corner = values[pl.ds(before_x * spans + before_z, 1), :]
-    functions = [group_lanes(LANES, b) for b in range(3)]
 
     def four(line, back, a):
         return [back[:, 3 * a + 1 : 3 * a + 2]] + [line[:, 3 * a + b : 3 * a + b + 1] for b in range(3)]
@@ -751,8 +777,6 @@
         return total
 
     near, right, left = four(here, behind, 0), four(here, behind, 1), four(aside, corner, 0)
-    line_near = sum(near[1 + b] * functions[b] for b in range(3))
-    line_right = sum(right[1 + b] * functions[b] for b in range(3))
     whole = [mix(near, pieces.at[0, k]) for k in range(2)]
     low = [mix(near, pieces.at[1, k]) for k in range(2)]
     high = [mix(right, pieces.at[1, k]) for k in range(2)]
@@ -766,15 +790,32 @@
             stiff(1, i) * low[0] + stiff(2, i) * high[0] + WEIGHTS[i] * (LOW[i] * low[1] + HIGH[i] * high[1])
         )
     extra = join_middle(extra)
-    beyond_x, beyond_w = face_pieces.at[0, 0], face_pieces.at[0, 1]
-    extra[0] = extra[0] + (
-        stiff(1, 7) * mix(left, beyond_x) + stiff(2, 7) * mix(near, beyond_x) + WEIGHTS[7] * mix(near, beyond_w)
-    )
-    extra[15] = extra[15] + stiff(0, 0) * mix(right, face_pieces.at[1, 0]) + WEIGHTS[0] * mix(right, face_pieces.at[1, 1])
-    keep = solid(Geometry(LANES).keep)
+    geo = Geometry(WIDE)
+
+    def line(numbers, at):
+        total = numbers[0] * waves[at : at + 1, :]
+        for b in range(1, 4):
+            total = total + numbers[b] * waves[at + b : at + b + 1, :]
+        return total
+
+    def wide_stiff(k, i):
+        return jnp.concatenate([stiff(k, i)] * (WIDE // LANES), axis=1)
+
+    def beyond(side, stiff_x, plain, turned):
+        fx, fy, fz = (split(face_factors[side, c]) for c in range(3))
+        value = fx * geo.keep * stiff_x[None]
+        value = value + WEIGHTS[0] * (fy * split(stiff_keep[...]) * plain[None] + fz * geo.keep * turned[None])
+        return solid(own(geo.assemble(value)))
+
+    wave_near, wave_right = line(near, 0), line(right, 0)
+    across = wide_stiff(1, 7) * line(left, 0) + wide_stiff(2, 7) * wave_near
+    extra[0] = extra[0] + beyond(0, across, wave_near, line(near, 4))
+    extra[15] = extra[15] + beyond(1, wide_stiff(0, 0) * wave_right, wave_right, line(right, 4))
+    keep = solid(own(geo.keep))
+    line_near, line_right = wave_near[:, :LANES], wave_right[:, :LANES]
     for x in range(ROWS):
         begin = start_faces[x // 15] if x in (0, 15) else start[x]
-        mine = faces[x // 15] if x in (0, 15) else local[x, :, :LANES]
+        mine = local[x, :, :LANES]
         new_residual[x] = residual[x] - alpha * (image[x] + extra[x])
         coarse_line = GROUP_X[0][x] * line_near
         if GROUP_X[1][x] != 0.0:
@@ -811,6 +852,15 @@
     one = lax.ppermute(first, axis, [(i, i ^ 1) for i in range(size)])
     two = lax.ppermute(second, axis, odd + [(b, a) for a, b in odd])
     return one, two
+
+
+def second_neighbours(common, axis):
+    size = lax.axis_size(axis)
+    if size == 4:
+        return lax.ppermute(common, axis, [(i, i ^ 2) for i in range(size)])
+    left = lax.ppermute(common[:FIRST_ROWS], axis, [(i, (i - 2) % size) for i in range(size)])
+    right = lax.ppermute(common[FIRST_ROWS:], axis, [(i, (i + 2) % size) for i in range(size)])
+    return jnp.concatenate([left, right], axis=0)
 
 
 def body(
@@ -832,61 +882,57 @@
         [pltpu.VMEM(coefficients.shape, jnp.float32), pltpu.VMEM((16, 16), jnp.float32), pltpu.SemaphoreType.DMA((3,))],
     )(*(pltpu.with_memory_space_constraint(v, pltpu.HBM) for v in (source, previous, coefficients)))
     first, second = swap(first, second, "gz")
-    upper, lower, diagonals, stiff, vectors, lam, lines, fixed, tables = call(
+    upper, lower, diagonals, stiff, vectors, bend, lam, lines, fixed, tables = call(
         functools.partial(prepare_kernel, small),
         [
             ("half", 3, WIDE, WIDE), ("half", 3, WIDE, LANES), (3, 8, 8, LANES),
-            (64, LANES), (64, LANES), (2, 8, LANES), (3, 8, LANES), (24, LANES), (3, 8, LANES),
+            (64, LANES), (64, LANES), (16, LANES), (2, 8, LANES), (3, 8, LANES), (24, LANES), (3, 8, LANES),
         ],
         [VMEM] * 3 + [SMEM] * 2 + [VMEM if small else FAR, VMEM],
         "prepare",
     )(own_metrics, stiffness, fdm_vectors, fdm_values, vertex_map, coarse_inverse, jnp.asarray(lane_tables()))
 
-    message = (FIRST_ROWS, LANES)
-    start, rest, metrics, factors, halves, own_a, own_b = call(
+    message = (2 * FIRST_ROWS + SECOND_ROWS, LANES)
+    start, known, factors, halves, remainders, spectrum, inverse, side_a, side_b, common = call(
         start_kernel,
-        [block, wide, (16, WIDE), (3, 2, ROWS, WIDE), (2, ROWS, WIDE), message, message],
-        [VMEM] * 9,
+        [
+            block, wide, (3, 2, ROWS, WIDE), (2, ROWS, WIDE), (2, ROWS, WIDE), wide, wide,
+            message, message, (2 * FIRST_ROWS, LANES),
+        ],
+        [VMEM] * 12,
         "start",
-    )(source, previous, own_metrics, first, second, stiff, upper, lower, diagonals)
-    far_a, far_b = swap(own_a, own_b, "gx")
-    known, inverse, pieces = call(
-        ready_kernel, [wide, wide, (2, 2, 4, ROWS, LANES)], [VMEM] * 8, "ready"
-    )(rest, metrics, factors, lam, stiff, lines, upper, lower)
-
-    message = (SECOND_ROWS, LANES)
-    start_faces, residual, local, face_values, face_factors, side_a, side_b, sums = call(
+        [pltpu.VMEM((16, WIDE), jnp.float32)],
+    )(source, previous, own_metrics, first, second, stiff, vectors, bend, lam, upper, lower, diagonals)
+    beyond = second_neighbours(common, "gx")
+    side_a, side_b = swap(side_a, side_b, "gx")
+    pieces, waves, stiff_keep = call(
+        ready_kernel, [(2, 2, 4, ROWS, LANES), (8, WIDE), (ROWS, WIDE)], [VMEM] * 5, "ready"
+    )(factors, stiff, lines, upper, lower)
+
+    start_faces, residual, local, beside, face_factors, sums = call(
         solve_kernel,
-        [(2, ROWS, LANES), block, wide, (2, 2, ROWS, WIDE), (2, 3, ROWS, WIDE), message, message, (8, LANES)],
-        [VMEM] * 12,
+        [(2, ROWS, LANES), block, wide, (2, ROWS, WIDE), (2, 3, ROWS, WIDE), (8, LANES)],
+        [VMEM] * 17,
         "solve",
-    )(rest, known, factors, inverse, halves, far_a, far_b, stiff, vectors, upper, lower, diagonals)
-    got_a, got_b = swap(side_a, side_b, "gx")
-    image, more_sums, face_pieces = call(
-        ahead_kernel,
-        [block, (8, LANES), (2, 2, 4, ROWS, LANES)],
-        [VMEM] * 8,
-        "ahead",
-    )(local, factors, face_factors, stiff, lines, upper, lower, diagonals)
-
-    image, faces, payload = call(
-        image_kernel, [block, (2, ROWS, LANES), (2 * devices, LANES)], [VMEM] * 14, "image"
     )(
-        image, factors, face_factors, face_values, got_a, got_b, sums, more_sums, fixed,
-        stiff, lines, upper, lower, diagonals,
+        known, factors, halves, remainders, spectrum, inverse, side_a, side_b, beyond, waves,
+        stiff, vectors, bend, lam, upper, lower, diagonals,
+    )
+    image, payload = call(image_kernel, [block, (2 * devices, LANES)], [VMEM] * 11, "image")(
+        local, factors, face_factors, beside, sums, fixed, stiff, lines, upper, lower, diagonals
     )
     gathered = lax.all_to_all(payload.reshape(devices, 2, LANES), ("gx", "gz"), 0, 0)
     gathered = gathered.reshape(2 * devices, LANES)
 
     operands = [
-        start, start_faces, residual, local, faces, image, pieces, face_pieces, lines,
+        start, start_faces, residual, local, image, pieces, face_factors, waves, stiff_keep, lines,
         tables, gathered,
     ]
     finish = functools.partial(final_kernel, devices, spans, count, per)
     if small:
 
         def kernel(*refs):
-            finish(*refs[:11], None, *refs[11:])
+            finish(*refs[:12], None, *refs[12:])
 
     else:
         kernel = finish

time: 35.5 us -> 33 us (0.930)
  starting transfers between devices: 11.3 us -> 8.76 us
  waiting for transfers between devices: 4.45 us -> 3.62 us
  Pallas kernels: 8.11 us -> 8.54 us
  blocking collectives: 10.8 us -> 11.2 us
    ppermute x3 -> x2, waiting for transfers between devices: 3.83 us -> 0.01 us  [swap(): two = lax.ppermute(second, axis, odd + [(b, a) for a, b in odd])]
    ppermute x0 -> x1, waiting for transfers between devices: none -> 3.61 us  [second_neighbours(): return lax.ppermute(common, axis, [(i, i ^ 2) for i in range(size)])]
    ppermute x3 -> x2, starting transfers between devices: 8.65 us -> 6.2 us  [swap(): two = lax.ppermute(second, axis, odd + [(b, a) for a, b in odd])]
    ppermute x3 -> x2, waiting for transfers between devices: 0.62 us -> 0.01 us  [swap(): one = lax.ppermute(first, axis, [(i, i ^ 1) for i in range(size)])]
    ppermute x3 -> x2, starting transfers between devices: 2.6 us -> 2.05 us  [swap(): one = lax.ppermute(first, axis, [(i, i ^ 1) for i in range(size)])]
    ppermute x0 -> x1, starting transfers between devices: none -> 0.51 us  [second_neighbours(): return lax.ppermute(common, axis, [(i, i ^ 2) for i in range(size)])]
    all_to_all x1, blocking collectives: 10.8 us -> 11.2 us  [body(): lax.all_to_all(payload.reshape(devices, 2, LANES), ('gx', 'gz'), 0, 0)]
    pallas_call x5 -> x4, Pallas kernels: 3.57 us -> 4.01 us  [the longest x1 1.43 us: body(): call(solve_kernel, [(2, ROWS, LANES), block, wide, (2, ROWS, WIDE), (2, 3...]
  transfers between devices with their start and end apart: 6 -> 5, of which waited for: 4 -> 1; matrix products, arithmetic and copies ran while one was open for 0% -> 0% of each run, Pallas kernels for 9% -> 7%
where the time goes in v4:
time: 33 us; the launch traced here: 32.9 us
  blocking collectives  11.2 us (34%)
  starting transfers between devices  8.76 us (27%)
  Pallas kernels  8.54 us (26%)
  waiting for transfers between devices  3.62 us (11%)
  between operations  0.73 us (2%)
    all_to_all x1, blocking collectives, body(): lax.all_to_all(payload.reshape(devices, 2, LANES), ('gx', 'gz'), 0, 0)  11.2 us
    ppermute x2, starting transfers between devices, swap(): two = lax.ppermute(second, axis, odd + [(b, a) for a, b in odd])  6.2 us
    ppermute x1, waiting for transfers between devices, second_neighbours(): return lax.ppermute(common, axis, [(i, i ^ 2) for i in range(size)])  3.61 us
    ppermute x2, starting transfers between devices, swap(): one = lax.ppermute(first, axis, [(i, i ^ 1) for i in range(size)])  2.05 us
    pallas_call x1, Pallas kernels, body(): call(functools.partial(prepare_kernel, small), [('half', 3, WIDE, WIDE),...  2.01 us
    pallas_call x1, Pallas kernels, body(): call(solve_kernel, [(2, ROWS, LANES), block, wide, (2, ROWS, WIDE), (2, 3...  1.43 us
    pallas_call x1, Pallas kernels, body(): call(start_kernel, [block, wide, (3, 2, ROWS, WIDE), (2, ROWS, WIDE), (2,...  1.39 us
    pallas_call x1, Pallas kernels, body(): call(kernel, [block, block], [VMEM] * len(operands), 'finish', [pltpu.VME...  1.3 us
  transfers between devices with their start and end apart: 5, of which 1 were waited for; matrix products, arithmetic and copies ran while one was open for 0% of the time, Pallas kernels for 7%

profile of v4, /device:TPU:0, one launch (start us, length us, event | category | flops | bytes accessed | tf_op | source)
XLA Modules:
  0.0 32.9 jit_solution(1945696007565419560)
XLA Ops:
  0.6 0.0 copy-start
  0.6 0.0 copy-start.1
  0.7 0.0 copy-start.3
  0.7 1.2 %pack.1 = (f32[13,8,128]{2,1,0:T(8,128)S(1)}, f32[13,8,128]{2,1,0:T(8,128)S(1)}, f32[16,128]{1,0:T(8,128)S(1)}, f32[16,16,128]{2,1,0:T(8,128)S(1)}, f32[16,16,128]{2,1,0:T(8,128)S(1)}) custom-call(f32[16,16,128]{2,1,0:T(8,128)} %source.1, f32[16,16,128]{2,1,0:T(8,128)} %previous.1, f32[3,2,2,16]{3,2,1,0:T(2,128)} %coefficients.1), custom_call_target="tpu_custom_call" | custom-call | tf_op jit(solution)/shard_map/pack/pallas_call | solution.py:877
  1.9 0.0 copy-start.2
  1.9 0.5 %collective-permute-start = (f32[13,8,128]{2,1,0:T(8,128)S(1)}, f32[13,8,128]{2,1,0:T(8,128)S(1)}, u32[]{:S(2)}, u32[]{:S(2)}) collective-permute-start(f32[13,8,128]{2,1,0:T(8,128)S(1)} %get-tuple-element.41), channel_id=1, source_target_pairs={{0,1},{1,0},{2,3},{3,2},{4,5},{5,4},{6,7},{7,6},{8,9},{9,8},{10,11... | collective-permute-start | bytes 159752 | tf_op jit(solution)/shard_map/ppermute | solution.py:852
  2.4 4.7 %collective-permute-start.1 = (f32[13,8,128]{2,1,0:T(8,128)S(1)}, f32[13,8,128]{2,1,0:T(8,128)S(1)}, u32[]{:S(2)}, u32[]{:S(2)}) collective-permute-start(f32[13,8,128]{2,1,0:T(8,128)S(1)} %get-tuple-element.42), channel_id=1, source_target_pairs={{1,2},{3,4},{5,6},{7,0},{2,1},{4,3},{6,5},{0,7},{9,10},{11,12},{13... | collective-permute-start | bytes 159752 | tf_op jit(solution)/shard_map/ppermute | solution.py:853
  7.1 0.0 copy-done.1
  7.1 0.0 copy-done.2
  7.2 2.0 %prepare.1 = (bf16[3,256,256]{2,1,0:T(8,128)(2,1)S(1)}, bf16[3,256,128]{2,1,0:T(8,128)(2,1)S(1)}, f32[3,8,8,128]{3,2,1,0:T(8,128)S(1)}, f32[64,128]{1,0:T(8,128)...) custom-call(f32[16,128]{1,0:T(8,128)S(1)} %get-tuple-element.40.metr, ...), custom_call_target="tpu_custom_call" | custom-call | tf_op jit(solution)/shard_map/prepare/pallas_call | solution.py:885
  9.2 0.0 collective-permute-done.first
  9.2 0.0 collective-permute-done.1.second
  9.2 1.4 %start.1 = (f32[16,16,128]{2,1,0:T(8,128)S(1)}, f32[16,16,256]{2,1,0:T(8,128)S(1)}, f32[3,2,16,256]{3,2,1,0:T(8,128)S(1)}, f32[2,16,256]{2,1,0:T(8,128)S(1)}, f3...) custom-call(f32[16,16,128]{2,1,0:T(8,128)S(1)} %get-tuple-element.38, ...), custom_call_target="tpu_custom_call" | custom-call | tf_op jit(solution)/shard_map/start/pallas_call | solution.py:896
  10.6 1.5 %collective-permute-start.2 = (f32[152,128]{1,0:T(8,128)S(1)}, f32[152,128]{1,0:T(8,128)S(1)}, u32[]{:S(2)}, u32[]{:S(2)}) collective-permute-start(f32[152,128]{1,0:T(8,128)S(1)} %get-tuple-element.57), channel_id=1, source_target_pairs={{0,8},{8,0},{16,24},{24,16},{1,9},{9,1},{17,25},{25,17},{2,10},{10... | collective-permute-start | bytes 233480 | tf_op jit(solution)/shard_map/ppermute | solution.py:852
  12.1 1.5 %collective-permute-start.3 = (f32[152,128]{1,0:T(8,128)S(1)}, f32[152,128]{1,0:T(8,128)S(1)}, u32[]{:S(2)}, u32[]{:S(2)}) collective-permute-start(f32[152,128]{1,0:T(8,128)S(1)} %get-tuple-element.58), channel_id=1, source_target_pairs={{8,16},{24,0},{16,8},{0,24},{9,17},{25,1},{17,9},{1,25},{10,18},{2... | collective-permute-start | bytes 233480 | tf_op jit(solution)/shard_map/ppermute | solution.py:853
  13.6 0.5 %collective-permute-start.4 = (f32[112,128]{1,0:T(8,128)S(1)}, f32[112,128]{1,0:T(8,128)S(1)}, u32[]{:S(2)}, u32[]{:S(2)}) collective-permute-start(f32[112,128]{1,0:T(8,128)S(1)} %get-tuple-element.59), channel_id=1, source_target_pairs={{0,16},{8,24},{16,0},{24,8},{1,17},{9,25},{17,1},{25,9},{2,18},{10... | collective-permute-start | bytes 172040 | tf_op jit(solution)/shard_map/ppermute | solution.py:860
  14.1 0.3 ready.1
  14.4 3.6 %collective-permute-done.4.got_c = f32[112,128]{1,0:T(8,128)S(1)} collective-permute-done((f32[112,128]{1,0:T(8,128)S(1)}, f32[112,128]{1,0:T(8,128)S(1)}, u32[]{:S(2)}, u32[]{:S(2)}) %collective-permute-start.4) | collective-permute-done | bytes 57376 | tf_op jit(solution)/shard_map/ppermute | solution.py:860
  18.0 0.0 collective-permute-done.2.got_a
  18.0 0.0 collective-permute-done.3.got_b
  18.0 1.4 %solve.1 = (f32[2,16,128]{2,1,0:T(8,128)S(1)}, f32[16,16,128]{2,1,0:T(8,128)S(1)}, f32[16,16,256]{2,1,0:T(8,128)S(1)}, f32[2,16,256]{2,1,0:T(8,128)S(1)}, f32[2,...) custom-call(f32[16,16,256]{2,1,0:T(8,128)S(1)} %get-tuple-element.51.known, ...), custom_call_target="tpu_custom_call" | custom-call | tf_op jit(solution)/shard_map/solve/pallas_call | solution.py:912
  19.5 0.9 %image.1 = (f32[16,16,128]{2,1,0:T(8,128)S(1)}, f32[64,128]{1,0:T(8,128)S(1)}) custom-call(f32[16,16,256]{2,1,0:T(8,128)S(1)} %get-tuple-element.64.local.refs_3_, f32[3,2,16,256]{3,2,1,0:T(8,128)S(1)} %get-tuple-element.52.factors, f32[2,3,16,256]{3,2,1,0:T(8,128)S(1)} %get-tuple-element.65.face_factors.refs_6_, ...), custom_call_target="tpu_custom_call" | custom-call | tf_op jit(solution)/shard_map/image/pallas_call | solution.py:921
  20.4 11.2 %all_to_all.5 = f32[32,2,128]{2,1,0:T(2,128)S(1)} all-to-all(f32[32,2,128]{2,1,0:T(2,128)S(1)} %bitcast.3), channel_id=1, replica_groups=mesh['gx'=4,'gz'=8] {'gx','gz'}, dimensions={0} | all-to-all | bytes 65536 | tf_op jit(solution)/shard_map/all_to_all | solution.py:924
  31.6 1.3 %finish.1 = (f32[16,16,128]{2,1,0:T(8,128)}, f32[16,16,128]{2,1,0:T(8,128)}) custom-call(f32[16,16,128]{2,1,0:T(8,128)S(1)} %get-tuple-element.50.refs_0_, f32[2,16,128]{2,1,0:T(8,128)S(1)} %get-tuple-element.62.refs_1_, f32[16,16,128]{2,1,0:T(8,128)S(1)} %get-tuple-element.63.refs_2_, f32[16,16,256]{2,1,0:T(8,128)S(1)} %get-tuple-element.64.local.refs_3_, ...), custom_call_target="tpu_custom_call" | custom-call | tf_op jit(solution)/shard_map/finish/pallas_call | solution.py:947
  (6 shorter events, 0.0 us)
Async XLA Ops:
  0.6 6.5 %copy-start = (s32[8,2,2,16]{3,2,1,0:T(2,128)S(1)}, s32[8,2,2,16]{3,2,1,0:T(2,128)}, u32[]{:S(2)}) copy-start(s32[8,2,2,16]{3,2,1,0:T(2,128)} %labels.1) | copy-start | bytes 6148
  0.6 6.5 %copy-start.1 = (f32[3,8,128]{2,1,0:T(8,128)S(1)}, f32[3,8,128]{2,1,0:T(8,128)}, u32[]{:S(2)}) copy-start(f32[3,8,128]{2,1,0:T(8,128)} %constant.2.clone.tables) | copy-start | bytes 36868
  0.7 6.5 %copy-start.3 = (f32[8,8]{1,0:T(8,128)S(1)}, f32[8,8]{1,0:T(8,128)}, u32[]{:S(2)}) copy-start(f32[8,8]{1,0:T(8,128)} %vectors.1) | copy-start | bytes 772
  1.9 5.3 %copy-start.2 = (f32[8,8]{1,0:T(8,128)S(1)}, f32[8,8]{1,0:T(8,128)}, u32[]{:S(2)}) copy-start(f32[8,8]{1,0:T(8,128)} %stiffness.1) | copy-start | bytes 772
  1.9 7.3 %collective-permute-start = (f32[13,8,128]{2,1,0:T(8,128)S(1)}, f32[13,8,128]{2,1,0:T(8,128)S(1)}, u32[]{:S(2)}, u32[]{:S(2)}) collective-permute-start(f32[13,8,128]{2,1,0:T(8,128)S(1)} %get-tuple-element.41), channel_id=1, source_target_pairs={{0,1},{1,0},{2,3},{3,2},{4,5},{5,4},{6,7},{7,6},{8,9},{9,8},{10,11... | collective-permute-start | bytes 159752 | tf_op jit(solution)/shard_map/ppermute | solution.py:852
  2.4 4.7 %copy-start.4 = (f32[2,64]{1,0:T(2,128)S(1)}, f32[2,64]{1,0:T(2,128)}, u32[]{:S(2)}) copy-start(f32[2,64]{1,0:T(2,128)} %coarse.1) | copy-start | bytes 1540
  2.4 4.7 %copy-start.5 = (f32[8]{0:T(128)S(1)}, f32[8]{0:T(128)}, u32[]{:S(2)}) copy-start(f32[8]{0:T(128)} %eigen.1) | copy-start | bytes 100
  2.4 6.8 %collective-permute-start.1 = (f32[13,8,128]{2,1,0:T(8,128)S(1)}, f32[13,8,128]{2,1,0:T(8,128)S(1)}, u32[]{:S(2)}, u32[]{:S(2)}) collective-permute-start(f32[13,8,128]{2,1,0:T(8,128)S(1)} %get-tuple-element.42), channel_id=1, source_target_pairs={{1,2},{3,4},{5,6},{7,0},{2,1},{4,3},{6,5},{0,7},{9,10},{11,12},{13... | collective-permute-start | bytes 159752 | tf_op jit(solution)/shard_map/ppermute | solution.py:853
  10.6 7.4 %collective-permute-start.2 = (f32[152,128]{1,0:T(8,128)S(1)}, f32[152,128]{1,0:T(8,128)S(1)}, u32[]{:S(2)}, u32[]{:S(2)}) collective-permute-start(f32[152,128]{1,0:T(8,128)S(1)} %get-tuple-element.57), channel_id=1, source_target_pairs={{0,8},{8,0},{16,24},{24,16},{1,9},{9,1},{17,25},{25,17},{2,10},{10... | collective-permute-start | bytes 233480 | tf_op jit(solution)/shard_map/ppermute | solution.py:852
  12.1 5.9 %collective-permute-start.3 = (f32[152,128]{1,0:T(8,128)S(1)}, f32[152,128]{1,0:T(8,128)S(1)}, u32[]{:S(2)}, u32[]{:S(2)}) collective-permute-start(f32[152,128]{1,0:T(8,128)S(1)} %get-tuple-element.58), channel_id=1, source_target_pairs={{8,16},{24,0},{16,8},{0,24},{9,17},{25,1},{17,9},{1,25},{10,18},{2... | collective-permute-start | bytes 233480 | tf_op jit(solution)/shard_map/ppermute | solution.py:853
  13.6 4.4 %collective-permute-start.4 = (f32[112,128]{1,0:T(8,128)S(1)}, f32[112,128]{1,0:T(8,128)S(1)}, u32[]{:S(2)}, u32[]{:S(2)}) collective-permute-start(f32[112,128]{1,0:T(8,128)S(1)} %get-tuple-element.59), channel_id=1, source_target_pairs={{0,16},{8,24},{16,0},{24,8},{1,17},{9,25},{17,1},{25,9},{2,18},{10... | collective-permute-start | bytes 172040 | tf_op jit(solution)/shard_map/ppermute | solution.py:860

commit v5 on v4

--- a/solution.py
+++ b/solution.py
@@ -41,7 +41,8 @@
 SLOT = DEEP + SHALLOW
 FIRST_FIELDS = ((0, 24), (41, 17), (75, 17))
 SECOND_FIELDS = ((0, 16), (32, 16), (64, 16), (96, 16))
-FIRST_ROWS, SECOND_ROWS = 56, 40
+FAR_FIELDS = ((0, 24), (48, 24))
+FIRST_ROWS, FAR_ROWS, SECOND_ROWS = 56, 32, 40
 PAIRS = ((0, 0), (0, 1), (1, 1))
 GROUP_X = (ONES + LOW, [0.0] * 8 + HIGH)
 INVERSE_X = [0.5] + [1.0] * 6 + [0.5] + [0.5] + [1.0] * 6 + [0.5]
@@ -134,11 +135,9 @@
     return [1.0 / (c[0] * line_of(lam.at[0], i, WIDE) + base) for i in range(8)]
 
 
-def contract_x(rows, table, i, transpose=False, without=None):
+def contract_x(rows, table, i, transpose=False):
     total = None
     for p in range(8):
-        if p == without:
-            continue
         factor = line_of(table, p * 8 + i if transpose else i * 8 + p, WIDE)
         term = factor * rows[p]
         total = term if total is None else total + term
@@ -146,11 +145,11 @@
 
 
 def contract_y(v, diagonals):
-    total = diagonals[0] * v
-    for d in range(1, 8):
-        rolled = jnp.stack([pltpu.roll(v[e], 8 - d, 0) for e in range(2)])
-        total = total + diagonals[d] * rolled
-    return total
+    def moved(value, rows):
+        return jnp.stack([pltpu.roll(value[e], 8 - rows, 0) for e in range(2)])
+
+    shifted = [v] + [moved(v, d) for d in range(1, 4)]
+    return weighted(diagonals[:4], shifted) + moved(weighted(diagonals[4:], shifted), 4)
 
 
 def thirds(v):
@@ -236,7 +235,7 @@
     return here + jnp.where(((element + 1) >> 3) == group, high, 0.0)
 
 
-def pack_kernel(source, previous, coefficients, first, second, metrics, near_source, near_previous, raw, scratch, ready):
+def pack_kernel(source, previous, coefficients, first, second, elements, near_source, near_previous, raw, ready):
     copies = [
         pltpu.make_async_copy(source, near_source, ready.at[0]),
         pltpu.make_async_copy(previous, near_previous, ready.at[1]),
@@ -245,16 +244,13 @@
     for copy in copies:
         copy.start()
     even = even_index("gz")
-    scratch[...] = jnp.zeros_like(scratch)
-    widen = (iota((16, LANES), 0) == (iota((16, LANES), 1) >> 3)).astype(jnp.float32)
+    elements[...] = jnp.zeros_like(elements)
     for copy in copies:
         copy.wait()
     for c in range(3):
         for element in range(2):
             at = (c * 2 + element) * 2
-            scratch[at : at + 2, :] = raw[c, element]
-    spread = jnp.dot(scratch[...], widen, precision=EXACT, preferred_element_type=jnp.float32)
-    metrics[...] = spread
+            elements[at : at + 2, 0:16] = raw[c, element]
     slot = iota((8, LANES), 1)
     for to_right, out in ((even, first), (jnp.logical_not(even), second)):
         for tile in range(11):
@@ -268,15 +264,21 @@
                     moved = pltpu.roll(ref[n // 2, 8 * (n % 2) : 8 * (n % 2) + 8], shift, 1)
                     packed = moved if packed is None else jnp.where(slot >= at, moved, packed)
             out[tile] = packed
-        out[11] = spread[:8]
-        out[12] = spread[8:]
+        out[11] = elements[:8]
+        out[12] = elements[8:]
+
+
+def lanes_of(elements):
+    widen = (iota((16, LANES), 0) == (iota((16, LANES), 1) >> 3)).astype(jnp.float32)
+    return jnp.dot(elements[:, 0:16], widen, precision=EXACT, preferred_element_type=jnp.float32)
 
 
 def prepare_kernel(
-    with_coarse, metrics, stiffness, vectors, eigen, labels, coarse, tables,
-    upper, lower, diagonals, stiff_table, vector_table, bend, lam, lines, fixed, near_tables,
+    with_coarse, elements, stiffness, vectors, eigen, labels, coarse, tables,
+    metrics, upper, lower, diagonals, stiff_table, vector_table, bend, lam, lines, fixed, near_tables,
 ):
     near_tables[...] = tables[...]
+    metrics[...] = lanes_of(elements[...])
     repeat = (iota((LANES, 8), 0) & 7 == iota((LANES, 8), 1)).astype(jnp.float32)
     same = (iota((LANES, LANES), 0) >> 3) == (iota((LANES, LANES), 1) >> 3)
     unit = (iota((8, 8), 0) == iota((8, 8), 1)).astype(jnp.float32)
@@ -287,15 +289,18 @@
 
     def put_block(at, matrix):
         half = dot(repeat, matrix, ((1,), (0,)))
-        block = jnp.where(same, dot(half, repeat, ((1,), (1,))), 0.0)
+        put_thirds(at, jnp.where(same, dot(half, repeat, ((1,), (1,))), 0.0))
+
+    def put_thirds(at, block):
         high, middle, low = thirds(block)
         both = jnp.concatenate([high, middle], axis=1)
         upper[at] = jnp.concatenate([both, both], axis=0)
         lower[at] = jnp.concatenate([high, low], axis=0)
 
     def put_diagonals(at, matrix):
+        turned = jnp.concatenate([matrix[4:], matrix[:4]], axis=0)
         for d in range(8):
-            chosen = jnp.where(column == ((row + d) & 7), matrix, 0.0)
+            chosen = jnp.where(column == ((row + d % 4) & 7), matrix if d < 4 else turned, 0.0)
             diagonals[at, d] = jnp.broadcast_to(jnp.sum(chosen, axis=1, keepdims=True), (8, LANES))
 
     def put_table(out, matrix):
@@ -303,6 +308,13 @@
         chosen = jnp.where(iota((64, 8), 0) & 7 == iota((64, 8), 1), dot(tall, matrix, ((1,), (0,))), 0.0)
         out[...] = jnp.broadcast_to(jnp.sum(chosen, axis=1, keepdims=True), (64, LANES))
 
+    lane = iota((LANES, LANES), 1) & 7
+    node = iota((LANES, LANES), 0)
+    element, position = node >> 3, node & 7
+    low, high = pick(position, LOW), pick(position, HIGH)
+    columns = jnp.where(lane == (element >> 3), low, 0.0) + jnp.where(lane == ((element + 1) >> 3), high, 0.0)
+    columns = jnp.where(lane == 3, 1.0, jnp.where(lane < 3, columns, 0.0))
+    put_thirds(3, columns)
     k, s = stiffness[...], vectors[...]
     k_turned, s_turned = dot(k, unit, ((0,), (0,))), dot(s, unit, ((0,), (0,)))
     for at, matrix in enumerate((k_turned, s, s_turned)):
@@ -394,16 +406,15 @@
 
     geo = Geometry(WIDE)
     metrics[:, :LANES] = own_metrics[...]
-    for e in range(2):
-        right, left = from_right[11 + e], from_left[11 + e]
-        metrics[8 * e : 8 * e + 8, LANES:] = jnp.where(
-            lane < HALO, right, jnp.where(lane >= LANES - HALO, left, 1.0)
-        )
+    around = lanes_of(jnp.concatenate([from_right[11], from_right[12], from_left[11], from_left[12]], axis=0))
+    wide_lane = iota((16, LANES), 1)
+    metrics[:, LANES:] = jnp.where(
+        wide_lane < HALO, around[:16], jnp.where(wide_lane >= LANES - HALO, around[16:], 1.0)
+    )
     factor = geo.keep * geo.inverse_y * geo.inverse_z
     rows = [geo.pair(wide(previous, x, 0, DEEP)) * (factor * INVERSE_X[x]) for x in range(ROWS)]
     rows = join_middle(rows)
     faces = (rows[0], rows[15])
-    rows[0] = rows[15] = jnp.zeros_like(rows[0])
     for x in range(ROWS):
         start[x] = solid(own(rows[x]))
     along_z = contract_z(jnp.concatenate([solid(v) for v in rows], axis=0), upper, lower, 0)
@@ -415,26 +426,32 @@
     rest = [wide(source, x, DEEP, SHALLOW) - applied[x] for x in range(ROWS)]
     halves[0], halves[1] = solid(faces[0]), solid(faces[1])
     remainders[0], remainders[1] = solid(rest[0]), solid(rest[15])
-    messages = []
+    coefficients = [
+        jnp.concatenate(
+            [metrics[(c * 2 + side) * 2 : (c * 2 + side) * 2 + 2] for c in range(3)] + [jnp.ones((2, WIDE), jnp.float32)],
+            axis=0,
+        )
+        for side in range(2)
+    ]
+    messages, distant = [], []
     for side, x in ((0, 0), (1, 15)):
         half, value = solid(faces[side]), solid(rest[x])
-        rows = [metrics[(c * 2 + side) * 2 : (c * 2 + side) * 2 + 2] for c in range(3)]
-        rows = jnp.concatenate(rows + [jnp.ones((2, WIDE), jnp.float32)], axis=0)
+        rows, others = coefficients[side], coefficients[1 - side]
         lower_fold = fold([half[:8, LANES:], value[:8, LANES:], rows[:, LANES:]], FIRST_FIELDS)
-        upper_fold = fold([half[8:, LANES:], value[8:, LANES:]], FIRST_FIELDS[:2])
-        messages += [half[:, :LANES], value[:, :LANES], lower_fold, upper_fold, rows[:, :LANES]]
-    messages = jnp.concatenate(messages, axis=0)
-    common[...] = messages
-    message_a[: 2 * FIRST_ROWS], message_b[: 2 * FIRST_ROWS] = messages, messages
-
-    rest = join_middle(rest)
-    zero = jnp.zeros((2, 8, WIDE), jnp.float32)
-    rest = [zero] + [geo.assemble(v) for v in rest[1:15]] + [zero]
+        upper_fold = fold([half[8:, LANES:], value[8:, LANES:], others[:, LANES:]], FIRST_FIELDS)
+        parts = [half[:, :LANES], value[:, :LANES], lower_fold, upper_fold, rows[:, :LANES]]
+        messages.append(jnp.concatenate(parts, axis=0))
+        folded = fold([half[:8, LANES:], half[8:, LANES:]], FAR_FIELDS)
+        distant.append(jnp.concatenate([half[:, :LANES], folded, rows[:, :LANES]], axis=0))
+    common[...] = jnp.concatenate(messages, axis=0)
+    both = [jnp.concatenate([messages[side], distant[1 - side]], axis=0) for side in range(2)]
+
+    rest = [geo.assemble(v) for v in join_middle(rest)]
     forward = wide_diagonals(diagonals, 1)
     moved = []
     for element in range(2):
         inside = rest[element * 8 : element * 8 + 8]
-        moved += [solid(contract_y(contract_x(inside, vectors, i, True, 7 * element), forward)) for i in range(8)]
+        moved += [solid(contract_y(contract_x(inside, vectors, i, True), forward)) for i in range(8)]
     for x in range(ROWS):
         known[x] = solid(rest[x])
     transformed = contract_z(jnp.concatenate(moved, axis=0), upper, lower, 1)
@@ -456,8 +473,9 @@
         folded = fold([v[at : at + 8, LANES:] for v in (value, beside) for at in (0, 8)], SECOND_FIELDS)
         messages.append(jnp.concatenate([value[:, :LANES], beside[:, :LANES], folded], axis=0))
     even_x = even_index("gx")
-    message_a[2 * FIRST_ROWS :] = jnp.where(even_x, messages[1], messages[0])
-    message_b[2 * FIRST_ROWS :] = jnp.where(even_x, messages[0], messages[1])
+    both = [jnp.concatenate([both[side], messages[side]], axis=0) for side in range(2)]
+    message_a[...] = jnp.where(even_x, both[1], both[0])
+    message_b[...] = jnp.where(even_x, both[0], both[1])
 
 
 def both_sides(even, a, b):
@@ -471,11 +489,20 @@
         widen(message[16 * k : 16 * k + 16], [unfold(lower_fold, FIRST_FIELDS[k]), unfold(upper_fold, FIRST_FIELDS[k])])
         for k in range(2)
     )
-    rows = widen(message[48:56], [unfold(lower_fold, FIRST_FIELDS[2], 1.0)])
-    metrics = [
+    return split(half), split(value), spread_metrics(message[48:56], lower_fold)
+
+
+def spread_metrics(tile, folded):
+    rows = widen(tile, [unfold(folded, FIRST_FIELDS[2], 1.0)])
+    return [
         jnp.stack([jnp.broadcast_to(rows[2 * c + e : 2 * c + e + 1], (8, WIDE)) for e in range(2)]) for c in range(3)
     ]
-    return split(half), split(value), metrics
+
+
+def read_far(message):
+    far = message[FIRST_ROWS : FIRST_ROWS + FAR_ROWS]
+    half = widen(far[0:16], [unfold(far[16:24], field) for field in FAR_FIELDS])
+    return split(half), spread_metrics(far[24:32], message[40:48])
 
 
 def read_second(message):
@@ -533,41 +560,43 @@
     geo = Geometry(WIDE)
     sides = both_sides(even, got_a, got_b)
     beyond = got_c[...]
-    at = [side[: 2 * FIRST_ROWS] for side in sides]
-    near = [read_first(at[0][FIRST_ROWS:]), read_first(at[1][:FIRST_ROWS])]
-    far = [read_first(at[0][:FIRST_ROWS]), read_first(at[1][FIRST_ROWS:])]
+    near = [read_first(side) for side in sides]
+    far = [read_far(side) for side in sides]
     last = [read_first(beyond[FIRST_ROWS:]), read_first(beyond[:FIRST_ROWS])]
     mine = [stored_factors(factors, e) for e in range(2)]
-    near_factors, far_factors, last_factors = ([scaled_metrics(geo, v[2]) for v in group] for group in (near, far, last))
+    near_factors, far_factors, last_factors = (
+        [scaled_metrics(geo, v[-1]) for v in group] for group in (near, far, last)
+    )
     for side in range(2):
         for c in range(3):
             face_factors[side, c] = solid(near_factors[side][c])
-    values = [split(halves[side]) + near[side][0] for side in range(2)]
-    values += [far[side][0] + last[side][0] for side in range(2)]
-    remains = [split(remainders[side]) + near[side][1] for side in range(2)]
-    remains += [far[side][1] + last[side][1] for side in range(2)]
-    beside_left = [near_factors[0], mine[1], last_factors[0], far_factors[1]]
-    beside_right = [mine[0], near_factors[1], far_factors[0], last_factors[1]]
+    half = [split(halves[side]) for side in range(2)]
+    remain = [split(remainders[side]) for side in range(2)]
+    left_half = [near[0][0], half[1], last[0][0], far[1][0]]
+    right_half = [half[0], near[1][0], far[0][0], last[1][0]]
+    left_factors = [near_factors[0], mine[1], last_factors[0], far_factors[1]]
+    right_factors = [mine[0], near_factors[1], far_factors[0], last_factors[1]]
     stiff = wide_diagonals(diagonals, 0)
-    along_z = contract_z(jnp.concatenate([solid(v) for v in values], axis=0), upper, lower, 0)
+    along_z = contract_z(jnp.concatenate([solid(v) for v in left_half + right_half], axis=0), upper, lower, 0)
     first, last_corner = line_of(stiffness, 0, WIDE), line_of(stiffness, 63, WIDE)
     cross = line_of(stiffness, 7, WIDE)
-    totals, into_left, into_right = [], [], []
+    taken, into_left, into_right = [], [], []
     for k in range(4):
-        one, two, value = beside_left[k], beside_right[k], values[k]
-        left, right = one[0] * value, two[0] * value
-        taken = last_corner * left + first * right + WEIGHTS[0] * (
-            (one[1] + two[1]) * contract_y(value, stiff) + (one[2] + two[2]) * split(along_z[k * 16 : k * 16 + 16])
-        )
-        totals.append(geo.assemble(remains[k] - taken))
+        left, right = left_factors[k][0] * right_half[k], right_factors[k][0] * left_half[k]
+        from_left, from_right = split(along_z[k * 16 : k * 16 + 16]), split(along_z[k * 16 + 64 : k * 16 + 80])
+        rest = left_factors[k][1] * contract_y(right_half[k], stiff) + right_factors[k][1] * contract_y(left_half[k], stiff)
+        rest = rest + left_factors[k][2] * from_right + right_factors[k][2] * from_left
+        taken.append(last_corner * left + first * right + WEIGHTS[0] * rest)
         into_left.append(geo.assemble(left) if k != 2 else None)
         into_right.append(geo.assemble(right) if k != 3 else None)
+    to_right = [geo.assemble(v - t) for v, t in zip((near[0][1], remain[1], last[0][1]), taken[:3])]
+    to_left = [geo.assemble(v - taken[k]) for k, v in ((0, remain[0]), (1, near[1][1]), (3, last[1][1]))]
     for side in range(2):
-        start_faces[side] = solid(own(values[side]))
+        start_faces[side] = solid(own(left_half[side] + right_half[side]))
 
     moved = [into_right[0], into_left[1]]
     rows = [own(split(known[x])) for x in range(ROWS)]
-    rows[0], rows[15] = own(totals[0]), own(totals[1])
+    rows[0], rows[15] = rows[0] + own(to_right[0]), rows[15] + own(to_left[1])
     for side, face in ((0, 0), (1, 7)):
         for i in range(8):
             if i != face:
@@ -588,12 +617,12 @@
         sums[a : a + 1] = down(parts[a] * weight)
 
     forward, backward = wide_diagonals(diagonals, 1), wide_diagonals(diagonals, 2)
-    fields = totals + [into_left[0], into_left[1], into_left[3], into_right[0], into_right[1], into_right[2]]
+    fields = to_right + to_left + [into_left[0], into_left[1], into_left[3], into_right[0], into_right[1], into_right[2]]
     flat = jnp.concatenate([solid(contract_y(v, forward)) for v in fields], axis=0)
     flat = contract_z(flat, upper, lower, 1)
     flat = [split(flat[k * 16 : k * 16 + 16]) for k in range(len(fields))]
-    totals, into_left = flat[:4], {0: flat[4], 1: flat[5], 3: flat[6]}
-    into_right = {0: flat[7], 1: flat[8], 2: flat[9]}
+    to_right, to_left = flat[:3], flat[3:6]
+    into_left, into_right = {0: flat[6], 1: flat[7], 3: flat[8]}, {0: flat[9], 1: flat[10], 2: flat[11]}
 
     def vector(p, i):
         return line_of(vectors, p * 8 + i, WIDE)
@@ -608,21 +637,21 @@
 
     moved = []
     for element, change in enumerate(
-        (changes(0, totals[0], into_right[0], into_left[1]), changes(1, totals[1], into_left[1], into_right[0]))
+        (changes(0, to_right[0], into_right[0], into_left[1]), changes(1, to_left[1], into_left[1], into_right[0]))
     ):
         moved += [solid((split(spectrum[element * 8 + i]) + change[i]) * split(inverse[element * 8 + i])) for i in range(8)]
     for side in range(2):
-        value, partial = (split(v) for v in read_second(sides[side][2 * FIRST_ROWS :]))
+        value, partial = (split(v) for v in read_second(sides[side][FIRST_ROWS + FAR_ROWS :]))
         near_element, far_element = 1 - side, side
         if side == 0:
-            close = changes(1, totals[0], into_left[0], into_right[2])
-            distant = changes(0, totals[2], into_right[2], into_left[0])
+            close = changes(1, to_left[0], into_left[0], into_right[2])
+            distant = changes(0, to_right[2], into_right[2], into_left[0])
         else:
-            close = changes(0, totals[1], into_right[1], into_left[3])
-            distant = changes(1, totals[3], into_left[3], into_right[1])
+            close = changes(0, to_right[1], into_right[1], into_left[3])
+            distant = changes(1, to_left[2], into_left[3], into_right[1])
         face = 7 * near_element
         close = [a * b for a, b in zip(close, divisors_of(geo, near[side][2], lam))]
-        distant = [a * b for a, b in zip(distant, divisors_of(geo, far[side][2], lam))]
+        distant = [a * b for a, b in zip(distant, divisors_of(geo, far[side][1], lam))]
         value = value + weighted([vector(face, i) for i in range(8)], close)
         partial = partial + weighted([line_of(bend, near_element * 8 + i, WIDE) for i in range(8)], close)
         partial = partial + cross * weighted([vector(face, i) for i in range(8)], distant)
@@ -680,18 +709,27 @@
     table = jnp.concatenate(
         [sums[0:2], extra[0], extra[1], fixed[0:9], sums[2:3], extra[2], zero], axis=0
     )
-    lane = iota((LANES, LANES), 1) & 7
-    node = iota((LANES, LANES), 0)
-    element, position = node >> 3, node & 7
-    low, high = pick(position, LOW), pick(position, HIGH)
-    columns = jnp.where(lane == (element >> 3), low, 0.0) + jnp.where(lane == ((element + 1) >> 3), high, 0.0)
-    columns = jnp.where(lane == 3, 1.0, jnp.where(lane < 3, columns, 0.0))
-    reduced = jnp.dot(table, columns, precision=EXACT, preferred_element_type=jnp.float32)
+    reduced = contract_z(table, upper, lower, 3)
     mine = (iota((16, LANES), 1) >> 3) == iota((16, LANES), 0)
     row = jnp.sum(jnp.where(mine, reduced, 0.0), axis=0, keepdims=True) + fixed[16:17]
     block = jnp.concatenate([row, fixed[17:18]] * 4, axis=0)
     copies = payload.shape[0] // 8
     payload[...] = jnp.broadcast_to(block[None], (copies, 8, LANES)).reshape(copies * 8, LANES)
+
+
+def middle_kernel(
+    known, factors, halves, remainders, spectrum, inverse, got_a, got_b, got_c, waves,
+    stiffness, vectors, bend, lam, upper, lower, diagonals, fixed, lines,
+    start_faces, residual, local, face_factors, image, payload, beside, sums,
+):
+    solve_kernel(
+        known, factors, halves, remainders, spectrum, inverse, got_a, got_b, got_c, waves,
+        stiffness, vectors, bend, lam, upper, lower, diagonals,
+        start_faces, residual, local, beside, face_factors, sums,
+    )
+    image_kernel(
+        local, factors, face_factors, beside, sums, fixed, stiffness, lines, upper, lower, diagonals, image, payload
+    )
 
 
 def lane_tables():
@@ -874,25 +912,25 @@
     block, wide, face = (ROWS, ROWS, LANES), (ROWS, ROWS, WIDE), (ROWS, LANES)
     halo = (13, 8, LANES)
 
-    first, second, own_metrics, source, previous = call(
+    first, second, elements, source, previous = call(
         pack_kernel,
         [halo, halo, face, block, block],
         [FAR] * 3,
         "pack",
-        [pltpu.VMEM(coefficients.shape, jnp.float32), pltpu.VMEM((16, 16), jnp.float32), pltpu.SemaphoreType.DMA((3,))],
+        [pltpu.VMEM(coefficients.shape, jnp.float32), pltpu.SemaphoreType.DMA((3,))],
     )(*(pltpu.with_memory_space_constraint(v, pltpu.HBM) for v in (source, previous, coefficients)))
     first, second = swap(first, second, "gz")
-    upper, lower, diagonals, stiff, vectors, bend, lam, lines, fixed, tables = call(
+    own_metrics, upper, lower, diagonals, stiff, vectors, bend, lam, lines, fixed, tables = call(
         functools.partial(prepare_kernel, small),
         [
-            ("half", 3, WIDE, WIDE), ("half", 3, WIDE, LANES), (3, 8, 8, LANES),
+            face, ("half", 4, WIDE, WIDE), ("half", 4, WIDE, LANES), (3, 8, 8, LANES),
             (64, LANES), (64, LANES), (16, LANES), (2, 8, LANES), (3, 8, LANES), (24, LANES), (3, 8, LANES),
         ],
         [VMEM] * 3 + [SMEM] * 2 + [VMEM if small else FAR, VMEM],
         "prepare",
-    )(own_metrics, stiffness, fdm_vectors, fdm_values, vertex_map, coarse_inverse, jnp.asarray(lane_tables()))
-
-    message = (2 * FIRST_ROWS + SECOND_ROWS, LANES)
+    )(elements, stiffness, fdm_vectors, fdm_values, vertex_map, coarse_inverse, jnp.asarray(lane_tables()))
+
+    message = (FIRST_ROWS + FAR_ROWS + SECOND_ROWS, LANES)
     start, known, factors, halves, remainders, spectrum, inverse, side_a, side_b, common = call(
         start_kernel,
         [
@@ -909,17 +947,15 @@
         ready_kernel, [(2, 2, 4, ROWS, LANES), (8, WIDE), (ROWS, WIDE)], [VMEM] * 5, "ready"
     )(factors, stiff, lines, upper, lower)
 
-    start_faces, residual, local, beside, face_factors, sums = call(
-        solve_kernel,
-        [(2, ROWS, LANES), block, wide, (2, ROWS, WIDE), (2, 3, ROWS, WIDE), (8, LANES)],
-        [VMEM] * 17,
-        "solve",
+    start_faces, residual, local, face_factors, image, payload = call(
+        middle_kernel,
+        [(2, ROWS, LANES), block, wide, (2, 3, ROWS, WIDE), block, (2 * devices, LANES)],
+        [VMEM] * 19,
+        "middle",
+        [pltpu.VMEM((2, ROWS, WIDE), jnp.float32), pltpu.VMEM((8, LANES), jnp.float32)],
     )(
         known, factors, halves, remainders, spectrum, inverse, side_a, side_b, beyond, waves,
-        stiff, vectors, bend, lam, upper, lower, diagonals,
-    )
-    image, payload = call(image_kernel, [block, (2 * devices, LANES)], [VMEM] * 11, "image")(
-        local, factors, face_factors, beside, sums, fixed, stiff, lines, upper, lower, diagonals
+        stiff, vectors, bend, lam, upper, lower, diagonals, fixed, lines,
     )
     gathered = lax.all_to_all(payload.reshape(devices, 2, LANES), ("gx", "gz"), 0, 0)
     gathered = gathered.reshape(2 * devices, LANES)

time: 33 us -> 32.6 us (0.988)
    pallas_call x3 -> x2, Pallas kernels: 4.34 us -> 4.12 us  [the longest x1 2.13 us: body(): call(middle_kernel, [(2, ROWS, LANES), block, wide, (2, 3, ROWS, WIDE), b...]
where the time goes in v5:
time: 32.6 us; the launch traced here: 32.4 us
  blocking collectives  11.1 us (34%)
  starting transfers between devices  8.73 us (27%)
  Pallas kernels  8.34 us (26%)
  waiting for transfers between devices  3.5 us (11%)
  between operations  0.73 us (2%)
    all_to_all x1, blocking collectives, body(): lax.all_to_all(payload.reshape(devices, 2, LANES), ('gx', 'gz'), 0, 0)  11.1 us
    ppermute x2, starting transfers between devices, swap(): two = lax.ppermute(second, axis, odd + [(b, a) for a, b in odd])  6.2 us
    ppermute x1, waiting for transfers between devices, second_neighbours(): return lax.ppermute(common, axis, [(i, i ^ 2) for i in range(size)])  3.48 us
    pallas_call x1, Pallas kernels, body(): call(middle_kernel, [(2, ROWS, LANES), block, wide, (2, 3, ROWS, WIDE), b...  2.13 us
    ppermute x2, starting transfers between devices, swap(): one = lax.ppermute(first, axis, [(i, i ^ 1) for i in range(size)])  2.03 us
    pallas_call x1, Pallas kernels, body(): call(functools.partial(prepare_kernel, small), [face, ('half', 4, WIDE, W...  1.98 us
    pallas_call x1, Pallas kernels, body(): call(start_kernel, [block, wide, (3, 2, ROWS, WIDE), (2, ROWS, WIDE), (2,...  1.41 us
    pallas_call x1, Pallas kernels, body(): call(kernel, [block, block], [VMEM] * len(operands), 'finish', [pltpu.VME...  1.3 us
  transfers between devices with their start and end apart: 5, of which 1 were waited for; matrix products, arithmetic and copies ran while one was open for 0% of the time, Pallas kernels for 7%

profile of v5, /device:TPU:0, one launch (start us, length us, event | category | flops | bytes accessed | tf_op | source)
XLA Modules:
  0.0 32.4 jit_solution(14571227369161413108)
XLA Ops:
  0.6 0.0 copy-start
  0.6 0.0 copy-start.1
  0.7 0.0 copy-start.3
  0.7 1.2 %pack.1 = (f32[13,8,128]{2,1,0:T(8,128)S(1)}, f32[13,8,128]{2,1,0:T(8,128)S(1)}, f32[16,128]{1,0:T(8,128)S(1)}, f32[16,16,128]{2,1,0:T(8,128)S(1)}, f32[16,16,128]{2,1,0:T(8,128)S(1)}) custom-call(f32[16,16,128]{2,1,0:T(8,128)} %source.1, f32[16,16,128]{2,1,0:T(8,128)} %previous.1, f32[3,2,2,16]{3,2,1,0:T(2,128)} %coefficients.1), custom_call_target="tpu_custom_call" | custom-call | tf_op jit(solution)/shard_map/pack/pallas_call | solution.py:915
  1.9 0.0 copy-start.2
  1.9 0.5 %collective-permute-start = (f32[13,8,128]{2,1,0:T(8,128)S(1)}, f32[13,8,128]{2,1,0:T(8,128)S(1)}, u32[]{:S(2)}, u32[]{:S(2)}) collective-permute-start(f32[13,8,128]{2,1,0:T(8,128)S(1)} %get-tuple-element.41), channel_id=1, source_target_pairs={{0,1},{1,0},{2,3},{3,2},{4,5},{5,4},{6,7},{7,6},{8,9},{9,8},{10,11... | collective-permute-start | bytes 159752 | tf_op jit(solution)/shard_map/ppermute | solution.py:890
  2.4 4.7 %collective-permute-start.1 = (f32[13,8,128]{2,1,0:T(8,128)S(1)}, f32[13,8,128]{2,1,0:T(8,128)S(1)}, u32[]{:S(2)}, u32[]{:S(2)}) collective-permute-start(f32[13,8,128]{2,1,0:T(8,128)S(1)} %get-tuple-element.42), channel_id=1, source_target_pairs={{1,2},{3,4},{5,6},{7,0},{2,1},{4,3},{6,5},{0,7},{9,10},{11,12},{13... | collective-permute-start | bytes 159752 | tf_op jit(solution)/shard_map/ppermute | solution.py:891
  7.1 0.0 copy-done
  7.1 0.0 copy-done.4
  7.2 0.0 copy-done.5
  7.2 2.0 %prepare.1 = (f32[16,128]{1,0:T(8,128)S(1)}, bf16[4,256,256]{2,1,0:T(8,128)(2,1)S(1)}, bf16[4,256,128]{2,1,0:T(8,128)(2,1)S(1)}, f32[3,8,8,128]{3,2,1,0:T(8,128)...) custom-call(f32[16,128]{1,0:T(8,128)S(1)} %get-tuple-element.39.elem, ...), custom_call_target="tpu_custom_call" | custom-call | tf_op jit(solution)/shard_map/prepare/pallas_call | solution.py:923
  9.2 0.0 collective-permute-done.first
  9.2 0.0 collective-permute-done.1.second
  9.2 1.4 %start.1 = (f32[16,16,128]{2,1,0:T(8,128)S(1)}, f32[16,16,256]{2,1,0:T(8,128)S(1)}, f32[3,2,16,256]{3,2,1,0:T(8,128)S(1)}, f32[2,16,256]{2,1,0:T(8,128)S(1)}, f3...) custom-call(f32[16,16,128]{2,1,0:T(8,128)S(1)} %get-tuple-element.37, ...), custom_call_target="tpu_custom_call" | custom-call | tf_op jit(solution)/shard_map/start/pallas_call | solution.py:934
  10.6 1.5 %collective-permute-start.2 = (f32[128,128]{1,0:T(8,128)S(1)}, f32[128,128]{1,0:T(8,128)S(1)}, u32[]{:S(2)}, u32[]{:S(2)}) collective-permute-start(f32[128,128]{1,0:T(8,128)S(1)} %get-tuple-element.57), channel_id=1, source_target_pairs={{0,8},{8,0},{16,24},{24,16},{1,9},{9,1},{17,25},{25,17},{2,10},{10... | collective-permute-start | bytes 196616 | tf_op jit(solution)/shard_map/ppermute | solution.py:890
  12.1 1.5 %collective-permute-start.3 = (f32[128,128]{1,0:T(8,128)S(1)}, f32[128,128]{1,0:T(8,128)S(1)}, u32[]{:S(2)}, u32[]{:S(2)}) collective-permute-start(f32[128,128]{1,0:T(8,128)S(1)} %get-tuple-element.58), channel_id=1, source_target_pairs={{8,16},{24,0},{16,8},{0,24},{9,17},{25,1},{17,9},{1,25},{10,18},{2... | collective-permute-start | bytes 196616 | tf_op jit(solution)/shard_map/ppermute | solution.py:891
  13.6 0.5 %collective-permute-start.4 = (f32[112,128]{1,0:T(8,128)S(1)}, f32[112,128]{1,0:T(8,128)S(1)}, u32[]{:S(2)}, u32[]{:S(2)}) collective-permute-start(f32[112,128]{1,0:T(8,128)S(1)} %get-tuple-element.59), channel_id=1, source_target_pairs={{0,16},{8,24},{16,0},{24,8},{1,17},{9,25},{17,1},{25,9},{2,18},{10... | collective-permute-start | bytes 172040 | tf_op jit(solution)/shard_map/ppermute | solution.py:898
  14.1 0.3 ready.1
  14.4 3.5 %collective-permute-done.4.got_c = f32[112,128]{1,0:T(8,128)S(1)} collective-permute-done((f32[112,128]{1,0:T(8,128)S(1)}, f32[112,128]{1,0:T(8,128)S(1)}, u32[]{:S(2)}, u32[]{:S(2)}) %collective-permute-start.4) | collective-permute-done | bytes 57376 | tf_op jit(solution)/shard_map/ppermute | solution.py:898
  17.9 0.0 collective-permute-done.2.got_a
  17.9 0.0 collective-permute-done.3.got_b
  17.9 2.1 %middle.1 = (f32[2,16,128]{2,1,0:T(8,128)S(1)}, f32[16,16,128]{2,1,0:T(8,128)S(1)}, f32[16,16,256]{2,1,0:T(8,128)S(1)}, f32[2,3,16,256]{3,2,1,0:T(8,128)S(1)}, f...) custom-call(f32[16,16,256]{2,1,0:T(8,128)S(1)} %get-tuple-element.51.known, ...), custom_call_target="tpu_custom_call" | custom-call | tf_op jit(solution)/shard_map/middle/pallas_call | solution.py:950
  20.0 11.1 %all_to_all.5 = f32[32,2,128]{2,1,0:T(2,128)S(1)} all-to-all(f32[32,2,128]{2,1,0:T(2,128)S(1)} %bitcast.3), channel_id=1, replica_groups=mesh['gx'=4,'gz'=8] {'gx','gz'}, dimensions={0} | all-to-all | bytes 65536 | tf_op jit(solution)/shard_map/all_to_all | solution.py:960
  31.1 1.3 %finish.1 = (f32[16,16,128]{2,1,0:T(8,128)}, f32[16,16,128]{2,1,0:T(8,128)}) custom-call(f32[16,16,128]{2,1,0:T(8,128)S(1)} %get-tuple-element.50.refs_0_, f32[2,16,128]{2,1,0:T(8,128)S(1)} %get-tuple-element.63.refs_1_, f32[16,16,128]{2,1,0:T(8,128)S(1)} %get-tuple-element.64.refs_2_, f32[16,16,256]{2,1,0:T(8,128)S(1)} %get-tuple-element.65.refs_3_, ...), custom_call_target="tpu_custom_call" | custom-call | tf_op jit(solution)/shard_map/finish/pallas_call | solution.py:983
  (5 shorter events, 0.0 us)
Async XLA Ops:
  0.6 6.5 %copy-start = (s32[8,2,2,16]{3,2,1,0:T(2,128)S(1)}, s32[8,2,2,16]{3,2,1,0:T(2,128)}, u32[]{:S(2)}) copy-start(s32[8,2,2,16]{3,2,1,0:T(2,128)} %labels.1) | copy-start | bytes 6148
  0.6 6.5 %copy-start.1 = (f32[3,8,128]{2,1,0:T(8,128)S(1)}, f32[3,8,128]{2,1,0:T(8,128)}, u32[]{:S(2)}) copy-start(f32[3,8,128]{2,1,0:T(8,128)} %constant.2.clone.tables) | copy-start | bytes 36868
  0.7 6.5 %copy-start.3 = (f32[8,8]{1,0:T(8,128)S(1)}, f32[8,8]{1,0:T(8,128)}, u32[]{:S(2)}) copy-start(f32[8,8]{1,0:T(8,128)} %vectors.1) | copy-start | bytes 772
  1.9 5.3 %copy-start.2 = (f32[8,8]{1,0:T(8,128)S(1)}, f32[8,8]{1,0:T(8,128)}, u32[]{:S(2)}) copy-start(f32[8,8]{1,0:T(8,128)} %stiffness.1) | copy-start | bytes 772
  1.9 7.3 %collective-permute-start = (f32[13,8,128]{2,1,0:T(8,128)S(1)}, f32[13,8,128]{2,1,0:T(8,128)S(1)}, u32[]{:S(2)}, u32[]{:S(2)}) collective-permute-start(f32[13,8,128]{2,1,0:T(8,128)S(1)} %get-tuple-element.41), channel_id=1, source_target_pairs={{0,1},{1,0},{2,3},{3,2},{4,5},{5,4},{6,7},{7,6},{8,9},{9,8},{10,11... | collective-permute-start | bytes 159752 | tf_op jit(solution)/shard_map/ppermute | solution.py:890
  2.4 4.7 %copy-start.4 = (f32[2,64]{1,0:T(2,128)S(1)}, f32[2,64]{1,0:T(2,128)}, u32[]{:S(2)}) copy-start(f32[2,64]{1,0:T(2,128)} %coarse.1) | copy-start | bytes 1540
  2.4 4.7 %copy-start.5 = (f32[8]{0:T(128)S(1)}, f32[8]{0:T(128)}, u32[]{:S(2)}) copy-start(f32[8]{0:T(128)} %eigen.1) | copy-start | bytes 100
  2.4 6.8 %collective-permute-start.1 = (f32[13,8,128]{2,1,0:T(8,128)S(1)}, f32[13,8,128]{2,1,0:T(8,128)S(1)}, u32[]{:S(2)}, u32[]{:S(2)}) collective-permute-start(f32[13,8,128]{2,1,0:T(8,128)S(1)} %get-tuple-element.42), channel_id=1, source_target_pairs={{1,2},{3,4},{5,6},{7,0},{2,1},{4,3},{6,5},{0,7},{9,10},{11,12},{13... | collective-permute-start | bytes 159752 | tf_op jit(solution)/shard_map/ppermute | solution.py:891
  10.6 7.3 %collective-permute-start.2 = (f32[128,128]{1,0:T(8,128)S(1)}, f32[128,128]{1,0:T(8,128)S(1)}, u32[]{:S(2)}, u32[]{:S(2)}) collective-permute-start(f32[128,128]{1,0:T(8,128)S(1)} %get-tuple-element.57), channel_id=1, source_target_pairs={{0,8},{8,0},{16,24},{24,16},{1,9},{9,1},{17,25},{25,17},{2,10},{10... | collective-permute-start | bytes 196616 | tf_op jit(solution)/shard_map/ppermute | solution.py:890
  12.1 5.8 %collective-permute-start.3 = (f32[128,128]{1,0:T(8,128)S(1)}, f32[128,128]{1,0:T(8,128)S(1)}, u32[]{:S(2)}, u32[]{:S(2)}) collective-permute-start(f32[128,128]{1,0:T(8,128)S(1)} %get-tuple-element.58), channel_id=1, source_target_pairs={{8,16},{24,0},{16,8},{0,24},{9,17},{25,1},{17,9},{1,25},{10,18},{2... | collective-permute-start | bytes 196616 | tf_op jit(solution)/shard_map/ppermute | solution.py:891
  13.6 4.3 %collective-permute-start.4 = (f32[112,128]{1,0:T(8,128)S(1)}, f32[112,128]{1,0:T(8,128)S(1)}, u32[]{:S(2)}, u32[]{:S(2)}) collective-permute-start(f32[112,128]{1,0:T(8,128)S(1)} %get-tuple-element.59), channel_id=1, source_target_pairs={{0,16},{8,24},{16,0},{24,8},{1,17},{9,25},{17,1},{25,9},{2,18},{10... | collective-permute-start | bytes 172040 | tf_op jit(solution)/shard_map/ppermute | solution.py:898

commit v6 on v5

--- a/solution.py
+++ b/solution.py
@@ -385,8 +385,8 @@
 
 
 def start_kernel(
-    source, previous, own_metrics, first, second, stiffness, vectors, bend, lam, upper, lower, diagonals,
-    start, known, factors, halves, remainders, spectrum, inverse, message_a, message_b, common, metrics,
+    source, previous, own_metrics, first, second, stiffness, upper, lower, diagonals,
+    start, remainder, factors, halves, common, part, metrics,
 ):
     even = even_index("gz")
     lane = iota((8, LANES), 1)
@@ -425,7 +425,8 @@
     applied = apply_rows(rows, along_z, scaled, stiffness, wide_diagonals(diagonals, 0))
     rest = [wide(source, x, DEEP, SHALLOW) - applied[x] for x in range(ROWS)]
     halves[0], halves[1] = solid(faces[0]), solid(faces[1])
-    remainders[0], remainders[1] = solid(rest[0]), solid(rest[15])
+    for x in range(ROWS):
+        remainder[x] = solid(rest[x])
     coefficients = [
         jnp.concatenate(
             [metrics[(c * 2 + side) * 2 : (c * 2 + side) * 2 + 2] for c in range(3)] + [jnp.ones((2, WIDE), jnp.float32)],
@@ -443,9 +444,18 @@
         messages.append(jnp.concatenate(parts, axis=0))
         folded = fold([half[:8, LANES:], half[8:, LANES:]], FAR_FIELDS)
         distant.append(jnp.concatenate([half[:, :LANES], folded, rows[:, :LANES]], axis=0))
-    common[...] = jnp.concatenate(messages, axis=0)
-    both = [jnp.concatenate([messages[side], distant[1 - side]], axis=0) for side in range(2)]
-
+    common[: 2 * FIRST_ROWS] = jnp.concatenate(messages, axis=0)
+    common[2 * FIRST_ROWS :] = jnp.zeros((16, LANES), jnp.float32)
+    for side in range(2):
+        part[side] = jnp.concatenate([messages[side], distant[1 - side]], axis=0)
+
+
+def guess_kernel(
+    remainder, metrics, part, stiffness, vectors, bend, lam, upper, lower, diagonals,
+    known, spectrum, inverse, message_a, message_b,
+):
+    geo = Geometry(WIDE)
+    rest = [split(remainder[x]) for x in range(ROWS)]
     rest = [geo.assemble(v) for v in join_middle(rest)]
     forward = wide_diagonals(diagonals, 1)
     moved = []
@@ -473,7 +483,7 @@
         folded = fold([v[at : at + 8, LANES:] for v in (value, beside) for at in (0, 8)], SECOND_FIELDS)
         messages.append(jnp.concatenate([value[:, :LANES], beside[:, :LANES], folded], axis=0))
     even_x = even_index("gx")
-    both = [jnp.concatenate([both[side], messages[side]], axis=0) for side in range(2)]
+    both = [jnp.concatenate([part[side], messages[side]], axis=0) for side in range(2)]
     message_a[...] = jnp.where(even_x, both[1], both[0])
     message_b[...] = jnp.where(even_x, both[0], both[1])
 
@@ -552,7 +562,7 @@
 
 
 def solve_kernel(
-    known, factors, halves, remainders, spectrum, inverse, got_a, got_b, got_c, _,
+    known, factors, halves, remainder, spectrum, inverse, got_a, got_b, got_c, _,
     stiffness, vectors, bend, lam, upper, lower, diagonals,
     start_faces, residual, local, beside, face_factors, sums,
 ):
@@ -562,7 +572,7 @@
     beyond = got_c[...]
     near = [read_first(side) for side in sides]
     far = [read_far(side) for side in sides]
-    last = [read_first(beyond[FIRST_ROWS:]), read_first(beyond[:FIRST_ROWS])]
+    last = [read_first(beyond[FIRST_ROWS : 2 * FIRST_ROWS]), read_first(beyond[:FIRST_ROWS])]
     mine = [stored_factors(factors, e) for e in range(2)]
     near_factors, far_factors, last_factors = (
         [scaled_metrics(geo, v[-1]) for v in group] for group in (near, far, last)
@@ -571,7 +581,7 @@
         for c in range(3):
             face_factors[side, c] = solid(near_factors[side][c])
     half = [split(halves[side]) for side in range(2)]
-    remain = [split(remainders[side]) for side in range(2)]
+    remain = [split(remainder[x]) for x in (0, 15)]
     left_half = [near[0][0], half[1], last[0][0], far[1][0]]
     right_half = [half[0], near[1][0], far[0][0], last[1][0]]
     left_factors = [near_factors[0], mine[1], last_factors[0], far_factors[1]]
@@ -718,12 +728,12 @@
 
 
 def middle_kernel(
-    known, factors, halves, remainders, spectrum, inverse, got_a, got_b, got_c, waves,
+    known, factors, halves, remainder, spectrum, inverse, got_a, got_b, got_c, waves,
     stiffness, vectors, bend, lam, upper, lower, diagonals, fixed, lines,
     start_faces, residual, local, face_factors, image, payload, beside, sums,
 ):
     solve_kernel(
-        known, factors, halves, remainders, spectrum, inverse, got_a, got_b, got_c, waves,
+        known, factors, halves, remainder, spectrum, inverse, got_a, got_b, got_c, waves,
         stiffness, vectors, bend, lam, upper, lower, diagonals,
         start_faces, residual, local, beside, face_factors, sums,
     )
@@ -866,7 +876,7 @@
 FAR = pl.BlockSpec(memory_space=pltpu.HBM)
 
 
-def call(kernel, shapes, specs, name, scratch=()):
+def call(kernel, shapes, specs, name, scratch=(), cost=None):
     def leaf(shape):
         kind = jnp.float32
         if shape[0] == "half":
@@ -881,6 +891,7 @@
         scratch_shapes=list(scratch),
         compiler_params=pltpu.CompilerParams(vmem_limit_bytes=16 * 1024 * 1024),
         name=name,
+        cost_estimate=cost,
     )
 
 
@@ -931,17 +942,20 @@
     )(elements, stiffness, fdm_vectors, fdm_values, vertex_map, coarse_inverse, jnp.asarray(lane_tables()))
 
     message = (FIRST_ROWS + FAR_ROWS + SECOND_ROWS, LANES)
-    start, known, factors, halves, remainders, spectrum, inverse, side_a, side_b, common = call(
+    start, remainder, factors, halves, common, part, metrics = call(
         start_kernel,
         [
-            block, wide, (3, 2, ROWS, WIDE), (2, ROWS, WIDE), (2, ROWS, WIDE), wide, wide,
-            message, message, (2 * FIRST_ROWS, LANES),
+            block, wide, (3, 2, ROWS, WIDE), (2, ROWS, WIDE), (2 * FIRST_ROWS + 16, LANES),
+            (2, FIRST_ROWS + FAR_ROWS, LANES), (16, WIDE),
         ],
-        [VMEM] * 12,
+        [VMEM] * 9,
         "start",
-        [pltpu.VMEM((16, WIDE), jnp.float32)],
-    )(source, previous, own_metrics, first, second, stiff, vectors, bend, lam, upper, lower, diagonals)
+    )(source, previous, own_metrics, first, second, stiff, upper, lower, diagonals)
     beyond = second_neighbours(common, "gx")
+    known, spectrum, inverse, side_a, side_b = call(
+        guess_kernel, [wide, wide, wide, message, message], [VMEM] * 10, "guess",
+        cost=pl.CostEstimate(flops=4000000000, bytes_accessed=4000000, transcendentals=0),
+    )(remainder, metrics, part, stiff, vectors, bend, lam, upper, lower, diagonals)
     side_a, side_b = swap(side_a, side_b, "gx")
     pieces, waves, stiff_keep = call(
         ready_kernel, [(2, 2, 4, ROWS, LANES), (8, WIDE), (ROWS, WIDE)], [VMEM] * 5, "ready"
@@ -954,7 +968,7 @@
         "middle",
         [pltpu.VMEM((2, ROWS, WIDE), jnp.float32), pltpu.VMEM((8, LANES), jnp.float32)],
     )(
-        known, factors, halves, remainders, spectrum, inverse, side_a, side_b, beyond, waves,
+        known, factors, halves, remainder, spectrum, inverse, side_a, side_b, beyond, waves,
         stiff, vectors, bend, lam, upper, lower, diagonals, fixed, lines,
     )
     gathered = lax.all_to_all(payload.reshape(devices, 2, LANES), ("gx", "gz"), 0, 0)

time: 32.6 us -> 32.4 us (level)
  blocking collectives: 11.1 us -> 9.87 us
  waiting for transfers between devices: 3.5 us -> 4.38 us
    ppermute x1, waiting for transfers between devices: 3.48 us -> 0.01 us  [second_neighbours(): return lax.ppermute(common, axis, [(i, i ^ 2) for i in range(size)])]
    ppermute x2, waiting for transfers between devices: 0.01 us -> 2.4 us  [swap(): two = lax.ppermute(second, axis, odd + [(b, a) for a, b in odd])]
    ppermute x2, waiting for transfers between devices: 0.01 us -> 1.98 us  [swap(): one = lax.ppermute(first, axis, [(i, i ^ 1) for i in range(size)])]
    all_to_all x1, blocking collectives: 11.1 us -> 9.87 us  [body(): lax.all_to_all(payload.reshape(devices, 2, LANES), ('gx', 'gz'), 0, 0)]
    ppermute x1, starting transfers between devices: 0.5 us -> 1.53 us  [second_neighbours(): return lax.ppermute(common, axis, [(i, i ^ 2) for i in range(size)])]
    ppermute x2, starting transfers between devices: 6.2 us -> 5.18 us  [swap(): two = lax.ppermute(second, axis, odd + [(b, a) for a, b in odd])]
    pallas_call x1 -> x2, Pallas kernels: 1.41 us -> 1.52 us  [the longest x1 0.79 us: body(): call(start_kernel, [block, wide, (3, 2, ROWS, WIDE), (2, ROWS, WIDE), (2...]
  transfers between devices with their start and end apart: 5 -> 5, of which waited for: 1 -> 2; matrix products, arithmetic and copies ran while one was open for 0% -> 0% of each run, Pallas kernels for 7% -> 9%
where the time goes in v6:
time: 32.4 us; the launch traced here: 32.2 us
  blocking collectives  9.87 us (30%)
  starting transfers between devices  8.74 us (27%)
  Pallas kernels  8.43 us (26%)
  waiting for transfers between devices  4.38 us (14%)
  between operations  0.74 us (2%)
    all_to_all x1, blocking collectives, body(): lax.all_to_all(payload.reshape(devices, 2, LANES), ('gx', 'gz'), 0, 0)  9.87 us
    ppermute x2, starting transfers between devices, swap(): two = lax.ppermute(second, axis, odd + [(b, a) for a, b in odd])  5.18 us
    ppermute x2, waiting for transfers between devices, swap(): two = lax.ppermute(second, axis, odd + [(b, a) for a, b in odd])  2.4 us
    pallas_call x1, Pallas kernels, body(): call(middle_kernel, [(2, ROWS, LANES), block, wide, (2, 3, ROWS, WIDE), b...  2.11 us
    ppermute x2, starting transfers between devices, swap(): one = lax.ppermute(first, axis, [(i, i ^ 1) for i in range(size)])  2.03 us
    pallas_call x1, Pallas kernels, body(): call(functools.partial(prepare_kernel, small), [face, ('half', 4, WIDE, W...  1.98 us
    ppermute x2, waiting for transfers between devices, swap(): one = lax.ppermute(first, axis, [(i, i ^ 1) for i in range(size)])  1.98 us
    ppermute x1, starting transfers between devices, second_neighbours(): return lax.ppermute(common, axis, [(i, i ^ 2) for i in range(size)])  1.53 us
  transfers between devices with their start and end apart: 5, of which 2 were waited for; matrix products, arithmetic and copies ran while one was open for 0% of the time, Pallas kernels for 9%

profile of v6, /device:TPU:0, one launch (start us, length us, event | category | flops | bytes accessed | tf_op | source)
XLA Modules:
  0.0 32.2 jit_solution(16214014687277449824)
XLA Ops:
  0.6 0.0 copy-start
  0.6 0.0 copy-start.1
  0.7 1.2 %pack.1 = (f32[13,8,128]{2,1,0:T(8,128)S(1)}, f32[13,8,128]{2,1,0:T(8,128)S(1)}, f32[16,128]{1,0:T(8,128)S(1)}, f32[16,16,128]{2,1,0:T(8,128)S(1)}, f32[16,16,128]{2,1,0:T(8,128)S(1)}) custom-call(f32[16,16,128]{2,1,0:T(8,128)} %source.1, f32[16,16,128]{2,1,0:T(8,128)} %previous.1, f32[3,2,2,16]{3,2,1,0:T(2,128)} %coefficients.1), custom_call_target="tpu_custom_call" | custom-call | tf_op jit(solution)/shard_map/pack/pallas_call | solution.py:926
  1.9 0.0 copy-start.2
  1.9 0.5 %collective-permute-start = (f32[13,8,128]{2,1,0:T(8,128)S(1)}, f32[13,8,128]{2,1,0:T(8,128)S(1)}, u32[]{:S(2)}, u32[]{:S(2)}) collective-permute-start(f32[13,8,128]{2,1,0:T(8,128)S(1)} %get-tuple-element.43), channel_id=1, source_target_pairs={{0,1},{1,0},{2,3},{3,2},{4,5},{5,4},{6,7},{7,6},{8,9},{9,8},{10,11... | collective-permute-start | bytes 159752 | tf_op jit(solution)/shard_map/ppermute | solution.py:901
  2.4 4.7 %collective-permute-start.1 = (f32[13,8,128]{2,1,0:T(8,128)S(1)}, f32[13,8,128]{2,1,0:T(8,128)S(1)}, u32[]{:S(2)}, u32[]{:S(2)}) collective-permute-start(f32[13,8,128]{2,1,0:T(8,128)S(1)} %get-tuple-element.44), channel_id=1, source_target_pairs={{1,2},{3,4},{5,6},{7,0},{2,1},{4,3},{6,5},{0,7},{9,10},{11,12},{13... | collective-permute-start | bytes 159752 | tf_op jit(solution)/shard_map/ppermute | solution.py:902
  7.1 0.0 copy-done
  7.1 0.0 copy-done.4
  7.2 0.0 copy-done.5
  7.2 2.0 %prepare.1 = (f32[16,128]{1,0:T(8,128)S(1)}, bf16[4,256,256]{2,1,0:T(8,128)(2,1)S(1)}, bf16[4,256,128]{2,1,0:T(8,128)(2,1)S(1)}, f32[3,8,8,128]{3,2,1,0:T(8,128)...) custom-call(f32[16,128]{1,0:T(8,128)S(1)} %get-tuple-element.41.elem, ...), custom_call_target="tpu_custom_call" | custom-call | tf_op jit(solution)/shard_map/prepare/pallas_call | solution.py:934
  9.2 0.0 collective-permute-done.first
  9.2 0.0 collective-permute-done.1.second
  9.2 0.8 %start.1 = (f32[16,16,128]{2,1,0:T(8,128)S(1)}, f32[16,16,256]{2,1,0:T(8,128)S(1)}, f32[3,2,16,256]{3,2,1,0:T(8,128)S(1)}, f32[2,16,256]{2,1,0:T(8,128)S(1)}, f3...) custom-call(f32[16,16,128]{2,1,0:T(8,128)S(1)} %get-tuple-element.39.source, ...), custom_call_target="tpu_custom_call" | custom-call | tf_op jit(solution)/shard_map/start/pallas_call | solution.py:945
  10.0 1.5 %collective-permute-start.4 = (f32[128,128]{1,0:T(8,128)S(1)}, f32[128,128]{1,0:T(8,128)S(1)}, u32[]{:S(2)}, u32[]{:S(2)}) collective-permute-start(f32[128,128]{1,0:T(8,128)S(1)} %get-tuple-element.63), channel_id=1, source_target_pairs={{0,16},{8,24},{16,0},{24,8},{1,17},{9,25},{17,1},{25,9},{2,18},{10... | collective-permute-start | bytes 196616 | tf_op jit(solution)/shard_map/ppermute | solution.py:909
  11.5 0.7 %guess.1 = (f32[16,16,256]{2,1,0:T(8,128)S(1)}, f32[16,16,256]{2,1,0:T(8,128)S(1)}, f32[16,16,256]{2,1,0:T(8,128)S(1)}, f32[128,128]{1,0:T(8,128)S(1)}, f32[128,128]{1,0:T(8,128)S(1)}) custom-call(f32[16,16,256]{2,1,0:T(8,128)S(1)} %get-tuple-element.50.remainder, f32[16,256]{1,0:T(8,128)S(1)} %get-tuple-element.51.metrics, ...), custom_call_target="tpu_custom_call" | custom-call | flops 4000000000 | bytes 4000000 | tf_op jit(solution)/shard_map/guess/pallas_call | solution.py:955
  12.2 1.5 %collective-permute-start.2 = (f32[128,128]{1,0:T(8,128)S(1)}, f32[128,128]{1,0:T(8,128)S(1)}, u32[]{:S(2)}, u32[]{:S(2)}) collective-permute-start(f32[128,128]{1,0:T(8,128)S(1)} %get-tuple-element.61), channel_id=1, source_target_pairs={{0,8},{8,0},{16,24},{24,16},{1,9},{9,1},{17,25},{25,17},{2,10},{10... | collective-permute-start | bytes 196616 | tf_op jit(solution)/shard_map/ppermute | solution.py:901
  13.7 0.5 %collective-permute-start.3 = (f32[128,128]{1,0:T(8,128)S(1)}, f32[128,128]{1,0:T(8,128)S(1)}, u32[]{:S(2)}, u32[]{:S(2)}) collective-permute-start(f32[128,128]{1,0:T(8,128)S(1)} %get-tuple-element.62), channel_id=1, source_target_pairs={{8,16},{24,0},{16,8},{0,24},{9,17},{25,1},{17,9},{1,25},{10,18},{2... | collective-permute-start | bytes 196616 | tf_op jit(solution)/shard_map/ppermute | solution.py:902
  14.2 0.3 ready.1
  14.5 0.0 collective-permute-done.4.got_c
  14.5 2.0 %collective-permute-done.2.got_a = f32[128,128]{1,0:T(8,128)S(1)} collective-permute-done((f32[128,128]{1,0:T(8,128)S(1)}, f32[128,128]{1,0:T(8,128)S(1)}, u32[]{:S(2)}, u32[]{:S(2)}) %collective-permute-start.2) | collective-permute-done | bytes 65568 | tf_op jit(solution)/shard_map/ppermute | solution.py:901
  16.5 2.4 %collective-permute-done.3.got_b = f32[128,128]{1,0:T(8,128)S(1)} collective-permute-done((f32[128,128]{1,0:T(8,128)S(1)}, f32[128,128]{1,0:T(8,128)S(1)}, u32[]{:S(2)}, u32[]{:S(2)}) %collective-permute-start.3) | collective-permute-done | bytes 65568 | tf_op jit(solution)/shard_map/ppermute | solution.py:902
  18.9 2.1 %middle.1 = (f32[2,16,128]{2,1,0:T(8,128)S(1)}, f32[16,16,128]{2,1,0:T(8,128)S(1)}, f32[16,16,256]{2,1,0:T(8,128)S(1)}, f32[2,3,16,256]{3,2,1,0:T(8,128)S(1)}, f...) custom-call(f32[16,16,256]{2,1,0:T(8,128)S(1)} %get-tuple-element.56.known, ...), custom_call_target="tpu_custom_call" | custom-call | tf_op jit(solution)/shard_map/middle/pallas_call | solution.py:964
  21.0 9.9 %all_to_all.5 = f32[32,2,128]{2,1,0:T(2,128)S(1)} all-to-all(f32[32,2,128]{2,1,0:T(2,128)S(1)} %bitcast.3), channel_id=1, replica_groups=mesh['gx'=4,'gz'=8] {'gx','gz'}, dimensions={0} | all-to-all | bytes 65536 | tf_op jit(solution)/shard_map/all_to_all | solution.py:974
  30.9 1.3 %finish.1 = (f32[16,16,128]{2,1,0:T(8,128)}, f32[16,16,128]{2,1,0:T(8,128)}) custom-call(f32[16,16,128]{2,1,0:T(8,128)S(1)} %get-tuple-element.49.refs_0_, f32[2,16,128]{2,1,0:T(8,128)S(1)} %get-tuple-element.67.refs_1_, f32[16,16,128]{2,1,0:T(8,128)S(1)} %get-tuple-element.68.refs_2_, f32[16,16,256]{2,1,0:T(8,128)S(1)} %get-tuple-element.69.refs_3_, ...), custom_call_target="tpu_custom_call" | custom-call | tf_op jit(solution)/shard_map/finish/pallas_call | solution.py:997
  (6 shorter events, 0.0 us)
Async XLA Ops:
  0.6 6.5 %copy-start = (s32[8,2,2,16]{3,2,1,0:T(2,128)S(1)}, s32[8,2,2,16]{3,2,1,0:T(2,128)}, u32[]{:S(2)}) copy-start(s32[8,2,2,16]{3,2,1,0:T(2,128)} %labels.1) | copy-start | bytes 6148
  0.6 6.5 %copy-start.1 = (f32[3,8,128]{2,1,0:T(8,128)S(1)}, f32[3,8,128]{2,1,0:T(8,128)}, u32[]{:S(2)}) copy-start(f32[3,8,128]{2,1,0:T(8,128)} %constant.2.clone.tables) | copy-start | bytes 36868
  0.7 6.5 %copy-start.3 = (f32[8,8]{1,0:T(8,128)S(1)}, f32[8,8]{1,0:T(8,128)}, u32[]{:S(2)}) copy-start(f32[8,8]{1,0:T(8,128)} %vectors.1) | copy-start | bytes 772
  1.9 5.3 %copy-start.2 = (f32[8,8]{1,0:T(8,128)S(1)}, f32[8,8]{1,0:T(8,128)}, u32[]{:S(2)}) copy-start(f32[8,8]{1,0:T(8,128)} %stiffness.1) | copy-start | bytes 772
  1.9 7.3 %collective-permute-start = (f32[13,8,128]{2,1,0:T(8,128)S(1)}, f32[13,8,128]{2,1,0:T(8,128)S(1)}, u32[]{:S(2)}, u32[]{:S(2)}) collective-permute-start(f32[13,8,128]{2,1,0:T(8,128)S(1)} %get-tuple-element.43), channel_id=1, source_target_pairs={{0,1},{1,0},{2,3},{3,2},{4,5},{5,4},{6,7},{7,6},{8,9},{9,8},{10,11... | collective-permute-start | bytes 159752 | tf_op jit(solution)/shard_map/ppermute | solution.py:901
  2.4 4.7 %copy-start.4 = (f32[2,64]{1,0:T(2,128)S(1)}, f32[2,64]{1,0:T(2,128)}, u32[]{:S(2)}) copy-start(f32[2,64]{1,0:T(2,128)} %coarse.1) | copy-start | bytes 1540
  2.4 4.7 %copy-start.5 = (f32[8]{0:T(128)S(1)}, f32[8]{0:T(128)}, u32[]{:S(2)}) copy-start(f32[8]{0:T(128)} %eigen.1) | copy-start | bytes 100
  2.4 6.8 %collective-permute-start.1 = (f32[13,8,128]{2,1,0:T(8,128)S(1)}, f32[13,8,128]{2,1,0:T(8,128)S(1)}, u32[]{:S(2)}, u32[]{:S(2)}) collective-permute-start(f32[13,8,128]{2,1,0:T(8,128)S(1)} %get-tuple-element.44), channel_id=1, source_target_pairs={{1,2},{3,4},{5,6},{7,0},{2,1},{4,3},{6,5},{0,7},{9,10},{11,12},{13... | collective-permute-start | bytes 159752 | tf_op jit(solution)/shard_map/ppermute | solution.py:902
  10.0 4.6 %collective-permute-start.4 = (f32[128,128]{1,0:T(8,128)S(1)}, f32[128,128]{1,0:T(8,128)S(1)}, u32[]{:S(2)}, u32[]{:S(2)}) collective-permute-start(f32[128,128]{1,0:T(8,128)S(1)} %get-tuple-element.63), channel_id=1, source_target_pairs={{0,16},{8,24},{16,0},{24,8},{1,17},{9,25},{17,1},{25,9},{2,18},{10... | collective-permute-start | bytes 196616 | tf_op jit(solution)/shard_map/ppermute | solution.py:909
  12.2 4.3 %collective-permute-start.2 = (f32[128,128]{1,0:T(8,128)S(1)}, f32[128,128]{1,0:T(8,128)S(1)}, u32[]{:S(2)}, u32[]{:S(2)}) collective-permute-start(f32[128,128]{1,0:T(8,128)S(1)} %get-tuple-element.61), channel_id=1, source_target_pairs={{0,8},{8,0},{16,24},{24,16},{1,9},{9,1},{17,25},{25,17},{2,10},{10... | collective-permute-start | bytes 196616 | tf_op jit(solution)/shard_map/ppermute | solution.py:901
  13.7 5.2 %collective-permute-start.3 = (f32[128,128]{1,0:T(8,128)S(1)}, f32[128,128]{1,0:T(8,128)S(1)}, u32[]{:S(2)}, u32[]{:S(2)}) collective-permute-start(f32[128,128]{1,0:T(8,128)S(1)} %get-tuple-element.62), channel_id=1, source_target_pairs={{8,16},{24,0},{16,8},{0,24},{9,17},{25,1},{17,9},{1,25},{10,18},{2... | collective-permute-start | bytes 196616 | tf_op jit(solution)/shard_map/ppermute | solution.py:902

commit v7 on v6

--- a/solution.py
+++ b/solution.py
@@ -37,12 +37,14 @@
 LANES = 128
 WIDE = 256
 HALO = 32
+ELEMENTS = 22
+CORNERS = (58, 80)
 DEEP, SHALLOW = 25, 17
 SLOT = DEEP + SHALLOW
-FIRST_FIELDS = ((0, 24), (41, 17), (75, 17))
+FIRST_FIELDS = ((0, 24), (41, 17))
 SECOND_FIELDS = ((0, 16), (32, 16), (64, 16), (96, 16))
 FAR_FIELDS = ((0, 24), (48, 24))
-FIRST_ROWS, FAR_ROWS, SECOND_ROWS = 56, 32, 40
+FIRST_ROWS, FAR_ROWS, SECOND_ROWS = 48, 24, 40
 PAIRS = ((0, 0), (0, 1), (1, 1))
 GROUP_X = (ONES + LOW, [0.0] * 8 + HIGH)
 INVERSE_X = [0.5] + [1.0] * 6 + [0.5] + [0.5] + [1.0] * 6 + [0.5]
@@ -159,13 +161,16 @@
     return high, middle, (rest - middle.astype(jnp.float32)).astype(jnp.bfloat16)
 
 
-def contract_z(flat, upper, lower, which):
+def contract_z(flat, upper, lower, which, short=False):
     pieces = []
     for at in range(0, flat.shape[1], LANES):
         high, middle, low = thirds(flat[:, at : at + LANES])
         one = jnp.dot(
             jnp.concatenate([high, middle], axis=1), upper[which], preferred_element_type=jnp.float32
         )
+        if short:
+            pieces.append(one[:, :LANES] + one[:, LANES:])
+            continue
         two = jnp.dot(jnp.concatenate([low, high], axis=1), lower[which], preferred_element_type=jnp.float32)
         pieces.append(one[:, :LANES] + (one[:, LANES:] + two))
     return pieces[0] if len(pieces) == 1 else jnp.concatenate(pieces, axis=1)
@@ -269,16 +274,29 @@
 
 
 def lanes_of(elements):
-    widen = (iota((16, LANES), 0) == (iota((16, LANES), 1) >> 3)).astype(jnp.float32)
-    return jnp.dot(elements[:, 0:16], widen, precision=EXACT, preferred_element_type=jnp.float32)
+    lane = iota((24, WIDE), 1)
+    beyond = lane - LANES
+    right, left = LANES + 3 * 8, WIDE - 3 * 8
+    index = jnp.where(lane < right, lane >> 3, jnp.where(lane >= left, 19 + ((beyond - (left - LANES)) >> 3), ELEMENTS))
+    spread = (iota((24, WIDE), 0) == index).astype(jnp.float32)
+    return jnp.dot(elements[:, 0:24], spread, precision=EXACT, preferred_element_type=jnp.float32)
+
+
+def elements_of(folded):
+    lane = iota((8, LANES), 1)
+    rest = jnp.where(lane == ELEMENTS, 1.0, 0.0)
+    return jnp.concatenate(
+        [jnp.where(lane < ELEMENTS, pltpu.roll(folded, LANES - at, 1), rest) for at in CORNERS], axis=0
+    )
 
 
 def prepare_kernel(
     with_coarse, elements, stiffness, vectors, eigen, labels, coarse, tables,
-    metrics, upper, lower, diagonals, stiff_table, vector_table, bend, lam, lines, fixed, near_tables,
+    upper, lower, diagonals, stiff_table, vector_table, bend, lam, lines, fixed, near_tables,
 ):
     near_tables[...] = tables[...]
-    metrics[...] = lanes_of(elements[...])
+    widen = (iota((16, LANES), 0) == (iota((16, LANES), 1) >> 3)).astype(jnp.float32)
+    metrics = jnp.dot(elements[:, 0:16], widen, precision=EXACT, preferred_element_type=jnp.float32)
     repeat = (iota((LANES, 8), 0) & 7 == iota((LANES, 8), 1)).astype(jnp.float32)
     same = (iota((LANES, LANES), 0) >> 3) == (iota((LANES, LANES), 1) >> 3)
     unit = (iota((8, 8), 0) == iota((8, 8), 1)).astype(jnp.float32)
@@ -357,7 +375,7 @@
             applied = stiff_lines[0 if fb == ONES else 1 + b]
             stiff_x = jnp.sum(applied * pick(node, fa), axis=0, keepdims=True)
             for e in range(2):
-                cx, cy, cz = (metrics[(c * 2 + element) * 2 + e, :].reshape(1, LANES) for c in range(3))
+                cx, cy, cz = (metrics[(c * 2 + element) * 2 + e].reshape(1, LANES) for c in range(3))
                 across = across + cx * (stiff_x * mass_y[e]) + cy * (stiff_y[e] * mass_x)
                 along = along + cz * (mass_x * mass_y[e])
         across = across * weight_z
@@ -385,7 +403,7 @@
 
 
 def start_kernel(
-    source, previous, own_metrics, first, second, stiffness, upper, lower, diagonals,
+    source, previous, elements, first, second, stiffness, upper, lower, diagonals,
     start, remainder, factors, halves, common, part, metrics,
 ):
     even = even_index("gz")
@@ -405,12 +423,11 @@
         return split(widen(ref[x], [beyond(2 * x + e, at, width) for e in range(2)]))
 
     geo = Geometry(WIDE)
-    metrics[:, :LANES] = own_metrics[...]
-    around = lanes_of(jnp.concatenate([from_right[11], from_right[12], from_left[11], from_left[12]], axis=0))
-    wide_lane = iota((16, LANES), 1)
-    metrics[:, LANES:] = jnp.where(
-        wide_lane < HALO, around[:16], jnp.where(wide_lane >= LANES - HALO, around[16:], 1.0)
-    )
+    right = pltpu.roll(jnp.concatenate([from_right[11], from_right[12]], axis=0), 16, 1)
+    left = pltpu.roll(jnp.concatenate([from_left[11], from_left[12]], axis=0), 6, 1)
+    place = iota((16, LANES), 1)
+    compact = jnp.where(place < 16, elements[...], jnp.where(place < 19, right, jnp.where(place < ELEMENTS, left, 1.0)))
+    metrics[...] = lanes_of(compact)
     factor = geo.keep * geo.inverse_y * geo.inverse_z
     rows = [geo.pair(wide(previous, x, 0, DEEP)) * (factor * INVERSE_X[x]) for x in range(ROWS)]
     rows = join_middle(rows)
@@ -427,23 +444,16 @@
     halves[0], halves[1] = solid(faces[0]), solid(faces[1])
     for x in range(ROWS):
         remainder[x] = solid(rest[x])
-    coefficients = [
-        jnp.concatenate(
-            [metrics[(c * 2 + side) * 2 : (c * 2 + side) * 2 + 2] for c in range(3)] + [jnp.ones((2, WIDE), jnp.float32)],
-            axis=0,
-        )
-        for side in range(2)
-    ]
     messages, distant = [], []
     for side, x in ((0, 0), (1, 15)):
         half, value = solid(faces[side]), solid(rest[x])
-        rows, others = coefficients[side], coefficients[1 - side]
-        lower_fold = fold([half[:8, LANES:], value[:8, LANES:], rows[:, LANES:]], FIRST_FIELDS)
-        upper_fold = fold([half[8:, LANES:], value[8:, LANES:], others[:, LANES:]], FIRST_FIELDS)
-        parts = [half[:, :LANES], value[:, :LANES], lower_fold, upper_fold, rows[:, :LANES]]
-        messages.append(jnp.concatenate(parts, axis=0))
+        lower_fold = fold([half[:8, LANES:], value[:8, LANES:]], FIRST_FIELDS)
+        upper_fold = fold([half[8:, LANES:], value[8:, LANES:]], FIRST_FIELDS)
+        for at, rows in zip(CORNERS, (compact[:8], compact[8:])):
+            upper_fold = jnp.where((lane >= at) & (lane < at + ELEMENTS), pltpu.roll(rows, at, 1), upper_fold)
+        messages.append(jnp.concatenate([half[:, :LANES], value[:, :LANES], lower_fold, upper_fold], axis=0))
         folded = fold([half[:8, LANES:], half[8:, LANES:]], FAR_FIELDS)
-        distant.append(jnp.concatenate([half[:, :LANES], folded, rows[:, :LANES]], axis=0))
+        distant.append(jnp.concatenate([half[:, :LANES], folded], axis=0))
     common[: 2 * FIRST_ROWS] = jnp.concatenate(messages, axis=0)
     common[2 * FIRST_ROWS :] = jnp.zeros((16, LANES), jnp.float32)
     for side in range(2):
@@ -464,7 +474,7 @@
         moved += [solid(contract_y(contract_x(inside, vectors, i, True), forward)) for i in range(8)]
     for x in range(ROWS):
         known[x] = solid(rest[x])
-    transformed = contract_z(jnp.concatenate(moved, axis=0), upper, lower, 1)
+    transformed = contract_z(jnp.concatenate(moved, axis=0), upper, lower, 1, True)
     damped = []
     for element in range(2):
         divisors = divisors_of(geo, [metric(metrics, c, element) for c in range(3)], lam)
@@ -499,20 +509,12 @@
         widen(message[16 * k : 16 * k + 16], [unfold(lower_fold, FIRST_FIELDS[k]), unfold(upper_fold, FIRST_FIELDS[k])])
         for k in range(2)
     )
-    return split(half), split(value), spread_metrics(message[48:56], lower_fold)
-
-
-def spread_metrics(tile, folded):
-    rows = widen(tile, [unfold(folded, FIRST_FIELDS[2], 1.0)])
-    return [
-        jnp.stack([jnp.broadcast_to(rows[2 * c + e : 2 * c + e + 1], (8, WIDE)) for e in range(2)]) for c in range(3)
-    ]
+    return split(half), split(value)
 
 
 def read_far(message):
     far = message[FIRST_ROWS : FIRST_ROWS + FAR_ROWS]
-    half = widen(far[0:16], [unfold(far[16:24], field) for field in FAR_FIELDS])
-    return split(half), spread_metrics(far[24:32], message[40:48])
+    return split(widen(far[0:16], [unfold(far[16:24], field) for field in FAR_FIELDS]))
 
 
 def read_second(message):
@@ -574,16 +576,24 @@
     far = [read_far(side) for side in sides]
     last = [read_first(beyond[FIRST_ROWS : 2 * FIRST_ROWS]), read_first(beyond[:FIRST_ROWS])]
     mine = [stored_factors(factors, e) for e in range(2)]
+    folds = [side[40:48] for side in sides] + [beyond[FIRST_ROWS + 40 : FIRST_ROWS + 48], beyond[40:48]]
+    spread = lanes_of(jnp.concatenate([elements_of(folded) for folded in folds], axis=0))
+
+    def metrics_of(device, element):
+        return [metric(spread[16 * device : 16 * device + 16], c, element) for c in range(3)]
+
+    near_metrics, far_metrics = [metrics_of(0, 1), metrics_of(1, 0)], [metrics_of(0, 0), metrics_of(1, 1)]
     near_factors, far_factors, last_factors = (
-        [scaled_metrics(geo, v[-1]) for v in group] for group in (near, far, last)
+        [scaled_metrics(geo, v) for v in group]
+        for group in (near_metrics, far_metrics, [metrics_of(2, 1), metrics_of(3, 0)])
     )
     for side in range(2):
         for c in range(3):
             face_factors[side, c] = solid(near_factors[side][c])
     half = [split(halves[side]) for side in range(2)]
     remain = [split(remainder[x]) for x in (0, 15)]
-    left_half = [near[0][0], half[1], last[0][0], far[1][0]]
-    right_half = [half[0], near[1][0], far[0][0], last[1][0]]
+    left_half = [near[0][0], half[1], last[0][0], far[1]]
+    right_half = [half[0], near[1][0], far[0], last[1][0]]
     left_factors = [near_factors[0], mine[1], last_factors[0], far_factors[1]]
     right_factors = [mine[0], near_factors[1], far_factors[0], last_factors[1]]
     stiff = wide_diagonals(diagonals, 0)
@@ -629,7 +639,7 @@
     forward, backward = wide_diagonals(diagonals, 1), wide_diagonals(diagonals, 2)
     fields = to_right + to_left + [into_left[0], into_left[1], into_left[3], into_right[0], into_right[1], into_right[2]]
     flat = jnp.concatenate([solid(contract_y(v, forward)) for v in fields], axis=0)
-    flat = contract_z(flat, upper, lower, 1)
+    flat = contract_z(flat, upper, lower, 1, True)
     flat = [split(flat[k * 16 : k * 16 + 16]) for k in range(len(fields))]
     to_right, to_left = flat[:3], flat[3:6]
     into_left, into_right = {0: flat[6], 1: flat[7], 3: flat[8]}, {0: flat[9], 1: flat[10], 2: flat[11]}
@@ -660,14 +670,14 @@
             close = changes(0, to_right[1], into_right[1], into_left[3])
             distant = changes(1, to_left[2], into_left[3], into_right[1])
         face = 7 * near_element
-        close = [a * b for a, b in zip(close, divisors_of(geo, near[side][2], lam))]
-        distant = [a * b for a, b in zip(distant, divisors_of(geo, far[side][1], lam))]
+        close = [a * b for a, b in zip(close, divisors_of(geo, near_metrics[side], lam))]
+        distant = [a * b for a, b in zip(distant, divisors_of(geo, far_metrics[side], lam))]
         value = value + weighted([vector(face, i) for i in range(8)], close)
         partial = partial + weighted([line_of(bend, near_element * 8 + i, WIDE) for i in range(8)], close)
         partial = partial + cross * weighted([vector(face, i) for i in range(8)], distant)
         moved += [solid(value), solid(partial)]
 
-    back = contract_z(jnp.concatenate(moved, axis=0), upper, lower, 2)
+    back = contract_z(jnp.concatenate(moved, axis=0), upper, lower, 2, True)
     back = [contract_y(split(back[k * 16 : k * 16 + 16]), backward) for k in range(ROWS + 4)]
     solved = []
     for element in range(2):
@@ -693,7 +703,7 @@
 ):
     geo = Geometry(WIDE)
     rows = [split(local[x]) for x in range(ROWS)]
-    along_z = contract_z(jnp.concatenate([solid(v) for v in rows], axis=0), upper, lower, 0)
+    along_z = contract_z(jnp.concatenate([solid(v) for v in rows], axis=0), upper, lower, 0, True)
     scaled = [stored_factors(factors, e) for e in range(2)]
     stiff = wide_diagonals(diagonals, 0)
     applied = apply_rows(rows, along_z, scaled, stiffness, stiff)
@@ -931,10 +941,10 @@
         [pltpu.VMEM(coefficients.shape, jnp.float32), pltpu.SemaphoreType.DMA((3,))],
     )(*(pltpu.with_memory_space_constraint(v, pltpu.HBM) for v in (source, previous, coefficients)))
     first, second = swap(first, second, "gz")
-    own_metrics, upper, lower, diagonals, stiff, vectors, bend, lam, lines, fixed, tables = call(
+    upper, lower, diagonals, stiff, vectors, bend, lam, lines, fixed, tables = call(
         functools.partial(prepare_kernel, small),
         [
-            face, ("half", 4, WIDE, WIDE), ("half", 4, WIDE, LANES), (3, 8, 8, LANES),
+            ("half", 4, WIDE, WIDE), ("half", 4, WIDE, LANES), (3, 8, 8, LANES),
             (64, LANES), (64, LANES), (16, LANES), (2, 8, LANES), (3, 8, LANES), (24, LANES), (3, 8, LANES),
         ],
         [VMEM] * 3 + [SMEM] * 2 + [VMEM if small else FAR, VMEM],
@@ -950,7 +960,7 @@
         ],
         [VMEM] * 9,
         "start",
-    )(source, previous, own_metrics, first, second, stiff, upper, lower, diagonals)
+    )(source, previous, elements, first, second, stiff, upper, lower, diagonals)
     beyond = second_neighbours(common, "gx")
     known, spectrum, inverse, side_a, side_b = call(
         guess_kernel, [wide, wide, wide, message, message], [VMEM] * 10, "guess",

time: 32.4 us -> 31.8 us (0.981)
  no operation moved by 1% of the time
where the time goes in v7:
time: 31.8 us; the launch traced here: 31.7 us
  blocking collectives  9.59 us (30%)
  starting transfers between devices  8.74 us (27%)
  Pallas kernels  8.29 us (26%)
  waiting for transfers between devices  4.3 us (14%)
  between operations  0.74 us (2%)
    all_to_all x1, blocking collectives, body(): lax.all_to_all(payload.reshape(devices, 2, LANES), ('gx', 'gz'), 0, 0)  9.59 us
    ppermute x2, starting transfers between devices, swap(): two = lax.ppermute(second, axis, odd + [(b, a) for a, b in odd])  5.19 us
    ppermute x2, waiting for transfers between devices, swap(): two = lax.ppermute(second, axis, odd + [(b, a) for a, b in odd])  2.4 us
    pallas_call x1, Pallas kernels, body(): call(middle_kernel, [(2, ROWS, LANES), block, wide, (2, 3, ROWS, WIDE), b...  2.05 us
    ppermute x2, starting transfers between devices, swap(): one = lax.ppermute(first, axis, [(i, i ^ 1) for i in range(size)])  2.02 us
    pallas_call x1, Pallas kernels, body(): call(functools.partial(prepare_kernel, small), [('half', 4, WIDE, WIDE),...  2 us
    ppermute x2, waiting for transfers between devices, swap(): one = lax.ppermute(first, axis, [(i, i ^ 1) for i in range(size)])  1.9 us
    ppermute x1, starting transfers between devices, second_neighbours(): return lax.ppermute(common, axis, [(i, i ^ 2) for i in range(size)])  1.53 us
  transfers between devices with their start and end apart: 5, of which 2 were waited for; matrix products, arithmetic and copies ran while one was open for 0% of the time, Pallas kernels for 9%

profile of v7, /device:TPU:0, one launch (start us, length us, event | category | flops | bytes accessed | tf_op | source)
XLA Modules:
  0.0 31.7 jit_solution(12886431187179635562)
XLA Ops:
  0.6 0.0 copy-start
  0.6 0.0 copy-start.1
  0.7 1.2 %pack.1 = (f32[13,8,128]{2,1,0:T(8,128)S(1)}, f32[13,8,128]{2,1,0:T(8,128)S(1)}, f32[16,128]{1,0:T(8,128)S(1)}, f32[16,16,128]{2,1,0:T(8,128)S(1)}, f32[16,16,128]{2,1,0:T(8,128)S(1)}) custom-call(f32[16,16,128]{2,1,0:T(8,128)} %source.1, f32[16,16,128]{2,1,0:T(8,128)} %previous.1, f32[3,2,2,16]{3,2,1,0:T(2,128)} %coefficients.1), custom_call_target="tpu_custom_call" | custom-call | tf_op jit(solution)/shard_map/pack/pallas_call | solution.py:936
  1.9 0.0 copy-start.2
  1.9 0.5 %collective-permute-start = (f32[13,8,128]{2,1,0:T(8,128)S(1)}, f32[13,8,128]{2,1,0:T(8,128)S(1)}, u32[]{:S(2)}, u32[]{:S(2)}) collective-permute-start(f32[13,8,128]{2,1,0:T(8,128)S(1)} %get-tuple-element.41), channel_id=1, source_target_pairs={{0,1},{1,0},{2,3},{3,2},{4,5},{5,4},{6,7},{7,6},{8,9},{9,8},{10,11... | collective-permute-start | bytes 159752 | tf_op jit(solution)/shard_map/ppermute | solution.py:911
  2.4 4.7 %collective-permute-start.1 = (f32[13,8,128]{2,1,0:T(8,128)S(1)}, f32[13,8,128]{2,1,0:T(8,128)S(1)}, u32[]{:S(2)}, u32[]{:S(2)}) collective-permute-start(f32[13,8,128]{2,1,0:T(8,128)S(1)} %get-tuple-element.42), channel_id=1, source_target_pairs={{1,2},{3,4},{5,6},{7,0},{2,1},{4,3},{6,5},{0,7},{9,10},{11,12},{13... | collective-permute-start | bytes 159752 | tf_op jit(solution)/shard_map/ppermute | solution.py:912
  7.1 0.0 copy-done
  7.1 0.0 copy-done.4
  7.2 0.0 copy-done.5
  7.2 2.0 %prepare.1 = (bf16[4,256,256]{2,1,0:T(8,128)(2,1)S(1)}, bf16[4,256,128]{2,1,0:T(8,128)(2,1)S(1)}, f32[3,8,8,128]{3,2,1,0:T(8,128)S(1)}, f32[64,128]{1,0:T(8,128)...) custom-call(f32[16,128]{1,0:T(8,128)S(1)} %get-tuple-element.40.elem, ...), custom_call_target="tpu_custom_call" | custom-call | tf_op jit(solution)/shard_map/prepare/pallas_call | solution.py:944
  9.2 0.0 collective-permute-done.first
  9.2 0.0 collective-permute-done.1.second
  9.2 0.8 %start.1 = (f32[16,16,128]{2,1,0:T(8,128)S(1)}, f32[16,16,256]{2,1,0:T(8,128)S(1)}, f32[3,2,16,256]{3,2,1,0:T(8,128)S(1)}, f32[2,16,256]{2,1,0:T(8,128)S(1)}, f3...) custom-call(f32[16,16,128]{2,1,0:T(8,128)S(1)} %get-tuple-element.38.source, ...), custom_call_target="tpu_custom_call" | custom-call | tf_op jit(solution)/shard_map/start/pallas_call | solution.py:955
  10.0 1.5 %collective-permute-start.4 = (f32[112,128]{1,0:T(8,128)S(1)}, f32[112,128]{1,0:T(8,128)S(1)}, u32[]{:S(2)}, u32[]{:S(2)}) collective-permute-start(f32[112,128]{1,0:T(8,128)S(1)} %get-tuple-element.61), channel_id=1, source_target_pairs={{0,16},{8,24},{16,0},{24,8},{1,17},{9,25},{17,1},{25,9},{2,18},{10... | collective-permute-start | bytes 172040 | tf_op jit(solution)/shard_map/ppermute | solution.py:919
  11.5 0.6 %guess.1 = (f32[16,16,256]{2,1,0:T(8,128)S(1)}, f32[16,16,256]{2,1,0:T(8,128)S(1)}, f32[16,16,256]{2,1,0:T(8,128)S(1)}, f32[112,128]{1,0:T(8,128)S(1)}, f32[112,128]{1,0:T(8,128)S(1)}) custom-call(f32[16,16,256]{2,1,0:T(8,128)S(1)} %get-tuple-element.48.remainder, f32[16,256]{1,0:T(8,128)S(1)} %get-tuple-element.49.metrics, ...), custom_call_target="tpu_custom_call" | custom-call | flops 4000000000 | bytes 4000000 | tf_op jit(solution)/shard_map/guess/pallas_call | solution.py:965
  12.2 1.5 %collective-permute-start.2 = (f32[112,128]{1,0:T(8,128)S(1)}, f32[112,128]{1,0:T(8,128)S(1)}, u32[]{:S(2)}, u32[]{:S(2)}) collective-permute-start(f32[112,128]{1,0:T(8,128)S(1)} %get-tuple-element.59), channel_id=1, source_target_pairs={{0,8},{8,0},{16,24},{24,16},{1,9},{9,1},{17,25},{25,17},{2,10},{10... | collective-permute-start | bytes 172040 | tf_op jit(solution)/shard_map/ppermute | solution.py:911
  13.7 0.5 %collective-permute-start.3 = (f32[112,128]{1,0:T(8,128)S(1)}, f32[112,128]{1,0:T(8,128)S(1)}, u32[]{:S(2)}, u32[]{:S(2)}) collective-permute-start(f32[112,128]{1,0:T(8,128)S(1)} %get-tuple-element.60), channel_id=1, source_target_pairs={{8,16},{24,0},{16,8},{0,24},{9,17},{25,1},{17,9},{1,25},{10,18},{2... | collective-permute-start | bytes 172040 | tf_op jit(solution)/shard_map/ppermute | solution.py:912
  14.1 0.3 ready.1
  14.4 0.0 collective-permute-done.4.got_c
  14.4 1.9 %collective-permute-done.2.got_a = f32[112,128]{1,0:T(8,128)S(1)} collective-permute-done((f32[112,128]{1,0:T(8,128)S(1)}, f32[112,128]{1,0:T(8,128)S(1)}, u32[]{:S(2)}, u32[]{:S(2)}) %collective-permute-start.2) | collective-permute-done | bytes 57376 | tf_op jit(solution)/shard_map/ppermute | solution.py:911
  16.3 2.4 %collective-permute-done.3.got_b = f32[112,128]{1,0:T(8,128)S(1)} collective-permute-done((f32[112,128]{1,0:T(8,128)S(1)}, f32[112,128]{1,0:T(8,128)S(1)}, u32[]{:S(2)}, u32[]{:S(2)}) %collective-permute-start.3) | collective-permute-done | bytes 57376 | tf_op jit(solution)/shard_map/ppermute | solution.py:912
  18.7 2.0 %middle.1 = (f32[2,16,128]{2,1,0:T(8,128)S(1)}, f32[16,16,128]{2,1,0:T(8,128)S(1)}, f32[16,16,256]{2,1,0:T(8,128)S(1)}, f32[2,3,16,256]{3,2,1,0:T(8,128)S(1)}, f...) custom-call(f32[16,16,256]{2,1,0:T(8,128)S(1)} %get-tuple-element.54.known, ...), custom_call_target="tpu_custom_call" | custom-call | tf_op jit(solution)/shard_map/middle/pallas_call | solution.py:974
  20.8 9.6 %all_to_all.5 = f32[32,2,128]{2,1,0:T(2,128)S(1)} all-to-all(f32[32,2,128]{2,1,0:T(2,128)S(1)} %bitcast.3), channel_id=1, replica_groups=mesh['gx'=4,'gz'=8] {'gx','gz'}, dimensions={0} | all-to-all | bytes 65536 | tf_op jit(solution)/shard_map/all_to_all | solution.py:984
  30.4 1.3 %finish.1 = (f32[16,16,128]{2,1,0:T(8,128)}, f32[16,16,128]{2,1,0:T(8,128)}) custom-call(f32[16,16,128]{2,1,0:T(8,128)S(1)} %get-tuple-element.47.refs_0_, f32[2,16,128]{2,1,0:T(8,128)S(1)} %get-tuple-element.65.refs_1_, f32[16,16,128]{2,1,0:T(8,128)S(1)} %get-tuple-element.66.refs_2_, f32[16,16,256]{2,1,0:T(8,128)S(1)} %get-tuple-element.67.refs_3_, ...), custom_call_target="tpu_custom_call" | custom-call | tf_op jit(solution)/shard_map/finish/pallas_call | solution.py:1007
  (6 shorter events, 0.0 us)
Async XLA Ops:
  0.6 6.5 %copy-start = (s32[8,2,2,16]{3,2,1,0:T(2,128)S(1)}, s32[8,2,2,16]{3,2,1,0:T(2,128)}, u32[]{:S(2)}) copy-start(s32[8,2,2,16]{3,2,1,0:T(2,128)} %labels.1) | copy-start | bytes 6148
  0.6 6.5 %copy-start.1 = (f32[3,8,128]{2,1,0:T(8,128)S(1)}, f32[3,8,128]{2,1,0:T(8,128)}, u32[]{:S(2)}) copy-start(f32[3,8,128]{2,1,0:T(8,128)} %constant.2.clone.tables) | copy-start | bytes 36868
  0.7 6.5 %copy-start.3 = (f32[8,8]{1,0:T(8,128)S(1)}, f32[8,8]{1,0:T(8,128)}, u32[]{:S(2)}) copy-start(f32[8,8]{1,0:T(8,128)} %vectors.1) | copy-start | bytes 772
  1.9 5.3 %copy-start.2 = (f32[8,8]{1,0:T(8,128)S(1)}, f32[8,8]{1,0:T(8,128)}, u32[]{:S(2)}) copy-start(f32[8,8]{1,0:T(8,128)} %stiffness.1) | copy-start | bytes 772
  1.9 7.3 %collective-permute-start = (f32[13,8,128]{2,1,0:T(8,128)S(1)}, f32[13,8,128]{2,1,0:T(8,128)S(1)}, u32[]{:S(2)}, u32[]{:S(2)}) collective-permute-start(f32[13,8,128]{2,1,0:T(8,128)S(1)} %get-tuple-element.41), channel_id=1, source_target_pairs={{0,1},{1,0},{2,3},{3,2},{4,5},{5,4},{6,7},{7,6},{8,9},{9,8},{10,11... | collective-permute-start | bytes 159752 | tf_op jit(solution)/shard_map/ppermute | solution.py:911
  2.4 4.7 %copy-start.4 = (f32[2,64]{1,0:T(2,128)S(1)}, f32[2,64]{1,0:T(2,128)}, u32[]{:S(2)}) copy-start(f32[2,64]{1,0:T(2,128)} %coarse.1) | copy-start | bytes 1540
  2.4 4.7 %copy-start.5 = (f32[8]{0:T(128)S(1)}, f32[8]{0:T(128)}, u32[]{:S(2)}) copy-start(f32[8]{0:T(128)} %eigen.1) | copy-start | bytes 100
  2.4 6.8 %collective-permute-start.1 = (f32[13,8,128]{2,1,0:T(8,128)S(1)}, f32[13,8,128]{2,1,0:T(8,128)S(1)}, u32[]{:S(2)}, u32[]{:S(2)}) collective-permute-start(f32[13,8,128]{2,1,0:T(8,128)S(1)} %get-tuple-element.42), channel_id=1, source_target_pairs={{1,2},{3,4},{5,6},{7,0},{2,1},{4,3},{6,5},{0,7},{9,10},{11,12},{13... | collective-permute-start | bytes 159752 | tf_op jit(solution)/shard_map/ppermute | solution.py:912
  10.0 4.5 %collective-permute-start.4 = (f32[112,128]{1,0:T(8,128)S(1)}, f32[112,128]{1,0:T(8,128)S(1)}, u32[]{:S(2)}, u32[]{:S(2)}) collective-permute-start(f32[112,128]{1,0:T(8,128)S(1)} %get-tuple-element.61), channel_id=1, source_target_pairs={{0,16},{8,24},{16,0},{24,8},{1,17},{9,25},{17,1},{25,9},{2,18},{10... | collective-permute-start | bytes 172040 | tf_op jit(solution)/shard_map/ppermute | solution.py:919
  12.2 4.2 %collective-permute-start.2 = (f32[112,128]{1,0:T(8,128)S(1)}, f32[112,128]{1,0:T(8,128)S(1)}, u32[]{:S(2)}, u32[]{:S(2)}) collective-permute-start(f32[112,128]{1,0:T(8,128)S(1)} %get-tuple-element.59), channel_id=1, source_target_pairs={{0,8},{8,0},{16,24},{24,16},{1,9},{9,1},{17,25},{25,17},{2,10},{10... | collective-permute-start | bytes 172040 | tf_op jit(solution)/shard_map/ppermute | solution.py:911
  13.7 5.1 %collective-permute-start.3 = (f32[112,128]{1,0:T(8,128)S(1)}, f32[112,128]{1,0:T(8,128)S(1)}, u32[]{:S(2)}, u32[]{:S(2)}) collective-permute-start(f32[112,128]{1,0:T(8,128)S(1)} %get-tuple-element.60), channel_id=1, source_target_pairs={{8,16},{24,0},{16,8},{0,24},{9,17},{25,1},{17,9},{1,25},{10,18},{2... | collective-permute-start | bytes 172040 | tf_op jit(solution)/shard_map/ppermute | solution.py:912

commit v8 on v7

--- a/solution.py
+++ b/solution.py
@@ -36,6 +36,7 @@
 ROWS = 16
 LANES = 128
 WIDE = 256
+BOTH = 384
 HALO = 32
 ELEMENTS = 22
 CORNERS = (58, 80)
@@ -130,17 +131,49 @@
     return total
 
 
-def divisors_of(geo, c, lam):
-    lam_y = jnp.concatenate([lam[0]] * (WIDE // LANES), axis=1)[None]
-    lam_z = jnp.concatenate([lam[1]] * (WIDE // LANES), axis=1)[None]
+def divisors_of(c, lam):
+    lanes = c[0].shape[-1]
+    lam_y = jnp.concatenate([lam[0]] * (lanes // LANES), axis=1)[None]
+    lam_z = jnp.concatenate([lam[1]] * (lanes // LANES), axis=1)[None]
     base = c[1] * lam_y + c[2] * lam_z
-    return [1.0 / (c[0] * line_of(lam.at[0], i, WIDE) + base) for i in range(8)]
+    return [1.0 / (c[0] * line_of(lam.at[0], i, lanes) + base) for i in range(8)]
+
+
+def halo_lanes():
+    lane = iota((1, 1, LANES), 2)
+    return (lane < HALO) | (lane >= LANES - HALO)
+
+
+def join_pair(low, high):
+    other = pltpu.roll(solid(high[:, :, LANES:]), LANES // 2, 1).reshape(2, 8, LANES)
+    return jnp.concatenate([own(low), own(high), jnp.where(halo_lanes(), low[:, :, LANES:], other)], axis=2)
+
+
+def part_pair(v):
+    last = v[:, :, WIDE:]
+    other = pltpu.roll(solid(last), LANES // 2, 1).reshape(2, 8, LANES)
+    return jnp.concatenate([own(v), last], axis=2), jnp.concatenate([v[:, :, LANES:WIDE], other], axis=2)
+
+
+def join_pairs(rows):
+    return [join_pair(rows[x], rows[x + 8]) for x in range(8)]
+
+
+def part_pairs(pairs):
+    parted = [part_pair(v) for v in pairs]
+    return [v[0] for v in parted] + [v[1] for v in parted]
+
+
+def pair_line(ref, low, high):
+    one, two = ref[low : low + 1, :], ref[high : high + 1, :]
+    mixed = jnp.where(halo_lanes()[0], one, two)
+    return jnp.concatenate([one, two, mixed], axis=1)[None]
 
 
 def contract_x(rows, table, i, transpose=False):
     total = None
     for p in range(8):
-        factor = line_of(table, p * 8 + i if transpose else i * 8 + p, WIDE)
+        factor = line_of(table, p * 8 + i if transpose else i * 8 + p, rows[p].shape[-1])
         term = factor * rows[p]
         total = term if total is None else total + term
     return total
@@ -176,8 +209,8 @@
     return pieces[0] if len(pieces) == 1 else jnp.concatenate(pieces, axis=1)
 
 
-def wide_diagonals(ref, which):
-    return [jnp.concatenate([ref[which, d]] * (WIDE // LANES), axis=1)[None] for d in range(8)]
+def wide_diagonals(ref, which, lanes=WIDE):
+    return [jnp.concatenate([ref[which, d]] * (lanes // LANES), axis=1)[None] for d in range(8)]
 
 
 def metric(ref, component, element):
@@ -193,17 +226,15 @@
     return [split(ref[c, element]) for c in range(3)]
 
 
-def apply_rows(rows, along_z, factors, stiffness, diagonals):
+def apply_pairs(pairs, factors, stiffness, upper, lower, diagonals, short=False):
+    factor_x, factor_y, factor_z = factors
+    along_z = contract_z(jnp.concatenate([solid(v) for v in pairs], axis=0), upper, lower, 0, short)
+    along_z = [split(along_z[x * 16 : x * 16 + 16]) for x in range(8)]
     result = []
-    for element in range(2):
-        factor_x, factor_y, factor_z = factors[element]
-        inside = rows[element * 8 : element * 8 + 8]
-        for i in range(8):
-            x = element * 8 + i
-            term_y = factor_y * contract_y(inside[i], diagonals)
-            term_z = factor_z * split(along_z[x * 16 : x * 16 + 16])
-            result.append(factor_x * contract_x(inside, stiffness, i) + WEIGHTS[i] * (term_y + term_z))
-    return result
+    for i in range(8):
+        terms = factor_y * contract_y(pairs[i], diagonals) + factor_z * along_z[i]
+        result.append(factor_x * contract_x(pairs, stiffness, i) + WEIGHTS[i] * terms)
+    return result, along_z
 
 
 def join_middle(rows):
@@ -278,8 +309,9 @@
     beyond = lane - LANES
     right, left = LANES + 3 * 8, WIDE - 3 * 8
     index = jnp.where(lane < right, lane >> 3, jnp.where(lane >= left, 19 + ((beyond - (left - LANES)) >> 3), ELEMENTS))
-    spread = (iota((24, WIDE), 0) == index).astype(jnp.float32)
-    return jnp.dot(elements[:, 0:24], spread, precision=EXACT, preferred_element_type=jnp.float32)
+    spread = (iota((24, WIDE), 0) == index).astype(jnp.bfloat16)
+    high, middle, low = (jnp.dot(v, spread, preferred_element_type=jnp.float32) for v in thirds(elements[:, 0:24]))
+    return high + (middle + low)
 
 
 def elements_of(folded):
@@ -404,7 +436,7 @@
 
 def start_kernel(
     source, previous, elements, first, second, stiffness, upper, lower, diagonals,
-    start, remainder, factors, halves, common, part, metrics,
+    start, remainder, factors, pair_factors, halves, common, part, metrics,
 ):
     even = even_index("gz")
     lane = iota((8, LANES), 1)
@@ -434,12 +466,14 @@
     faces = (rows[0], rows[15])
     for x in range(ROWS):
         start[x] = solid(own(rows[x]))
-    along_z = contract_z(jnp.concatenate([solid(v) for v in rows], axis=0), upper, lower, 0)
     scaled = [scaled_metrics(geo, [metric(metrics, c, e) for c in range(3)]) for e in range(2)]
-    for e in range(2):
-        for c in range(3):
+    joined = [join_pair(scaled[0][c], scaled[1][c]) for c in range(3)]
+    for c in range(3):
+        pair_factors[c] = solid(joined[c])
+        for e in range(2):
             factors[c, e] = solid(scaled[e][c])
-    applied = apply_rows(rows, along_z, scaled, stiffness, wide_diagonals(diagonals, 0))
+    applied, _ = apply_pairs(join_pairs(rows), joined, stiffness, upper, lower, wide_diagonals(diagonals, 0, BOTH))
+    applied = part_pairs(applied)
     rest = [wide(source, x, DEEP, SHALLOW) - applied[x] for x in range(ROWS)]
     halves[0], halves[1] = solid(faces[0]), solid(faces[1])
     for x in range(ROWS):
@@ -467,28 +501,24 @@
     geo = Geometry(WIDE)
     rest = [split(remainder[x]) for x in range(ROWS)]
     rest = [geo.assemble(v) for v in join_middle(rest)]
-    forward = wide_diagonals(diagonals, 1)
-    moved = []
-    for element in range(2):
-        inside = rest[element * 8 : element * 8 + 8]
-        moved += [solid(contract_y(contract_x(inside, vectors, i, True), forward)) for i in range(8)]
     for x in range(ROWS):
-        known[x] = solid(rest[x])
+        known[x] = solid(own(rest[x]))
+    pairs = join_pairs(rest)
+    forward = wide_diagonals(diagonals, 1, BOTH)
+    moved = [solid(contract_y(contract_x(pairs, vectors, i, True), forward)) for i in range(8)]
     transformed = contract_z(jnp.concatenate(moved, axis=0), upper, lower, 1, True)
+    divisors = divisors_of([join_pair(metric(metrics, c, 0), metric(metrics, c, 1)) for c in range(3)], lam)
     damped = []
-    for element in range(2):
-        divisors = divisors_of(geo, [metric(metrics, c, element) for c in range(3)], lam)
-        for i in range(8):
-            x = element * 8 + i
-            value = split(transformed[x * 16 : x * 16 + 16])
-            spectrum[x], inverse[x] = solid(value), solid(divisors[i])
-            damped.append(value * divisors[i])
+    for i in range(8):
+        value = split(transformed[i * 16 : i * 16 + 16])
+        spectrum[i], inverse[i] = solid(value), solid(divisors[i])
+        damped.append(value * divisors[i])
+    ends = [part_pair(contract_x(damped, vectors, near)) for near in (0, 7)]
     messages = []
     for side, near in ((0, 0), (1, 7)):
-        inside, across = damped[side * 8 : side * 8 + 8], damped[8 - side * 8 : 16 - side * 8]
-        value = contract_x(inside, vectors, near)
-        beside = weighted([line_of(bend, side * 8 + i, WIDE) for i in range(8)], inside)
-        beside = beside + line_of(stiffness, near * 8 + 7 - near, WIDE) * contract_x(across, vectors, near)
+        value = ends[side][side]
+        beside = part_pair(weighted([line_of(bend, side * 8 + i, BOTH) for i in range(8)], damped))[side]
+        beside = beside + line_of(stiffness, near * 8 + 7 - near, WIDE) * ends[side][1 - side]
         value, beside = solid(value), solid(beside)
         folded = fold([v[at : at + 8, LANES:] for v in (value, beside) for at in (0, 8)], SECOND_FIELDS)
         messages.append(jnp.concatenate([value[:, :LANES], beside[:, :LANES], folded], axis=0))
@@ -496,11 +526,6 @@
     both = [jnp.concatenate([part[side], messages[side]], axis=0) for side in range(2)]
     message_a[...] = jnp.where(even_x, both[1], both[0])
     message_b[...] = jnp.where(even_x, both[0], both[1])
-
-
-def both_sides(even, a, b):
-    one, two = a[...], b[...]
-    return jnp.where(even, two, one), jnp.where(even, one, two)
 
 
 def read_first(message):
@@ -563,64 +588,101 @@
                 pieces[element, k, b] = solid(own(made[b][k]))
 
 
+def side_kernel(
+    first, halves, remainder, factors, got, beyond, stiffness, vectors, bend, lam, upper, lower, diagonals,
+    start_face, additions, fields, answers, near_factors,
+):
+    right = even_index("gx") if first else jnp.logical_not(even_index("gx"))
+    side = jnp.where(right, 1, 0)
+    other = 1 - side
+    geo = Geometry(WIDE)
+    message = got[...]
+    near_half, near_value = read_first(message)
+    far_half = read_far(message)
+    block = beyond[pl.ds(pl.multiple_of(FIRST_ROWS * other, 8), FIRST_ROWS), :]
+    last_half, last_value = read_first(block)
+    spread = lanes_of(jnp.concatenate([elements_of(message[40:48]), elements_of(block[40:48])], axis=0))
+
+    def metrics_of(device, of_right, of_left):
+        rows = spread[16 * device : 16 * device + 16]
+        return [jnp.where(right, metric(rows, c, of_right), metric(rows, c, of_left)) for c in range(3)]
+
+    def row_of(ref, at):
+        row = ref[pl.ds(at, 1), :]
+        return jnp.concatenate([row] * (WIDE // LANES), axis=1)[None]
+
+    near, far, last = metrics_of(0, 0, 1), metrics_of(0, 1, 0), metrics_of(1, 0, 1)
+    near_scaled, far_scaled, last_scaled = (scaled_metrics(geo, c) for c in (near, far, last))
+    mine = [split(factors[c, side]) for c in range(3)]
+    for c in range(3):
+        near_factors[c] = solid(near_scaled[c])
+    half, value = split(halves[side]), split(remainder[15 * side])
+    start_face[...] = solid(own(half + near_half))
+    stiff = wide_diagonals(diagonals, 0)
+    parts = [half, near_half, far_half, last_half]
+    along_z = contract_z(jnp.concatenate([solid(v) for v in parts], axis=0), upper, lower, 0)
+    here, there = row_of(stiffness, 63 * side), row_of(stiffness, 63 * other)
+
+    def face_row(c, corner, k):
+        term = c[1] * contract_y(parts[k], stiff) + c[2] * split(along_z[k * 16 : k * 16 + 16])
+        return corner * (c[0] * parts[k]) + WEIGHTS[0] * term
+
+    taken = face_row(mine, here, 1) + face_row(near_scaled, there, 0)
+    taken_far = face_row(far_scaled, here, 3) + face_row(last_scaled, there, 2)
+    made = [
+        geo.assemble(v)
+        for v in (
+            near_value - taken, mine[0] * near_half, value - taken, near_scaled[0] * half,
+            last_value - taken_far, far_scaled[0] * last_half,
+        )
+    ]
+    for k in range(2):
+        additions[k] = solid(own(made[k]))
+    forward = wide_diagonals(diagonals, 1)
+    flat = jnp.concatenate([solid(contract_y(v, forward)) for v in made], axis=0)
+    flat = contract_z(flat, upper, lower, 1, True)
+    fields[0], fields[1] = flat[0:16], flat[16:32]
+    near_total, near_field, far_total, far_field = (split(flat[k * 16 : k * 16 + 16]) for k in range(2, 6))
+
+    cross = line_of(stiffness, 7, WIDE)
+    ends = [[row_of(vectors, 56 * at + i) for i in range(8)] for at in (other, side)]
+    bends = [[row_of(bend, 8 * at + i) for i in range(8)] for at in (other, side)]
+    result, partial = (split(v) for v in read_second(message[FIRST_ROWS + FAR_ROWS :]))
+    crossed, divisors = cross * far_field, divisors_of(near, lam)
+    close = [
+        (ends[0][i] * near_total - bends[0][i] * near_field - ends[1][i] * crossed) * divisors[i] for i in range(8)
+    ]
+    crossed, divisors = cross * near_field, divisors_of(far, lam)
+    distant = [
+        (ends[1][i] * far_total - bends[1][i] * far_field - ends[0][i] * crossed) * divisors[i] for i in range(8)
+    ]
+    result = result + weighted(ends[0], close)
+    partial = partial + weighted(bends[0], close) + cross * weighted(ends[0], distant)
+    answers[0], answers[1] = solid(result), solid(partial)
+
+
 def solve_kernel(
-    known, factors, halves, remainder, spectrum, inverse, got_a, got_b, got_c, _,
-    stiffness, vectors, bend, lam, upper, lower, diagonals,
+    known, spectrum, inverse, sides, stiffness, vectors, bend, upper, lower, diagonals,
     start_faces, residual, local, beside, face_factors, sums,
 ):
     even = even_index("gx")
     geo = Geometry(WIDE)
-    sides = both_sides(even, got_a, got_b)
-    beyond = got_c[...]
-    near = [read_first(side) for side in sides]
-    far = [read_far(side) for side in sides]
-    last = [read_first(beyond[FIRST_ROWS : 2 * FIRST_ROWS]), read_first(beyond[:FIRST_ROWS])]
-    mine = [stored_factors(factors, e) for e in range(2)]
-    folds = [side[40:48] for side in sides] + [beyond[FIRST_ROWS + 40 : FIRST_ROWS + 48], beyond[40:48]]
-    spread = lanes_of(jnp.concatenate([elements_of(folded) for folded in folds], axis=0))
-
-    def metrics_of(device, element):
-        return [metric(spread[16 * device : 16 * device + 16], c, element) for c in range(3)]
-
-    near_metrics, far_metrics = [metrics_of(0, 1), metrics_of(1, 0)], [metrics_of(0, 0), metrics_of(1, 1)]
-    near_factors, far_factors, last_factors = (
-        [scaled_metrics(geo, v) for v in group]
-        for group in (near_metrics, far_metrics, [metrics_of(2, 1), metrics_of(3, 0)])
-    )
-    for side in range(2):
-        for c in range(3):
-            face_factors[side, c] = solid(near_factors[side][c])
-    half = [split(halves[side]) for side in range(2)]
-    remain = [split(remainder[x]) for x in (0, 15)]
-    left_half = [near[0][0], half[1], last[0][0], far[1]]
-    right_half = [half[0], near[1][0], far[0], last[1][0]]
-    left_factors = [near_factors[0], mine[1], last_factors[0], far_factors[1]]
-    right_factors = [mine[0], near_factors[1], far_factors[0], last_factors[1]]
-    stiff = wide_diagonals(diagonals, 0)
-    along_z = contract_z(jnp.concatenate([solid(v) for v in left_half + right_half], axis=0), upper, lower, 0)
-    first, last_corner = line_of(stiffness, 0, WIDE), line_of(stiffness, 63, WIDE)
-    cross = line_of(stiffness, 7, WIDE)
-    taken, into_left, into_right = [], [], []
-    for k in range(4):
-        left, right = left_factors[k][0] * right_half[k], right_factors[k][0] * left_half[k]
-        from_left, from_right = split(along_z[k * 16 : k * 16 + 16]), split(along_z[k * 16 + 64 : k * 16 + 80])
-        rest = left_factors[k][1] * contract_y(right_half[k], stiff) + right_factors[k][1] * contract_y(left_half[k], stiff)
-        rest = rest + left_factors[k][2] * from_right + right_factors[k][2] * from_left
-        taken.append(last_corner * left + first * right + WEIGHTS[0] * rest)
-        into_left.append(geo.assemble(left) if k != 2 else None)
-        into_right.append(geo.assemble(right) if k != 3 else None)
-    to_right = [geo.assemble(v - t) for v, t in zip((near[0][1], remain[1], last[0][1]), taken[:3])]
-    to_left = [geo.assemble(v - taken[k]) for k, v in ((0, remain[0]), (1, near[1][1]), (3, last[1][1]))]
-    for side in range(2):
-        start_faces[side] = solid(own(left_half[side] + right_half[side]))
-
-    moved = [into_right[0], into_left[1]]
-    rows = [own(split(known[x])) for x in range(ROWS)]
-    rows[0], rows[15] = rows[0] + own(to_right[0]), rows[15] + own(to_left[1])
+
+    def both(which, *at):
+        one, two = sides[0][which][at], sides[1][which][at]
+        return jnp.where(even, two, one), jnp.where(even, one, two)
+
+    start_faces[0], start_faces[1] = both(0)
+    for c in range(3):
+        face_factors[0, c], face_factors[1, c] = both(4, c)
+    totals, moved = both(1, 0), both(1, 1)
+
+    rows = [split(known[x]) for x in range(ROWS)]
+    rows[0], rows[15] = rows[0] + split(totals[0]), rows[15] + split(totals[1])
     for side, face in ((0, 0), (1, 7)):
         for i in range(8):
             if i != face:
-                change = line_of(stiffness, i * 8 + face, LANES) * own(moved[side])
+                change = line_of(stiffness, i * 8 + face, LANES) * split(moved[side])
                 x = side * 8 + i
                 rows[x] = rows[x] - change
                 if x in (7, 8):
@@ -636,53 +698,24 @@
     for a in range(2):
         sums[a : a + 1] = down(parts[a] * weight)
 
-    forward, backward = wide_diagonals(diagonals, 1), wide_diagonals(diagonals, 2)
-    fields = to_right + to_left + [into_left[0], into_left[1], into_left[3], into_right[0], into_right[1], into_right[2]]
-    flat = jnp.concatenate([solid(contract_y(v, forward)) for v in fields], axis=0)
-    flat = contract_z(flat, upper, lower, 1, True)
-    flat = [split(flat[k * 16 : k * 16 + 16]) for k in range(len(fields))]
-    to_right, to_left = flat[:3], flat[3:6]
-    into_left, into_right = {0: flat[6], 1: flat[7], 3: flat[8]}, {0: flat[9], 1: flat[10], 2: flat[11]}
-
-    def vector(p, i):
-        return line_of(vectors, p * 8 + i, WIDE)
-
-    def changes(element, total, close, distant):
-        face, other = 7 * element, 7 - 7 * element
-        crossed = cross * distant
-        return [
-            vector(face, i) * total - line_of(bend, element * 8 + i, WIDE) * close - vector(other, i) * crossed
-            for i in range(8)
-        ]
-
-    moved = []
-    for element, change in enumerate(
-        (changes(0, to_right[0], into_right[0], into_left[1]), changes(1, to_left[1], into_left[1], into_right[0]))
-    ):
-        moved += [solid((split(spectrum[element * 8 + i]) + change[i]) * split(inverse[element * 8 + i])) for i in range(8)]
-    for side in range(2):
-        value, partial = (split(v) for v in read_second(sides[side][FIRST_ROWS + FAR_ROWS :]))
-        near_element, far_element = 1 - side, side
-        if side == 0:
-            close = changes(1, to_left[0], into_left[0], into_right[2])
-            distant = changes(0, to_right[2], into_right[2], into_left[0])
-        else:
-            close = changes(0, to_right[1], into_right[1], into_left[3])
-            distant = changes(1, to_left[2], into_left[3], into_right[1])
-        face = 7 * near_element
-        close = [a * b for a, b in zip(close, divisors_of(geo, near_metrics[side], lam))]
-        distant = [a * b for a, b in zip(distant, divisors_of(geo, far_metrics[side], lam))]
-        value = value + weighted([vector(face, i) for i in range(8)], close)
-        partial = partial + weighted([line_of(bend, near_element * 8 + i, WIDE) for i in range(8)], close)
-        partial = partial + cross * weighted([vector(face, i) for i in range(8)], distant)
-        moved += [solid(value), solid(partial)]
-
-    back = contract_z(jnp.concatenate(moved, axis=0), upper, lower, 2, True)
-    back = [contract_y(split(back[k * 16 : k * 16 + 16]), backward) for k in range(ROWS + 4)]
-    solved = []
-    for element in range(2):
-        inside = back[element * 8 : element * 8 + 8]
-        solved += [contract_x(inside, vectors, i) for i in range(8)]
+    backward = wide_diagonals(diagonals, 2)
+    totals, moved = [split(v) for v in both(2, 0)], [split(v) for v in both(2, 1)]
+
+    total, close = join_pair(*totals), join_pair(*moved)
+    crossed = line_of(stiffness, 7, BOTH) * join_pair(moved[1], moved[0])
+    ready = []
+    for i in range(8):
+        change = pair_line(vectors, i, 56 + i) * total - pair_line(bend, i, 8 + i) * close
+        change = change - pair_line(vectors, 56 + i, i) * crossed
+        ready.append(solid((split(spectrum[i]) + change) * split(inverse[i])))
+    answers = [both(3, k) for k in range(2)]
+    answers = jnp.concatenate([answers[k][side] for side in range(2) for k in range(2)], axis=0)
+    back = contract_z(jnp.concatenate(ready, axis=0), upper, lower, 2, True)
+    answers = contract_z(answers, upper, lower, 2, True)
+    wide_backward = wide_diagonals(diagonals, 2, BOTH)
+    back = [contract_y(split(back[k * 16 : k * 16 + 16]), wide_backward) for k in range(8)]
+    answers = [contract_y(split(answers[k * 16 : k * 16 + 16]), backward) for k in range(4)]
+    solved = part_pairs([contract_x(back, vectors, i) for i in range(8)])
     total = None
     for x in range(ROWS):
         term = own(solved[x]) * rows[x]
@@ -690,11 +723,11 @@
     sums[2:3] = down(total)
     sums[3:8] = jnp.zeros((5, LANES), jnp.float32)
     solved = join_middle(solved)
-    solved[0], solved[15] = solved[0] + back[16], solved[15] + back[18]
+    solved[0], solved[15] = solved[0] + answers[0], solved[15] + answers[2]
     for x in range(ROWS):
         local[x] = solid(geo.assemble(solved[x]))
     for side in range(2):
-        beside[side] = solid(geo.assemble(back[17 + 2 * side]))
+        beside[side] = solid(geo.assemble(answers[1 + 2 * side]))
 
 
 def image_kernel(
@@ -703,10 +736,13 @@
 ):
     geo = Geometry(WIDE)
     rows = [split(local[x]) for x in range(ROWS)]
-    along_z = contract_z(jnp.concatenate([solid(v) for v in rows], axis=0), upper, lower, 0, True)
-    scaled = [stored_factors(factors, e) for e in range(2)]
     stiff = wide_diagonals(diagonals, 0)
-    applied = apply_rows(rows, along_z, scaled, stiffness, stiff)
+    applied, along_z = apply_pairs(
+        join_pairs(rows), [split(factors[c]) for c in range(3)], stiffness, upper, lower,
+        wide_diagonals(diagonals, 0, BOTH), True,
+    )
+    applied = part_pairs(applied)
+    along_z = (part_pair(along_z[0])[0], part_pair(along_z[7])[1])
     total, parts = None, [None, None]
     for x in range(ROWS):
         term = own(applied[x]) * own(rows[x])
@@ -719,8 +755,7 @@
     for side, x, across in ((0, 0, 63), (1, 15, 0)):
         there = [split(face_factors[side, c]) for c in range(3)]
         other = there[0] * (split(beside[side]) + line_of(stiffness, across, WIDE) * rows[x])
-        turned = split(along_z[x * 16 : x * 16 + 16])
-        other = other + WEIGHTS[0] * (there[1] * contract_y(rows[x], stiff) + there[2] * turned)
+        other = other + WEIGHTS[0] * (there[1] * contract_y(rows[x], stiff) + there[2] * along_z[side])
         applied[x] = applied[x] + other
     applied = join_middle(applied)
     for x in range(ROWS):
@@ -738,13 +773,11 @@
 
 
 def middle_kernel(
-    known, factors, halves, remainder, spectrum, inverse, got_a, got_b, got_c, waves,
-    stiffness, vectors, bend, lam, upper, lower, diagonals, fixed, lines,
-    start_faces, residual, local, face_factors, image, payload, beside, sums,
+    known, factors, spectrum, inverse, _, stiffness, vectors, bend, upper, lower, diagonals, fixed, lines, *refs
 ):
+    sides, (start_faces, residual, local, face_factors, image, payload, beside, sums) = (refs[5:10], refs[:5]), refs[10:]
     solve_kernel(
-        known, factors, halves, remainder, spectrum, inverse, got_a, got_b, got_c, waves,
-        stiffness, vectors, bend, lam, upper, lower, diagonals,
+        known, spectrum, inverse, sides, stiffness, vectors, bend, upper, lower, diagonals,
         start_faces, residual, local, beside, face_factors, sums,
     )
     image_kernel(
@@ -952,10 +985,10 @@
     )(elements, stiffness, fdm_vectors, fdm_values, vertex_map, coarse_inverse, jnp.asarray(lane_tables()))
 
     message = (FIRST_ROWS + FAR_ROWS + SECOND_ROWS, LANES)
-    start, remainder, factors, halves, common, part, metrics = call(
+    start, remainder, factors, pair_factors, halves, common, part, metrics = call(
         start_kernel,
         [
-            block, wide, (3, 2, ROWS, WIDE), (2, ROWS, WIDE), (2 * FIRST_ROWS + 16, LANES),
+            block, wide, (3, 2, ROWS, WIDE), (3, ROWS, BOTH), (2, ROWS, WIDE), (2 * FIRST_ROWS + 16, LANES),
             (2, FIRST_ROWS + FAR_ROWS, LANES), (16, WIDE),
         ],
         [VMEM] * 9,
@@ -963,7 +996,7 @@
     )(source, previous, elements, first, second, stiff, upper, lower, diagonals)
     beyond = second_neighbours(common, "gx")
     known, spectrum, inverse, side_a, side_b = call(
-        guess_kernel, [wide, wide, wide, message, message], [VMEM] * 10, "guess",
+        guess_kernel, [block, (8, ROWS, BOTH), (8, ROWS, BOTH), message, message], [VMEM] * 10, "guess",
         cost=pl.CostEstimate(flops=4000000000, bytes_accessed=4000000, transcendentals=0),
     )(remainder, metrics, part, stiff, vectors, bend, lam, upper, lower, diagonals)
     side_a, side_b = swap(side_a, side_b, "gx")
@@ -971,16 +1004,21 @@
         ready_kernel, [(2, 2, 4, ROWS, LANES), (8, WIDE), (ROWS, WIDE)], [VMEM] * 5, "ready"
     )(factors, stiff, lines, upper, lower)
 
+    sides = []
+    for at, got in ((1, side_b), (0, side_a)):
+        sides += call(
+            functools.partial(side_kernel, at == 0),
+            [face, (2, ROWS, LANES), (2, ROWS, WIDE), (2, ROWS, WIDE), (3, ROWS, WIDE)],
+            [VMEM] * 12,
+            ("side_first", "side_second")[at],
+        )(halves, remainder, factors, got, beyond, stiff, vectors, bend, lam, upper, lower, diagonals)
     start_faces, residual, local, face_factors, image, payload = call(
         middle_kernel,
         [(2, ROWS, LANES), block, wide, (2, 3, ROWS, WIDE), block, (2 * devices, LANES)],
-        [VMEM] * 19,
+        [VMEM] * 23,
         "middle",
         [pltpu.VMEM((2, ROWS, WIDE), jnp.float32), pltpu.VMEM((8, LANES), jnp.float32)],
-    )(
-        known, factors, halves, remainder, spectrum, inverse, side_a, side_b, beyond, waves,
-        stiff, vectors, bend, lam, upper, lower, diagonals, fixed, lines,
-    )
+    )(known, pair_factors, spectrum, inverse, waves, stiff, vectors, bend, upper, lower, diagonals, fixed, lines, *sides)
     gathered = lax.all_to_all(payload.reshape(devices, 2, LANES), ("gx", "gz"), 0, 0)
     gathered = gathered.reshape(2 * devices, LANES)
 

time: 31.8 us -> 31.6 us (level)
  waiting for transfers between devices: 4.3 us -> 3.67 us
  Pallas kernels: 8.29 us -> 8.61 us
    pallas_call x2 -> x4, Pallas kernels: 1.42 us -> 2.64 us  [the longest x2 1.23 us: body(): call(functools.partial(side_kernel, at == 0), [face, (2, ROWS, LANES), (2...]
    pallas_call x1, Pallas kernels: 2.05 us -> 1.15 us  [body(): call(middle_kernel, [(2, ROWS, LANES), block, wide, (2, 3, ROWS, WIDE), b...]
    ppermute x2, waiting for transfers between devices: 2.4 us -> 1.77 us  [swap(): two = lax.ppermute(second, axis, odd + [(b, a) for a, b in odd])]
  transfers between devices with their start and end apart: 5 -> 5, of which waited for: 2 -> 2; matrix products, arithmetic and copies ran while one was open for 0% -> 0% of each run, Pallas kernels for 9% -> 11%
where the time goes in v8:
time: 31.6 us; the launch traced here: 31.4 us
  blocking collectives  9.59 us (30%)
  starting transfers between devices  8.77 us (28%)
  Pallas kernels  8.61 us (27%)
  waiting for transfers between devices  3.67 us (12%)
  between operations  0.76 us (2%)
    all_to_all x1, blocking collectives, body(): lax.all_to_all(payload.reshape(devices, 2, LANES), ('gx', 'gz'), 0, 0)  9.59 us
    ppermute x2, starting transfers between devices, swap(): two = lax.ppermute(second, axis, odd + [(b, a) for a, b in odd])  5.19 us
    ppermute x2, starting transfers between devices, swap(): one = lax.ppermute(first, axis, [(i, i ^ 1) for i in range(size)])  2.02 us
    pallas_call x1, Pallas kernels, body(): call(functools.partial(prepare_kernel, small), [('half', 4, WIDE, WIDE),...  2 us
    ppermute x2, waiting for transfers between devices, swap(): one = lax.ppermute(first, axis, [(i, i ^ 1) for i in range(size)])  1.9 us
    ppermute x2, waiting for transfers between devices, swap(): two = lax.ppermute(second, axis, odd + [(b, a) for a, b in odd])  1.77 us
    ppermute x1, starting transfers between devices, second_neighbours(): return lax.ppermute(common, axis, [(i, i ^ 2) for i in range(size)])  1.56 us
    pallas_call x1, Pallas kernels, body(): call(kernel, [block, block], [VMEM] * len(operands), 'finish', [pltpu.VME...  1.3 us
  transfers between devices with their start and end apart: 5, of which 2 were waited for; matrix products, arithmetic and copies ran while one was open for 0% of the time, Pallas kernels for 11%

profile of v8, /device:TPU:0, one launch (start us, length us, event | category | flops | bytes accessed | tf_op | source)
XLA Modules:
  0.0 31.4 jit_solution(10681067497658820542)
XLA Ops:
  0.6 0.0 copy-start.1
  0.7 1.2 %pack.1 = (f32[13,8,128]{2,1,0:T(8,128)S(1)}, f32[13,8,128]{2,1,0:T(8,128)S(1)}, f32[16,128]{1,0:T(8,128)S(1)}, f32[16,16,128]{2,1,0:T(8,128)S(1)}, f32[16,16,128]{2,1,0:T(8,128)S(1)}) custom-call(f32[16,16,128]{2,1,0:T(8,128)} %source.1, f32[16,16,128]{2,1,0:T(8,128)} %previous.1, f32[3,2,2,16]{3,2,1,0:T(2,128)} %coefficients.1), custom_call_target="tpu_custom_call" | custom-call | tf_op jit(solution)/shard_map/pack/pallas_call | solution.py:969
  1.9 0.0 copy-start.2
  1.9 0.5 %collective-permute-start = (f32[13,8,128]{2,1,0:T(8,128)S(1)}, f32[13,8,128]{2,1,0:T(8,128)S(1)}, u32[]{:S(2)}, u32[]{:S(2)}) collective-permute-start(f32[13,8,128]{2,1,0:T(8,128)S(1)} %get-tuple-element.52), channel_id=1, source_target_pairs={{0,1},{1,0},{2,3},{3,2},{4,5},{5,4},{6,7},{7,6},{8,9},{9,8},{10,11... | collective-permute-start | bytes 159752 | tf_op jit(solution)/shard_map/ppermute | solution.py:944
  2.4 4.7 %collective-permute-start.1 = (f32[13,8,128]{2,1,0:T(8,128)S(1)}, f32[13,8,128]{2,1,0:T(8,128)S(1)}, u32[]{:S(2)}, u32[]{:S(2)}) collective-permute-start(f32[13,8,128]{2,1,0:T(8,128)S(1)} %get-tuple-element.53), channel_id=1, source_target_pairs={{1,2},{3,4},{5,6},{7,0},{2,1},{4,3},{6,5},{0,7},{9,10},{11,12},{13... | collective-permute-start | bytes 159752 | tf_op jit(solution)/shard_map/ppermute | solution.py:945
  7.1 0.0 copy-done
  7.1 0.0 copy-done.4
  7.2 2.0 %prepare.1 = (bf16[4,256,256]{2,1,0:T(8,128)(2,1)S(1)}, bf16[4,256,128]{2,1,0:T(8,128)(2,1)S(1)}, f32[3,8,8,128]{3,2,1,0:T(8,128)S(1)}, f32[64,128]{1,0:T(8,128)...) custom-call(f32[16,128]{1,0:T(8,128)S(1)} %get-tuple-element.51.elem, ...), custom_call_target="tpu_custom_call" | custom-call | tf_op jit(solution)/shard_map/prepare/pallas_call | solution.py:977
  9.2 0.0 collective-permute-done.first
  9.2 0.0 collective-permute-done.1.second
  9.2 0.7 %start.1 = (f32[16,16,128]{2,1,0:T(8,128)S(1)}, f32[16,16,256]{2,1,0:T(8,128)S(1)}, f32[3,2,16,256]{3,2,1,0:T(8,128)S(1)}, f32[3,16,384]{2,1,0:T(8,128)S(1)}, f3...) custom-call(f32[16,16,128]{2,1,0:T(8,128)S(1)} %get-tuple-element.49.source, ...), custom_call_target="tpu_custom_call" | custom-call | tf_op jit(solution)/shard_map/start/pallas_call | solution.py:988
  9.9 1.6 %collective-permute-start.3 = (f32[112,128]{1,0:T(8,128)S(1)}, f32[112,128]{1,0:T(8,128)S(1)}, u32[]{:S(2)}, u32[]{:S(2)}) collective-permute-start(f32[112,128]{1,0:T(8,128)S(1)} %get-tuple-element.75), channel_id=1, source_target_pairs={{0,16},{8,24},{16,0},{24,8},{1,17},{9,25},{17,1},{25,9},{2,18},{10... | collective-permute-start | bytes 172040 | tf_op jit(solution)/shard_map/ppermute | solution.py:952
  11.5 0.7 %guess.1 = (f32[16,16,128]{2,1,0:T(8,128)S(1)}, f32[8,16,384]{2,1,0:T(8,128)S(1)}, f32[8,16,384]{2,1,0:T(8,128)S(1)}, f32[112,128]{1,0:T(8,128)S(1)}, f32[112,128]{1,0:T(8,128)S(1)}) custom-call(f32[16,16,256]{2,1,0:T(8,128)S(1)} %get-tuple-element.59.remainder, f32[16,256]{1,0:T(8,128)S(1)} %get-tuple-element.60.metrics, ...), custom_call_target="tpu_custom_call" | custom-call | flops 4000000000 | bytes 4000000 | tf_op jit(solution)/shard_map/guess/pallas_call | solution.py:998
  12.2 1.5 %collective-permute-start.4 = (f32[112,128]{1,0:T(8,128)S(1)}, f32[112,128]{1,0:T(8,128)S(1)}, u32[]{:S(2)}, u32[]{:S(2)}) collective-permute-start(f32[112,128]{1,0:T(8,128)S(1)} %get-tuple-element.81), channel_id=1, source_target_pairs={{0,8},{8,0},{16,24},{24,16},{1,9},{9,1},{17,25},{25,17},{2,10},{10... | collective-permute-start | bytes 172040 | tf_op jit(solution)/shard_map/ppermute | solution.py:944
  13.7 0.5 %collective-permute-start.2 = (f32[112,128]{1,0:T(8,128)S(1)}, f32[112,128]{1,0:T(8,128)S(1)}, u32[]{:S(2)}, u32[]{:S(2)}) collective-permute-start(f32[112,128]{1,0:T(8,128)S(1)} %get-tuple-element.74), channel_id=1, source_target_pairs={{8,16},{24,0},{16,8},{0,24},{9,17},{25,1},{17,9},{1,25},{10,18},{2... | collective-permute-start | bytes 172040 | tf_op jit(solution)/shard_map/ppermute | solution.py:945
  14.2 0.3 ready.1
  14.5 0.0 collective-permute-done.3.beyond
  14.5 1.9 %collective-permute-done.4.got = f32[112,128]{1,0:T(8,128)S(1)} collective-permute-done((f32[112,128]{1,0:T(8,128)S(1)}, f32[112,128]{1,0:T(8,128)S(1)}, u32[]{:S(2)}, u32[]{:S(2)}) %collective-permute-start.4) | collective-permute-done | bytes 57376 | tf_op jit(solution)/shard_map/ppermute | solution.py:944
  16.4 0.6 %side_first.1 = (f32[16,128]{1,0:T(8,128)S(1)}, f32[2,16,128]{2,1,0:T(8,128)S(1)}, f32[2,16,256]{2,1,0:T(8,128)S(1)}, f32[2,16,256]{2,1,0:T(8,128)S(1)}, f32[3,16,256]{2,1,0:T(8,128)S(1)}) custom-call(f32[2,16,256]{2,1,0:T(8,128)S(1)} %get-tuple-element.73.halves, f32[16,16,256]{2,1,0:T(8,128)S(1)} %get-tuple-element.59.remainder, ...), custom_call_target="tpu_custom_call" | custom-call | tf_op jit(solution)/shard_map/side_first/pallas_call | solution.py:1009
  17.0 1.8 %collective-permute-done.2.got = f32[112,128]{1,0:T(8,128)S(1)} collective-permute-done((f32[112,128]{1,0:T(8,128)S(1)}, f32[112,128]{1,0:T(8,128)S(1)}, u32[]{:S(2)}, u32[]{:S(2)}) %collective-permute-start.2) | collective-permute-done | bytes 57376 | tf_op jit(solution)/shard_map/ppermute | solution.py:945
  18.7 0.6 %side_second.1 = (f32[16,128]{1,0:T(8,128)S(1)}, f32[2,16,128]{2,1,0:T(8,128)S(1)}, f32[2,16,256]{2,1,0:T(8,128)S(1)}, f32[2,16,256]{2,1,0:T(8,128)S(1)}, f32[3,16,256]{2,1,0:T(8,128)S(1)}) custom-call(f32[2,16,256]{2,1,0:T(8,128)S(1)} %get-tuple-element.73.halves, f32[16,16,256]{2,1,0:T(8,128)S(1)} %get-tuple-element.59.remainder, ...), custom_call_target="tpu_custom_call" | custom-call | tf_op jit(solution)/shard_map/side_second/pallas_call | solution.py:1009
  19.4 1.2 %middle.1 = (f32[2,16,128]{2,1,0:T(8,128)S(1)}, f32[16,16,128]{2,1,0:T(8,128)S(1)}, f32[16,16,256]{2,1,0:T(8,128)S(1)}, f32[2,3,16,256]{3,2,1,0:T(8,128)S(1)}, f...) custom-call(f32[16,16,128]{2,1,0:T(8,128)S(1)} %get-tuple-element.65.known, ...), custom_call_target="tpu_custom_call" | custom-call | tf_op jit(solution)/shard_map/middle/pallas_call | solution.py:1015
  20.5 9.6 %all_to_all.5 = f32[32,2,128]{2,1,0:T(2,128)S(1)} all-to-all(f32[32,2,128]{2,1,0:T(2,128)S(1)} %bitcast.3), channel_id=1, replica_groups=mesh['gx'=4,'gz'=8] {'gx','gz'}, dimensions={0} | all-to-all | bytes 65536 | tf_op jit(solution)/shard_map/all_to_all | solution.py:1022
  30.1 1.3 %finish.1 = (f32[16,16,128]{2,1,0:T(8,128)}, f32[16,16,128]{2,1,0:T(8,128)}) custom-call(f32[16,16,128]{2,1,0:T(8,128)S(1)} %get-tuple-element.58.refs_0_, f32[2,16,128]{2,1,0:T(8,128)S(1)} %get-tuple-element.87.refs_1_, f32[16,16,128]{2,1,0:T(8,128)S(1)} %get-tuple-element.88.refs_2_, f32[16,16,256]{2,1,0:T(8,128)S(1)} %get-tuple-element.89.refs_3_, ...), custom_call_target="tpu_custom_call" | custom-call | tf_op jit(solution)/shard_map/finish/pallas_call | solution.py:1045
  (8 shorter events, 0.0 us)
Async XLA Ops:
  0.6 6.5 %copy-start = (s32[8,2,2,16]{3,2,1,0:T(2,128)S(1)}, s32[8,2,2,16]{3,2,1,0:T(2,128)}, u32[]{:S(2)}) copy-start(s32[8,2,2,16]{3,2,1,0:T(2,128)} %labels.1) | copy-start | bytes 6148
  0.6 6.5 %copy-start.1 = (f32[3,8,128]{2,1,0:T(8,128)S(1)}, f32[3,8,128]{2,1,0:T(8,128)}, u32[]{:S(2)}) copy-start(f32[3,8,128]{2,1,0:T(8,128)} %constant.2.clone.tables) | copy-start | bytes 36868
  0.7 6.5 %copy-start.3 = (f32[8,8]{1,0:T(8,128)S(1)}, f32[8,8]{1,0:T(8,128)}, u32[]{:S(2)}) copy-start(f32[8,8]{1,0:T(8,128)} %vectors.1) | copy-start | bytes 772
  1.9 5.3 %copy-start.2 = (f32[8,8]{1,0:T(8,128)S(1)}, f32[8,8]{1,0:T(8,128)}, u32[]{:S(2)}) copy-start(f32[8,8]{1,0:T(8,128)} %stiffness.1) | copy-start | bytes 772
  1.9 7.3 %collective-permute-start = (f32[13,8,128]{2,1,0:T(8,128)S(1)}, f32[13,8,128]{2,1,0:T(8,128)S(1)}, u32[]{:S(2)}, u32[]{:S(2)}) collective-permute-start(f32[13,8,128]{2,1,0:T(8,128)S(1)} %get-tuple-element.52), channel_id=1, source_target_pairs={{0,1},{1,0},{2,3},{3,2},{4,5},{5,4},{6,7},{7,6},{8,9},{9,8},{10,11... | collective-permute-start | bytes 159752 | tf_op jit(solution)/shard_map/ppermute | solution.py:944
  2.4 4.7 %copy-start.4 = (f32[2,64]{1,0:T(2,128)S(1)}, f32[2,64]{1,0:T(2,128)}, u32[]{:S(2)}) copy-start(f32[2,64]{1,0:T(2,128)} %coarse.1) | copy-start | bytes 1540
  2.4 4.7 %copy-start.5 = (f32[8]{0:T(128)S(1)}, f32[8]{0:T(128)}, u32[]{:S(2)}) copy-start(f32[8]{0:T(128)} %eigen.1) | copy-start | bytes 100
  2.4 6.8 %collective-permute-start.1 = (f32[13,8,128]{2,1,0:T(8,128)S(1)}, f32[13,8,128]{2,1,0:T(8,128)S(1)}, u32[]{:S(2)}, u32[]{:S(2)}) collective-permute-start(f32[13,8,128]{2,1,0:T(8,128)S(1)} %get-tuple-element.53), channel_id=1, source_target_pairs={{1,2},{3,4},{5,6},{7,0},{2,1},{4,3},{6,5},{0,7},{9,10},{11,12},{13... | collective-permute-start | bytes 159752 | tf_op jit(solution)/shard_map/ppermute | solution.py:945
  9.9 4.5 %collective-permute-start.3 = (f32[112,128]{1,0:T(8,128)S(1)}, f32[112,128]{1,0:T(8,128)S(1)}, u32[]{:S(2)}, u32[]{:S(2)}) collective-permute-start(f32[112,128]{1,0:T(8,128)S(1)} %get-tuple-element.75), channel_id=1, source_target_pairs={{0,16},{8,24},{16,0},{24,8},{1,17},{9,25},{17,1},{25,9},{2,18},{10... | collective-permute-start | bytes 172040 | tf_op jit(solution)/shard_map/ppermute | solution.py:952
  12.2 4.2 %collective-permute-start.4 = (f32[112,128]{1,0:T(8,128)S(1)}, f32[112,128]{1,0:T(8,128)S(1)}, u32[]{:S(2)}, u32[]{:S(2)}) collective-permute-start(f32[112,128]{1,0:T(8,128)S(1)} %get-tuple-element.81), channel_id=1, source_target_pairs={{0,8},{8,0},{16,24},{24,16},{1,9},{9,1},{17,25},{25,17},{2,10},{10... | collective-permute-start | bytes 172040 | tf_op jit(solution)/shard_map/ppermute | solution.py:944
  13.7 5.1 %collective-permute-start.2 = (f32[112,128]{1,0:T(8,128)S(1)}, f32[112,128]{1,0:T(8,128)S(1)}, u32[]{:S(2)}, u32[]{:S(2)}) collective-permute-start(f32[112,128]{1,0:T(8,128)S(1)} %get-tuple-element.74), channel_id=1, source_target_pairs={{8,16},{24,0},{16,8},{0,24},{9,17},{25,1},{17,9},{1,25},{10,18},{2... | collective-permute-start | bytes 172040 | tf_op jit(solution)/shard_map/ppermute | solution.py:945

commit v9 on v8

--- a/solution.py
+++ b/solution.py
@@ -40,6 +40,7 @@
 HALO = 32
 ELEMENTS = 22
 CORNERS = (58, 80)
+SPARE = (84, 100)
 DEEP, SHALLOW = 25, 17
 SLOT = DEEP + SHALLOW
 FIRST_FIELDS = ((0, 24), (41, 17))
@@ -299,9 +300,10 @@
                     shift = jnp.where(to_right, (at + width) % LANES, at)
                     moved = pltpu.roll(ref[n // 2, 8 * (n % 2) : 8 * (n % 2) + 8], shift, 1)
                     packed = moved if packed is None else jnp.where(slot >= at, moved, packed)
+            if tile == 10:
+                for at, rows in zip(SPARE, (elements[:8], elements[8:])):
+                    packed = jnp.where(slot >= at, pltpu.roll(rows, at, 1), packed)
             out[tile] = packed
-        out[11] = elements[:8]
-        out[12] = elements[8:]
 
 
 def lanes_of(elements):
@@ -455,8 +457,10 @@
         return split(widen(ref[x], [beyond(2 * x + e, at, width) for e in range(2)]))
 
     geo = Geometry(WIDE)
-    right = pltpu.roll(jnp.concatenate([from_right[11], from_right[12]], axis=0), 16, 1)
-    left = pltpu.roll(jnp.concatenate([from_left[11], from_left[12]], axis=0), 6, 1)
+    right, left = (
+        jnp.concatenate([pltpu.roll(tiles[10], (LANES + to - at) % LANES, 1) for at in SPARE], axis=0)
+        for tiles, to in ((from_right, 16), (from_left, 6))
+    )
     place = iota((16, LANES), 1)
     compact = jnp.where(place < 16, elements[...], jnp.where(place < 19, right, jnp.where(place < ELEMENTS, left, 1.0)))
     metrics[...] = lanes_of(compact)
@@ -773,15 +777,20 @@
 
 
 def middle_kernel(
-    known, factors, spectrum, inverse, _, stiffness, vectors, bend, upper, lower, diagonals, fixed, lines, *refs
+    known, pair_factors, spectrum, inverse, _, stiffness, vectors, bend, upper, lower, diagonals, fixed, lines,
+    halves, remainder, factors, got, beyond, lam, *refs
 ):
-    sides, (start_faces, residual, local, face_factors, image, payload, beside, sums) = (refs[5:10], refs[:5]), refs[10:]
+    one, refs = refs[:5], refs[5:]
+    (start_faces, residual, local, face_factors, image, payload, beside, sums), two = refs[:8], refs[8:]
+    side_kernel(
+        False, halves, remainder, factors, got, beyond, stiffness, vectors, bend, lam, upper, lower, diagonals, *two
+    )
     solve_kernel(
-        known, spectrum, inverse, sides, stiffness, vectors, bend, upper, lower, diagonals,
+        known, spectrum, inverse, (one, two), stiffness, vectors, bend, upper, lower, diagonals,
         start_faces, residual, local, beside, face_factors, sums,
     )
     image_kernel(
-        local, factors, face_factors, beside, sums, fixed, stiffness, lines, upper, lower, diagonals, image, payload
+        local, pair_factors, face_factors, beside, sums, fixed, stiffness, lines, upper, lower, diagonals, image, payload
     )
 
 
@@ -964,7 +973,7 @@
     per, count = coarse_inverse.shape
     small = per * count <= LANES
     block, wide, face = (ROWS, ROWS, LANES), (ROWS, ROWS, WIDE), (ROWS, LANES)
-    halo = (13, 8, LANES)
+    halo = (11, 8, LANES)
 
     first, second, elements, source, previous = call(
         pack_kernel,
@@ -1004,21 +1013,20 @@
         ready_kernel, [(2, 2, 4, ROWS, LANES), (8, WIDE), (ROWS, WIDE)], [VMEM] * 5, "ready"
     )(factors, stiff, lines, upper, lower)
 
-    sides = []
-    for at, got in ((1, side_b), (0, side_a)):
-        sides += call(
-            functools.partial(side_kernel, at == 0),
-            [face, (2, ROWS, LANES), (2, ROWS, WIDE), (2, ROWS, WIDE), (3, ROWS, WIDE)],
-            [VMEM] * 12,
-            ("side_first", "side_second")[at],
-        )(halves, remainder, factors, got, beyond, stiff, vectors, bend, lam, upper, lower, diagonals)
+    shapes = [face, (2, ROWS, LANES), (2, ROWS, WIDE), (2, ROWS, WIDE), (3, ROWS, WIDE)]
+    one = call(functools.partial(side_kernel, True), shapes, [VMEM] * 12, "side")(
+        halves, remainder, factors, side_a, beyond, stiff, vectors, bend, lam, upper, lower, diagonals
+    )
     start_faces, residual, local, face_factors, image, payload = call(
         middle_kernel,
         [(2, ROWS, LANES), block, wide, (2, 3, ROWS, WIDE), block, (2 * devices, LANES)],
-        [VMEM] * 23,
+        [VMEM] * 24,
         "middle",
-        [pltpu.VMEM((2, ROWS, WIDE), jnp.float32), pltpu.VMEM((8, LANES), jnp.float32)],
-    )(known, pair_factors, spectrum, inverse, waves, stiff, vectors, bend, upper, lower, diagonals, fixed, lines, *sides)
+        [pltpu.VMEM(shape, jnp.float32) for shape in [(2, ROWS, WIDE), (8, LANES)] + shapes],
+    )(
+        known, pair_factors, spectrum, inverse, waves, stiff, vectors, bend, upper, lower, diagonals, fixed, lines,
+        halves, remainder, factors, side_b, beyond, lam, *one,
+    )
     gathered = lax.all_to_all(payload.reshape(devices, 2, LANES), ("gx", "gz"), 0, 0)
     gathered = gathered.reshape(2 * devices, LANES)
 

time: 31.6 us -> 31.4 us (level)
    pallas_call x2 -> x1, Pallas kernels: 1.23 us -> 0.61 us  [body(): call(functools.partial(side_kernel, True), shapes, [VMEM] * 12, 'side')]
    pallas_call x1, Pallas kernels: 1.15 us -> 1.68 us  [body(): call(middle_kernel, [(2, ROWS, LANES), block, wide, (2, 3, ROWS, WIDE), b...]
where the time goes in v9:
time: 31.4 us; the launch traced here: 31.2 us
  blocking collectives  9.5 us (30%)
  starting transfers between devices  8.77 us (28%)
  Pallas kernels  8.52 us (27%)
  waiting for transfers between devices  3.68 us (12%)
  between operations  0.75 us (2%)
    all_to_all x1, blocking collectives, body(): lax.all_to_all(payload.reshape(devices, 2, LANES), ('gx', 'gz'), 0, 0)  9.5 us
    ppermute x2, starting transfers between devices, swap(): two = lax.ppermute(second, axis, odd + [(b, a) for a, b in odd])  5.18 us
    ppermute x2, starting transfers between devices, swap(): one = lax.ppermute(first, axis, [(i, i ^ 1) for i in range(size)])  2.03 us
    pallas_call x1, Pallas kernels, body(): call(functools.partial(prepare_kernel, small), [('half', 4, WIDE, WIDE),...  2 us
    ppermute x2, waiting for transfers between devices, swap(): one = lax.ppermute(first, axis, [(i, i ^ 1) for i in range(size)])  1.9 us
    ppermute x2, waiting for transfers between devices, swap(): two = lax.ppermute(second, axis, odd + [(b, a) for a, b in odd])  1.78 us
    pallas_call x1, Pallas kernels, body(): call(middle_kernel, [(2, ROWS, LANES), block, wide, (2, 3, ROWS, WIDE), b...  1.68 us
    ppermute x1, starting transfers between devices, second_neighbours(): return lax.ppermute(common, axis, [(i, i ^ 2) for i in range(size)])  1.56 us
  transfers between devices with their start and end apart: 5, of which 2 were waited for; matrix products, arithmetic and copies ran while one was open for 0% of the time, Pallas kernels for 11%

profile of v9, /device:TPU:0, one launch (start us, length us, event | category | flops | bytes accessed | tf_op | source)
XLA Modules:
  0.0 31.2 jit_solution(3928876737894960356)
XLA Ops:
  0.6 0.0 copy-start.1
  0.7 1.2 %pack.1 = (f32[11,8,128]{2,1,0:T(8,128)S(1)}, f32[11,8,128]{2,1,0:T(8,128)S(1)}, f32[16,128]{1,0:T(8,128)S(1)}, f32[16,16,128]{2,1,0:T(8,128)S(1)}, f32[16,16,128]{2,1,0:T(8,128)S(1)}) custom-call(f32[16,16,128]{2,1,0:T(8,128)} %source.1, f32[16,16,128]{2,1,0:T(8,128)} %previous.1, f32[3,2,2,16]{3,2,1,0:T(2,128)} %coefficients.1), custom_call_target="tpu_custom_call" | custom-call | tf_op jit(solution)/shard_map/pack/pallas_call | solution.py:978
  1.9 0.0 copy-start.2
  1.9 0.5 %collective-permute-start = (f32[11,8,128]{2,1,0:T(8,128)S(1)}, f32[11,8,128]{2,1,0:T(8,128)S(1)}, u32[]{:S(2)}, u32[]{:S(2)}) collective-permute-start(f32[11,8,128]{2,1,0:T(8,128)S(1)} %get-tuple-element.47), channel_id=1, source_target_pairs={{0,1},{1,0},{2,3},{3,2},{4,5},{5,4},{6,7},{7,6},{8,9},{9,8},{10,11... | collective-permute-start | bytes 135176 | tf_op jit(solution)/shard_map/ppermute | solution.py:953
  2.4 4.7 %collective-permute-start.1 = (f32[11,8,128]{2,1,0:T(8,128)S(1)}, f32[11,8,128]{2,1,0:T(8,128)S(1)}, u32[]{:S(2)}, u32[]{:S(2)}) collective-permute-start(f32[11,8,128]{2,1,0:T(8,128)S(1)} %get-tuple-element.48), channel_id=1, source_target_pairs={{1,2},{3,4},{5,6},{7,0},{2,1},{4,3},{6,5},{0,7},{9,10},{11,12},{13... | collective-permute-start | bytes 135176 | tf_op jit(solution)/shard_map/ppermute | solution.py:954
  7.1 0.0 copy-done
  7.2 0.0 copy-done.4
  7.2 0.0 copy-done.5
  7.2 2.0 %prepare.1 = (bf16[4,256,256]{2,1,0:T(8,128)(2,1)S(1)}, bf16[4,256,128]{2,1,0:T(8,128)(2,1)S(1)}, f32[3,8,8,128]{3,2,1,0:T(8,128)S(1)}, f32[64,128]{1,0:T(8,128)...) custom-call(f32[16,128]{1,0:T(8,128)S(1)} %get-tuple-element.46.elem, ...), custom_call_target="tpu_custom_call" | custom-call | tf_op jit(solution)/shard_map/prepare/pallas_call | solution.py:986
  9.2 0.0 collective-permute-done.first
  9.2 0.0 collective-permute-done.1.second
  9.2 0.7 %start.1 = (f32[16,16,128]{2,1,0:T(8,128)S(1)}, f32[16,16,256]{2,1,0:T(8,128)S(1)}, f32[3,2,16,256]{3,2,1,0:T(8,128)S(1)}, f32[3,16,384]{2,1,0:T(8,128)S(1)}, f3...) custom-call(f32[16,16,128]{2,1,0:T(8,128)S(1)} %get-tuple-element.44.source, ...), custom_call_target="tpu_custom_call" | custom-call | tf_op jit(solution)/shard_map/start/pallas_call | solution.py:997
  9.9 1.6 %collective-permute-start.3 = (f32[112,128]{1,0:T(8,128)S(1)}, f32[112,128]{1,0:T(8,128)S(1)}, u32[]{:S(2)}, u32[]{:S(2)}) collective-permute-start(f32[112,128]{1,0:T(8,128)S(1)} %get-tuple-element.70), channel_id=1, source_target_pairs={{0,16},{8,24},{16,0},{24,8},{1,17},{9,25},{17,1},{25,9},{2,18},{10... | collective-permute-start | bytes 172040 | tf_op jit(solution)/shard_map/ppermute | solution.py:961
  11.5 0.7 %guess.1 = (f32[16,16,128]{2,1,0:T(8,128)S(1)}, f32[8,16,384]{2,1,0:T(8,128)S(1)}, f32[8,16,384]{2,1,0:T(8,128)S(1)}, f32[112,128]{1,0:T(8,128)S(1)}, f32[112,128]{1,0:T(8,128)S(1)}) custom-call(f32[16,16,256]{2,1,0:T(8,128)S(1)} %get-tuple-element.54.remainder, f32[16,256]{1,0:T(8,128)S(1)} %get-tuple-element.55.metrics, ...), custom_call_target="tpu_custom_call" | custom-call | flops 4000000000 | bytes 4000000 | tf_op jit(solution)/shard_map/guess/pallas_call | solution.py:1007
  12.2 1.5 %collective-permute-start.4 = (f32[112,128]{1,0:T(8,128)S(1)}, f32[112,128]{1,0:T(8,128)S(1)}, u32[]{:S(2)}, u32[]{:S(2)}) collective-permute-start(f32[112,128]{1,0:T(8,128)S(1)} %get-tuple-element.71), channel_id=1, source_target_pairs={{0,8},{8,0},{16,24},{24,16},{1,9},{9,1},{17,25},{25,17},{2,10},{10... | collective-permute-start | bytes 172040 | tf_op jit(solution)/shard_map/ppermute | solution.py:953
  13.7 0.5 %collective-permute-start.2 = (f32[112,128]{1,0:T(8,128)S(1)}, f32[112,128]{1,0:T(8,128)S(1)}, u32[]{:S(2)}, u32[]{:S(2)}) collective-permute-start(f32[112,128]{1,0:T(8,128)S(1)} %get-tuple-element.69), channel_id=1, source_target_pairs={{8,16},{24,0},{16,8},{0,24},{9,17},{25,1},{17,9},{1,25},{10,18},{2... | collective-permute-start | bytes 172040 | tf_op jit(solution)/shard_map/ppermute | solution.py:954
  14.2 0.3 ready.1
  14.5 0.0 collective-permute-done.3.beyond
  14.5 1.9 %collective-permute-done.4.got = f32[112,128]{1,0:T(8,128)S(1)} collective-permute-done((f32[112,128]{1,0:T(8,128)S(1)}, f32[112,128]{1,0:T(8,128)S(1)}, u32[]{:S(2)}, u32[]{:S(2)}) %collective-permute-start.4) | collective-permute-done | bytes 57376 | tf_op jit(solution)/shard_map/ppermute | solution.py:953
  16.4 0.6 %side.1 = (f32[16,128]{1,0:T(8,128)S(1)}, f32[2,16,128]{2,1,0:T(8,128)S(1)}, f32[2,16,256]{2,1,0:T(8,128)S(1)}, f32[2,16,256]{2,1,0:T(8,128)S(1)}, f32[3,16,256]{2,1,0:T(8,128)S(1)}) custom-call(f32[2,16,256]{2,1,0:T(8,128)S(1)} %get-tuple-element.68.halves, f32[16,16,256]{2,1,0:T(8,128)S(1)} %get-tuple-element.54.remainder, ...), custom_call_target="tpu_custom_call" | custom-call | tf_op jit(solution)/shard_map/side/pallas_call | solution.py:1017
  17.0 1.8 %collective-permute-done.2.got = f32[112,128]{1,0:T(8,128)S(1)} collective-permute-done((f32[112,128]{1,0:T(8,128)S(1)}, f32[112,128]{1,0:T(8,128)S(1)}, u32[]{:S(2)}, u32[]{:S(2)}) %collective-permute-start.2) | collective-permute-done | bytes 57376 | tf_op jit(solution)/shard_map/ppermute | solution.py:954
  18.8 1.7 %middle.1 = (f32[2,16,128]{2,1,0:T(8,128)S(1)}, f32[16,16,128]{2,1,0:T(8,128)S(1)}, f32[16,16,256]{2,1,0:T(8,128)S(1)}, f32[2,3,16,256]{3,2,1,0:T(8,128)S(1)}, f...) custom-call(f32[16,16,128]{2,1,0:T(8,128)S(1)} %get-tuple-element.60.known, ...), custom_call_target="tpu_custom_call" | custom-call | tf_op jit(solution)/shard_map/middle/pallas_call | solution.py:1020
  20.4 9.5 %all_to_all.5 = f32[32,2,128]{2,1,0:T(2,128)S(1)} all-to-all(f32[32,2,128]{2,1,0:T(2,128)S(1)} %bitcast.3), channel_id=1, replica_groups=mesh['gx'=4,'gz'=8] {'gx','gz'}, dimensions={0} | all-to-all | bytes 65536 | tf_op jit(solution)/shard_map/all_to_all | solution.py:1030
  29.9 1.3 %finish.1 = (f32[16,16,128]{2,1,0:T(8,128)}, f32[16,16,128]{2,1,0:T(8,128)}) custom-call(f32[16,16,128]{2,1,0:T(8,128)S(1)} %get-tuple-element.53.refs_0_, f32[2,16,128]{2,1,0:T(8,128)S(1)} %get-tuple-element.77.refs_1_, f32[16,16,128]{2,1,0:T(8,128)S(1)} %get-tuple-element.78.refs_2_, f32[16,16,256]{2,1,0:T(8,128)S(1)} %get-tuple-element.79.refs_3_, ...), custom_call_target="tpu_custom_call" | custom-call | tf_op jit(solution)/shard_map/finish/pallas_call | solution.py:1053
  (7 shorter events, 0.0 us)
Async XLA Ops:
  0.6 6.5 %copy-start = (s32[8,2,2,16]{3,2,1,0:T(2,128)S(1)}, s32[8,2,2,16]{3,2,1,0:T(2,128)}, u32[]{:S(2)}) copy-start(s32[8,2,2,16]{3,2,1,0:T(2,128)} %labels.1) | copy-start | bytes 6148
  0.6 6.5 %copy-start.1 = (f32[3,8,128]{2,1,0:T(8,128)S(1)}, f32[3,8,128]{2,1,0:T(8,128)}, u32[]{:S(2)}) copy-start(f32[3,8,128]{2,1,0:T(8,128)} %constant.2.clone.tables) | copy-start | bytes 36868
  0.7 6.5 %copy-start.3 = (f32[8,8]{1,0:T(8,128)S(1)}, f32[8,8]{1,0:T(8,128)}, u32[]{:S(2)}) copy-start(f32[8,8]{1,0:T(8,128)} %vectors.1) | copy-start | bytes 772
  1.9 5.3 %copy-start.2 = (f32[8,8]{1,0:T(8,128)S(1)}, f32[8,8]{1,0:T(8,128)}, u32[]{:S(2)}) copy-start(f32[8,8]{1,0:T(8,128)} %stiffness.1) | copy-start | bytes 772
  1.9 7.3 %collective-permute-start = (f32[11,8,128]{2,1,0:T(8,128)S(1)}, f32[11,8,128]{2,1,0:T(8,128)S(1)}, u32[]{:S(2)}, u32[]{:S(2)}) collective-permute-start(f32[11,8,128]{2,1,0:T(8,128)S(1)} %get-tuple-element.47), channel_id=1, source_target_pairs={{0,1},{1,0},{2,3},{3,2},{4,5},{5,4},{6,7},{7,6},{8,9},{9,8},{10,11... | collective-permute-start | bytes 135176 | tf_op jit(solution)/shard_map/ppermute | solution.py:953
  2.4 4.7 %copy-start.4 = (f32[2,64]{1,0:T(2,128)S(1)}, f32[2,64]{1,0:T(2,128)}, u32[]{:S(2)}) copy-start(f32[2,64]{1,0:T(2,128)} %coarse.1) | copy-start | bytes 1540
  2.4 4.7 %copy-start.5 = (f32[8]{0:T(128)S(1)}, f32[8]{0:T(128)}, u32[]{:S(2)}) copy-start(f32[8]{0:T(128)} %eigen.1) | copy-start | bytes 100
  2.4 6.8 %collective-permute-start.1 = (f32[11,8,128]{2,1,0:T(8,128)S(1)}, f32[11,8,128]{2,1,0:T(8,128)S(1)}, u32[]{:S(2)}, u32[]{:S(2)}) collective-permute-start(f32[11,8,128]{2,1,0:T(8,128)S(1)} %get-tuple-element.48), channel_id=1, source_target_pairs={{1,2},{3,4},{5,6},{7,0},{2,1},{4,3},{6,5},{0,7},{9,10},{11,12},{13... | collective-permute-start | bytes 135176 | tf_op jit(solution)/shard_map/ppermute | solution.py:954
  9.9 4.5 %collective-permute-start.3 = (f32[112,128]{1,0:T(8,128)S(1)}, f32[112,128]{1,0:T(8,128)S(1)}, u32[]{:S(2)}, u32[]{:S(2)}) collective-permute-start(f32[112,128]{1,0:T(8,128)S(1)} %get-tuple-element.70), channel_id=1, source_target_pairs={{0,16},{8,24},{16,0},{24,8},{1,17},{9,25},{17,1},{25,9},{2,18},{10... | collective-permute-start | bytes 172040 | tf_op jit(solution)/shard_map/ppermute | solution.py:961
  12.2 4.2 %collective-permute-start.4 = (f32[112,128]{1,0:T(8,128)S(1)}, f32[112,128]{1,0:T(8,128)S(1)}, u32[]{:S(2)}, u32[]{:S(2)}) collective-permute-start(f32[112,128]{1,0:T(8,128)S(1)} %get-tuple-element.71), channel_id=1, source_target_pairs={{0,8},{8,0},{16,24},{24,16},{1,9},{9,1},{17,25},{25,17},{2,10},{10... | collective-permute-start | bytes 172040 | tf_op jit(solution)/shard_map/ppermute | solution.py:953
  13.7 5.1 %collective-permute-start.2 = (f32[112,128]{1,0:T(8,128)S(1)}, f32[112,128]{1,0:T(8,128)S(1)}, u32[]{:S(2)}, u32[]{:S(2)}) collective-permute-start(f32[112,128]{1,0:T(8,128)S(1)} %get-tuple-element.69), channel_id=1, source_target_pairs={{8,16},{24,0},{16,8},{0,24},{9,17},{25,1},{17,9},{1,25},{10,18},{2... | collective-permute-start | bytes 172040 | tf_op jit(solution)/shard_map/ppermute | solution.py:954

commit v10 on v9

--- a/solution.py
+++ b/solution.py
@@ -272,11 +272,16 @@
     return here + jnp.where(((element + 1) >> 3) == group, high, 0.0)
 
 
-def pack_kernel(source, previous, coefficients, first, second, elements, near_source, near_previous, raw, ready):
+def pack_kernel(
+    source, previous, coefficients, eigen, coarse,
+    first, second, elements, near_source, near_previous, near_eigen, near_coarse, raw, ready,
+):
     copies = [
         pltpu.make_async_copy(source, near_source, ready.at[0]),
         pltpu.make_async_copy(previous, near_previous, ready.at[1]),
         pltpu.make_async_copy(coefficients, raw, ready.at[2]),
+        pltpu.make_async_copy(eigen, near_eigen, ready.at[3]),
+        pltpu.make_async_copy(coarse, near_coarse, ready.at[4]),
     ]
     for copy in copies:
         copy.start()
@@ -379,9 +384,10 @@
         chosen = jnp.where(column == near, 0.0, s_turned * k[near : near + 1, :])
         total = jnp.sum(chosen, axis=1, keepdims=True)
         bend[8 * side : 8 * side + 8] = jnp.broadcast_to(total, (8, LANES))
-    values = [eigen[i] for i in range(8)]
-    lam[0] = pick(iota((8, LANES), 0), values)
-    lam[1] = pick(iota((8, LANES), 1) & 7, values)
+    values = eigen[...]
+    total = jnp.sum(jnp.where(row == column, values, 0.0), axis=1, keepdims=True)
+    lam[0] = jnp.broadcast_to(total, (8, LANES))
+    lam[1] = jnp.broadcast_to(dot(values, repeat, ((1,), (1,))), (8, LANES))
     stiff_lines = []
     for at, line in enumerate((ONES, LOW, HIGH)):
         total = jnp.sum(k * pick(column, line), axis=1, keepdims=True)
@@ -422,7 +428,7 @@
     for a in range(2):
         for b in range(3):
             corner, x, z = 4 * a + (b == 2), a, (0, 8, 15)[b]
-            number = labels[corner, x, 0, z].astype(jnp.float32)
+            number = labels[corner, x][0:1, z : z + 1].astype(jnp.float32)
             numbers = jnp.where(place == 8 * (3 * a + b) + 4, number, numbers)
     fixed[16:17] = numbers
     below = jnp.zeros((1, LANES), jnp.float32)
@@ -975,13 +981,15 @@
     block, wide, face = (ROWS, ROWS, LANES), (ROWS, ROWS, WIDE), (ROWS, LANES)
     halo = (11, 8, LANES)
 
-    first, second, elements, source, previous = call(
+    coarse = coarse_inverse if small else coarse_inverse[:, :LANES]
+    operands = (source, previous, coefficients, fdm_values.reshape(1, 8), coarse)
+    first, second, elements, source, previous, eigen, coarse = call(
         pack_kernel,
-        [halo, halo, face, block, block],
-        [FAR] * 3,
+        [halo, halo, face, block, block, (1, 8), coarse.shape],
+        [FAR] * 5,
         "pack",
-        [pltpu.VMEM(coefficients.shape, jnp.float32), pltpu.SemaphoreType.DMA((3,))],
-    )(*(pltpu.with_memory_space_constraint(v, pltpu.HBM) for v in (source, previous, coefficients)))
+        [pltpu.VMEM(coefficients.shape, jnp.float32), pltpu.SemaphoreType.DMA((5,))],
+    )(*(pltpu.with_memory_space_constraint(v, pltpu.HBM) for v in operands))
     first, second = swap(first, second, "gz")
     upper, lower, diagonals, stiff, vectors, bend, lam, lines, fixed, tables = call(
         functools.partial(prepare_kernel, small),
@@ -989,9 +997,9 @@
             ("half", 4, WIDE, WIDE), ("half", 4, WIDE, LANES), (3, 8, 8, LANES),
             (64, LANES), (64, LANES), (16, LANES), (2, 8, LANES), (3, 8, LANES), (24, LANES), (3, 8, LANES),
         ],
-        [VMEM] * 3 + [SMEM] * 2 + [VMEM if small else FAR, VMEM],
+        [VMEM] * 7,
         "prepare",
-    )(elements, stiffness, fdm_vectors, fdm_values, vertex_map, coarse_inverse, jnp.asarray(lane_tables()))
+    )(elements, stiffness, fdm_vectors, eigen, vertex_map, coarse, jnp.asarray(lane_tables()))
 
     message = (FIRST_ROWS + FAR_ROWS + SECOND_ROWS, LANES)
     start, remainder, factors, pair_factors, halves, common, part, metrics = call(

time: 31.4 us -> 31.4 us (level)
  Pallas kernels: 8.52 us -> 7.81 us
  waiting for transfers between devices: 3.68 us -> 4.2 us
    pallas_call x1, Pallas kernels: 2 us -> 1.28 us  [body(): call(functools.partial(prepare_kernel, small), [('half', 4, WIDE, WIDE),...]
    ppermute x2, waiting for transfers between devices: 1.78 us -> 2.29 us  [swap(): two = lax.ppermute(second, axis, odd + [(b, a) for a, b in odd])]
  transfers between devices with their start and end apart: 5 -> 5, of which waited for: 2 -> 3; matrix products, arithmetic and copies ran while one was open for 0% -> 0% of each run, Pallas kernels for 11% -> 9%
where the time goes in v10:
time: 31.4 us; the launch traced here: 31.2 us
  blocking collectives  9.72 us (31%)
  starting transfers between devices  8.77 us (28%)
  Pallas kernels  7.81 us (25%)
  waiting for transfers between devices  4.2 us (13%)
  between operations  0.72 us (2%)
    all_to_all x1, blocking collectives, body(): lax.all_to_all(payload.reshape(devices, 2, LANES), ('gx', 'gz'), 0, 0)  9.72 us
    ppermute x2, starting transfers between devices, swap(): two = lax.ppermute(second, axis, odd + [(b, a) for a, b in odd])  5.19 us
    ppermute x2, waiting for transfers between devices, swap(): two = lax.ppermute(second, axis, odd + [(b, a) for a, b in odd])  2.29 us
    ppermute x2, starting transfers between devices, swap(): one = lax.ppermute(first, axis, [(i, i ^ 1) for i in range(size)])  2.02 us
    ppermute x2, waiting for transfers between devices, swap(): one = lax.ppermute(first, axis, [(i, i ^ 1) for i in range(size)])  1.91 us
    pallas_call x1, Pallas kernels, body(): call(middle_kernel, [(2, ROWS, LANES), block, wide, (2, 3, ROWS, WIDE), b...  1.68 us
    ppermute x1, starting transfers between devices, second_neighbours(): return lax.ppermute(common, axis, [(i, i ^ 2) for i in range(size)])  1.56 us
    pallas_call x1, Pallas kernels, body(): call(kernel, [block, block], [VMEM] * len(operands), 'finish', [pltpu.VME...  1.3 us
  transfers between devices with their start and end apart: 5, of which 3 were waited for; matrix products, arithmetic and copies ran while one was open for 0% of the time, Pallas kernels for 9%

profile of v10, /device:TPU:0, one launch (start us, length us, event | category | flops | bytes accessed | tf_op | source)
XLA Modules:
  0.0 31.2 jit_solution(14668451948987053176)
XLA Ops:
  0.6 0.0 copy-start
  0.6 0.0 copy-start.1
  0.7 1.2 %pack.1 = (f32[11,8,128]{2,1,0:T(8,128)S(1)}, f32[11,8,128]{2,1,0:T(8,128)S(1)}, f32[16,128]{1,0:T(8,128)S(1)}, f32[16,16,128]{2,1,0:T(8,128)S(1)}, f32[16,16,12...) custom-call(f32[16,16,128]{2,1,0:T(8,128)} %source.1, f32[16,16,128]{2,1,0:T(8,128)} %previous.1, ...), custom_call_target="tpu_custom_call" | custom-call | tf_op jit(solution)/shard_map/pack/pallas_call | solution.py:986
  1.9 0.0 copy-start.3
  1.9 0.0 copy-start.2
  1.9 0.5 %collective-permute-start = (f32[11,8,128]{2,1,0:T(8,128)S(1)}, f32[11,8,128]{2,1,0:T(8,128)S(1)}, u32[]{:S(2)}, u32[]{:S(2)}) collective-permute-start(f32[11,8,128]{2,1,0:T(8,128)S(1)} %get-tuple-element.49), channel_id=1, source_target_pairs={{0,1},{1,0},{2,3},{3,2},{4,5},{5,4},{6,7},{7,6},{8,9},{9,8},{10,11... | collective-permute-start | bytes 135176 | tf_op jit(solution)/shard_map/ppermute | solution.py:959
  2.4 4.7 %collective-permute-start.1 = (f32[11,8,128]{2,1,0:T(8,128)S(1)}, f32[11,8,128]{2,1,0:T(8,128)S(1)}, u32[]{:S(2)}, u32[]{:S(2)}) collective-permute-start(f32[11,8,128]{2,1,0:T(8,128)S(1)} %get-tuple-element.50), channel_id=1, source_target_pairs={{1,2},{3,4},{5,6},{7,0},{2,1},{4,3},{6,5},{0,7},{9,10},{11,12},{13... | collective-permute-start | bytes 135176 | tf_op jit(solution)/shard_map/ppermute | solution.py:960
  7.2 0.0 copy-done.2
  7.2 1.3 %prepare.1 = (bf16[4,256,256]{2,1,0:T(8,128)(2,1)S(1)}, bf16[4,256,128]{2,1,0:T(8,128)(2,1)S(1)}, f32[3,8,8,128]{3,2,1,0:T(8,128)S(1)}, f32[64,128]{1,0:T(8,128)...) custom-call(f32[16,128]{1,0:T(8,128)S(1)} %get-tuple-element.48.elem, ...), custom_call_target="tpu_custom_call" | custom-call | tf_op jit(solution)/shard_map/prepare/pallas_call | solution.py:994
  8.5 0.0 collective-permute-done.first
  8.5 0.5 %collective-permute-done.1.second = f32[11,8,128]{2,1,0:T(8,128)S(1)} collective-permute-done((f32[11,8,128]{2,1,0:T(8,128)S(1)}, f32[11,8,128]{2,1,0:T(8,128)S(1)}, u32[]{:S(2)}, u32[]{:S(2)}) %collective-permute-start.1) | collective-permute-done | bytes 45088 | tf_op jit(solution)/shard_map/ppermute | solution.py:960
  9.0 0.7 %start.1 = (f32[16,16,128]{2,1,0:T(8,128)S(1)}, f32[16,16,256]{2,1,0:T(8,128)S(1)}, f32[3,2,16,256]{3,2,1,0:T(8,128)S(1)}, f32[3,16,384]{2,1,0:T(8,128)S(1)}, f3...) custom-call(f32[16,16,128]{2,1,0:T(8,128)S(1)} %get-tuple-element.46.source, ...), custom_call_target="tpu_custom_call" | custom-call | tf_op jit(solution)/shard_map/start/pallas_call | solution.py:1005
  9.7 1.6 %collective-permute-start.3 = (f32[112,128]{1,0:T(8,128)S(1)}, f32[112,128]{1,0:T(8,128)S(1)}, u32[]{:S(2)}, u32[]{:S(2)}) collective-permute-start(f32[112,128]{1,0:T(8,128)S(1)} %get-tuple-element.74), channel_id=1, source_target_pairs={{0,16},{8,24},{16,0},{24,8},{1,17},{9,25},{17,1},{25,9},{2,18},{10... | collective-permute-start | bytes 172040 | tf_op jit(solution)/shard_map/ppermute | solution.py:967
  11.3 0.7 %guess.1 = (f32[16,16,128]{2,1,0:T(8,128)S(1)}, f32[8,16,384]{2,1,0:T(8,128)S(1)}, f32[8,16,384]{2,1,0:T(8,128)S(1)}, f32[112,128]{1,0:T(8,128)S(1)}, f32[112,128]{1,0:T(8,128)S(1)}) custom-call(f32[16,16,256]{2,1,0:T(8,128)S(1)} %get-tuple-element.58.remainder, f32[16,256]{1,0:T(8,128)S(1)} %get-tuple-element.59.metrics, ...), custom_call_target="tpu_custom_call" | custom-call | flops 4000000000 | bytes 4000000 | tf_op jit(solution)/shard_map/guess/pallas_call | solution.py:1015
  12.0 1.5 %collective-permute-start.4 = (f32[112,128]{1,0:T(8,128)S(1)}, f32[112,128]{1,0:T(8,128)S(1)}, u32[]{:S(2)}, u32[]{:S(2)}) collective-permute-start(f32[112,128]{1,0:T(8,128)S(1)} %get-tuple-element.75), channel_id=1, source_target_pairs={{0,8},{8,0},{16,24},{24,16},{1,9},{9,1},{17,25},{25,17},{2,10},{10... | collective-permute-start | bytes 172040 | tf_op jit(solution)/shard_map/ppermute | solution.py:959
  13.5 0.5 %collective-permute-start.2 = (f32[112,128]{1,0:T(8,128)S(1)}, f32[112,128]{1,0:T(8,128)S(1)}, u32[]{:S(2)}, u32[]{:S(2)}) collective-permute-start(f32[112,128]{1,0:T(8,128)S(1)} %get-tuple-element.73), channel_id=1, source_target_pairs={{8,16},{24,0},{16,8},{0,24},{9,17},{25,1},{17,9},{1,25},{10,18},{2... | collective-permute-start | bytes 172040 | tf_op jit(solution)/shard_map/ppermute | solution.py:960
  13.9 0.3 ready.1
  14.2 0.0 collective-permute-done.3.beyond
  14.2 1.9 %collective-permute-done.4.got = f32[112,128]{1,0:T(8,128)S(1)} collective-permute-done((f32[112,128]{1,0:T(8,128)S(1)}, f32[112,128]{1,0:T(8,128)S(1)}, u32[]{:S(2)}, u32[]{:S(2)}) %collective-permute-start.4) | collective-permute-done | bytes 57376 | tf_op jit(solution)/shard_map/ppermute | solution.py:959
  16.1 0.6 %side.1 = (f32[16,128]{1,0:T(8,128)S(1)}, f32[2,16,128]{2,1,0:T(8,128)S(1)}, f32[2,16,256]{2,1,0:T(8,128)S(1)}, f32[2,16,256]{2,1,0:T(8,128)S(1)}, f32[3,16,256]{2,1,0:T(8,128)S(1)}) custom-call(f32[2,16,256]{2,1,0:T(8,128)S(1)} %get-tuple-element.72.halves, f32[16,16,256]{2,1,0:T(8,128)S(1)} %get-tuple-element.58.remainder, ...), custom_call_target="tpu_custom_call" | custom-call | tf_op jit(solution)/shard_map/side/pallas_call | solution.py:1025
  16.8 1.8 %collective-permute-done.2.got = f32[112,128]{1,0:T(8,128)S(1)} collective-permute-done((f32[112,128]{1,0:T(8,128)S(1)}, f32[112,128]{1,0:T(8,128)S(1)}, u32[]{:S(2)}, u32[]{:S(2)}) %collective-permute-start.2) | collective-permute-done | bytes 57376 | tf_op jit(solution)/shard_map/ppermute | solution.py:960
  18.5 1.7 %middle.1 = (f32[2,16,128]{2,1,0:T(8,128)S(1)}, f32[16,16,128]{2,1,0:T(8,128)S(1)}, f32[16,16,256]{2,1,0:T(8,128)S(1)}, f32[2,3,16,256]{3,2,1,0:T(8,128)S(1)}, f...) custom-call(f32[16,16,128]{2,1,0:T(8,128)S(1)} %get-tuple-element.64.known, ...), custom_call_target="tpu_custom_call" | custom-call | tf_op jit(solution)/shard_map/middle/pallas_call | solution.py:1028
  20.2 9.7 %all_to_all.5 = f32[32,2,128]{2,1,0:T(2,128)S(1)} all-to-all(f32[32,2,128]{2,1,0:T(2,128)S(1)} %bitcast.4), channel_id=1, replica_groups=mesh['gx'=4,'gz'=8] {'gx','gz'}, dimensions={0} | all-to-all | bytes 65536 | tf_op jit(solution)/shard_map/all_to_all | solution.py:1038
  29.9 1.3 %finish.1 = (f32[16,16,128]{2,1,0:T(8,128)}, f32[16,16,128]{2,1,0:T(8,128)}) custom-call(f32[16,16,128]{2,1,0:T(8,128)S(1)} %get-tuple-element.57.refs_0_, f32[2,16,128]{2,1,0:T(8,128)S(1)} %get-tuple-element.81.refs_1_, f32[16,16,128]{2,1,0:T(8,128)S(1)} %get-tuple-element.82.refs_2_, f32[16,16,256]{2,1,0:T(8,128)S(1)} %get-tuple-element.83.refs_3_, ...), custom_call_target="tpu_custom_call" | custom-call | tf_op jit(solution)/shard_map/finish/pallas_call | solution.py:1061
  (3 shorter events, 0.0 us)
Async XLA Ops:
  0.6 6.5 %copy-start = (s32[8,2,2,16]{3,2,1,0:T(2,128)S(1)}, s32[8,2,2,16]{3,2,1,0:T(2,128)}, u32[]{:S(2)}) copy-start(s32[8,2,2,16]{3,2,1,0:T(2,128)} %labels.1) | copy-start | bytes 6148
  0.6 6.5 %copy-start.1 = (f32[3,8,128]{2,1,0:T(8,128)S(1)}, f32[3,8,128]{2,1,0:T(8,128)}, u32[]{:S(2)}) copy-start(f32[3,8,128]{2,1,0:T(8,128)} %constant.2.clone.tables) | copy-start | bytes 36868
  1.9 5.3 %copy-start.3 = (f32[8,8]{1,0:T(8,128)S(1)}, f32[8,8]{1,0:T(8,128)}, u32[]{:S(2)}) copy-start(f32[8,8]{1,0:T(8,128)} %vectors.1) | copy-start | bytes 772
  1.9 5.3 %copy-start.2 = (f32[8,8]{1,0:T(8,128)S(1)}, f32[8,8]{1,0:T(8,128)}, u32[]{:S(2)}) copy-start(f32[8,8]{1,0:T(8,128)} %stiffness.1) | copy-start | bytes 772
  1.9 6.5 %collective-permute-start = (f32[11,8,128]{2,1,0:T(8,128)S(1)}, f32[11,8,128]{2,1,0:T(8,128)S(1)}, u32[]{:S(2)}, u32[]{:S(2)}) collective-permute-start(f32[11,8,128]{2,1,0:T(8,128)S(1)} %get-tuple-element.49), channel_id=1, source_target_pairs={{0,1},{1,0},{2,3},{3,2},{4,5},{5,4},{6,7},{7,6},{8,9},{9,8},{10,11... | collective-permute-start | bytes 135176 | tf_op jit(solution)/shard_map/ppermute | solution.py:959
  2.4 6.5 %collective-permute-start.1 = (f32[11,8,128]{2,1,0:T(8,128)S(1)}, f32[11,8,128]{2,1,0:T(8,128)S(1)}, u32[]{:S(2)}, u32[]{:S(2)}) collective-permute-start(f32[11,8,128]{2,1,0:T(8,128)S(1)} %get-tuple-element.50), channel_id=1, source_target_pairs={{1,2},{3,4},{5,6},{7,0},{2,1},{4,3},{6,5},{0,7},{9,10},{11,12},{13... | collective-permute-start | bytes 135176 | tf_op jit(solution)/shard_map/ppermute | solution.py:960
  9.7 4.5 %collective-permute-start.3 = (f32[112,128]{1,0:T(8,128)S(1)}, f32[112,128]{1,0:T(8,128)S(1)}, u32[]{:S(2)}, u32[]{:S(2)}) collective-permute-start(f32[112,128]{1,0:T(8,128)S(1)} %get-tuple-element.74), channel_id=1, source_target_pairs={{0,16},{8,24},{16,0},{24,8},{1,17},{9,25},{17,1},{25,9},{2,18},{10... | collective-permute-start | bytes 172040 | tf_op jit(solution)/shard_map/ppermute | solution.py:967
  12.0 4.2 %collective-permute-start.4 = (f32[112,128]{1,0:T(8,128)S(1)}, f32[112,128]{1,0:T(8,128)S(1)}, u32[]{:S(2)}, u32[]{:S(2)}) collective-permute-start(f32[112,128]{1,0:T(8,128)S(1)} %get-tuple-element.75), channel_id=1, source_target_pairs={{0,8},{8,0},{16,24},{24,16},{1,9},{9,1},{17,25},{25,17},{2,10},{10... | collective-permute-start | bytes 172040 | tf_op jit(solution)/shard_map/ppermute | solution.py:959
  13.5 5.1 %collective-permute-start.2 = (f32[112,128]{1,0:T(8,128)S(1)}, f32[112,128]{1,0:T(8,128)S(1)}, u32[]{:S(2)}, u32[]{:S(2)}) collective-permute-start(f32[112,128]{1,0:T(8,128)S(1)} %get-tuple-element.73), channel_id=1, source_target_pairs={{8,16},{24,0},{16,8},{0,24},{9,17},{25,1},{17,9},{1,25},{10,18},{2... | collective-permute-start | bytes 172040 | tf_op jit(solution)/shard_map/ppermute | solution.py:960

commit v11 on v10

--- a/solution.py
+++ b/solution.py
@@ -824,8 +824,9 @@
 def final_kernel(
     devices, spans, count, per,
     start, start_faces, residual, local, image, pieces, face_factors, waves, stiff_keep, lines, tables,
-    gathered, given, new_solution, new_residual, values,
+    arrived, given, new_solution, new_residual, values, gathered,
 ):
+    gathered[: 2 * devices] = arrived[...]
     rows = gathered[pl.ds(0, devices, stride=2), :]
     if given is None:
         spot = iota((devices, count), 1)
@@ -1057,8 +1058,9 @@
         mine = jnp.dot(coarse_inverse, rhs, precision=EXACT)
         coarse = lax.all_gather(mine, ("gx", "gz"), axis=0, tiled=True)
         operands.append(jnp.pad(coarse[labels], ((0, 0), (0, LANES - 6))))
+    scratch = [pltpu.VMEM((devices, LANES), jnp.float32), pltpu.VMEM((2 * devices + 8, LANES), jnp.float32)]
     return tuple(
-        call(kernel, [block, block], [VMEM] * len(operands), "finish", [pltpu.VMEM((devices, LANES), jnp.float32)])(
+        call(kernel, [block, block], [VMEM] * len(operands), "finish", scratch)(
             *operands
         )
     )

time: 31.4 us -> 31.4 us (level)
  no operation moved by 1% of the time
where the time goes in v11:
time: 31.4 us; the launch traced here: 31.2 us
  blocking collectives  9.72 us (31%)
  starting transfers between devices  8.77 us (28%)
  Pallas kernels  7.81 us (25%)
  waiting for transfers between devices  4.2 us (13%)
  between operations  0.72 us (2%)
    all_to_all x1, blocking collectives, body(): lax.all_to_all(payload.reshape(devices, 2, LANES), ('gx', 'gz'), 0, 0)  9.72 us
    ppermute x2, starting transfers between devices, swap(): two = lax.ppermute(second, axis, odd + [(b, a) for a, b in odd])  5.19 us
    ppermute x2, waiting for transfers between devices, swap(): two = lax.ppermute(second, axis, odd + [(b, a) for a, b in odd])  2.29 us
    ppermute x2, starting transfers between devices, swap(): one = lax.ppermute(first, axis, [(i, i ^ 1) for i in range(size)])  2.02 us
    ppermute x2, waiting for transfers between devices, swap(): one = lax.ppermute(first, axis, [(i, i ^ 1) for i in range(size)])  1.91 us
    pallas_call x1, Pallas kernels, body(): call(middle_kernel, [(2, ROWS, LANES), block, wide, (2, 3, ROWS, WIDE), b...  1.68 us
    ppermute x1, starting transfers between devices, second_neighbours(): return lax.ppermute(common, axis, [(i, i ^ 2) for i in range(size)])  1.56 us
    pallas_call x1, Pallas kernels, body(): call(kernel, [block, block], [VMEM] * len(operands), 'finish', scratch)  1.3 us
  transfers between devices with their start and end apart: 5, of which 3 were waited for; matrix products, arithmetic and copies ran while one was open for 0% of the time, Pallas kernels for 9%

profile of v11, /device:TPU:0, one launch (start us, length us, event | category | flops | bytes accessed | tf_op | source)
XLA Modules:
  0.0 31.2 jit_solution(7279529080205691591)
XLA Ops:
  0.6 0.0 copy-start
  0.6 0.0 copy-start.1
  0.7 1.2 %pack.1 = (f32[11,8,128]{2,1,0:T(8,128)S(1)}, f32[11,8,128]{2,1,0:T(8,128)S(1)}, f32[16,128]{1,0:T(8,128)S(1)}, f32[16,16,128]{2,1,0:T(8,128)S(1)}, f32[16,16,12...) custom-call(f32[16,16,128]{2,1,0:T(8,128)} %source.1, f32[16,16,128]{2,1,0:T(8,128)} %previous.1, ...), custom_call_target="tpu_custom_call" | custom-call | tf_op jit(solution)/shard_map/pack/pallas_call | solution.py:987
  1.9 0.0 copy-start.3
  1.9 0.0 copy-start.2
  1.9 0.5 %collective-permute-start = (f32[11,8,128]{2,1,0:T(8,128)S(1)}, f32[11,8,128]{2,1,0:T(8,128)S(1)}, u32[]{:S(2)}, u32[]{:S(2)}) collective-permute-start(f32[11,8,128]{2,1,0:T(8,128)S(1)} %get-tuple-element.49), channel_id=1, source_target_pairs={{0,1},{1,0},{2,3},{3,2},{4,5},{5,4},{6,7},{7,6},{8,9},{9,8},{10,11... | collective-permute-start | bytes 135176 | tf_op jit(solution)/shard_map/ppermute | solution.py:960
  2.4 4.7 %collective-permute-start.1 = (f32[11,8,128]{2,1,0:T(8,128)S(1)}, f32[11,8,128]{2,1,0:T(8,128)S(1)}, u32[]{:S(2)}, u32[]{:S(2)}) collective-permute-start(f32[11,8,128]{2,1,0:T(8,128)S(1)} %get-tuple-element.50), channel_id=1, source_target_pairs={{1,2},{3,4},{5,6},{7,0},{2,1},{4,3},{6,5},{0,7},{9,10},{11,12},{13... | collective-permute-start | bytes 135176 | tf_op jit(solution)/shard_map/ppermute | solution.py:961
  7.2 0.0 copy-done.2
  7.2 1.3 %prepare.1 = (bf16[4,256,256]{2,1,0:T(8,128)(2,1)S(1)}, bf16[4,256,128]{2,1,0:T(8,128)(2,1)S(1)}, f32[3,8,8,128]{3,2,1,0:T(8,128)S(1)}, f32[64,128]{1,0:T(8,128)...) custom-call(f32[16,128]{1,0:T(8,128)S(1)} %get-tuple-element.48.elem, ...), custom_call_target="tpu_custom_call" | custom-call | tf_op jit(solution)/shard_map/prepare/pallas_call | solution.py:995
  8.5 0.0 collective-permute-done.first
  8.5 0.5 %collective-permute-done.1.second = f32[11,8,128]{2,1,0:T(8,128)S(1)} collective-permute-done((f32[11,8,128]{2,1,0:T(8,128)S(1)}, f32[11,8,128]{2,1,0:T(8,128)S(1)}, u32[]{:S(2)}, u32[]{:S(2)}) %collective-permute-start.1) | collective-permute-done | bytes 45088 | tf_op jit(solution)/shard_map/ppermute | solution.py:961
  9.0 0.7 %start.1 = (f32[16,16,128]{2,1,0:T(8,128)S(1)}, f32[16,16,256]{2,1,0:T(8,128)S(1)}, f32[3,2,16,256]{3,2,1,0:T(8,128)S(1)}, f32[3,16,384]{2,1,0:T(8,128)S(1)}, f3...) custom-call(f32[16,16,128]{2,1,0:T(8,128)S(1)} %get-tuple-element.46.source, ...), custom_call_target="tpu_custom_call" | custom-call | tf_op jit(solution)/shard_map/start/pallas_call | solution.py:1006
  9.7 1.6 %collective-permute-start.3 = (f32[112,128]{1,0:T(8,128)S(1)}, f32[112,128]{1,0:T(8,128)S(1)}, u32[]{:S(2)}, u32[]{:S(2)}) collective-permute-start(f32[112,128]{1,0:T(8,128)S(1)} %get-tuple-element.74), channel_id=1, source_target_pairs={{0,16},{8,24},{16,0},{24,8},{1,17},{9,25},{17,1},{25,9},{2,18},{10... | collective-permute-start | bytes 172040 | tf_op jit(solution)/shard_map/ppermute | solution.py:968
  11.3 0.7 %guess.1 = (f32[16,16,128]{2,1,0:T(8,128)S(1)}, f32[8,16,384]{2,1,0:T(8,128)S(1)}, f32[8,16,384]{2,1,0:T(8,128)S(1)}, f32[112,128]{1,0:T(8,128)S(1)}, f32[112,128]{1,0:T(8,128)S(1)}) custom-call(f32[16,16,256]{2,1,0:T(8,128)S(1)} %get-tuple-element.58.remainder, f32[16,256]{1,0:T(8,128)S(1)} %get-tuple-element.59.metrics, ...), custom_call_target="tpu_custom_call" | custom-call | flops 4000000000 | bytes 4000000 | tf_op jit(solution)/shard_map/guess/pallas_call | solution.py:1016
  12.0 1.5 %collective-permute-start.4 = (f32[112,128]{1,0:T(8,128)S(1)}, f32[112,128]{1,0:T(8,128)S(1)}, u32[]{:S(2)}, u32[]{:S(2)}) collective-permute-start(f32[112,128]{1,0:T(8,128)S(1)} %get-tuple-element.75), channel_id=1, source_target_pairs={{0,8},{8,0},{16,24},{24,16},{1,9},{9,1},{17,25},{25,17},{2,10},{10... | collective-permute-start | bytes 172040 | tf_op jit(solution)/shard_map/ppermute | solution.py:960
  13.5 0.5 %collective-permute-start.2 = (f32[112,128]{1,0:T(8,128)S(1)}, f32[112,128]{1,0:T(8,128)S(1)}, u32[]{:S(2)}, u32[]{:S(2)}) collective-permute-start(f32[112,128]{1,0:T(8,128)S(1)} %get-tuple-element.73), channel_id=1, source_target_pairs={{8,16},{24,0},{16,8},{0,24},{9,17},{25,1},{17,9},{1,25},{10,18},{2... | collective-permute-start | bytes 172040 | tf_op jit(solution)/shard_map/ppermute | solution.py:961
  13.9 0.3 ready.1
  14.2 0.0 collective-permute-done.3.beyond
  14.2 1.9 %collective-permute-done.4.got = f32[112,128]{1,0:T(8,128)S(1)} collective-permute-done((f32[112,128]{1,0:T(8,128)S(1)}, f32[112,128]{1,0:T(8,128)S(1)}, u32[]{:S(2)}, u32[]{:S(2)}) %collective-permute-start.4) | collective-permute-done | bytes 57376 | tf_op jit(solution)/shard_map/ppermute | solution.py:960
  16.1 0.6 %side.1 = (f32[16,128]{1,0:T(8,128)S(1)}, f32[2,16,128]{2,1,0:T(8,128)S(1)}, f32[2,16,256]{2,1,0:T(8,128)S(1)}, f32[2,16,256]{2,1,0:T(8,128)S(1)}, f32[3,16,256]{2,1,0:T(8,128)S(1)}) custom-call(f32[2,16,256]{2,1,0:T(8,128)S(1)} %get-tuple-element.72.halves, f32[16,16,256]{2,1,0:T(8,128)S(1)} %get-tuple-element.58.remainder, ...), custom_call_target="tpu_custom_call" | custom-call | tf_op jit(solution)/shard_map/side/pallas_call | solution.py:1026
  16.8 1.8 %collective-permute-done.2.got = f32[112,128]{1,0:T(8,128)S(1)} collective-permute-done((f32[112,128]{1,0:T(8,128)S(1)}, f32[112,128]{1,0:T(8,128)S(1)}, u32[]{:S(2)}, u32[]{:S(2)}) %collective-permute-start.2) | collective-permute-done | bytes 57376 | tf_op jit(solution)/shard_map/ppermute | solution.py:961
  18.5 1.7 %middle.1 = (f32[2,16,128]{2,1,0:T(8,128)S(1)}, f32[16,16,128]{2,1,0:T(8,128)S(1)}, f32[16,16,256]{2,1,0:T(8,128)S(1)}, f32[2,3,16,256]{3,2,1,0:T(8,128)S(1)}, f...) custom-call(f32[16,16,128]{2,1,0:T(8,128)S(1)} %get-tuple-element.64.known, ...), custom_call_target="tpu_custom_call" | custom-call | tf_op jit(solution)/shard_map/middle/pallas_call | solution.py:1029
  20.2 9.7 %all_to_all.5 = f32[32,2,128]{2,1,0:T(2,128)S(1)} all-to-all(f32[32,2,128]{2,1,0:T(2,128)S(1)} %bitcast.4), channel_id=1, replica_groups=mesh['gx'=4,'gz'=8] {'gx','gz'}, dimensions={0} | all-to-all | bytes 65536 | tf_op jit(solution)/shard_map/all_to_all | solution.py:1039
  29.9 1.3 %finish.1 = (f32[16,16,128]{2,1,0:T(8,128)}, f32[16,16,128]{2,1,0:T(8,128)}) custom-call(f32[16,16,128]{2,1,0:T(8,128)S(1)} %get-tuple-element.57.refs_0_, f32[2,16,128]{2,1,0:T(8,128)S(1)} %get-tuple-element.81.refs_1_, f32[16,16,128]{2,1,0:T(8,128)S(1)} %get-tuple-element.82.refs_2_, f32[16,16,256]{2,1,0:T(8,128)S(1)} %get-tuple-element.83.refs_3_, ...), custom_call_target="tpu_custom_call" | custom-call | tf_op jit(solution)/shard_map/finish/pallas_call | solution.py:1063
  (3 shorter events, 0.0 us)
Async XLA Ops:
  0.6 6.5 %copy-start = (s32[8,2,2,16]{3,2,1,0:T(2,128)S(1)}, s32[8,2,2,16]{3,2,1,0:T(2,128)}, u32[]{:S(2)}) copy-start(s32[8,2,2,16]{3,2,1,0:T(2,128)} %labels.1) | copy-start | bytes 6148
  0.6 6.5 %copy-start.1 = (f32[3,8,128]{2,1,0:T(8,128)S(1)}, f32[3,8,128]{2,1,0:T(8,128)}, u32[]{:S(2)}) copy-start(f32[3,8,128]{2,1,0:T(8,128)} %constant.2.clone.tables) | copy-start | bytes 36868
  1.9 5.3 %copy-start.3 = (f32[8,8]{1,0:T(8,128)S(1)}, f32[8,8]{1,0:T(8,128)}, u32[]{:S(2)}) copy-start(f32[8,8]{1,0:T(8,128)} %vectors.1) | copy-start | bytes 772
  1.9 5.3 %copy-start.2 = (f32[8,8]{1,0:T(8,128)S(1)}, f32[8,8]{1,0:T(8,128)}, u32[]{:S(2)}) copy-start(f32[8,8]{1,0:T(8,128)} %stiffness.1) | copy-start | bytes 772
  1.9 6.5 %collective-permute-start = (f32[11,8,128]{2,1,0:T(8,128)S(1)}, f32[11,8,128]{2,1,0:T(8,128)S(1)}, u32[]{:S(2)}, u32[]{:S(2)}) collective-permute-start(f32[11,8,128]{2,1,0:T(8,128)S(1)} %get-tuple-element.49), channel_id=1, source_target_pairs={{0,1},{1,0},{2,3},{3,2},{4,5},{5,4},{6,7},{7,6},{8,9},{9,8},{10,11... | collective-permute-start | bytes 135176 | tf_op jit(solution)/shard_map/ppermute | solution.py:960
  2.4 6.5 %collective-permute-start.1 = (f32[11,8,128]{2,1,0:T(8,128)S(1)}, f32[11,8,128]{2,1,0:T(8,128)S(1)}, u32[]{:S(2)}, u32[]{:S(2)}) collective-permute-start(f32[11,8,128]{2,1,0:T(8,128)S(1)} %get-tuple-element.50), channel_id=1, source_target_pairs={{1,2},{3,4},{5,6},{7,0},{2,1},{4,3},{6,5},{0,7},{9,10},{11,12},{13... | collective-permute-start | bytes 135176 | tf_op jit(solution)/shard_map/ppermute | solution.py:961
  9.7 4.5 %collective-permute-start.3 = (f32[112,128]{1,0:T(8,128)S(1)}, f32[112,128]{1,0:T(8,128)S(1)}, u32[]{:S(2)}, u32[]{:S(2)}) collective-permute-start(f32[112,128]{1,0:T(8,128)S(1)} %get-tuple-element.74), channel_id=1, source_target_pairs={{0,16},{8,24},{16,0},{24,8},{1,17},{9,25},{17,1},{25,9},{2,18},{10... | collective-permute-start | bytes 172040 | tf_op jit(solution)/shard_map/ppermute | solution.py:968
  12.0 4.2 %collective-permute-start.4 = (f32[112,128]{1,0:T(8,128)S(1)}, f32[112,128]{1,0:T(8,128)S(1)}, u32[]{:S(2)}, u32[]{:S(2)}) collective-permute-start(f32[112,128]{1,0:T(8,128)S(1)} %get-tuple-element.75), channel_id=1, source_target_pairs={{0,8},{8,0},{16,24},{24,16},{1,9},{9,1},{17,25},{25,17},{2,10},{10... | collective-permute-start | bytes 172040 | tf_op jit(solution)/shard_map/ppermute | solution.py:960
  13.5 5.1 %collective-permute-start.2 = (f32[112,128]{1,0:T(8,128)S(1)}, f32[112,128]{1,0:T(8,128)S(1)}, u32[]{:S(2)}, u32[]{:S(2)}) collective-permute-start(f32[112,128]{1,0:T(8,128)S(1)} %get-tuple-element.73), channel_id=1, source_target_pairs={{8,16},{24,0},{16,8},{0,24},{9,17},{25,1},{17,9},{1,25},{10,18},{2... | collective-permute-start | bytes 172040 | tf_op jit(solution)/shard_map/ppermute | solution.py:961

commit v12 on v11

--- a/solution.py
+++ b/solution.py
@@ -102,6 +102,19 @@
 
     def assemble(self, v):
         return self.pair(v) * self.keep
+
+    def assemble_own(self, v):
+        v = self.pair_y(v)
+        mine, halo = v[:, :, :LANES], v[:, :, LANES:]
+        lane = iota((1, 1, LANES), 2)
+        edge, last, keep = (mask[:, :, :LANES] for mask in (self.edge, self.last, self.keep))
+
+        def turned(mixed, lanes):
+            return pltpu.roll(mixed.reshape(16, LANES), lanes, 1).reshape(2, 8, LANES)
+
+        after = turned(jnp.where(lane == 0, halo, mine), LANES - 1)
+        before = turned(jnp.where(lane == LANES - 1, halo, mine), 1)
+        return (mine + jnp.where(edge, jnp.where(last, after, before), 0.0)) * keep
 
 
 def solid(v):
@@ -769,7 +782,7 @@
         applied[x] = applied[x] + other
     applied = join_middle(applied)
     for x in range(ROWS):
-        image[x] = solid(own(geo.assemble(applied[x])))
+        image[x] = solid(geo.assemble_own(applied[x]))
     zero = jnp.zeros((1, LANES), jnp.float32)
     table = jnp.concatenate(
         [sums[0:2], extra[0], extra[1], fixed[0:9], sums[2:3], extra[2], zero], axis=0
@@ -912,7 +925,7 @@
         fx, fy, fz = (split(face_factors[side, c]) for c in range(3))
         value = fx * geo.keep * stiff_x[None]
         value = value + WEIGHTS[0] * (fy * split(stiff_keep[...]) * plain[None] + fz * geo.keep * turned[None])
-        return solid(own(geo.assemble(value)))
+        return solid(geo.assemble_own(value))
 
     wave_near, wave_right = line(near, 0), line(right, 0)
     across = wide_stiff(1, 7) * line(left, 0) + wide_stiff(2, 7) * wave_near

time: 31.4 us -> 31.4 us (level)
  no operation moved by 1% of the time
where the time goes in v12:
time: 31.4 us; the launch traced here: 31.2 us
  blocking collectives  9.72 us (31%)
  starting transfers between devices  8.77 us (28%)
  Pallas kernels  7.79 us (25%)
  waiting for transfers between devices  4.2 us (13%)
  between operations  0.72 us (2%)
    all_to_all x1, blocking collectives, body(): lax.all_to_all(payload.reshape(devices, 2, LANES), ('gx', 'gz'), 0, 0)  9.72 us
    ppermute x2, starting transfers between devices, swap(): two = lax.ppermute(second, axis, odd + [(b, a) for a, b in odd])  5.19 us
    ppermute x2, waiting for transfers between devices, swap(): two = lax.ppermute(second, axis, odd + [(b, a) for a, b in odd])  2.29 us
    ppermute x2, starting transfers between devices, swap(): one = lax.ppermute(first, axis, [(i, i ^ 1) for i in range(size)])  2.02 us
    ppermute x2, waiting for transfers between devices, swap(): one = lax.ppermute(first, axis, [(i, i ^ 1) for i in range(size)])  1.91 us
    pallas_call x1, Pallas kernels, body(): call(middle_kernel, [(2, ROWS, LANES), block, wide, (2, 3, ROWS, WIDE), b...  1.66 us
    ppermute x1, starting transfers between devices, second_neighbours(): return lax.ppermute(common, axis, [(i, i ^ 2) for i in range(size)])  1.56 us
    pallas_call x1, Pallas kernels, body(): call(kernel, [block, block], [VMEM] * len(operands), 'finish', scratch)  1.3 us
  transfers between devices with their start and end apart: 5, of which 3 were waited for; matrix products, arithmetic and copies ran while one was open for 0% of the time, Pallas kernels for 9%

profile of v12, /device:TPU:0, one launch (start us, length us, event | category | flops | bytes accessed | tf_op | source)
XLA Modules:
  0.0 31.2 jit_solution(1688951165875932052)
XLA Ops:
  0.6 0.0 copy-start
  0.6 0.0 copy-start.1
  0.7 1.2 %pack.1 = (f32[11,8,128]{2,1,0:T(8,128)S(1)}, f32[11,8,128]{2,1,0:T(8,128)S(1)}, f32[16,128]{1,0:T(8,128)S(1)}, f32[16,16,128]{2,1,0:T(8,128)S(1)}, f32[16,16,12...) custom-call(f32[16,16,128]{2,1,0:T(8,128)} %source.1, f32[16,16,128]{2,1,0:T(8,128)} %previous.1, ...), custom_call_target="tpu_custom_call" | custom-call | tf_op jit(solution)/shard_map/pack/pallas_call | solution.py:1000
  1.9 0.0 copy-start.3
  1.9 0.0 copy-start.2
  1.9 0.5 %collective-permute-start = (f32[11,8,128]{2,1,0:T(8,128)S(1)}, f32[11,8,128]{2,1,0:T(8,128)S(1)}, u32[]{:S(2)}, u32[]{:S(2)}) collective-permute-start(f32[11,8,128]{2,1,0:T(8,128)S(1)} %get-tuple-element.49), channel_id=1, source_target_pairs={{0,1},{1,0},{2,3},{3,2},{4,5},{5,4},{6,7},{7,6},{8,9},{9,8},{10,11... | collective-permute-start | bytes 135176 | tf_op jit(solution)/shard_map/ppermute | solution.py:973
  2.4 4.7 %collective-permute-start.1 = (f32[11,8,128]{2,1,0:T(8,128)S(1)}, f32[11,8,128]{2,1,0:T(8,128)S(1)}, u32[]{:S(2)}, u32[]{:S(2)}) collective-permute-start(f32[11,8,128]{2,1,0:T(8,128)S(1)} %get-tuple-element.50), channel_id=1, source_target_pairs={{1,2},{3,4},{5,6},{7,0},{2,1},{4,3},{6,5},{0,7},{9,10},{11,12},{13... | collective-permute-start | bytes 135176 | tf_op jit(solution)/shard_map/ppermute | solution.py:974
  7.2 0.0 copy-done.2
  7.2 1.3 %prepare.1 = (bf16[4,256,256]{2,1,0:T(8,128)(2,1)S(1)}, bf16[4,256,128]{2,1,0:T(8,128)(2,1)S(1)}, f32[3,8,8,128]{3,2,1,0:T(8,128)S(1)}, f32[64,128]{1,0:T(8,128)...) custom-call(f32[16,128]{1,0:T(8,128)S(1)} %get-tuple-element.48.elem, ...), custom_call_target="tpu_custom_call" | custom-call | tf_op jit(solution)/shard_map/prepare/pallas_call | solution.py:1008
  8.5 0.0 collective-permute-done.first
  8.5 0.5 %collective-permute-done.1.second = f32[11,8,128]{2,1,0:T(8,128)S(1)} collective-permute-done((f32[11,8,128]{2,1,0:T(8,128)S(1)}, f32[11,8,128]{2,1,0:T(8,128)S(1)}, u32[]{:S(2)}, u32[]{:S(2)}) %collective-permute-start.1) | collective-permute-done | bytes 45088 | tf_op jit(solution)/shard_map/ppermute | solution.py:974
  9.0 0.7 %start.1 = (f32[16,16,128]{2,1,0:T(8,128)S(1)}, f32[16,16,256]{2,1,0:T(8,128)S(1)}, f32[3,2,16,256]{3,2,1,0:T(8,128)S(1)}, f32[3,16,384]{2,1,0:T(8,128)S(1)}, f3...) custom-call(f32[16,16,128]{2,1,0:T(8,128)S(1)} %get-tuple-element.46.source, ...), custom_call_target="tpu_custom_call" | custom-call | tf_op jit(solution)/shard_map/start/pallas_call | solution.py:1019
  9.7 1.6 %collective-permute-start.3 = (f32[112,128]{1,0:T(8,128)S(1)}, f32[112,128]{1,0:T(8,128)S(1)}, u32[]{:S(2)}, u32[]{:S(2)}) collective-permute-start(f32[112,128]{1,0:T(8,128)S(1)} %get-tuple-element.74), channel_id=1, source_target_pairs={{0,16},{8,24},{16,0},{24,8},{1,17},{9,25},{17,1},{25,9},{2,18},{10... | collective-permute-start | bytes 172040 | tf_op jit(solution)/shard_map/ppermute | solution.py:981
  11.3 0.7 %guess.1 = (f32[16,16,128]{2,1,0:T(8,128)S(1)}, f32[8,16,384]{2,1,0:T(8,128)S(1)}, f32[8,16,384]{2,1,0:T(8,128)S(1)}, f32[112,128]{1,0:T(8,128)S(1)}, f32[112,128]{1,0:T(8,128)S(1)}) custom-call(f32[16,16,256]{2,1,0:T(8,128)S(1)} %get-tuple-element.58.remainder, f32[16,256]{1,0:T(8,128)S(1)} %get-tuple-element.59.metrics, ...), custom_call_target="tpu_custom_call" | custom-call | flops 4000000000 | bytes 4000000 | tf_op jit(solution)/shard_map/guess/pallas_call | solution.py:1029
  12.0 1.5 %collective-permute-start.4 = (f32[112,128]{1,0:T(8,128)S(1)}, f32[112,128]{1,0:T(8,128)S(1)}, u32[]{:S(2)}, u32[]{:S(2)}) collective-permute-start(f32[112,128]{1,0:T(8,128)S(1)} %get-tuple-element.75), channel_id=1, source_target_pairs={{0,8},{8,0},{16,24},{24,16},{1,9},{9,1},{17,25},{25,17},{2,10},{10... | collective-permute-start | bytes 172040 | tf_op jit(solution)/shard_map/ppermute | solution.py:973
  13.5 0.5 %collective-permute-start.2 = (f32[112,128]{1,0:T(8,128)S(1)}, f32[112,128]{1,0:T(8,128)S(1)}, u32[]{:S(2)}, u32[]{:S(2)}) collective-permute-start(f32[112,128]{1,0:T(8,128)S(1)} %get-tuple-element.73), channel_id=1, source_target_pairs={{8,16},{24,0},{16,8},{0,24},{9,17},{25,1},{17,9},{1,25},{10,18},{2... | collective-permute-start | bytes 172040 | tf_op jit(solution)/shard_map/ppermute | solution.py:974
  13.9 0.3 ready.1
  14.2 0.0 collective-permute-done.3.beyond
  14.2 1.9 %collective-permute-done.4.got = f32[112,128]{1,0:T(8,128)S(1)} collective-permute-done((f32[112,128]{1,0:T(8,128)S(1)}, f32[112,128]{1,0:T(8,128)S(1)}, u32[]{:S(2)}, u32[]{:S(2)}) %collective-permute-start.4) | collective-permute-done | bytes 57376 | tf_op jit(solution)/shard_map/ppermute | solution.py:973
  16.1 0.6 %side.1 = (f32[16,128]{1,0:T(8,128)S(1)}, f32[2,16,128]{2,1,0:T(8,128)S(1)}, f32[2,16,256]{2,1,0:T(8,128)S(1)}, f32[2,16,256]{2,1,0:T(8,128)S(1)}, f32[3,16,256]{2,1,0:T(8,128)S(1)}) custom-call(f32[2,16,256]{2,1,0:T(8,128)S(1)} %get-tuple-element.72.halves, f32[16,16,256]{2,1,0:T(8,128)S(1)} %get-tuple-element.58.remainder, ...), custom_call_target="tpu_custom_call" | custom-call | tf_op jit(solution)/shard_map/side/pallas_call | solution.py:1039
  16.8 1.8 %collective-permute-done.2.got = f32[112,128]{1,0:T(8,128)S(1)} collective-permute-done((f32[112,128]{1,0:T(8,128)S(1)}, f32[112,128]{1,0:T(8,128)S(1)}, u32[]{:S(2)}, u32[]{:S(2)}) %collective-permute-start.2) | collective-permute-done | bytes 57376 | tf_op jit(solution)/shard_map/ppermute | solution.py:974
  18.5 1.7 %middle.1 = (f32[2,16,128]{2,1,0:T(8,128)S(1)}, f32[16,16,128]{2,1,0:T(8,128)S(1)}, f32[16,16,256]{2,1,0:T(8,128)S(1)}, f32[2,3,16,256]{3,2,1,0:T(8,128)S(1)}, f...) custom-call(f32[16,16,128]{2,1,0:T(8,128)S(1)} %get-tuple-element.64.known, ...), custom_call_target="tpu_custom_call" | custom-call | tf_op jit(solution)/shard_map/middle/pallas_call | solution.py:1042
  20.2 9.7 %all_to_all.5 = f32[32,2,128]{2,1,0:T(2,128)S(1)} all-to-all(f32[32,2,128]{2,1,0:T(2,128)S(1)} %bitcast.4), channel_id=1, replica_groups=mesh['gx'=4,'gz'=8] {'gx','gz'}, dimensions={0} | all-to-all | bytes 65536 | tf_op jit(solution)/shard_map/all_to_all | solution.py:1052
  29.9 1.3 %finish.1 = (f32[16,16,128]{2,1,0:T(8,128)}, f32[16,16,128]{2,1,0:T(8,128)}) custom-call(f32[16,16,128]{2,1,0:T(8,128)S(1)} %get-tuple-element.57.refs_0_, f32[2,16,128]{2,1,0:T(8,128)S(1)} %get-tuple-element.81.refs_1_, f32[16,16,128]{2,1,0:T(8,128)S(1)} %get-tuple-element.82.refs_2_, f32[16,16,256]{2,1,0:T(8,128)S(1)} %get-tuple-element.83.refs_3_, ...), custom_call_target="tpu_custom_call" | custom-call | tf_op jit(solution)/shard_map/finish/pallas_call | solution.py:1076
  (3 shorter events, 0.0 us)
Async XLA Ops:
  0.6 6.5 %copy-start = (s32[8,2,2,16]{3,2,1,0:T(2,128)S(1)}, s32[8,2,2,16]{3,2,1,0:T(2,128)}, u32[]{:S(2)}) copy-start(s32[8,2,2,16]{3,2,1,0:T(2,128)} %labels.1) | copy-start | bytes 6148
  0.6 6.5 %copy-start.1 = (f32[3,8,128]{2,1,0:T(8,128)S(1)}, f32[3,8,128]{2,1,0:T(8,128)}, u32[]{:S(2)}) copy-start(f32[3,8,128]{2,1,0:T(8,128)} %constant.2.clone.tables) | copy-start | bytes 36868
  1.9 5.3 %copy-start.3 = (f32[8,8]{1,0:T(8,128)S(1)}, f32[8,8]{1,0:T(8,128)}, u32[]{:S(2)}) copy-start(f32[8,8]{1,0:T(8,128)} %vectors.1) | copy-start | bytes 772
  1.9 5.3 %copy-start.2 = (f32[8,8]{1,0:T(8,128)S(1)}, f32[8,8]{1,0:T(8,128)}, u32[]{:S(2)}) copy-start(f32[8,8]{1,0:T(8,128)} %stiffness.1) | copy-start | bytes 772
  1.9 6.5 %collective-permute-start = (f32[11,8,128]{2,1,0:T(8,128)S(1)}, f32[11,8,128]{2,1,0:T(8,128)S(1)}, u32[]{:S(2)}, u32[]{:S(2)}) collective-permute-start(f32[11,8,128]{2,1,0:T(8,128)S(1)} %get-tuple-element.49), channel_id=1, source_target_pairs={{0,1},{1,0},{2,3},{3,2},{4,5},{5,4},{6,7},{7,6},{8,9},{9,8},{10,11... | collective-permute-start | bytes 135176 | tf_op jit(solution)/shard_map/ppermute | solution.py:973
  2.4 6.5 %collective-permute-start.1 = (f32[11,8,128]{2,1,0:T(8,128)S(1)}, f32[11,8,128]{2,1,0:T(8,128)S(1)}, u32[]{:S(2)}, u32[]{:S(2)}) collective-permute-start(f32[11,8,128]{2,1,0:T(8,128)S(1)} %get-tuple-element.50), channel_id=1, source_target_pairs={{1,2},{3,4},{5,6},{7,0},{2,1},{4,3},{6,5},{0,7},{9,10},{11,12},{13... | collective-permute-start | bytes 135176 | tf_op jit(solution)/shard_map/ppermute | solution.py:974
  9.7 4.5 %collective-permute-start.3 = (f32[112,128]{1,0:T(8,128)S(1)}, f32[112,128]{1,0:T(8,128)S(1)}, u32[]{:S(2)}, u32[]{:S(2)}) collective-permute-start(f32[112,128]{1,0:T(8,128)S(1)} %get-tuple-element.74), channel_id=1, source_target_pairs={{0,16},{8,24},{16,0},{24,8},{1,17},{9,25},{17,1},{25,9},{2,18},{10... | collective-permute-start | bytes 172040 | tf_op jit(solution)/shard_map/ppermute | solution.py:981
  12.0 4.2 %collective-permute-start.4 = (f32[112,128]{1,0:T(8,128)S(1)}, f32[112,128]{1,0:T(8,128)S(1)}, u32[]{:S(2)}, u32[]{:S(2)}) collective-permute-start(f32[112,128]{1,0:T(8,128)S(1)} %get-tuple-element.75), channel_id=1, source_target_pairs={{0,8},{8,0},{16,24},{24,16},{1,9},{9,1},{17,25},{25,17},{2,10},{10... | collective-permute-start | bytes 172040 | tf_op jit(solution)/shard_map/ppermute | solution.py:973
  13.5 5.1 %collective-permute-start.2 = (f32[112,128]{1,0:T(8,128)S(1)}, f32[112,128]{1,0:T(8,128)S(1)}, u32[]{:S(2)}, u32[]{:S(2)}) collective-permute-start(f32[112,128]{1,0:T(8,128)S(1)} %get-tuple-element.73), channel_id=1, source_target_pairs={{8,16},{24,0},{16,8},{0,24},{9,17},{25,1},{17,9},{1,25},{10,18},{2... | collective-permute-start | bytes 172040 | tf_op jit(solution)/shard_map/ppermute | solution.py:974

commit v13 on v12

--- a/solution.py
+++ b/solution.py
@@ -290,12 +290,14 @@
     first, second, elements, near_source, near_previous, near_eigen, near_coarse, raw, ready,
 ):
     copies = [
-        pltpu.make_async_copy(source, near_source, ready.at[0]),
-        pltpu.make_async_copy(previous, near_previous, ready.at[1]),
         pltpu.make_async_copy(coefficients, raw, ready.at[2]),
         pltpu.make_async_copy(eigen, near_eigen, ready.at[3]),
         pltpu.make_async_copy(coarse, near_coarse, ready.at[4]),
     ]
+    for k in range(4):
+        part = pl.ds(4 * k, 4)
+        copies.append(pltpu.make_async_copy(source.at[part], near_source.at[part], ready.at[5 + k]))
+        copies.append(pltpu.make_async_copy(previous.at[part], near_previous.at[part], ready.at[9 + k]))
     for copy in copies:
         copy.start()
     even = even_index("gz")
@@ -1002,7 +1004,7 @@
         [halo, halo, face, block, block, (1, 8), coarse.shape],
         [FAR] * 5,
         "pack",
-        [pltpu.VMEM(coefficients.shape, jnp.float32), pltpu.SemaphoreType.DMA((5,))],
+        [pltpu.VMEM(coefficients.shape, jnp.float32), pltpu.SemaphoreType.DMA((13,))],
     )(*(pltpu.with_memory_space_constraint(v, pltpu.HBM) for v in operands))
     first, second = swap(first, second, "gz")
     upper, lower, diagonals, stiff, vectors, bend, lam, lines, fixed, tables = call(

time: 31.4 us -> 31.4 us (level)
  no operation moved by 1% of the time
where the time goes in v13:
time: 31.4 us; the launch traced here: 31.2 us
  blocking collectives  9.72 us (31%)
  starting transfers between devices  8.77 us (28%)
  Pallas kernels  7.8 us (25%)
  waiting for transfers between devices  4.2 us (13%)
  between operations  0.72 us (2%)
    all_to_all x1, blocking collectives, body(): lax.all_to_all(payload.reshape(devices, 2, LANES), ('gx', 'gz'), 0, 0)  9.72 us
    ppermute x2, starting transfers between devices, swap(): two = lax.ppermute(second, axis, odd + [(b, a) for a, b in odd])  5.19 us
    ppermute x2, waiting for transfers between devices, swap(): two = lax.ppermute(second, axis, odd + [(b, a) for a, b in odd])  2.29 us
    ppermute x2, starting transfers between devices, swap(): one = lax.ppermute(first, axis, [(i, i ^ 1) for i in range(size)])  2.02 us
    ppermute x2, waiting for transfers between devices, swap(): one = lax.ppermute(first, axis, [(i, i ^ 1) for i in range(size)])  1.91 us
    pallas_call x1, Pallas kernels, body(): call(middle_kernel, [(2, ROWS, LANES), block, wide, (2, 3, ROWS, WIDE), b...  1.66 us
    ppermute x1, starting transfers between devices, second_neighbours(): return lax.ppermute(common, axis, [(i, i ^ 2) for i in range(size)])  1.56 us
    pallas_call x1, Pallas kernels, body(): call(kernel, [block, block], [VMEM] * len(operands), 'finish', scratch)  1.3 us
  transfers between devices with their start and end apart: 5, of which 3 were waited for; matrix products, arithmetic and copies ran while one was open for 0% of the time, Pallas kernels for 9%

profile of v13, /device:TPU:0, one launch (start us, length us, event | category | flops | bytes accessed | tf_op | source)
XLA Modules:
  0.0 31.2 jit_solution(12413314456884117293)
XLA Ops:
  0.6 0.0 copy-start
  0.6 0.0 copy-start.1
  0.7 1.3 %pack.1 = (f32[11,8,128]{2,1,0:T(8,128)S(1)}, f32[11,8,128]{2,1,0:T(8,128)S(1)}, f32[16,128]{1,0:T(8,128)S(1)}, f32[16,16,128]{2,1,0:T(8,128)S(1)}, f32[16,16,12...) custom-call(f32[16,16,128]{2,1,0:T(8,128)} %source.1, f32[16,16,128]{2,1,0:T(8,128)} %previous.1, ...), custom_call_target="tpu_custom_call" | custom-call | tf_op jit(solution)/shard_map/pack/pallas_call | solution.py:1002
  1.9 0.0 copy-start.3
  1.9 0.0 copy-start.2
  1.9 0.5 %collective-permute-start = (f32[11,8,128]{2,1,0:T(8,128)S(1)}, f32[11,8,128]{2,1,0:T(8,128)S(1)}, u32[]{:S(2)}, u32[]{:S(2)}) collective-permute-start(f32[11,8,128]{2,1,0:T(8,128)S(1)} %get-tuple-element.49), channel_id=1, source_target_pairs={{0,1},{1,0},{2,3},{3,2},{4,5},{5,4},{6,7},{7,6},{8,9},{9,8},{10,11... | collective-permute-start | bytes 135176 | tf_op jit(solution)/shard_map/ppermute | solution.py:975
  2.5 4.7 %collective-permute-start.1 = (f32[11,8,128]{2,1,0:T(8,128)S(1)}, f32[11,8,128]{2,1,0:T(8,128)S(1)}, u32[]{:S(2)}, u32[]{:S(2)}) collective-permute-start(f32[11,8,128]{2,1,0:T(8,128)S(1)} %get-tuple-element.50), channel_id=1, source_target_pairs={{1,2},{3,4},{5,6},{7,0},{2,1},{4,3},{6,5},{0,7},{9,10},{11,12},{13... | collective-permute-start | bytes 135176 | tf_op jit(solution)/shard_map/ppermute | solution.py:976
  7.2 0.0 copy-done
  7.2 1.3 %prepare.1 = (bf16[4,256,256]{2,1,0:T(8,128)(2,1)S(1)}, bf16[4,256,128]{2,1,0:T(8,128)(2,1)S(1)}, f32[3,8,8,128]{3,2,1,0:T(8,128)S(1)}, f32[64,128]{1,0:T(8,128)...) custom-call(f32[16,128]{1,0:T(8,128)S(1)} %get-tuple-element.48.elem, ...), custom_call_target="tpu_custom_call" | custom-call | tf_op jit(solution)/shard_map/prepare/pallas_call | solution.py:1010
  8.5 0.0 collective-permute-done.first
  8.5 0.5 %collective-permute-done.1.second = f32[11,8,128]{2,1,0:T(8,128)S(1)} collective-permute-done((f32[11,8,128]{2,1,0:T(8,128)S(1)}, f32[11,8,128]{2,1,0:T(8,128)S(1)}, u32[]{:S(2)}, u32[]{:S(2)}) %collective-permute-start.1) | collective-permute-done | bytes 45088 | tf_op jit(solution)/shard_map/ppermute | solution.py:976
  9.0 0.7 %start.1 = (f32[16,16,128]{2,1,0:T(8,128)S(1)}, f32[16,16,256]{2,1,0:T(8,128)S(1)}, f32[3,2,16,256]{3,2,1,0:T(8,128)S(1)}, f32[3,16,384]{2,1,0:T(8,128)S(1)}, f3...) custom-call(f32[16,16,128]{2,1,0:T(8,128)S(1)} %get-tuple-element.46.source, ...), custom_call_target="tpu_custom_call" | custom-call | tf_op jit(solution)/shard_map/start/pallas_call | solution.py:1021
  9.7 1.6 %collective-permute-start.3 = (f32[112,128]{1,0:T(8,128)S(1)}, f32[112,128]{1,0:T(8,128)S(1)}, u32[]{:S(2)}, u32[]{:S(2)}) collective-permute-start(f32[112,128]{1,0:T(8,128)S(1)} %get-tuple-element.74), channel_id=1, source_target_pairs={{0,16},{8,24},{16,0},{24,8},{1,17},{9,25},{17,1},{25,9},{2,18},{10... | collective-permute-start | bytes 172040 | tf_op jit(solution)/shard_map/ppermute | solution.py:983
  11.3 0.7 %guess.1 = (f32[16,16,128]{2,1,0:T(8,128)S(1)}, f32[8,16,384]{2,1,0:T(8,128)S(1)}, f32[8,16,384]{2,1,0:T(8,128)S(1)}, f32[112,128]{1,0:T(8,128)S(1)}, f32[112,128]{1,0:T(8,128)S(1)}) custom-call(f32[16,16,256]{2,1,0:T(8,128)S(1)} %get-tuple-element.58.remainder, f32[16,256]{1,0:T(8,128)S(1)} %get-tuple-element.59.metrics, ...), custom_call_target="tpu_custom_call" | custom-call | flops 4000000000 | bytes 4000000 | tf_op jit(solution)/shard_map/guess/pallas_call | solution.py:1031
  12.0 1.5 %collective-permute-start.4 = (f32[112,128]{1,0:T(8,128)S(1)}, f32[112,128]{1,0:T(8,128)S(1)}, u32[]{:S(2)}, u32[]{:S(2)}) collective-permute-start(f32[112,128]{1,0:T(8,128)S(1)} %get-tuple-element.75), channel_id=1, source_target_pairs={{0,8},{8,0},{16,24},{24,16},{1,9},{9,1},{17,25},{25,17},{2,10},{10... | collective-permute-start | bytes 172040 | tf_op jit(solution)/shard_map/ppermute | solution.py:975
  13.5 0.5 %collective-permute-start.2 = (f32[112,128]{1,0:T(8,128)S(1)}, f32[112,128]{1,0:T(8,128)S(1)}, u32[]{:S(2)}, u32[]{:S(2)}) collective-permute-start(f32[112,128]{1,0:T(8,128)S(1)} %get-tuple-element.73), channel_id=1, source_target_pairs={{8,16},{24,0},{16,8},{0,24},{9,17},{25,1},{17,9},{1,25},{10,18},{2... | collective-permute-start | bytes 172040 | tf_op jit(solution)/shard_map/ppermute | solution.py:976
  13.9 0.3 ready.1
  14.3 0.0 collective-permute-done.3.beyond
  14.3 1.9 %collective-permute-done.4.got = f32[112,128]{1,0:T(8,128)S(1)} collective-permute-done((f32[112,128]{1,0:T(8,128)S(1)}, f32[112,128]{1,0:T(8,128)S(1)}, u32[]{:S(2)}, u32[]{:S(2)}) %collective-permute-start.4) | collective-permute-done | bytes 57376 | tf_op jit(solution)/shard_map/ppermute | solution.py:975
  16.2 0.6 %side.1 = (f32[16,128]{1,0:T(8,128)S(1)}, f32[2,16,128]{2,1,0:T(8,128)S(1)}, f32[2,16,256]{2,1,0:T(8,128)S(1)}, f32[2,16,256]{2,1,0:T(8,128)S(1)}, f32[3,16,256]{2,1,0:T(8,128)S(1)}) custom-call(f32[2,16,256]{2,1,0:T(8,128)S(1)} %get-tuple-element.72.halves, f32[16,16,256]{2,1,0:T(8,128)S(1)} %get-tuple-element.58.remainder, ...), custom_call_target="tpu_custom_call" | custom-call | tf_op jit(solution)/shard_map/side/pallas_call | solution.py:1041
  16.8 1.8 %collective-permute-done.2.got = f32[112,128]{1,0:T(8,128)S(1)} collective-permute-done((f32[112,128]{1,0:T(8,128)S(1)}, f32[112,128]{1,0:T(8,128)S(1)}, u32[]{:S(2)}, u32[]{:S(2)}) %collective-permute-start.2) | collective-permute-done | bytes 57376 | tf_op jit(solution)/shard_map/ppermute | solution.py:976
  18.5 1.7 %middle.1 = (f32[2,16,128]{2,1,0:T(8,128)S(1)}, f32[16,16,128]{2,1,0:T(8,128)S(1)}, f32[16,16,256]{2,1,0:T(8,128)S(1)}, f32[2,3,16,256]{3,2,1,0:T(8,128)S(1)}, f...) custom-call(f32[16,16,128]{2,1,0:T(8,128)S(1)} %get-tuple-element.64.known, ...), custom_call_target="tpu_custom_call" | custom-call | tf_op jit(solution)/shard_map/middle/pallas_call | solution.py:1044
  20.2 9.7 %all_to_all.5 = f32[32,2,128]{2,1,0:T(2,128)S(1)} all-to-all(f32[32,2,128]{2,1,0:T(2,128)S(1)} %bitcast.4), channel_id=1, replica_groups=mesh['gx'=4,'gz'=8] {'gx','gz'}, dimensions={0} | all-to-all | bytes 65536 | tf_op jit(solution)/shard_map/all_to_all | solution.py:1054
  29.9 1.3 %finish.1 = (f32[16,16,128]{2,1,0:T(8,128)}, f32[16,16,128]{2,1,0:T(8,128)}) custom-call(f32[16,16,128]{2,1,0:T(8,128)S(1)} %get-tuple-element.57.refs_0_, f32[2,16,128]{2,1,0:T(8,128)S(1)} %get-tuple-element.81.refs_1_, f32[16,16,128]{2,1,0:T(8,128)S(1)} %get-tuple-element.82.refs_2_, f32[16,16,256]{2,1,0:T(8,128)S(1)} %get-tuple-element.83.refs_3_, ...), custom_call_target="tpu_custom_call" | custom-call | tf_op jit(solution)/shard_map/finish/pallas_call | solution.py:1078
  (3 shorter events, 0.0 us)
Async XLA Ops:
  0.6 6.5 %copy-start = (s32[8,2,2,16]{3,2,1,0:T(2,128)S(1)}, s32[8,2,2,16]{3,2,1,0:T(2,128)}, u32[]{:S(2)}) copy-start(s32[8,2,2,16]{3,2,1,0:T(2,128)} %labels.1) | copy-start | bytes 6148
  0.6 6.5 %copy-start.1 = (f32[3,8,128]{2,1,0:T(8,128)S(1)}, f32[3,8,128]{2,1,0:T(8,128)}, u32[]{:S(2)}) copy-start(f32[3,8,128]{2,1,0:T(8,128)} %constant.2.clone.tables) | copy-start | bytes 36868
  1.9 5.3 %copy-start.3 = (f32[8,8]{1,0:T(8,128)S(1)}, f32[8,8]{1,0:T(8,128)}, u32[]{:S(2)}) copy-start(f32[8,8]{1,0:T(8,128)} %vectors.1) | copy-start | bytes 772
  1.9 5.3 %copy-start.2 = (f32[8,8]{1,0:T(8,128)S(1)}, f32[8,8]{1,0:T(8,128)}, u32[]{:S(2)}) copy-start(f32[8,8]{1,0:T(8,128)} %stiffness.1) | copy-start | bytes 772
  1.9 6.5 %collective-permute-start = (f32[11,8,128]{2,1,0:T(8,128)S(1)}, f32[11,8,128]{2,1,0:T(8,128)S(1)}, u32[]{:S(2)}, u32[]{:S(2)}) collective-permute-start(f32[11,8,128]{2,1,0:T(8,128)S(1)} %get-tuple-element.49), channel_id=1, source_target_pairs={{0,1},{1,0},{2,3},{3,2},{4,5},{5,4},{6,7},{7,6},{8,9},{9,8},{10,11... | collective-permute-start | bytes 135176 | tf_op jit(solution)/shard_map/ppermute | solution.py:975
  2.5 6.5 %collective-permute-start.1 = (f32[11,8,128]{2,1,0:T(8,128)S(1)}, f32[11,8,128]{2,1,0:T(8,128)S(1)}, u32[]{:S(2)}, u32[]{:S(2)}) collective-permute-start(f32[11,8,128]{2,1,0:T(8,128)S(1)} %get-tuple-element.50), channel_id=1, source_target_pairs={{1,2},{3,4},{5,6},{7,0},{2,1},{4,3},{6,5},{0,7},{9,10},{11,12},{13... | collective-permute-start | bytes 135176 | tf_op jit(solution)/shard_map/ppermute | solution.py:976
  9.7 4.5 %collective-permute-start.3 = (f32[112,128]{1,0:T(8,128)S(1)}, f32[112,128]{1,0:T(8,128)S(1)}, u32[]{:S(2)}, u32[]{:S(2)}) collective-permute-start(f32[112,128]{1,0:T(8,128)S(1)} %get-tuple-element.74), channel_id=1, source_target_pairs={{0,16},{8,24},{16,0},{24,8},{1,17},{9,25},{17,1},{25,9},{2,18},{10... | collective-permute-start | bytes 172040 | tf_op jit(solution)/shard_map/ppermute | solution.py:983
  12.0 4.2 %collective-permute-start.4 = (f32[112,128]{1,0:T(8,128)S(1)}, f32[112,128]{1,0:T(8,128)S(1)}, u32[]{:S(2)}, u32[]{:S(2)}) collective-permute-start(f32[112,128]{1,0:T(8,128)S(1)} %get-tuple-element.75), channel_id=1, source_target_pairs={{0,8},{8,0},{16,24},{24,16},{1,9},{9,1},{17,25},{25,17},{2,10},{10... | collective-permute-start | bytes 172040 | tf_op jit(solution)/shard_map/ppermute | solution.py:975
  13.5 5.1 %collective-permute-start.2 = (f32[112,128]{1,0:T(8,128)S(1)}, f32[112,128]{1,0:T(8,128)S(1)}, u32[]{:S(2)}, u32[]{:S(2)}) collective-permute-start(f32[112,128]{1,0:T(8,128)S(1)} %get-tuple-element.73), channel_id=1, source_target_pairs={{8,16},{24,0},{16,8},{0,24},{9,17},{25,1},{17,9},{1,25},{10,18},{2... | collective-permute-start | bytes 172040 | tf_op jit(solution)/shard_map/ppermute | solution.py:976
